TPU v7x, 32 devices: a whole 2x2x4 slice. The times are simulated.
32 devices in a mesh: dp: 4 (over x, core), fsdp: 8 (over z, y).
Axes of the slice: x: 2, y: 2, z: 4, core: 2. Of those that a mesh axis runs over, the one named last changes fastest.
Arguments:
- query_key_value: bfloat16 [3, 14336, 1664], P(None, ('dp', 'fsdp')), may hold values from -60 to 60
- cotangent: bfloat16 [14336, 3200], P(('dp', 'fsdp')), may hold values from -6 to 6
- proj_weight: bfloat16 [1664, 3200], P('fsdp'), may hold values from -0.15625 to 0.15625
- layer_scale: float32 [3200], replicated, may hold values from 0.3 to 3
- lengths: int32 [4, 8, 4], P(None, 'fsdp'), may hold values from 0 to 192, as said below
Outputs:
- grad_qkv: bfloat16 [3, 14336, 1664], P(None, ('dp', 'fsdp'))
- grad_proj: float32 [1664, 3200], P('fsdp', 'dp')
Inputs may be any that keep to these rules, and one draw needn't show every extreme that they name: lengths[a, b, 0] + lengths[a, b, 1] = 256, each at least 64; lengths[a, b, 2] and lengths[a, b, 3] are both 0 or both from 64 to 96; of the devices a and a + 4 / 2 (a < 2) of one fsdp index exactly one has them nonzero; in every fsdp index the nonzero one of the pair a = 0 has lengths[., b, 3] = 96.
All inputs are finite; a program needn't handle non-finite values.
Results may differ from a plain program's by a relative error of at most 0.011.
Values may be sent and summed in bfloat16 or wider, within the bound.
No kernel may reach another device: no remote copies, remote signals or barrier semaphores. Data moves between devices by JAX's collectives and lax.ppermute only.
A program may use at most 128 MiB of HBM per device.

v0:
```python
import jax
import jax.numpy as jnp
from jax import lax
from jax.sharding import PartitionSpec as P

HS = 128
MAIN = 256
SLOT = 96


def slot_ids(count, label):
    slot_pos = jnp.arange(SLOT, dtype=jnp.int32)
    return jnp.where(slot_pos < count, label, -1).astype(jnp.int32)


def attend(query_rows, key_rows, value_rows, grad_rows, segment):
    rows = query_rows.shape[0]
    width = query_rows.shape[1]
    heads = width // HS
    factor = HS ** (-0.5)
    query_h = query_rows.reshape(rows, heads, HS)
    key_h = key_rows.reshape(rows, heads, HS)
    value_h = value_rows.reshape(rows, heads, HS)
    grad_h = grad_rows.reshape(rows, heads, HS)
    scores = jnp.einsum("qhd,khd->hqk", query_h, key_h, preferred_element_type=jnp.float32) * factor
    valid = segment >= 0
    allowed = (segment[:, None] == segment[None, :]) & valid[:, None]
    scores = jnp.where(allowed[None], scores, -1e30)
    highest = jnp.max(scores, axis=2, keepdims=True)
    weights = jnp.exp(scores - highest)
    probs = weights / jnp.sum(weights, axis=2, keepdims=True)
    probs = jnp.where(valid[None, :, None], probs, jnp.zeros_like(probs))
    probs_b = probs.astype(jnp.bfloat16)
    attended = jnp.einsum("hqk,khd->qhd", probs_b, value_h, preferred_element_type=jnp.float32)
    attended = attended.reshape(rows, width).astype(jnp.bfloat16)
    dprob = jnp.einsum("qhd,khd->hqk", grad_h, value_h, preferred_element_type=jnp.float32)
    delta = jnp.sum(probs * dprob, axis=2, keepdims=True)
    dscore = (probs * (dprob - delta) * factor).astype(jnp.bfloat16)
    grad_query = jnp.einsum("hqk,khd->qhd", dscore, key_h, preferred_element_type=jnp.float32)
    grad_key = jnp.einsum("hqk,qhd->khd", dscore, query_h, preferred_element_type=jnp.float32)
    grad_value = jnp.einsum("hqk,qhd->khd", probs_b, grad_h, preferred_element_type=jnp.float32)
    return (
        attended,
        grad_query.reshape(rows, width).astype(jnp.bfloat16),
        grad_key.reshape(rows, width).astype(jnp.bfloat16),
        grad_value.reshape(rows, width).astype(jnp.bfloat16),
    )


def local(query_key_value, cotangent, proj_weight, layer_scale, lengths):
    member = lax.axis_index("dp")
    table = lengths[:, 0, :]
    counts = lax.dynamic_index_in_dim(table, member, 0, keepdims=False)
    scaled = (cotangent.astype(jnp.float32) * layer_scale[None, :]).astype(jnp.bfloat16)
    grad_out = lax.dot_general(
        scaled,
        lax.all_gather(proj_weight, "fsdp", axis=0, tiled=True),
        (((1,), (1,)), ((), ())),
        preferred_element_type=jnp.float32,
    ).astype(jnp.bfloat16)
    stop_first = MAIN + SLOT
    main_pos = jnp.arange(MAIN, dtype=jnp.int32)
    main_seg = (main_pos >= counts[0]).astype(jnp.int32)
    main_res = attend(
        query_key_value[0][:MAIN],
        query_key_value[1][:MAIN],
        query_key_value[2][:MAIN],
        grad_out[:MAIN],
        main_seg,
    )
    first_res = attend(
        query_key_value[0][MAIN:stop_first],
        query_key_value[1][MAIN:stop_first],
        query_key_value[2][MAIN:stop_first],
        grad_out[MAIN:stop_first],
        slot_ids(counts[2], 2),
    )
    second_res = attend(
        query_key_value[0][stop_first:],
        query_key_value[1][stop_first:],
        query_key_value[2][stop_first:],
        grad_out[stop_first:],
        slot_ids(counts[3], 3),
    )
    joined = [
        jnp.concatenate([main_res[index], first_res[index], second_res[index]], axis=0)
        for index in range(4)
    ]
    attended = joined[0]
    partial_rows = lax.psum_scatter(
        lax.dot_general(
            attended, scaled, (((0,), (0,)), ((), ())), preferred_element_type=jnp.float32
        ),
        "fsdp",
        scatter_dimension=0,
        tiled=True,
    )
    grad_proj = lax.psum_scatter(partial_rows, "dp", scatter_dimension=1, tiled=True)
    return (jnp.stack([joined[1], joined[2], joined[3]]), grad_proj)


def solution(mesh):
    placed = (
        P(None, ("dp", "fsdp"), None),
        P(("dp", "fsdp"), None),
        P("fsdp", None),
        P(),
        P(None, "fsdp", None),
    )
    return jax.shard_map(
        local,
        mesh=mesh,
        in_specs=placed,
        out_specs=(P(None, ("dp", "fsdp"), None), P("fsdp", "dp")),
        check_vma=False,
    )
```

profile of v0, /device:TPU:0, one launch (start us, length us, event | category | flops | bytes accessed | tf_op | source)
XLA Modules:
  0.0 577.9 jit_solution(992279779710918498)
XLA Ops:
  7.2 0.7 all-gather.2.cloned.1.call-update
  8.0 1.6 fusion.113
  10.9 1.0 reshape.286
  11.9 0.6 fusion.114
  12.5 0.6 broadcast_compare_fusion.2
  13.2 0.6 compare_select_fusion.1
  14.2 1.1 fusion.116
  15.7 1.0 copy.129
  16.7 0.6 broadcast_compare_fusion.1
  17.3 0.7 compare_select_fusion
  18.1 1.4 fusion.40
  19.5 1.0 fusion.115
  20.9 1.0 copy.130
  21.9 2.1 fusion.112
  24.0 0.6 copy.137
  24.6 0.6 copy.136
  25.2 0.6 copy.135
  25.8 0.7 compare_convert_fusion
  26.6 3.1 fusion.117
  29.7 2.6 convolution_convert_fusion.1
  32.3 0.5 copy-done.23
  32.8 10.3 %fusion.10 = f32[1664,3200]{1,0:T(8,128)} fusion(bf16[448,3200]{1,0:T(8,128)(2,1)S(1)} %copy-done.23, f32[3200]{0:T(1024)S(1)} %copy-done.24, bf16[96,1664]{0,1:T(8,128)(2,1)S(1)} %bitcast.108, bf16[96,1664]{0,1:T(8,128)(2,1)S(1)} %bitcast.107, bf16[256,1664]{0,1:T(8,128)(2,1)S(1)} %bitcast.109), kind=kOutput, calls=%fused_computation.16 | convolution fusion | flops 4779794432 | bytes 25670144 | tf_op jit(solution)/shard_map/dot_general | solution.py:91
  43.4 122.4 %all-gather.2.cloned.1.call-done = bf16[1664,3200]{1,0:T(8,128)(2,1)} async-done(((bf16[208,3200]{1,0:T(8,128)(2,1)}), bf16[1664,3200]{1,0:T(8,128)(2,1)}) %all-gather.2.cloned.1.call-update) | async-done | bytes 10649616 | tf_op jit(solution)/shard_map/all_gather | solution.py:57
  165.8 11.2 %convolution_convert_fusion = bf16[448,1664]{1,0:T(8,128)(2,1)S(1)} fusion(bf16[1664,3200]{1,0:T(8,128)(2,1)} %all-gather.2.cloned.1.call-done, bf16[448,3200]{1,0:T(8,128)(2,1)} %param.6, f32[3200]{0:T(1024)S(1)} %copy-done.24), kind=kOutput, calls=%fused_computation.14 | convolution fusion | flops 4776067072 | bytes 15020544 | tf_op jit(solution)/shard_map/dot_general | solution.py:55
  177.0 1.2 copy-done.2
  178.2 0.6 copy.76
  178.8 335.9 %reduce-scatter.5.cloned.1.call-done = f32[208,3200]{1,0:T(8,128)} async-done(((f32[1664,3200]{1,0:T(8,128)}), f32[208,3200]{1,0:T(8,128)}) %reduce-scatter.5.cloned.1.call-update) | async-done | bytes 2662416 | tf_op jit(solution)/shard_map/reduce_scatter | solution.py:90
  514.7 3.6 copy.131
  518.3 3.6 convolution_convert_fusion.2
  521.9 1.6 copy.107
  523.5 2.6 fusion.118
  526.1 7.6 %fusion.30 = bf16[13,256,128]{1,2,0:T(8,128)(2,1)} fusion(bf16[256,13,128]{0,2,1:T(8,128)(2,1)S(1)} %bitcast.102, f32[13,256,256]{1,2,0:T(8,128)} %fusion.118, f32[13,256,256]{1,2,0:T(8,128)} %get-tuple-element.21, f32[13,256]{1,0:T(8,128)S(1)} %get-tuple-element.20, pred[256]{0:T(512)(128)(4,1)S(1)} %get-tuple-element.23), kind=kOutput, calls=%fused_computation.33 | convolution fusion | flops 226201088 | bytes 8533248 | tf_op jit(solution)/shard_map/hqk,qhd->khd/dot_general | solution.py:40
  533.7 1.5 copy.101
  535.3 7.4 %fusion.27 = bf16[13,256,128]{1,2,0:T(8,128)(2,1)} fusion(bf16[256,13,128]{0,2,1:T(8,128)(2,1)S(1)} %bitcast.100, f32[13,256,256]{1,2,0:T(8,128)} %fusion.118, f32[13,256,256]{1,2,0:T(8,128)} %get-tuple-element.21, f32[13,256]{1,0:T(8,128)S(1)} %get-tuple-element.20, pred[256]{0:T(512)(128)(4,1)S(1)} %get-tuple-element.23), kind=kOutput, calls=%fused_computation.32 | convolution fusion | flops 226201088 | bytes 8533248 | tf_op jit(solution)/shard_map/hqk,khd->qhd/dot_general | solution.py:39
  542.7 1.5 copy.95
  544.2 1.9 slice_bitcast_fusion.1
  546.1 1.2 fusion.69
  547.3 3.0 fusion.47
  550.3 1.2 fusion.66
  551.5 3.0 fusion.48
  554.5 2.3 fusion.53
  556.8 2.4 fusion.54
  559.2 2.2 fusion.49
  561.4 2.8 fusion.50
  564.3 1.2 copy_bitcast_fusion
  565.7 0.6 copy-done.20
  566.7 2.4 pad_maximum_fusion
  569.1 2.3 copy.132
  (71 shorter events, 3.6 us)
Async XLA Ops:
  7.2 4.8 copy-start
  7.2 158.6 %all-gather.2.cloned.1.call-start = ((), (), s32[]{:S(2)}) async-start(), calls=%async_computation.2 | async-start | bytes 11980800 | tf_op jit(solution)/shard_map/all_gather | solution.py:57
  7.9 506.8 %reduce-scatter.5.cloned.1.call-start = ((), (), s32[]{:S(2)}) async-start(), calls=%async_computation.3 | async-start | bytes 23961600 | tf_op jit(solution)/shard_map/reduce_scatter | solution.py:90
  9.8 5.8 %copy-start.3 = (bf16[96,13,128]{2,1,0:T(8,128)(2,1)}, bf16[96,13,128]{2,1,0:T(8,128)(2,1)S(1)}, u32[]{:S(2)}) copy-start(bf16[96,13,128]{2,1,0:T(8,128)(2,1)S(1)} %reshape.284) | copy-start | bytes 958468
  10.1 5.6 copy-start.19
  10.3 5.3 copy-start.18
  10.6 7.5 %copy-start.16 = (bf16[96,13,128]{2,1,0:T(8,128)(2,1)}, bf16[96,13,128]{2,1,0:T(8,128)(2,1)S(1)}, u32[]{:S(2)}) copy-start(bf16[96,13,128]{2,1,0:T(8,128)(2,1)S(1)} %reshape.285) | copy-start | bytes 958468
  10.9 9.6 %copy-start.5 = (bf16[96,13,128]{2,1,0:T(8,128)(2,1)}, bf16[96,13,128]{2,1,0:T(8,128)(2,1)S(1)}, u32[]{:S(2)}) copy-start(bf16[96,13,128]{2,1,0:T(8,128)(2,1)S(1)} %reshape.288) | copy-start | bytes 958468
  14.2 6.3 %copy-start.12 = (f32[13,96,96]{1,2,0:T(8,128)}, f32[13,96,96]{1,2,0:T(8,128)S(1)}, u32[]{:S(2)}) copy-start(f32[13,96,96]{1,2,0:T(8,128)S(1)} %fusion.39) | copy-start | bytes 1437700
  19.5 1.4 copy-start.13
  25.8 3.9 copy-start.10
  29.7 2.6 copy-start.14
  29.7 2.6 copy-start.15
  29.7 3.1 copy-start.23
  29.7 3.1 copy-start.24
  43.2 525.9 %reduce-scatter.7.cloned.1.call-start = ((), (), s32[]{:S(2)}) async-start(), calls=%async_computation.4 | async-start | bytes 4096000
  177.0 1.2 copy-start.2
  526.1 9.2 %copy-start.11 = (bf16[1,256,1664]{1,2,0:T(8,128)(2,1)S(1)}, bf16[1,256,1664]{1,2,0:T(8,128)(2,1)}, u32[]{:S(2)}) copy-start(bf16[1,256,1664]{1,2,0:T(8,128)(2,1)} %copy-done.10) | copy-start | bytes 2555908
  535.3 10.9 %copy-start.4 = (bf16[96,13,128]{2,1,0:T(8,128)(2,1)S(1)}, bf16[96,13,128]{2,1,0:T(8,128)(2,1)}, u32[]{:S(2)}) copy-start(bf16[96,13,128]{2,1,0:T(8,128)(2,1)} %copy-done.3) | copy-start | bytes 958468
  544.2 6.1 %copy-start.6 = (bf16[96,13,128]{2,1,0:T(8,128)(2,1)S(1)}, bf16[96,13,128]{2,1,0:T(8,128)(2,1)}, u32[]{:S(2)}) copy-start(bf16[96,13,128]{2,1,0:T(8,128)(2,1)} %copy-done.5) | copy-start | bytes 958468
  546.1 1.2 copy-start.8
  547.3 3.0 copy-start.7
  551.5 3.0 copy-start.9
  556.8 4.6 copy-start.17
  564.3 1.3 copy-start.22
  565.4 1.0 copy-start.20
  565.4 1.1 copy-start.21
  566.5 4.9 copy-start.1
Sparse Core Ops, SparseCore 0:
  10.2 155.5 all-gather.1
  169.4 345.2 reduce-scatter.4
  518.4 37.8 reduce-scatter.6
where the time goes:
time: 579 us; the launch traced here: 578 us
  waiting for transfers between devices  459 us (79%)
  matrix products  69 us (12%)
  local copies, waits for them, and re-layouts  27.2 us (5%)
  between operations  14.2 us (2%)
  other arithmetic  8.32 us (1%)
    reduce_scatter x1, waiting for transfers between devices, local(): lax.psum_scatter(lax.dot_general(attended, scaled, (((0,), (0,)), ((), ()...  336 us
    all_gather x1, waiting for transfers between devices, local(): lax.all_gather(proj_weight, 'fsdp', axis=0, tiled=True)  122 us
    dot_general x3, matrix products, attend(): jnp.einsum('hqk,khd->qhd', dscore, key_h, preferred_element_type=jnp.floa...  13.4 us
    dot_general x3, matrix products, attend(): jnp.einsum('hqk,qhd->khd', dscore, query_h, preferred_element_type=jnp.fl...  12.7 us
    unnamed x56, local copies, waits for them, and re-layouts  12.1 us
  transfers between devices with their start and end apart: 3, of which 2 were waited for; matrix products, arithmetic and copies ran while one was open for 17% of the time, Pallas kernels for 0%

commit v1 on v0

v1 whole, which is shorter than its diff:
```python
import functools

import jax
import jax.numpy as jnp
from jax import lax
from jax.experimental import pallas as pl
from jax.experimental.pallas import tpu as pltpu
from jax.sharding import PartitionSpec as P

HS = 128
MAIN = 256
SLOT = 96
LANE = 128
FACTOR = HS ** (-0.5)
VMEM_BYTES = 32 * 1024 * 1024
LONG = pl.CostEstimate(flops=10 ** 11, bytes_accessed=10 ** 8, transcendentals=0)
SHORT = pl.CostEstimate(flops=1000, bytes_accessed=1000, transcendentals=0)


def dot(left, right, left_dim, right_dim):
    return lax.dot_general(left, right, (((left_dim,), (right_dim,)), ((), ())), preferred_element_type=jnp.float32)


def prepare_kernel(steps, width, starts, cotangent, layer_scale, scaled, turned, *windows):
    block = cotangent.shape[1]
    values = cotangent[...].astype(jnp.float32) * layer_scale[...]
    at = pl.ds(pl.multiple_of(pl.program_id(0) * block, LANE), block)
    scaled[:, at] = values.astype(jnp.bfloat16)
    spare = jnp.zeros((turned.shape[1] - values.shape[0], block), jnp.float32)
    turned[...] = jnp.concatenate([values, spare], axis=0).T.astype(jnp.bfloat16)

    @pl.when(pl.program_id(0) == steps - 1)
    def _():
        for k, window in enumerate(windows):
            window[...] = scaled[:, pl.ds(pl.multiple_of(starts[k], LANE), width)]


def prepare(starts, cotangent, layer_scale, peers, width):
    rows, total = cotangent.shape
    lanes = -(-rows // LANE) * LANE
    steps = 5
    block = total // steps
    return pl.pallas_call(
        functools.partial(prepare_kernel, steps, width),
        grid_spec=pltpu.PrefetchScalarGridSpec(
            num_scalar_prefetch=1,
            grid=(steps,),
            in_specs=[
                pl.BlockSpec((rows, block), lambda i, s: (0, i)),
                pl.BlockSpec((1, block), lambda i, s: (0, i)),
            ],
            out_specs=[
                pl.BlockSpec((rows, total), lambda i, s: (0, 0)),
                pl.BlockSpec((block, lanes), lambda i, s: (i, 0)),
            ]
            + [pl.BlockSpec((rows, width), lambda i, s: (0, 0))] * peers,
        ),
        out_shape=[
            jax.ShapeDtypeStruct((rows, total), jnp.bfloat16),
            jax.ShapeDtypeStruct((total, lanes), jnp.bfloat16),
        ]
        + [jax.ShapeDtypeStruct((rows, width), jnp.bfloat16)] * peers,
        compiler_params=pltpu.CompilerParams(vmem_limit_bytes=VMEM_BYTES),
        cost_estimate=LONG,
        name="scaled_cotangent",
    )(starts, cotangent, layer_scale.reshape(1, total))


def arrange_kernel(sizes, order, attended, *refs):
    *outs, sems = refs
    copies = []
    for out, size in zip(outs, sizes):
        for j in range(size):
            n = len(copies)
            copies.append(pltpu.make_async_copy(attended.at[order[n]], out.at[j], sems.at[n]))
    for copy in copies:
        copy.start()
    for copy in copies:
        copy.wait()


def arrange(order, attended, sizes):
    _, depth, rows = attended.shape
    return pl.pallas_call(
        functools.partial(arrange_kernel, sizes),
        grid_spec=pltpu.PrefetchScalarGridSpec(
            num_scalar_prefetch=1,
            grid=(1,),
            in_specs=[pl.BlockSpec(memory_space=pl.ANY)],
            out_specs=[pl.BlockSpec(memory_space=pl.ANY)] * len(sizes),
            scratch_shapes=[pltpu.SemaphoreType.DMA((sum(sizes),))],
        ),
        out_shape=[jax.ShapeDtypeStruct((size, depth, rows), attended.dtype) for size in sizes],
        compiler_params=pltpu.CompilerParams(vmem_limit_bytes=VMEM_BYTES),
        cost_estimate=SHORT,
        name="attended_chunks",
    )(order, attended)


PAIR = 2
EXPONENT = FACTOR * 1.4426950408889634


def forward_kernel(counts, qkv, attended, main_probs, slot_probs):
    def marks(image, ids):
        lane = lax.broadcasted_iota(jnp.int32, (image.shape[0], HS), 1)
        first = jnp.where(image == ids[0], 1.0, 0.0)
        second = jnp.where(image == ids[1], 1.0, 0.0)
        own = jnp.where(lane == 0, first, jnp.where(lane == 1, second, 0.0))
        other = jnp.where(lane == 0, 1.0 - first, jnp.where(lane == 1, 1.0 - second, 0.0)) * -1e30
        return own.astype(jnp.bfloat16), other.astype(jnp.bfloat16)

    main_at = lax.broadcasted_iota(jnp.int32, (MAIN, HS), 0)
    main_marks = marks(jnp.where(main_at >= counts[0], 1, 0), (0, 1))

    def image(at):
        first = jnp.where(at < counts[2], 2, -1)
        return jnp.where(at < SLOT, first, jnp.where(at - SLOT < counts[3], 3, -1))

    slot_marks = marks(image(lax.broadcasted_iota(jnp.int32, (2 * SLOT, HS), 0)), (2, 3))
    valid = image(lax.broadcasted_iota(jnp.int32, (1, 2 * SLOT), 1)) >= 0
    parts = []
    for head in range(PAIR):
        lanes = slice(head * HS, (head + 1) * HS)
        parts.append((head, 0, MAIN, lanes, main_marks, None, main_probs))
        parts.append((head, MAIN, 2 * SLOT, lanes, slot_marks, valid, slot_probs))
    scores = []
    for head, first, rows, lanes, (mark_query, mark_key), _, _ in parts:
        query = jnp.concatenate([qkv[0, first:first + rows, lanes], mark_query], axis=1)
        key = jnp.concatenate([qkv[1, first:first + rows, lanes], mark_key], axis=1)
        scores.append(dot(key, query, 1, 1))
    probs = []
    for score, (_, _, _, _, _, good, _) in zip(scores, parts):
        weights = jnp.exp2((score - jnp.max(score, axis=0, keepdims=True)) * EXPONENT)
        scale = 1.0 / jnp.sum(weights, axis=0, keepdims=True)
        probs.append(weights * (scale if good is None else jnp.where(good, scale, 0.0)))
    for prob, (head, first, rows, lanes, _, _, probs_ref) in zip(probs, parts):
        probs_ref[head] = prob
        result = dot(qkv[2, first:first + rows, lanes], prob.astype(jnp.bfloat16), 0, 0)
        attended[lanes, first:first + rows] = result.astype(jnp.bfloat16)


def forward(counts, qkv):
    _, rows, width = qkv.shape
    heads = width // HS
    return pl.pallas_call(
        forward_kernel,
        grid_spec=pltpu.PrefetchScalarGridSpec(
            num_scalar_prefetch=1,
            grid=(-(-heads // PAIR),),
            in_specs=[pl.BlockSpec((3, rows, PAIR * HS), lambda h, c: (0, 0, h))],
            out_specs=[
                pl.BlockSpec((PAIR * HS, rows), lambda h, c: (h, 0)),
                pl.BlockSpec((PAIR, MAIN, MAIN), lambda h, c: (h, 0, 0)),
                pl.BlockSpec((PAIR, 2 * SLOT, 2 * SLOT), lambda h, c: (h, 0, 0)),
            ],
        ),
        out_shape=[
            jax.ShapeDtypeStruct((width, rows), jnp.bfloat16),
            jax.ShapeDtypeStruct((heads, MAIN, MAIN), jnp.float32),
            jax.ShapeDtypeStruct((heads, 2 * SLOT, 2 * SLOT), jnp.float32),
        ],
        compiler_params=pltpu.CompilerParams(vmem_limit_bytes=VMEM_BYTES),
        cost_estimate=LONG,
        name="attention_forward",
    )(counts, qkv)


def backward_kernel(qkv, grad_mine, grad_other, main_probs, slot_probs, *rest):
    grads = rest[-1]
    parts = []
    for head in range(PAIR):
        lanes = slice(head * HS, (head + 1) * HS)
        for first, rows, probs_ref in ((0, MAIN, main_probs), (MAIN, 2 * SLOT, slot_probs)):
            parts.append((head, slice(first, first + rows), lanes, probs_ref))
    grad, dprobs, dscores = [], [], []
    for head, at, lanes, _ in parts:
        both = grad_mine[lanes, at] + grad_other[lanes, at].astype(jnp.float32)
        grad.append(both.astype(jnp.bfloat16))
    for g, (head, at, lanes, _) in zip(grad, parts):
        dprobs.append(dot(qkv[2, at, lanes], g, 1, 0))
    for g, (head, at, lanes, probs_ref) in zip(grad, parts):
        grads[2, at, lanes] = dot(probs_ref[head].astype(jnp.bfloat16), g, 1, 1).astype(jnp.bfloat16)
    for dprob, (head, at, lanes, probs_ref) in zip(dprobs, parts):
        probs = probs_ref[head]
        delta = jnp.sum(probs * dprob, axis=0, keepdims=True)
        dscores.append((probs * (dprob - delta) * FACTOR).astype(jnp.bfloat16))
    for dscore, (head, at, lanes, _) in zip(dscores, parts):
        grads[1, at, lanes] = dot(dscore, qkv[0, at, lanes], 1, 0).astype(jnp.bfloat16)
        grads[0, at, lanes] = dot(dscore, qkv[1, at, lanes], 0, 0).astype(jnp.bfloat16)


def backward(qkv, grad_mine, grad_other, main_probs, slot_probs, low, high, grads):
    _, rows, width = qkv.shape
    held = [] if grads is None else [grads]
    return pl.pallas_call(
        backward_kernel,
        grid=(high - low,),
        in_specs=[
            pl.BlockSpec((3, rows, PAIR * HS), lambda h: (0, 0, h + low)),
            pl.BlockSpec((PAIR * HS, rows), lambda h: (h + low, 0)),
            pl.BlockSpec((PAIR * HS, rows), lambda h: (h + low, 0)),
            pl.BlockSpec((PAIR, MAIN, MAIN), lambda h: (h + low, 0, 0)),
            pl.BlockSpec((PAIR, 2 * SLOT, 2 * SLOT), lambda h: (h + low, 0, 0)),
        ] + [pl.BlockSpec(memory_space=pl.ANY)] * len(held),
        out_specs=pl.BlockSpec((3, rows, PAIR * HS), lambda h: (0, 0, h + low)),
        out_shape=jax.ShapeDtypeStruct(qkv.shape, jnp.bfloat16),
        input_output_aliases={5: 0} if held else {},
        compiler_params=pltpu.CompilerParams(vmem_limit_bytes=VMEM_BYTES),
        cost_estimate=LONG,
        name="attention_backward",
    )(qkv, grad_mine, grad_other, main_probs, slot_probs, *held)


def grad_out_kernel(sizes, split, total, info, turned, turned_other, *refs):
    columns, sems = refs[-2:]
    mine, other = refs[-4:-2]
    step = pl.program_id(0)
    core = info[0]
    at = pl.ds(pl.multiple_of(core * (total - split), LANE), split)
    copies = [
        pltpu.make_async_copy(source.at[at], columns.at[i], sems.at[i]) for i, source in enumerate((turned, turned_other))
    ]

    @pl.when(step == 0)
    def _():
        for copy in copies:
            copy.start()
        for copy in copies:
            copy.wait()

        @pl.when(core == 1)
        def _():
            shared = 2 * split - total
            columns[:, :shared, :] = jnp.zeros((2, shared, columns.shape[2]), jnp.bfloat16)

    index = 0
    for j, size in enumerate(sizes):

        @pl.when(step == j)
        def _(index=index, size=size):
            first = 0
            for piece in refs[index:index + size]:
                at = slice(first, first + piece.shape[0])
                rows = mine.shape[2]
                mine[0, at, :] = dot(piece[...], columns[0], 1, 0)[:, :rows]
                other[0, at, :] = dot(piece[...], columns[1], 1, 0)[:, :rows].astype(jnp.bfloat16)
                first += piece.shape[0]

        index += size


def grad_out_rows(info, turned, turned_other, rows, pieces, shards, held):
    total, lanes = turned.shape
    split = pieces[0][0].shape[1]
    depth = sum(p.shape[0] for p in pieces[0])
    sizes = [len(p) for p in pieces]
    arrays = [a for p in pieces for a in p]
    held = [] if held is None else list(held)
    return pl.pallas_call(
        functools.partial(grad_out_kernel, sizes, split, total),
        grid_spec=pltpu.PrefetchScalarGridSpec(
            num_scalar_prefetch=1,
            grid=(len(pieces),),
            in_specs=[pl.BlockSpec(memory_space=pl.ANY)] * 2
            + [pl.BlockSpec(a.shape, lambda j, info: (0, 0)) for a in arrays]
            + [pl.BlockSpec(memory_space=pl.ANY)] * len(held),
            out_specs=[pl.BlockSpec((1, depth, rows), lambda j, info: (info[1 + j], 0, 0))] * 2,
            scratch_shapes=[pltpu.VMEM((2, split, lanes), jnp.bfloat16), pltpu.SemaphoreType.DMA((2,))],
        ),
        out_shape=[
            jax.ShapeDtypeStruct((shards, depth, rows), jnp.float32),
            jax.ShapeDtypeStruct((shards, depth, rows), jnp.bfloat16),
        ],
        input_output_aliases={3 + len(arrays) + i: i for i in range(len(held))},
        compiler_params=pltpu.CompilerParams(vmem_limit_bytes=VMEM_BYTES),
        cost_estimate=LONG,
        name="grad_out_rows",
    )(info, turned, turned_other, *arrays, *held)


def partial_kernel(sources, count, window, order, starts, *refs):
    attended, columns = refs[:sources], refs[sources:2 * sources]
    outs, (chunks, held, sems) = refs[2 * sources:-3], refs[-3:]
    depth = chunks.shape[2]
    copies = []
    for i in range(sources):
        at = pl.ds(pl.multiple_of(starts[min(i // 2, 1)], LANE), window)
        some = [pltpu.make_async_copy(columns[i].at[:, at], held.at[i], sems.at[i, count])]
        for j in range(count):
            source = attended[i].at[order[j] if i < 2 else j]
            some.append(pltpu.make_async_copy(source, chunks.at[i, j], sems.at[i, j]))
        copies.append(some)
    for some in copies:
        for copy in some:
            copy.start()
    together = depth % 16 == 0
    for i, some in enumerate(copies):
        for copy in some:
            copy.wait()
        if together:
            product = dot(chunks[i].reshape(count * depth, chunks.shape[3]), held[i], 1, 0)
        for j, out in enumerate(outs):
            part = product[j * depth:(j + 1) * depth] if together else dot(chunks[i, j], held[i], 1, 0)
            if i == 0:
                out[...] = part
            else:
                out[...] += part


def partial_products(order, starts, attended, columns, window):
    _, depth, rows = attended[0].shape
    count, sources = order.shape[0], len(attended)
    return pl.pallas_call(
        functools.partial(partial_kernel, sources, count, window),
        grid_spec=pltpu.PrefetchScalarGridSpec(
            num_scalar_prefetch=2,
            grid=(1,),
            in_specs=[pl.BlockSpec(memory_space=pl.ANY)] * (2 * sources),
            out_specs=[pl.BlockSpec((depth, window), lambda j, o, s: (0, 0))] * count,
            scratch_shapes=[
                pltpu.VMEM((sources, count, depth, rows), jnp.bfloat16),
                pltpu.VMEM((sources, rows, window), jnp.bfloat16),
                pltpu.SemaphoreType.DMA((sources, count + 1)),
            ],
        ),
        out_shape=[jax.ShapeDtypeStruct((depth, window), jnp.float32)] * count,
        compiler_params=pltpu.CompilerParams(vmem_limit_bytes=VMEM_BYTES),
        cost_estimate=LONG,
        name="projection_partial",
    )(order, starts, *attended, *columns)


def windows_of(groups, owned, total):
    lows = [g * owned // LANE * LANE for g in range(groups)]
    width = max(-(-((g + 1) * owned) // LANE) * LANE - low for g, low in enumerate(lows))
    return width


def ring_of(count):
    return list(range(0, count, 2)) + list(range(count - 1, 0, -2))


def local(members, shards, query_key_value, cotangent, proj_weight, layer_scale, lengths):
    member = lax.axis_index("dp")
    shard = lax.axis_index("fsdp")
    core, chip, peers = member % 2, member // 2, members // 2
    ring = ring_of(shards)
    place = jnp.where(shard % 2 == 0, shard // 2, shards - 1 - shard // 2)
    ahead = [(ring[i], ring[(i + 1) % shards]) for i in range(shards)]
    behind = [(ring[i], ring[(i - 1) % shards]) for i in range(shards)]
    half = shards // 2
    depth, total = proj_weight.shape
    rows, width = query_key_value.shape[1:]
    owned = total // members
    counts = lax.dynamic_index_in_dim(lengths[:, 0, :], member, 0, keepdims=False)

    def swap(array, bit):
        return lax.ppermute(array, "dp", [(i, i ^ bit) for i in range(members)])

    def shard_at(offset):
        at = (place + offset + shards) % shards
        return jnp.where(at < half, 2 * at, 2 * (shards - 1 - at) + 1)

    def table(values):
        return jnp.stack([jnp.asarray(v) for v in values]).astype(jnp.int32)

    chip_width, window = windows_of(peers, 2 * owned, total), windows_of(members, owned, total)

    def chip_start(chip):
        return jnp.minimum(chip * 2 * owned // LANE * LANE, total - chip_width)

    my_start = jnp.minimum(member * owned // LANE * LANE, chip_start(chip) + chip_width - window)
    starts = table([my_start, my_start - chip_start(chip)])

    split = -(-(total // LANE) // 2) * LANE
    mine = jnp.where(core == 0, proj_weight[:, :split], proj_weight[:, total - split:])
    cut = -(-depth // 32) * 16
    up, down = [mine], [mine]
    up.append(lax.ppermute(up[-1], "fsdp", ahead))
    down.append(lax.ppermute(down[-1], "fsdp", behind))

    mine, cotangent = lax.optimization_barrier((mine, cotangent))
    scaled, turned, *sent = prepare(
        table([chip_start(chip ^ k) for k in range(1, peers)] or [0]), cotangent, layer_scale, peers - 1, chip_width
    )
    columns = [scaled, swap(scaled, 1)]
    turned_other = swap(turned, 1)
    attended, main_probs, slot_probs = forward(counts, query_key_value)
    attended = attended.reshape(shards, depth, rows)
    near = [[o, -o] for o in range(half - 1, 0, -1)]
    groups = [[half] + near[0]] + near[1:-1] + [near[-1] + [0]]
    came_columns = [swap(sent[k - 1], 2 * k) for k in range(1, peers)]
    flat = table([shard_at(o) for group in groups for o in group])
    sizes = [len(group) for group in groups]
    orders = [flat[sum(sizes[:g]):sum(sizes[:g + 1])] for g in range(len(groups))]
    chunks = list(arrange(flat, attended, sizes))
    came = [[swap(chunks[0], 2 * k) for k in range(1, peers)]]

    def rows_of(some, held):
        info = table([core] + [shard_at(o) for _, o in some])
        return grad_out_rows(info, turned, turned_other, rows, [p for p, _ in some], shards, held)

    up[1], down[1], attended = lax.optimization_barrier((up[1], down[1], attended))
    both = [attended, swap(attended, 1)]
    for _ in range(half - 3):
        up.append(lax.ppermute(up[-1], "fsdp", ahead))
        down.append(lax.ppermute(down[-1], "fsdp", behind))
    up[-1], down[-1], columns[1], turned_other = lax.optimization_barrier((up[-1], down[-1], columns[1], turned_other))
    came_columns, near_up, near_down, chunks = lax.optimization_barrier((came_columns, up[-1], down[-1], chunks))
    came.append([swap(chunks[1], 2 * k) for k in range(1, peers)])
    pieces = [([mine], 0)]
    for step in range(1, half - 1):
        last = step == half - 2
        pieces += [([near_up if last else up[step]], -step), ([near_down if last else down[step]], step)]
    grad_out = rows_of(pieces, None)
    for c in came_columns:
        columns += [c, swap(c, 1)]
    up.append(lax.ppermute(up[-1], "fsdp", ahead))
    down.append(lax.ppermute(down[-1], "fsdp", behind))
    up[-1], down[-1], grad_out, both[1] = lax.optimization_barrier((up[-1], down[-1], grad_out, both[1]))
    came[0], near_up, near_down, chunks = lax.optimization_barrier((came[0], up[-1], down[-1], chunks))
    came += [[swap(some, 2 * k) for k in range(1, peers)] for some in chunks[2:]]
    far_up = lax.ppermute(up[-1][:cut], "fsdp", ahead)
    far_down = lax.ppermute(down[-1][cut:], "fsdp", behind)

    def products(index):
        taken = list(both)
        for c in came[index]:
            taken += [c, swap(c, 1)]
        result = partial_products(orders[index], starts, taken, columns, window)
        return {o: result[j] for j, o in enumerate(groups[index])}

    terms = products(0)
    first = terms[half].astype(jnp.bfloat16)
    far_up, far_down, terms = lax.optimization_barrier((far_up, far_down, terms))
    going_up, going_down = first[:cut], first[cut:]
    came_up = lax.ppermute(going_up, "fsdp", ahead)
    came_down = lax.ppermute(going_down, "fsdp", behind)

    grad_out = rows_of([([near_up], 1 - half), ([near_down], half - 1), ([far_up, far_down], half)], grad_out)
    grad_mine = grad_out[0].reshape(width, rows)
    grad_other = swap(grad_out[1], 1).reshape(width, rows)
    pairs = -(-(width // HS) // PAIR)
    bounds = [0, 3, 5, pairs]

    def back(index, held):
        return backward(
            query_key_value, grad_mine, grad_other, main_probs, slot_probs, bounds[index], bounds[index + 1], held
        )

    grads = None
    for step in range(half, 1, -1):
        if step == half:
            came_up = jnp.pad(came_up, ((0, depth - cut), (0, 0)))
            came_down = jnp.pad(came_down, ((cut, 0), (0, 0)))
        else:
            terms.update(products(half - step))
        going_up = (terms[step - 1] + came_up.astype(jnp.float32)).astype(jnp.bfloat16)
        going_down = (terms[1 - step] + came_down.astype(jnp.float32)).astype(jnp.bfloat16)
        beside = []
        if step > 2:
            beside.append(came[half - step + 1])
        if step == 3:
            beside.append(grad_mine)
        if step == 2:
            grads = back(0, grads)
            beside.append(grads)
        going_up, going_down, *beside = lax.optimization_barrier((going_up, going_down, *beside))
        if step > 2:
            came[half - step + 1] = beside[0]
        if step == 3:
            grad_mine = beside[1]
        if step == 2:
            grads = beside[0]
        came_up = lax.ppermute(going_up, "fsdp", ahead)
        came_down = lax.ppermute(going_down, "fsdp", behind)
    grads = back(2, back(1, grads))
    came_up, came_down, grads = lax.optimization_barrier((came_up, came_down, grads))
    reduced = terms[0] + came_up.astype(jnp.float32) + came_down.astype(jnp.float32)
    grad_proj = lax.dynamic_slice_in_dim(reduced, member * owned - my_start, owned, 1)
    return grads, grad_proj


def solution(mesh):
    members, shards = mesh.shape["dp"], mesh.shape["fsdp"]
    placed = (
        P(None, ("dp", "fsdp"), None),
        P(("dp", "fsdp"), None),
        P("fsdp", None),
        P(),
        P(None, "fsdp", None),
    )
    return jax.shard_map(
        functools.partial(local, members, shards),
        mesh=mesh,
        in_specs=placed,
        out_specs=(P(None, ("dp", "fsdp"), None), P("fsdp", "dp")),
        check_vma=False,
    )
```

time: 579 us -> 140 us (0.24)
  waiting for transfers between devices: 459 us -> 37 us
  matrix products: 69 us -> 0 us
  Pallas kernels: 0 us -> 54.3 us
  starting transfers between devices: 0.3 us -> 22.7 us
  between operations: 14.2 us -> 0.96 us
  local copies, waits for them, and re-layouts: 27.2 us -> 15.9 us
    reduce_scatter x1 -> x0, waiting for transfers between devices: 336 us -> none  [local(): lax.psum_scatter(lax.dot_general(attended, scaled, (((0,), (0,)), ((), ()...]
    all_gather x1 -> x0, waiting for transfers between devices: 122 us -> none  [local(): lax.all_gather(proj_weight, 'fsdp', axis=0, tiled=True)]
    dot_general x19 -> x0, matrix products: 65.9 us -> none  [the longest x3 13.4 us: attend(): jnp.einsum('hqk,khd->qhd', dscore, key_h, preferred_element_type=jnp.floa...]
    pallas_call x0 -> x11, Pallas kernels: none -> 54.3 us  [the longest x3 16.7 us: partial_products(): pl.pallas_call(functools.partial(partial_kernel, sources, count, window),...]
    ppermute x0 -> x28, waiting for transfers between devices: none -> 37 us  [the longest x3 14.1 us: local(): up.append(lax.ppermute(up[-1], 'fsdp', ahead))]
    ppermute x0 -> x28, starting transfers between devices: none -> 22.7 us  [the longest x4 6.35 us: local(): came_up = lax.ppermute(going_up, 'fsdp', ahead)]
    convert_element_type x8 -> x0, local copies, waits for them, and re-layouts: 7.89 us -> none  [the longest x2 2.75 us: attend(): grad_value.reshape(rows, width).astype(jnp.bfloat16)]
    unnamed x56 -> x44, local copies, waits for them, and re-layouts: 12.1 us -> 14.9 us
  transfers between devices with their start and end apart: 3 -> 28, of which waited for: 2 -> 14; matrix products, arithmetic and copies ran while one was open for 17% -> 3% of each run, Pallas kernels for 0% -> 37%
where the time goes in v1:
time: 140 us; the launch traced here: 139 us
  Pallas kernels  54.3 us (39%)
  waiting for transfers between devices  37 us (26%)
  starting transfers between devices  22.7 us (16%)
  local copies, waits for them, and re-layouts  15.9 us (11%)
  other arithmetic  8.48 us (6%)
    pallas_call x3, Pallas kernels, partial_products(): pl.pallas_call(functools.partial(partial_kernel, sources, count, window),...  16.7 us
    unnamed x44, local copies, waits for them, and re-layouts  14.9 us
    pallas_call x2, Pallas kernels, grad_out_rows(): pl.pallas_call(functools.partial(grad_out_kernel, sizes, split, total), g...  14.8 us
    ppermute x3, waiting for transfers between devices, local(): up.append(lax.ppermute(up[-1], 'fsdp', ahead))  14.1 us
    ppermute x4, waiting for transfers between devices, local(): came_up = lax.ppermute(going_up, 'fsdp', ahead)  12 us
    pallas_call x3, Pallas kernels, backward(): pl.pallas_call(backward_kernel, grid=(high - low,), in_specs=[pl.BlockSpe...  8.46 us
    pallas_call x1, Pallas kernels, forward(): pl.pallas_call(forward_kernel, grid_spec=pltpu.PrefetchScalarGridSpec(num...  7.26 us
    ppermute x4, starting transfers between devices, local(): came_up = lax.ppermute(going_up, 'fsdp', ahead)  6.35 us
  transfers between devices with their start and end apart: 28, of which 14 were waited for; matrix products, arithmetic and copies ran while one was open for 3% of the time, Pallas kernels for 37%

profile of v1, /device:TPU:0, one launch (start us, length us, event | category | flops | bytes accessed | tf_op | source)
XLA Modules:
  0.0 139.3 jit_solution(11229409180907893040)
XLA Ops:
  0.7 2.2 %slice_select_fusion.refs_0_ = bf16[208,1664]{1,0:T(8,128)(2,1)} fusion(bf16[208,3200]{1,0:T(8,128)(2,1)} %param.7, pred[]{:T(512)S(6)} %eq.26), kind=kLoop, calls=%fused_computation.8 | loop fusion | flops 346112 | bytes 2076673 | tf_op jit(solution)/shard_map/jit(_where)/select_n | solution.py:377
  2.9 3.0 %collective-permute-start = (bf16[208,1664]{1,0:T(8,128)(2,1)}, bf16[208,1664]{1,0:T(8,128)(2,1)}, u32[]{:S(2)}, u32[]{:S(2)}) collective-permute-start(bf16[208,1664]{1,0:T(8,128)(2,1)} %slice_select_fusion.refs_0_), channel_id=1, source_target_pairs={{0,2},{2,4},{4,6},{6,7},{7,5},{5,3},{3,1},{1,0},{8,10},{10,12},{12... | collective-permute-start | bytes 2076680 | tf_op jit(solution)/shard_map/ppermute | solution.py:380
  6.7 1.8 %copy-done.4 = bf16[448,3200]{1,0:T(8,128)(2,1)S(1)} copy-done((bf16[448,3200]{1,0:T(8,128)(2,1)S(1)}, bf16[448,3200]{1,0:T(8,128)(2,1)}, u32[]{:S(2)}) %copy-start.4) | copy-done | bytes 2867224
  8.5 5.0 %scaled_cotangent.1 = (bf16[448,3200]{1,0:T(8,128)(2,1)}, bf16[3200,512]{1,0:T(8,128)(2,1)}, bf16[448,1664]{1,0:T(8,128)(2,1)}) custom-call(s32[1]{0:T(128)} %bitcast.7.starts, bf16[448,3200]{1,0:T(8,128)(2,1)S(1)} %copy-done.4, f32[1,3200]{1,0:T(1,128)S(1)} %reshape.19.layer_scale), custom_call_target="tpu_custom_call" | custom-call | flops 99999997952 | bytes 100000000 | tf_op jit(solution)/shard_map/scaled_cotangent/pallas_call | solution.py:43
  14.0 1.9 %collective-permute-start.8 = (bf16[448,1664]{1,0:T(8,128)(2,1)}, bf16[448,1664]{1,0:T(8,128)(2,1)}, u32[]{:S(2)}, u32[]{:S(2)}) collective-permute-start(bf16[448,1664]{1,0:T(8,128)(2,1)} %get-tuple-element.74), channel_id=1, source_target_pairs={{0,16},{8,24},{16,0},{24,8},{1,17},{9,25},{17,1},{25,9},{2,18},{10... | collective-permute-start | bytes 4472840 | tf_op jit(solution)/shard_map/ppermute | solution.py:359
  16.0 2.3 %copy-done.2 = bf16[3,448,1664]{2,1,0:T(8,128)(2,1)S(1)} copy-done((bf16[3,448,1664]{2,1,0:T(8,128)(2,1)S(1)}, bf16[3,448,1664]{2,1,0:T(8,128)(2,1)}, u32[]{:S(2)}) %copy-start.2) | copy-done | bytes 4472856
  18.2 7.3 %attention_forward.1 = (bf16[1664,448]{1,0:T(8,128)(2,1)S(1)}, f32[13,256,256]{2,1,0:T(8,128)S(1)}, f32[13,192,192]{2,1,0:T(8,128)S(1)}) custom-call(s32[4]{0:T(128)S(1)} %fusion.1.counts, bf16[3,448,1664]{2,1,0:T(8,128)(2,1)S(1)} %copy-done.2), custom_call_target="tpu_custom_call" | custom-call | flops 99999997952 | bytes 100000000 | tf_op jit(solution)/shard_map/attention_forward/pallas_call | solution.py:146
  25.5 1.7 %copy-done.18 = f32[13,256,256]{2,1,0:T(8,128)} copy-done((f32[13,256,256]{2,1,0:T(8,128)}, f32[13,256,256]{2,1,0:T(8,128)S(1)}, u32[]{:S(2)}) %copy-start.18) | copy-done | bytes 3407896
  27.2 1.5 %copy-done.20 = f32[13,192,192]{2,1,0:T(8,128)} copy-done((f32[13,192,192]{2,1,0:T(8,128)}, f32[13,192,192]{2,1,0:T(8,128)S(1)}, u32[]{:S(2)}) %copy-start.20) | copy-done | bytes 1916952
  28.7 1.6 %collective-permute-start.2 = (bf16[208,1664]{1,0:T(8,128)(2,1)}, bf16[208,1664]{1,0:T(8,128)(2,1)}, u32[]{:S(2)}, u32[]{:S(2)}) collective-permute-start(bf16[208,1664]{1,0:T(8,128)(2,1)} %collective-permute-done.refs_1_), channel_id=1, source_target_pairs={{0,2},{2,4},{4,6},{6,7},{7,5},{5,3},{3,1},{1,0},{8,10},{10,12},{12... | collective-permute-start | bytes 2076680 | tf_op jit(solution)/shard_map/ppermute | solution.py:407
  30.8 2.0 %attended_chunks.1 = (bf16[3,208,448]{2,1,0:T(8,128)(2,1)}, bf16[2,208,448]{2,1,0:T(8,128)(2,1)S(1)}, bf16[3,208,448]{2,1,0:T(8,128)(2,1)}) custom-call(s32[8]{0:T(128)S(1)} %stack.78.order, bf16[8,208,448]{2,1,0:T(8,128)(2,1)S(1)} %bitcast.17), custom_call_target="tpu_custom_call" | custom-call | flops 1000 | bytes 1000 | tf_op jit(solution)/shard_map/attended_chunks/pallas_call | solution.py:84
  33.0 13.2 %collective-permute-done.2.refs_3_ = bf16[208,1664]{1,0:T(8,128)(2,1)} collective-permute-done((bf16[208,1664]{1,0:T(8,128)(2,1)}, bf16[208,1664]{1,0:T(8,128)(2,1)}, u32[]{:S(2)}, u32[]{:S(2)}) %collective-permute-start.2) | collective-permute-done | bytes 692256 | tf_op jit(solution)/shard_map/ppermute | solution.py:407
  46.5 0.9 collective-permute-done.3.refs_4_
  47.4 0.8 copy-done.12
  48.2 1.6 %collective-permute-start.6 = (bf16[208,1664]{1,0:T(8,128)(2,1)}, bf16[208,1664]{1,0:T(8,128)(2,1)S(1)}, u32[]{:S(2)}, u32[]{:S(2)}) collective-permute-start(bf16[208,1664]{1,0:T(8,128)(2,1)} %collective-permute-done.2.refs_3_), channel_id=1, source_target_pairs={{0,2},{2,4},{4,6},{6,7},{7,5},{5,3},{3,1},{1,0},{8,10},{10,12},{12... | collective-permute-start | bytes 2076680 | tf_op jit(solution)/shard_map/ppermute | solution.py:419
  50.3 1.1 copy-done.13
  51.4 9.1 %grad_out_rows.2 = (f32[8,208,448]{2,1,0:T(8,128)S(1)}, bf16[8,208,448]{2,1,0:T(8,128)(2,1)S(1)}) custom-call(s32[6]{0:T(128)S(1)} %stack.74.info, bf16[3200,512]{1,0:T(8,128)(2,1)} %get-tuple-element.69.turned, bf16[3200,512]{1,0:T(8,128)(2,1)} %collective-permute-done.5.turned_other, bf16[208,1664]{1,0:T(8,128)(2,1)} %slice_select_fusion.refs_0_, ...), custom_call_target="tpu_custom_call" | custom-call | flops 99999997952 | bytes 100000000 | tf_op jit(solution)/shard_map/grad_out_rows/pallas_call | solution.py:260
  60.6 1.2 copy-done.9
  61.8 1.7 %copy-done.14 = f32[8,208,448]{2,1,0:T(8,128)} copy-done((f32[8,208,448]{2,1,0:T(8,128)}, f32[8,208,448]{2,1,0:T(8,128)S(1)}, u32[]{:S(2)}) %copy-start.14) | copy-done | bytes 2981912
  63.5 1.2 copy-done.5
  64.7 0.9 collective-permute-done.6.refs_0_
  65.6 1.3 collective-permute-done.7.refs_1_
  67.1 1.6 %collective-permute-start.10 = (bf16[112,1664]{1,0:T(8,128)(2,1)S(1)}, bf16[112,1664]{1,0:T(8,128)(2,1)S(1)}, u32[]{:S(2)}, u32[]{:S(2)}) collective-permute-start(bf16[112,1664]{1,0:T(8,128)(2,1)S(1)} %slice.26), channel_id=1, source_target_pairs={{0,2},{2,4},{4,6},{6,7},{7,5},{5,3},{3,1},{1,0},{8,10},{10,12},{12... | collective-permute-start | bytes 1118216 | tf_op jit(solution)/shard_map/ppermute | solution.py:424
  69.3 1.5 %copy-done.6 = bf16[8,208,448]{2,1,0:T(8,128)(2,1)S(1)} copy-done((bf16[8,208,448]{2,1,0:T(8,128)(2,1)S(1)}, bf16[8,208,448]{2,1,0:T(8,128)(2,1)}, u32[]{:S(2)}) %copy-start.6) | copy-done | bytes 1490968
  70.8 5.7 %projection_partial.3 = (f32[208,896]{1,0:T(8,128)S(1)}, f32[208,896]{1,0:T(8,128)S(1)}, f32[208,896]{1,0:T(8,128)S(1)}) custom-call(s32[3]{0:T(128)S(1)} %pad_add_fusion.3.order, s32[2]{0:T(128)S(1)} %pad_add_fusion.1.starts, bf16[8,208,448]{2,1,0:T(8,128)(2,1)S(1)} %bitcast.19, bf16[8,208,448]{2,1,0:T(8,128)(2,1)S(1)} %copy-done.6, ...), custom_call_target="tpu_custom_call" | custom-call | flops 99999997952 | bytes 100000000 | tf_op jit(solution)/shard_map/projection_partial/pallas_call | solution.py:314
  77.2 0.9 collective-permute-start.17
  78.1 1.1 collective-permute-start.21
  79.2 1.6 %collective-permute-start.15 = (bf16[112,896]{1,0:T(8,128)(2,1)S(1)}, bf16[112,896]{1,0:T(8,128)(2,1)S(1)}, u32[]{:S(2)}, u32[]{:S(2)}) collective-permute-start(bf16[112,896]{1,0:T(8,128)(2,1)S(1)} %slice.30), channel_id=1, source_target_pairs={{0,2},{2,4},{4,6},{6,7},{7,5},{5,3},{3,1},{1,0},{8,10},{10,12},{12... | collective-permute-start | bytes 602120 | tf_op jit(solution)/shard_map/ppermute | solution.py:438
  80.9 2.1 %collective-permute-done.16 = bf16[96,896]{1,0:T(8,128)(2,1)S(1)} collective-permute-done((bf16[96,896]{1,0:T(8,128)(2,1)S(1)}, bf16[96,896]{1,0:T(8,128)(2,1)S(1)}, u32[]{:S(2)}, u32[]{:S(2)}) %collective-permute-start.16) | collective-permute-done | bytes 172064 | tf_op jit(solution)/shard_map/ppermute | solution.py:439
  83.0 2.4 %collective-permute-done.15 = bf16[112,896]{1,0:T(8,128)(2,1)S(1)} collective-permute-done((bf16[112,896]{1,0:T(8,128)(2,1)S(1)}, bf16[112,896]{1,0:T(8,128)(2,1)S(1)}, u32[]{:S(2)}, u32[]{:S(2)}) %collective-permute-start.15) | collective-permute-done | bytes 200736 | tf_op jit(solution)/shard_map/ppermute | solution.py:438
  85.6 4.3 %collective-permute-done.17.refs_2_ = bf16[2,208,448]{2,1,0:T(8,128)(2,1)S(1)} collective-permute-done((bf16[2,208,448]{2,1,0:T(8,128)(2,1)S(1)}, bf16[2,208,448]{2,1,0:T(8,128)(2,1)S(1)}, u32[]{:S(2)}, u32[]{:S(2)}) %collective-permute-start.17) | collective-permute-done | bytes 372768 | tf_op jit(solution)/shard_map/ppermute | solution.py:359
  89.9 5.7 %grad_out_rows.3 = (f32[8,208,448]{2,1,0:T(8,128)S(1)}, bf16[8,208,448]{2,1,0:T(8,128)(2,1)S(1)}) custom-call(s32[4]{0:T(128)S(1)} %pad_add_fusion.4.info, bf16[3200,512]{1,0:T(8,128)(2,1)} %get-tuple-element.69.turned, bf16[3200,512]{1,0:T(8,128)(2,1)} %collective-permute-done.5.turned_other, ...), custom_call_target="tpu_custom_call", output_to_operand_aliasing={{0}: (7, {}), {1}: (8, {})} | custom-call | flops 99999997952 | bytes 100000000 | tf_op jit(solution)/shard_map/grad_out_rows/pallas_call | solution.py:260
  95.6 1.6 %collective-permute-start.19 = (bf16[208,896]{1,0:T(8,128)(2,1)S(1)}, bf16[208,896]{1,0:T(8,128)(2,1)S(1)}, u32[]{:S(2)}, u32[]{:S(2)}) collective-permute-start(bf16[208,896]{1,0:T(8,128)(2,1)S(1)} %add_convert_fusion.5), channel_id=1, source_target_pairs={{0,2},{2,4},{4,6},{6,7},{7,5},{5,3},{3,1},{1,0},{8,10},{10,12},{12... | collective-permute-start | bytes 1118216 | tf_op jit(solution)/shard_map/ppermute | solution.py:476
  97.7 4.9 %projection_partial.4 = (f32[208,896]{1,0:T(8,128)S(1)}, f32[208,896]{1,0:T(8,128)S(1)}) custom-call(s32[2]{0:T(128)S(1)} %pad_add_fusion.2.order, s32[2]{0:T(128)S(1)} %pad_add_fusion.1.starts, bf16[8,208,448]{2,1,0:T(8,128)(2,1)S(1)} %bitcast.20, bf16[8,208,448]{2,1,0:T(8,128)(2,1)S(1)} %copy-done.7, ...), custom_call_target="tpu_custom_call" | custom-call | flops 99999997952 | bytes 100000000 | tf_op jit(solution)/shard_map/projection_partial/pallas_call | solution.py:314
  102.6 4.1 %collective-permute-done.19 = bf16[208,896]{1,0:T(8,128)(2,1)S(1)} collective-permute-done((bf16[208,896]{1,0:T(8,128)(2,1)S(1)}, bf16[208,896]{1,0:T(8,128)(2,1)S(1)}, u32[]{:S(2)}, u32[]{:S(2)}) %collective-permute-start.19) | collective-permute-done | bytes 372768 | tf_op jit(solution)/shard_map/ppermute | solution.py:476
  106.8 0.8 add_convert_fusion.3
  108.0 0.8 add_convert_fusion.2
  109.5 1.6 %collective-permute-start.23 = (bf16[208,896]{1,0:T(8,128)(2,1)}, bf16[208,896]{1,0:T(8,128)(2,1)S(1)}, u32[]{:S(2)}, u32[]{:S(2)}) collective-permute-start(bf16[208,896]{1,0:T(8,128)(2,1)} %add_convert_fusion.3), channel_id=1, source_target_pairs={{0,2},{2,4},{4,6},{6,7},{7,5},{5,3},{3,1},{1,0},{8,10},{10,12},{12... | collective-permute-start | bytes 1118216 | tf_op jit(solution)/shard_map/ppermute | solution.py:476
  111.5 6.1 %projection_partial.5 = (f32[208,896]{1,0:T(8,128)S(1)}, f32[208,896]{1,0:T(8,128)S(1)}, f32[208,896]{1,0:T(8,128)S(1)}) custom-call(s32[3]{0:T(128)S(1)} %pad_add_fusion.order, s32[2]{0:T(128)S(1)} %pad_add_fusion.1.starts, bf16[8,208,448]{2,1,0:T(8,128)(2,1)S(1)} %bitcast.21, bf16[8,208,448]{2,1,0:T(8,128)(2,1)S(1)} %copy-done.8, ...), custom_call_target="tpu_custom_call" | custom-call | flops 99999997952 | bytes 100000000 | tf_op jit(solution)/shard_map/projection_partial/pallas_call | solution.py:314
  117.6 2.7 %collective-permute-done.23 = bf16[208,896]{1,0:T(8,128)(2,1)S(1)} collective-permute-done((bf16[208,896]{1,0:T(8,128)(2,1)}, bf16[208,896]{1,0:T(8,128)(2,1)S(1)}, u32[]{:S(2)}, u32[]{:S(2)}) %collective-permute-start.23) | collective-permute-done | bytes 372768 | tf_op jit(solution)/shard_map/ppermute | solution.py:476
  120.3 0.8 add_convert_fusion.1
  122.5 3.4 %attention_backward.3.rest_0_ = bf16[3,448,1664]{2,1,0:T(8,128)(2,1)} custom-call(bf16[3,448,1664]{2,1,0:T(8,128)(2,1)S(1)} %copy-done.3, f32[1664,448]{1,0:T(8,128)S(1)} %bitcast.25, bf16[1664,448]{1,0:T(8,128)(2,1)S(1)} %bitcast.22, f32[13,256,256]{2,1,0:T(8,128)S(1)} %copy-done.19, f32[13,192,192]{2,1,0:T(8,128)S(1)} %copy-done.21), custom_call_target="tpu_custom_call" | custom-call | flops 99999997952 | bytes 100000000 | tf_op jit(solution)/shard_map/attention_backward/pallas_call | solution.py:196
  125.9 1.5 %collective-permute-start.26 = (bf16[208,896]{1,0:T(8,128)(2,1)}, bf16[208,896]{1,0:T(8,128)(2,1)}, u32[]{:S(2)}, u32[]{:S(2)}) collective-permute-start(bf16[208,896]{1,0:T(8,128)(2,1)} %add_convert_fusion.1), channel_id=1, source_target_pairs={{0,2},{2,4},{4,6},{6,7},{7,5},{5,3},{3,1},{1,0},{8,10},{10,12},{12... | collective-permute-start | bytes 1118216 | tf_op jit(solution)/shard_map/ppermute | solution.py:476
  127.9 2.6 %attention_backward.4.rest_0_ = bf16[3,448,1664]{2,1,0:T(8,128)(2,1)} custom-call(bf16[3,448,1664]{2,1,0:T(8,128)(2,1)S(1)} %copy-done.3, f32[1664,448]{1,0:T(8,128)S(1)} %bitcast.26, bf16[1664,448]{1,0:T(8,128)(2,1)S(1)} %bitcast.23, f32[13,256,256]{2,1,0:T(8,128)S(1)} %copy-done.19, ...), custom_call_target="tpu_custom_call", output_to_operand_aliasing={{}: (5, {})} | custom-call | flops 99999997952 | bytes 100000000 | tf_op jit(solution)/shard_map/attention_backward/pallas_call | solution.py:196
  130.5 2.5 %attention_backward.5 = bf16[3,448,1664]{2,1,0:T(8,128)(2,1)} custom-call(bf16[3,448,1664]{2,1,0:T(8,128)(2,1)S(1)} %copy-done.3, f32[1664,448]{1,0:T(8,128)S(1)} %bitcast.27, bf16[1664,448]{1,0:T(8,128)(2,1)S(1)} %bitcast.24, f32[13,256,256]{2,1,0:T(8,128)S(1)} %copy-done.19, f32[13,192,192]{2,1,0:T(8,128)S(1)} %copy-done.21, ...), custom_call_target="tpu_custom_call", output_to_operand_aliasing={{}: (5, {})} | custom-call | flops 99999997952 | bytes 100000000 | tf_op jit(solution)/shard_map/attention_backward/pallas_call | solution.py:196
  132.9 2.7 %collective-permute-done.26 = bf16[208,896]{1,0:T(8,128)(2,1)} collective-permute-done((bf16[208,896]{1,0:T(8,128)(2,1)}, bf16[208,896]{1,0:T(8,128)(2,1)}, u32[]{:S(2)}, u32[]{:S(2)}) %collective-permute-start.26) | collective-permute-done | bytes 372768 | tf_op jit(solution)/shard_map/ppermute | solution.py:476
  135.7 1.2 collective-permute-done.27
  136.9 2.4 %fusion = f32[208,800]{1,0:T(8,128)} fusion(f32[208,896]{1,0:T(8,128)S(1)} %get-tuple-element.121, s32[]{:T(128)S(6)} %select_n.154, bf16[208,896]{1,0:T(8,128)(2,1)} %collective-permute-done.27, bf16[208,896]{1,0:T(8,128)(2,1)} %collective-permute-done.26), kind=kLoop, calls=%fused_computation.1 | loop fusion | flops 665600 | bytes 1996804 | tf_op jit(solution)/shard_map/add | solution.py:480
  (85 shorter events, 8.1 us)
Async XLA Ops:
  0.6 15.3 %copy-start = (s32[4,1,4]{2,1,0:T(1,128)S(1)}, s32[4,1,4]{2,1,0:T(1,128)}, u32[]{:S(2)}) copy-start(s32[4,1,4]{2,1,0:T(1,128)} %param.9) | copy-start | bytes 196
  2.9 25.8 %collective-permute-start = (bf16[208,1664]{1,0:T(8,128)(2,1)}, bf16[208,1664]{1,0:T(8,128)(2,1)}, u32[]{:S(2)}, u32[]{:S(2)}) collective-permute-start(bf16[208,1664]{1,0:T(8,128)(2,1)} %slice_select_fusion.refs_0_), channel_id=1, source_target_pairs={{0,2},{2,4},{4,6},{6,7},{7,5},{5,3},{3,1},{1,0},{8,10},{10,12},{12... | collective-permute-start | bytes 2076680 | tf_op jit(solution)/shard_map/ppermute | solution.py:380
  5.9 22.8 %collective-permute-start.1 = (bf16[208,1664]{1,0:T(8,128)(2,1)}, bf16[208,1664]{1,0:T(8,128)(2,1)}, u32[]{:S(2)}, u32[]{:S(2)}) collective-permute-start(bf16[208,1664]{1,0:T(8,128)(2,1)} %slice_select_fusion.refs_0_), channel_id=1, source_target_pairs={{0,1},{2,0},{4,2},{6,4},{7,6},{5,7},{3,5},{1,3},{8,9},{10,8},{12,1... | collective-permute-start | bytes 2076680 | tf_op jit(solution)/shard_map/ppermute | solution.py:381
  6.7 1.8 %copy-start.4 = (bf16[448,3200]{1,0:T(8,128)(2,1)S(1)}, bf16[448,3200]{1,0:T(8,128)(2,1)}, u32[]{:S(2)}) copy-start(bf16[448,3200]{1,0:T(8,128)(2,1)} %cotangent) | copy-start | bytes 8601604
  13.5 33.9 %collective-permute-start.4 = (bf16[448,3200]{1,0:T(8,128)(2,1)}, bf16[448,3200]{1,0:T(8,128)(2,1)}, u32[]{:S(2)}, u32[]{:S(2)}) collective-permute-start(bf16[448,3200]{1,0:T(8,128)(2,1)} %get-tuple-element.68.refs_4_), channel_id=1, source_target_pairs={{0,8},{8,0},{16,24},{24,16},{1,9},{9,1},{17,25},{25,17},{2,10},{10... | collective-permute-start | bytes 8601608 | tf_op jit(solution)/shard_map/ppermute | solution.py:359
  13.5 34.7 %collective-permute-start.5 = (bf16[3200,512]{1,0:T(8,128)(2,1)}, bf16[3200,512]{1,0:T(8,128)(2,1)}, u32[]{:S(2)}, u32[]{:S(2)}) collective-permute-start(bf16[3200,512]{1,0:T(8,128)(2,1)} %get-tuple-element.69.turned), channel_id=1, source_target_pairs={{0,8},{8,0},{16,24},{24,16},{1,9},{9,1},{17,25},{25,17},{2,10},{10... | collective-permute-start | bytes 9830408 | tf_op jit(solution)/shard_map/ppermute | solution.py:359
  14.0 36.2 %collective-permute-start.8 = (bf16[448,1664]{1,0:T(8,128)(2,1)}, bf16[448,1664]{1,0:T(8,128)(2,1)}, u32[]{:S(2)}, u32[]{:S(2)}) collective-permute-start(bf16[448,1664]{1,0:T(8,128)(2,1)} %get-tuple-element.74), channel_id=1, source_target_pairs={{0,16},{8,24},{16,0},{24,8},{1,17},{9,25},{17,1},{25,9},{2,18},{10... | collective-permute-start | bytes 4472840 | tf_op jit(solution)/shard_map/ppermute | solution.py:359
  16.0 2.3 %copy-start.2 = (bf16[3,448,1664]{2,1,0:T(8,128)(2,1)S(1)}, bf16[3,448,1664]{2,1,0:T(8,128)(2,1)}, u32[]{:S(2)}) copy-start(bf16[3,448,1664]{2,1,0:T(8,128)(2,1)} %qkv.7) | copy-start | bytes 13418500
  25.5 1.7 %copy-start.18 = (f32[13,256,256]{2,1,0:T(8,128)}, f32[13,256,256]{2,1,0:T(8,128)S(1)}, u32[]{:S(2)}) copy-start(f32[13,256,256]{2,1,0:T(8,128)S(1)} %get-tuple-element.115.main_probs) | copy-start | bytes 10223620
  27.2 1.5 %copy-start.20 = (f32[13,192,192]{2,1,0:T(8,128)}, f32[13,192,192]{2,1,0:T(8,128)S(1)}, u32[]{:S(2)}) copy-start(f32[13,192,192]{2,1,0:T(8,128)S(1)} %get-tuple-element.116.slot_probs) | copy-start | bytes 5750788
  28.7 17.5 %collective-permute-start.2 = (bf16[208,1664]{1,0:T(8,128)(2,1)}, bf16[208,1664]{1,0:T(8,128)(2,1)}, u32[]{:S(2)}, u32[]{:S(2)}) collective-permute-start(bf16[208,1664]{1,0:T(8,128)(2,1)} %collective-permute-done.refs_1_), channel_id=1, source_target_pairs={{0,2},{2,4},{4,6},{6,7},{7,5},{5,3},{3,1},{1,0},{8,10},{10,12},{12... | collective-permute-start | bytes 2076680 | tf_op jit(solution)/shard_map/ppermute | solution.py:407
  30.3 17.1 %collective-permute-start.3 = (bf16[208,1664]{1,0:T(8,128)(2,1)}, bf16[208,1664]{1,0:T(8,128)(2,1)S(1)}, u32[]{:S(2)}, u32[]{:S(2)}) collective-permute-start(bf16[208,1664]{1,0:T(8,128)(2,1)} %collective-permute-done.1.refs_2_), channel_id=1, source_target_pairs={{0,1},{2,0},{4,2},{6,4},{7,6},{5,7},{3,5},{1,3},{8,9},{10,8},{12,1... | collective-permute-start | bytes 2076680 | tf_op jit(solution)/shard_map/ppermute | solution.py:408
  46.2 20.7 %collective-permute-start.12 = (bf16[3,208,448]{2,1,0:T(8,128)(2,1)}, bf16[3,208,448]{2,1,0:T(8,128)(2,1)}, u32[]{:S(2)}, u32[]{:S(2)}) collective-permute-start(bf16[3,208,448]{2,1,0:T(8,128)(2,1)} %get-tuple-element.75), channel_id=1, source_target_pairs={{0,16},{8,24},{16,0},{24,8},{1,17},{9,25},{17,1},{25,9},{2,18},{10... | collective-permute-start | bytes 1677320 | tf_op jit(solution)/shard_map/ppermute | solution.py:359
  47.4 16.2 %collective-permute-start.9 = (bf16[8,208,448]{2,1,0:T(8,128)(2,1)S(1)}, bf16[8,208,448]{2,1,0:T(8,128)(2,1)S(1)}, u32[]{:S(2)}, u32[]{:S(2)}) collective-permute-start(bf16[8,208,448]{2,1,0:T(8,128)(2,1)S(1)} %bitcast.18), channel_id=1, source_target_pairs={{0,8},{8,0},{16,24},{24,16},{1,9},{9,1},{17,25},{25,17},{2,10},{10... | collective-permute-start | bytes 4472840 | tf_op jit(solution)/shard_map/ppermute | solution.py:359
  48.2 17.4 %collective-permute-start.6 = (bf16[208,1664]{1,0:T(8,128)(2,1)}, bf16[208,1664]{1,0:T(8,128)(2,1)S(1)}, u32[]{:S(2)}, u32[]{:S(2)}) collective-permute-start(bf16[208,1664]{1,0:T(8,128)(2,1)} %collective-permute-done.2.refs_3_), channel_id=1, source_target_pairs={{0,2},{2,4},{4,6},{6,7},{7,5},{5,3},{3,1},{1,0},{8,10},{10,12},{12... | collective-permute-start | bytes 2076680 | tf_op jit(solution)/shard_map/ppermute | solution.py:419
  49.8 17.1 %collective-permute-start.7 = (bf16[208,1664]{1,0:T(8,128)(2,1)}, bf16[208,1664]{1,0:T(8,128)(2,1)S(1)}, u32[]{:S(2)}, u32[]{:S(2)}) collective-permute-start(bf16[208,1664]{1,0:T(8,128)(2,1)} %copy-done.12), channel_id=1, source_target_pairs={{0,1},{2,0},{4,2},{6,4},{7,6},{5,7},{3,5},{1,3},{8,9},{10,8},{12,1... | collective-permute-start | bytes 2076680 | tf_op jit(solution)/shard_map/ppermute | solution.py:420
  50.3 19.1 %collective-permute-start.14 = (bf16[448,1664]{1,0:T(8,128)(2,1)}, bf16[448,1664]{1,0:T(8,128)(2,1)}, u32[]{:S(2)}, u32[]{:S(2)}) collective-permute-start(bf16[448,1664]{1,0:T(8,128)(2,1)} %collective-permute-done.8.refs_6_), channel_id=1, source_target_pairs={{0,8},{8,0},{16,24},{24,16},{1,9},{9,1},{17,25},{25,17},{2,10},{10... | collective-permute-start | bytes 4472840 | tf_op jit(solution)/shard_map/ppermute | solution.py:359
  60.5 1.2 copy-start.9
  61.8 1.7 %copy-start.14 = (f32[8,208,448]{2,1,0:T(8,128)}, f32[8,208,448]{2,1,0:T(8,128)S(1)}, u32[]{:S(2)}) copy-start(f32[8,208,448]{2,1,0:T(8,128)S(1)} %get-tuple-element.105.refs_4_) | copy-start | bytes 8945668
  63.5 1.2 copy-start.5
  66.9 2.4 %collective-permute-start.13 = (bf16[3,208,448]{2,1,0:T(8,128)(2,1)}, bf16[3,208,448]{2,1,0:T(8,128)(2,1)}, u32[]{:S(2)}, u32[]{:S(2)}) collective-permute-start(bf16[3,208,448]{2,1,0:T(8,128)(2,1)} %collective-permute-done.12.refs_2_), channel_id=1, source_target_pairs={{0,8},{8,0},{16,24},{24,16},{1,9},{9,1},{17,25},{25,17},{2,10},{10... | collective-permute-start | bytes 1677320 | tf_op jit(solution)/shard_map/ppermute | solution.py:359
  67.1 12.1 %collective-permute-start.10 = (bf16[112,1664]{1,0:T(8,128)(2,1)S(1)}, bf16[112,1664]{1,0:T(8,128)(2,1)S(1)}, u32[]{:S(2)}, u32[]{:S(2)}) collective-permute-start(bf16[112,1664]{1,0:T(8,128)(2,1)S(1)} %slice.26), channel_id=1, source_target_pairs={{0,2},{2,4},{4,6},{6,7},{7,5},{5,3},{3,1},{1,0},{8,10},{10,12},{12... | collective-permute-start | bytes 1118216 | tf_op jit(solution)/shard_map/ppermute | solution.py:424
  68.7 10.5 %collective-permute-start.11 = (bf16[96,1664]{1,0:T(8,128)(2,1)S(1)}, bf16[96,1664]{1,0:T(8,128)(2,1)S(1)}, u32[]{:S(2)}, u32[]{:S(2)}) collective-permute-start(bf16[96,1664]{1,0:T(8,128)(2,1)S(1)} %slice.27), channel_id=1, source_target_pairs={{0,1},{2,0},{4,2},{6,4},{7,6},{5,7},{3,5},{1,3},{8,9},{10,8},{12,1... | collective-permute-start | bytes 958472 | tf_op jit(solution)/shard_map/ppermute | solution.py:425
  69.3 1.5 %copy-start.6 = (bf16[8,208,448]{2,1,0:T(8,128)(2,1)S(1)}, bf16[8,208,448]{2,1,0:T(8,128)(2,1)}, u32[]{:S(2)}) copy-start(bf16[8,208,448]{2,1,0:T(8,128)(2,1)} %copy-done.5) | copy-start | bytes 4472836
  70.8 19.1 %copy-start.15 = (f32[8,208,448]{2,1,0:T(8,128)S(1)}, f32[8,208,448]{2,1,0:T(8,128)}, u32[]{:S(2)}) copy-start(f32[8,208,448]{2,1,0:T(8,128)} %copy-done.14) | copy-start | bytes 8945668
  76.4 13.4 %copy-start.10 = (bf16[8,208,448]{2,1,0:T(8,128)(2,1)S(1)}, bf16[8,208,448]{2,1,0:T(8,128)(2,1)}, u32[]{:S(2)}) copy-start(bf16[8,208,448]{2,1,0:T(8,128)(2,1)} %copy-done.9) | copy-start | bytes 4472836
  76.5 6.5 %collective-permute-start.16 = (bf16[96,896]{1,0:T(8,128)(2,1)S(1)}, bf16[96,896]{1,0:T(8,128)(2,1)S(1)}, u32[]{:S(2)}, u32[]{:S(2)}) collective-permute-start(bf16[96,896]{1,0:T(8,128)(2,1)S(1)} %slice.31), channel_id=1, source_target_pairs={{0,1},{2,0},{4,2},{6,4},{7,6},{5,7},{3,5},{1,3},{8,9},{10,8},{12,1... | collective-permute-start | bytes 516104 | tf_op jit(solution)/shard_map/ppermute | solution.py:439
  77.2 12.7 %collective-permute-start.17 = (bf16[2,208,448]{2,1,0:T(8,128)(2,1)S(1)}, bf16[2,208,448]{2,1,0:T(8,128)(2,1)S(1)}, u32[]{:S(2)}, u32[]{:S(2)}) collective-permute-start(bf16[2,208,448]{2,1,0:T(8,128)(2,1)S(1)} %get-tuple-element.85), channel_id=1, source_target_pairs={{0,16},{8,24},{16,0},{24,8},{1,17},{9,25},{17,1},{25,9},{2,18},{10... | collective-permute-start | bytes 1118216 | tf_op jit(solution)/shard_map/ppermute | solution.py:359
  78.1 30.8 %collective-permute-start.21 = (bf16[3,208,448]{2,1,0:T(8,128)(2,1)}, bf16[3,208,448]{2,1,0:T(8,128)(2,1)}, u32[]{:S(2)}, u32[]{:S(2)}) collective-permute-start(bf16[3,208,448]{2,1,0:T(8,128)(2,1)} %get-tuple-element.100), channel_id=1, source_target_pairs={{0,16},{8,24},{16,0},{24,8},{1,17},{9,25},{17,1},{25,9},{2,18},{10... | collective-permute-start | bytes 1677320 | tf_op jit(solution)/shard_map/ppermute | solution.py:359
  79.2 6.2 %collective-permute-start.15 = (bf16[112,896]{1,0:T(8,128)(2,1)S(1)}, bf16[112,896]{1,0:T(8,128)(2,1)S(1)}, u32[]{:S(2)}, u32[]{:S(2)}) collective-permute-start(bf16[112,896]{1,0:T(8,128)(2,1)S(1)} %slice.30), channel_id=1, source_target_pairs={{0,2},{2,4},{4,6},{6,7},{7,5},{5,3},{3,1},{1,0},{8,10},{10,12},{12... | collective-permute-start | bytes 602120 | tf_op jit(solution)/shard_map/ppermute | solution.py:438
  85.5 12.1 %copy-start.7 = (bf16[8,208,448]{2,1,0:T(8,128)(2,1)S(1)}, bf16[8,208,448]{2,1,0:T(8,128)(2,1)}, u32[]{:S(2)}) copy-start(bf16[8,208,448]{2,1,0:T(8,128)(2,1)} %copy-done.5) | copy-start | bytes 4472836
  89.9 7.8 %collective-permute-start.18 = (bf16[2,208,448]{2,1,0:T(8,128)(2,1)S(1)}, bf16[2,208,448]{2,1,0:T(8,128)(2,1)S(1)}, u32[]{:S(2)}, u32[]{:S(2)}) collective-permute-start(bf16[2,208,448]{2,1,0:T(8,128)(2,1)S(1)} %collective-permute-done.17.refs_2_), channel_id=1, source_target_pairs={{0,8},{8,0},{16,24},{24,16},{1,9},{9,1},{17,25},{25,17},{2,10},{10... | collective-permute-start | bytes 1118216 | tf_op jit(solution)/shard_map/ppermute | solution.py:359
  95.6 7.0 %copy-start.11 = (bf16[8,208,448]{2,1,0:T(8,128)(2,1)}, bf16[8,208,448]{2,1,0:T(8,128)(2,1)S(1)}, u32[]{:S(2)}) copy-start(bf16[8,208,448]{2,1,0:T(8,128)(2,1)S(1)} %get-tuple-element.114) | copy-start | bytes 4472836
  95.6 7.0 %copy-start.16 = (f32[8,208,448]{2,1,0:T(8,128)}, f32[8,208,448]{2,1,0:T(8,128)S(1)}, u32[]{:S(2)}) copy-start(f32[8,208,448]{2,1,0:T(8,128)S(1)} %get-tuple-element.107) | copy-start | bytes 8945668
  95.6 11.2 %collective-permute-start.19 = (bf16[208,896]{1,0:T(8,128)(2,1)S(1)}, bf16[208,896]{1,0:T(8,128)(2,1)S(1)}, u32[]{:S(2)}, u32[]{:S(2)}) collective-permute-start(bf16[208,896]{1,0:T(8,128)(2,1)S(1)} %add_convert_fusion.5), channel_id=1, source_target_pairs={{0,2},{2,4},{4,6},{6,7},{7,5},{5,3},{3,1},{1,0},{8,10},{10,12},{12... | collective-permute-start | bytes 1118216 | tf_op jit(solution)/shard_map/ppermute | solution.py:476
  97.2 10.8 %collective-permute-start.20 = (bf16[208,896]{1,0:T(8,128)(2,1)S(1)}, bf16[208,896]{1,0:T(8,128)(2,1)S(1)}, u32[]{:S(2)}, u32[]{:S(2)}) collective-permute-start(bf16[208,896]{1,0:T(8,128)(2,1)S(1)} %add_convert_fusion.4), channel_id=1, source_target_pairs={{0,1},{2,0},{4,2},{6,4},{7,6},{5,7},{3,5},{1,3},{8,9},{10,8},{12,1... | collective-permute-start | bytes 1118216 | tf_op jit(solution)/shard_map/ppermute | solution.py:477
  102.6 8.9 %copy-start.8 = (bf16[8,208,448]{2,1,0:T(8,128)(2,1)S(1)}, bf16[8,208,448]{2,1,0:T(8,128)(2,1)}, u32[]{:S(2)}) copy-start(bf16[8,208,448]{2,1,0:T(8,128)(2,1)} %copy-done.5) | copy-start | bytes 4472836
  108.9 2.6 %collective-permute-start.22 = (bf16[3,208,448]{2,1,0:T(8,128)(2,1)}, bf16[3,208,448]{2,1,0:T(8,128)(2,1)}, u32[]{:S(2)}, u32[]{:S(2)}) collective-permute-start(bf16[3,208,448]{2,1,0:T(8,128)(2,1)} %collective-permute-done.21.refs_2_), channel_id=1, source_target_pairs={{0,8},{8,0},{16,24},{24,16},{1,9},{9,1},{17,25},{25,17},{2,10},{10... | collective-permute-start | bytes 1677320 | tf_op jit(solution)/shard_map/ppermute | solution.py:359
  109.0 13.5 %collective-permute-start.25 = (bf16[8,208,448]{2,1,0:T(8,128)(2,1)}, bf16[8,208,448]{2,1,0:T(8,128)(2,1)S(1)}, u32[]{:S(2)}, u32[]{:S(2)}) collective-permute-start(bf16[8,208,448]{2,1,0:T(8,128)(2,1)} %copy-done.11), channel_id=1, source_target_pairs={{0,8},{8,0},{16,24},{24,16},{1,9},{9,1},{17,25},{25,17},{2,10},{10... | collective-permute-start | bytes 4472840 | tf_op jit(solution)/shard_map/ppermute | solution.py:359
  109.5 10.9 %collective-permute-start.23 = (bf16[208,896]{1,0:T(8,128)(2,1)}, bf16[208,896]{1,0:T(8,128)(2,1)S(1)}, u32[]{:S(2)}, u32[]{:S(2)}) collective-permute-start(bf16[208,896]{1,0:T(8,128)(2,1)} %add_convert_fusion.3), channel_id=1, source_target_pairs={{0,2},{2,4},{4,6},{6,7},{7,5},{5,3},{3,1},{1,0},{8,10},{10,12},{12... | collective-permute-start | bytes 1118216 | tf_op jit(solution)/shard_map/ppermute | solution.py:476
  111.0 10.6 %collective-permute-start.24 = (bf16[208,896]{1,0:T(8,128)(2,1)}, bf16[208,896]{1,0:T(8,128)(2,1)S(1)}, u32[]{:S(2)}, u32[]{:S(2)}) collective-permute-start(bf16[208,896]{1,0:T(8,128)(2,1)} %add_convert_fusion.2), channel_id=1, source_target_pairs={{0,1},{2,0},{4,2},{6,4},{7,6},{5,7},{3,5},{1,3},{8,9},{10,8},{12,1... | collective-permute-start | bytes 1118216 | tf_op jit(solution)/shard_map/ppermute | solution.py:477
  111.5 10.9 %copy-start.3 = (bf16[3,448,1664]{2,1,0:T(8,128)(2,1)S(1)}, bf16[3,448,1664]{2,1,0:T(8,128)(2,1)}, u32[]{:S(2)}) copy-start(bf16[3,448,1664]{2,1,0:T(8,128)(2,1)} %qkv.7) | copy-start | bytes 13418500
  111.5 10.9 %copy-start.17 = (f32[8,208,448]{2,1,0:T(8,128)S(1)}, f32[8,208,448]{2,1,0:T(8,128)}, u32[]{:S(2)}) copy-start(f32[8,208,448]{2,1,0:T(8,128)} %copy-done.16) | copy-start | bytes 8945668
  111.5 10.9 %copy-start.19 = (f32[13,256,256]{2,1,0:T(8,128)S(1)}, f32[13,256,256]{2,1,0:T(8,128)}, u32[]{:S(2)}) copy-start(f32[13,256,256]{2,1,0:T(8,128)} %copy-done.18) | copy-start | bytes 10223620
  117.6 4.8 %copy-start.21 = (f32[13,192,192]{2,1,0:T(8,128)S(1)}, f32[13,192,192]{2,1,0:T(8,128)}, u32[]{:S(2)}) copy-start(f32[13,192,192]{2,1,0:T(8,128)} %copy-done.20) | copy-start | bytes 5750788
  125.9 9.8 %collective-permute-start.26 = (bf16[208,896]{1,0:T(8,128)(2,1)}, bf16[208,896]{1,0:T(8,128)(2,1)}, u32[]{:S(2)}, u32[]{:S(2)}) collective-permute-start(bf16[208,896]{1,0:T(8,128)(2,1)} %add_convert_fusion.1), channel_id=1, source_target_pairs={{0,2},{2,4},{4,6},{6,7},{7,5},{5,3},{3,1},{1,0},{8,10},{10,12},{12... | collective-permute-start | bytes 1118216 | tf_op jit(solution)/shard_map/ppermute | solution.py:476
  127.4 9.5 %collective-permute-start.27 = (bf16[208,896]{1,0:T(8,128)(2,1)}, bf16[208,896]{1,0:T(8,128)(2,1)}, u32[]{:S(2)}, u32[]{:S(2)}) collective-permute-start(bf16[208,896]{1,0:T(8,128)(2,1)} %add_convert_fusion), channel_id=1, source_target_pairs={{0,1},{2,0},{4,2},{6,4},{7,6},{5,7},{3,5},{1,3},{8,9},{10,8},{12,1... | collective-permute-start | bytes 1118216 | tf_op jit(solution)/shard_map/ppermute | solution.py:477
  130.5 8.9 %copy-start.1 = (s32[4,1,4]{2,1,0:T(1,128)S(1)}, s32[4,1,4]{2,1,0:T(1,128)}, u32[]{:S(2)}) copy-start(s32[4,1,4]{2,1,0:T(1,128)} %param.9) | copy-start | bytes 196
  (2 other events, 2.0 us)

commit v2 on v1

--- a/solution.py
+++ b/solution.py
@@ -19,6 +19,10 @@
 
 def dot(left, right, left_dim, right_dim):
     return lax.dot_general(left, right, (((left_dim,), (right_dim,)), ((), ())), preferred_element_type=jnp.float32)
+
+
+def in_hbm(array):
+    return pltpu.with_memory_space_constraint(array, pltpu.HBM)
 
 
 def prepare_kernel(steps, width, starts, cotangent, layer_scale, scaled, turned, *windows):
@@ -63,7 +67,7 @@
         compiler_params=pltpu.CompilerParams(vmem_limit_bytes=VMEM_BYTES),
         cost_estimate=LONG,
         name="scaled_cotangent",
-    )(starts, cotangent, layer_scale.reshape(1, total))
+    )(starts, in_hbm(cotangent), layer_scale.reshape(1, total))
 
 
 def arrange_kernel(sizes, order, attended, *refs):
@@ -156,14 +160,14 @@
             ],
         ),
         out_shape=[
-            jax.ShapeDtypeStruct((width, rows), jnp.bfloat16),
-            jax.ShapeDtypeStruct((heads, MAIN, MAIN), jnp.float32),
-            jax.ShapeDtypeStruct((heads, 2 * SLOT, 2 * SLOT), jnp.float32),
+            pltpu.HBM((width, rows), jnp.bfloat16),
+            pltpu.HBM((heads, MAIN, MAIN), jnp.float32),
+            pltpu.HBM((heads, 2 * SLOT, 2 * SLOT), jnp.float32),
         ],
         compiler_params=pltpu.CompilerParams(vmem_limit_bytes=VMEM_BYTES),
         cost_estimate=LONG,
         name="attention_forward",
-    )(counts, qkv)
+    )(counts, in_hbm(qkv))
 
 
 def backward_kernel(qkv, grad_mine, grad_other, main_probs, slot_probs, *rest):
@@ -204,50 +208,53 @@
             pl.BlockSpec((PAIR, 2 * SLOT, 2 * SLOT), lambda h: (h + low, 0, 0)),
         ] + [pl.BlockSpec(memory_space=pl.ANY)] * len(held),
         out_specs=pl.BlockSpec((3, rows, PAIR * HS), lambda h: (0, 0, h + low)),
-        out_shape=jax.ShapeDtypeStruct(qkv.shape, jnp.bfloat16),
+        out_shape=pltpu.HBM(qkv.shape, jnp.bfloat16),
         input_output_aliases={5: 0} if held else {},
         compiler_params=pltpu.CompilerParams(vmem_limit_bytes=VMEM_BYTES),
         cost_estimate=LONG,
         name="attention_backward",
-    )(qkv, grad_mine, grad_other, main_probs, slot_probs, *held)
+    )(in_hbm(qkv), in_hbm(grad_mine), grad_other, in_hbm(main_probs), in_hbm(slot_probs), *map(in_hbm, held))
 
 
 def grad_out_kernel(sizes, split, total, info, turned, turned_other, *refs):
-    columns, sems = refs[-2:]
-    mine, other = refs[-4:-2]
-    step = pl.program_id(0)
+    mine, other, columns, tall, mine_rows, other_rows, in_sems, out_sems = refs[-8:]
+    count, depth, rows = mine_rows.shape
     core = info[0]
     at = pl.ds(pl.multiple_of(core * (total - split), LANE), split)
-    copies = [
-        pltpu.make_async_copy(source.at[at], columns.at[i], sems.at[i]) for i, source in enumerate((turned, turned_other))
+    loads = [
+        pltpu.make_async_copy(source.at[at], columns.at[i], in_sems.at[i]) for i, source in enumerate((turned, turned_other))
     ]
-
-    @pl.when(step == 0)
-    def _():
-        for copy in copies:
-            copy.start()
-        for copy in copies:
-            copy.wait()
-
-        @pl.when(core == 1)
-        def _():
-            shared = 2 * split - total
-            columns[:, :shared, :] = jnp.zeros((2, shared, columns.shape[2]), jnp.bfloat16)
-
     index = 0
     for j, size in enumerate(sizes):
-
-        @pl.when(step == j)
-        def _(index=index, size=size):
-            first = 0
-            for piece in refs[index:index + size]:
-                at = slice(first, first + piece.shape[0])
-                rows = mine.shape[2]
-                mine[0, at, :] = dot(piece[...], columns[0], 1, 0)[:, :rows]
-                other[0, at, :] = dot(piece[...], columns[1], 1, 0)[:, :rows].astype(jnp.bfloat16)
-                first += piece.shape[0]
-
+        first = 0
+        for piece in refs[index:index + size]:
+            target = tall.at[j] if size == 1 else tall.at[j, pl.ds(first, piece.shape[0])]
+            loads.append(pltpu.make_async_copy(piece, target, in_sems.at[len(loads)]))
+            first += piece.shape[0]
         index += size
+    for load in loads:
+        load.start()
+    for load in loads:
+        load.wait()
+
+    @pl.when(core == 1)
+    def _():
+        shared = 2 * split - total
+        columns[:, :shared, :] = jnp.zeros((2, shared, columns.shape[2]), jnp.bfloat16)
+
+    stores = []
+    for i, (result, out) in enumerate(((mine_rows, mine), (other_rows, other))):
+        if depth % 16 == 0:
+            product = dot(tall[...].reshape(count * depth, split), columns[i], 1, 0)[:, :rows]
+            result[...] = product.astype(result.dtype).reshape(count, depth, rows)
+        else:
+            for j in range(count):
+                result[j] = dot(tall[j], columns[i], 1, 0)[:, :rows].astype(result.dtype)
+        for j in range(count):
+            stores.append(pltpu.make_async_copy(result.at[j], out.at[info[1 + j]], out_sems.at[i, j]))
+            stores[-1].start()
+    for store in stores:
+        store.wait()
 
 
 def grad_out_rows(info, turned, turned_other, rows, pieces, shards, held):
@@ -256,27 +263,83 @@
     depth = sum(p.shape[0] for p in pieces[0])
     sizes = [len(p) for p in pieces]
     arrays = [a for p in pieces for a in p]
+    count = len(pieces)
     held = [] if held is None else list(held)
     return pl.pallas_call(
         functools.partial(grad_out_kernel, sizes, split, total),
         grid_spec=pltpu.PrefetchScalarGridSpec(
             num_scalar_prefetch=1,
-            grid=(len(pieces),),
-            in_specs=[pl.BlockSpec(memory_space=pl.ANY)] * 2
-            + [pl.BlockSpec(a.shape, lambda j, info: (0, 0)) for a in arrays]
-            + [pl.BlockSpec(memory_space=pl.ANY)] * len(held),
-            out_specs=[pl.BlockSpec((1, depth, rows), lambda j, info: (info[1 + j], 0, 0))] * 2,
-            scratch_shapes=[pltpu.VMEM((2, split, lanes), jnp.bfloat16), pltpu.SemaphoreType.DMA((2,))],
+            grid=(1,),
+            in_specs=[pl.BlockSpec(memory_space=pl.ANY)] * (2 + len(arrays) + len(held)),
+            out_specs=[pl.BlockSpec(memory_space=pl.ANY)] * 2,
+            scratch_shapes=[
+                pltpu.VMEM((2, split, lanes), jnp.bfloat16),
+                pltpu.VMEM((count, depth, split), jnp.bfloat16),
+                pltpu.VMEM((count, depth, rows), jnp.float32),
+                pltpu.VMEM((count, depth, rows), jnp.bfloat16),
+                pltpu.SemaphoreType.DMA((2 + len(arrays),)),
+                pltpu.SemaphoreType.DMA((2, count)),
+            ],
         ),
         out_shape=[
-            jax.ShapeDtypeStruct((shards, depth, rows), jnp.float32),
-            jax.ShapeDtypeStruct((shards, depth, rows), jnp.bfloat16),
+            pltpu.HBM((shards, depth, rows), jnp.float32),
+            pltpu.HBM((shards, depth, rows), jnp.bfloat16),
         ],
         input_output_aliases={3 + len(arrays) + i: i for i in range(len(held))},
         compiler_params=pltpu.CompilerParams(vmem_limit_bytes=VMEM_BYTES),
         cost_estimate=LONG,
         name="grad_out_rows",
-    )(info, turned, turned_other, *arrays, *held)
+    )(info, turned, turned_other, *arrays, *map(in_hbm, held))
+
+
+def half_kernel(starts, weight, out, sem):
+    copy = pltpu.make_async_copy(weight.at[:, pl.ds(pl.multiple_of(starts[0], LANE), out.shape[1])], out, sem)
+    copy.start()
+    copy.wait()
+
+
+def half_columns(start, weight, width):
+    return pl.pallas_call(
+        half_kernel,
+        grid_spec=pltpu.PrefetchScalarGridSpec(
+            num_scalar_prefetch=1,
+            grid=(1,),
+            in_specs=[pl.BlockSpec(memory_space=pl.ANY)],
+            out_specs=pl.BlockSpec(memory_space=pl.ANY),
+            scratch_shapes=[pltpu.SemaphoreType.DMA],
+        ),
+        out_shape=jax.ShapeDtypeStruct((weight.shape[0], width), weight.dtype),
+        compiler_params=pltpu.CompilerParams(vmem_limit_bytes=VMEM_BYTES),
+        cost_estimate=SHORT,
+        name="own_half_of_weight",
+    )(start, weight)
+
+
+def finish_kernel(offsets, start, term, came_up, came_down, out):
+    total = term[...] + came_up[...].astype(jnp.float32) + came_down[...].astype(jnp.float32)
+    for offset in offsets:
+
+        @pl.when(start[0] == offset)
+        def _():
+            out[...] = total[:, offset:offset + out.shape[1]]
+
+
+def finish(start, term, came_up, came_down, owned, offsets):
+    depth, window = term.shape
+    block = pl.BlockSpec((depth, window), lambda i, s: (0, 0))
+    return pl.pallas_call(
+        functools.partial(finish_kernel, offsets),
+        grid_spec=pltpu.PrefetchScalarGridSpec(
+            num_scalar_prefetch=1,
+            grid=(1,),
+            in_specs=[block] * 3,
+            out_specs=pl.BlockSpec((depth, owned), lambda i, s: (0, 0)),
+        ),
+        out_shape=jax.ShapeDtypeStruct((depth, owned), jnp.float32),
+        compiler_params=pltpu.CompilerParams(vmem_limit_bytes=VMEM_BYTES),
+        cost_estimate=SHORT,
+        name="last_sum",
+    )(start, term, came_up, came_down)
 
 
 def partial_kernel(sources, count, window, order, starts, *refs):
@@ -374,7 +437,7 @@
     starts = table([my_start, my_start - chip_start(chip)])
 
     split = -(-(total // LANE) // 2) * LANE
-    mine = jnp.where(core == 0, proj_weight[:, :split], proj_weight[:, total - split:])
+    mine = half_columns(table([core * (total - split)]), proj_weight, split)
     cut = -(-depth // 32) * 16
     up, down = [mine], [mine]
     up.append(lax.ppermute(up[-1], "fsdp", ahead))
@@ -419,8 +482,7 @@
     up.append(lax.ppermute(up[-1], "fsdp", ahead))
     down.append(lax.ppermute(down[-1], "fsdp", behind))
     up[-1], down[-1], grad_out, both[1] = lax.optimization_barrier((up[-1], down[-1], grad_out, both[1]))
-    came[0], near_up, near_down, chunks = lax.optimization_barrier((came[0], up[-1], down[-1], chunks))
-    came += [[swap(some, 2 * k) for k in range(1, peers)] for some in chunks[2:]]
+    came[0], near_up, near_down = lax.optimization_barrier((came[0], up[-1], down[-1]))
     far_up = lax.ppermute(up[-1][:cut], "fsdp", ahead)
     far_down = lax.ppermute(down[-1][cut:], "fsdp", behind)
 
@@ -433,7 +495,8 @@
 
     terms = products(0)
     first = terms[half].astype(jnp.bfloat16)
-    far_up, far_down, terms = lax.optimization_barrier((far_up, far_down, terms))
+    far_up, far_down, terms, chunks = lax.optimization_barrier((far_up, far_down, terms, chunks))
+    came += [[swap(some, 2 * k) for k in range(1, peers)] for some in chunks[2:]]
     going_up, going_down = first[:cut], first[cut:]
     came_up = lax.ppermute(going_up, "fsdp", ahead)
     came_down = lax.ppermute(going_down, "fsdp", behind)
@@ -477,8 +540,11 @@
         came_down = lax.ppermute(going_down, "fsdp", behind)
     grads = back(2, back(1, grads))
     came_up, came_down, grads = lax.optimization_barrier((came_up, came_down, grads))
-    reduced = terms[0] + came_up.astype(jnp.float32) + came_down.astype(jnp.float32)
-    grad_proj = lax.dynamic_slice_in_dim(reduced, member * owned - my_start, owned, 1)
+    offsets = set()
+    for m in range(members):
+        low = min((m // 2) * 2 * owned // LANE * LANE, total - chip_width)
+        offsets.add(m * owned - min(m * owned // LANE * LANE, low + chip_width - window))
+    grad_proj = finish(table([member * owned - my_start]), terms[0], came_up, came_down, owned, sorted(offsets))
     return grads, grad_proj
 
 

time: 140 us -> 139 us (level)
  Pallas kernels: 54.3 us -> 65.6 us
  local copies, waits for them, and re-layouts: 15.9 us -> 10.1 us
  other arithmetic: 8.48 us -> 3.81 us
  waiting for transfers between devices: 37 us -> 34.6 us
    unnamed x44 -> x30, local copies, waits for them, and re-layouts: 14.9 us -> 9.16 us
    pallas_call x3, Pallas kernels: 8.46 us -> 13.5 us  [backward(): pl.pallas_call(backward_kernel, grid=(high - low,), in_specs=[pl.BlockSpe...]
    ppermute x3, waiting for transfers between devices: 14.1 us -> 10.4 us  [local(): up.append(lax.ppermute(up[-1], 'fsdp', ahead))]
    ppermute x12, waiting for transfers between devices: 4.45 us -> 8.01 us  [swap(): return lax.ppermute(array, 'dp', [(i, i ^ bit) for i in range(members)])]
    pallas_call x0 -> x2, Pallas kernels: none -> 3.07 us  [the longest x1 2.21 us: finish(): pl.pallas_call(functools.partial(finish_kernel, offsets), grid_spec=pltpu...]
    add x1 -> x0, other arithmetic: 2.43 us -> none  [local(): terms[0] + came_up.astype(jnp.float32) + came_down.astype(jnp.float32)]
    pallas_call x1, Pallas kernels: 7.26 us -> 9.63 us  [forward(): pl.pallas_call(forward_kernel, grid_spec=pltpu.PrefetchScalarGridSpec(num...]
    select_n x1 -> x0, other arithmetic: 2.24 us -> none  [local(): jnp.where(core == 0, proj_weight[:, :split], proj_weight[:, total - split:])]
  transfers between devices with their start and end apart: 28 -> 28, of which waited for: 14 -> 15; matrix products, arithmetic and copies ran while one was open for 3% -> 3% of each run, Pallas kernels for 37% -> 41%
where the time goes in v2:
time: 139 us; the launch traced here: 138 us
  Pallas kernels  65.6 us (47%)
  waiting for transfers between devices  34.6 us (25%)
  starting transfers between devices  22.9 us (16%)
  local copies, waits for them, and re-layouts  10.1 us (7%)
  other arithmetic  3.81 us (3%)
    pallas_call x3, Pallas kernels, partial_products(): pl.pallas_call(functools.partial(partial_kernel, sources, count, window),...  16.3 us
    pallas_call x2, Pallas kernels, grad_out_rows(): pl.pallas_call(functools.partial(grad_out_kernel, sizes, split, total), g...  14.1 us
    pallas_call x3, Pallas kernels, backward(): pl.pallas_call(backward_kernel, grid=(high - low,), in_specs=[pl.BlockSpe...  13.5 us
    ppermute x3, waiting for transfers between devices, local(): up.append(lax.ppermute(up[-1], 'fsdp', ahead))  10.4 us
    ppermute x4, waiting for transfers between devices, local(): came_up = lax.ppermute(going_up, 'fsdp', ahead)  9.8 us
    pallas_call x1, Pallas kernels, forward(): pl.pallas_call(forward_kernel, grid_spec=pltpu.PrefetchScalarGridSpec(num...  9.63 us
    unnamed x30, local copies, waits for them, and re-layouts  9.16 us
    ppermute x12, waiting for transfers between devices, swap(): return lax.ppermute(array, 'dp', [(i, i ^ bit) for i in range(members)])  8.01 us
  transfers between devices with their start and end apart: 28, of which 15 were waited for; matrix products, arithmetic and copies ran while one was open for 3% of the time, Pallas kernels for 41%

profile of v2, /device:TPU:0, one launch (start us, length us, event | category | flops | bytes accessed | tf_op | source)
XLA Modules:
  0.0 137.9 jit_solution(14775712487744560464)
XLA Ops:
  0.7 1.3 copy-done.4
  2.0 0.9 own_half_of_weight.1.refs_0_
  2.8 3.1 %collective-permute-start = (bf16[208,1664]{1,0:T(8,128)(2,1)}, bf16[208,1664]{1,0:T(8,128)(2,1)}, u32[]{:S(2)}, u32[]{:S(2)}) collective-permute-start(bf16[208,1664]{1,0:T(8,128)(2,1)} %own_half_of_weight.1.refs_0_), channel_id=1, source_target_pairs={{0,2},{2,4},{4,6},{6,7},{7,5},{5,3},{3,1},{1,0},{8,10},{10,12},{12... | collective-permute-start | bytes 2076680 | tf_op jit(solution)/shard_map/ppermute | solution.py:443
  5.9 0.7 reshape.19.layer_scale
  6.7 6.1 %scaled_cotangent.1 = (bf16[448,3200]{1,0:T(8,128)(2,1)}, bf16[3200,512]{1,0:T(8,128)(2,1)S(1)}, bf16[448,1664]{1,0:T(8,128)(2,1)}) custom-call(s32[1]{0:T(128)} %bitcast.8.starts, bf16[448,3200]{1,0:T(8,128)(2,1)} %cotangent, f32[1,3200]{1,0:T(1,128)S(1)} %reshape.19.layer_scale), custom_call_target="tpu_custom_call" | custom-call | flops 99999997952 | bytes 100000000 | tf_op jit(solution)/shard_map/scaled_cotangent/pallas_call | solution.py:47
  13.3 1.9 %collective-permute-start.8 = (bf16[448,1664]{1,0:T(8,128)(2,1)}, bf16[448,1664]{1,0:T(8,128)(2,1)}, u32[]{:S(2)}, u32[]{:S(2)}) collective-permute-start(bf16[448,1664]{1,0:T(8,128)(2,1)} %get-tuple-element.74), channel_id=1, source_target_pairs={{0,16},{8,24},{16,0},{24,8},{1,17},{9,25},{17,1},{25,9},{2,18},{10... | collective-permute-start | bytes 4472840 | tf_op jit(solution)/shard_map/ppermute | solution.py:422
  15.3 9.6 %attention_forward.1 = (bf16[1664,448]{1,0:T(8,128)(2,1)}, f32[13,256,256]{2,1,0:T(8,128)}, f32[13,192,192]{2,1,0:T(8,128)}) custom-call(s32[4]{0:T(128)S(1)} %dynamic-slice_bitcast_fusion.counts, bf16[3,448,1664]{2,1,0:T(8,128)(2,1)} %qkv.7), custom_call_target="tpu_custom_call" | custom-call | flops 99999997952 | bytes 100000000 | tf_op jit(solution)/shard_map/attention_forward/pallas_call | solution.py:150
  24.9 1.6 %collective-permute-start.2 = (bf16[208,1664]{1,0:T(8,128)(2,1)}, bf16[208,1664]{1,0:T(8,128)(2,1)}, u32[]{:S(2)}, u32[]{:S(2)}) collective-permute-start(bf16[208,1664]{1,0:T(8,128)(2,1)} %collective-permute-done.refs_1_), channel_id=1, source_target_pairs={{0,2},{2,4},{4,6},{6,7},{7,5},{5,3},{3,1},{1,0},{8,10},{10,12},{12... | collective-permute-start | bytes 2076680 | tf_op jit(solution)/shard_map/ppermute | solution.py:470
  27.1 1.5 %copy-done.2 = bf16[1664,448]{1,0:T(8,128)(2,1)S(1)} copy-done((bf16[1664,448]{1,0:T(8,128)(2,1)S(1)}, bf16[1664,448]{1,0:T(8,128)(2,1)}, u32[]{:S(2)}) %copy-start.2) | copy-done | bytes 1490968
  28.5 2.8 %attended_chunks.1 = (bf16[3,208,448]{2,1,0:T(8,128)(2,1)S(1)}, bf16[2,208,448]{2,1,0:T(8,128)(2,1)S(1)}, bf16[3,208,448]{2,1,0:T(8,128)(2,1)}) custom-call(s32[8]{0:T(128)S(1)} %stack.85.order, bf16[8,208,448]{2,1,0:T(8,128)(2,1)S(1)} %bitcast.20), custom_call_target="tpu_custom_call" | custom-call | flops 1000 | bytes 1000 | tf_op jit(solution)/shard_map/attended_chunks/pallas_call | solution.py:88
  31.4 0.9 copy-done.12
  32.2 0.8 copy-done.13
  33.1 9.3 %collective-permute-done.2.refs_3_ = bf16[208,1664]{1,0:T(8,128)(2,1)} collective-permute-done((bf16[208,1664]{1,0:T(8,128)(2,1)}, bf16[208,1664]{1,0:T(8,128)(2,1)}, u32[]{:S(2)}, u32[]{:S(2)}) %collective-permute-start.2) | collective-permute-done | bytes 692256 | tf_op jit(solution)/shard_map/ppermute | solution.py:470
  42.7 1.0 collective-permute-done.3.refs_4_
  43.7 1.6 %collective-permute-start.6 = (bf16[208,1664]{1,0:T(8,128)(2,1)}, bf16[208,1664]{1,0:T(8,128)(2,1)S(1)}, u32[]{:S(2)}, u32[]{:S(2)}) collective-permute-start(bf16[208,1664]{1,0:T(8,128)(2,1)} %collective-permute-done.2.refs_3_), channel_id=1, source_target_pairs={{0,2},{2,4},{4,6},{6,7},{7,5},{5,3},{3,1},{1,0},{8,10},{10,12},{12... | collective-permute-start | bytes 2076680 | tf_op jit(solution)/shard_map/ppermute | solution.py:482
  45.8 3.3 %collective-permute-done.8.refs_6_ = bf16[448,1664]{1,0:T(8,128)(2,1)} collective-permute-done((bf16[448,1664]{1,0:T(8,128)(2,1)}, bf16[448,1664]{1,0:T(8,128)(2,1)}, u32[]{:S(2)}, u32[]{:S(2)}) %collective-permute-start.8) | collective-permute-done | bytes 1490976 | tf_op jit(solution)/shard_map/ppermute | solution.py:422
  49.1 2.1 %copy-done.6 = bf16[3200,512]{1,0:T(8,128)(2,1)S(1)} copy-done((bf16[3200,512]{1,0:T(8,128)(2,1)S(1)}, bf16[3200,512]{1,0:T(8,128)(2,1)}, u32[]{:S(2)}) %copy-start.6) | copy-done | bytes 3276824
  51.2 8.4 %grad_out_rows.2 = (f32[8,208,448]{2,1,0:T(8,128)}, bf16[8,208,448]{2,1,0:T(8,128)(2,1)}) custom-call(s32[6]{0:T(128)S(1)} %stack.81.info, bf16[3200,512]{1,0:T(8,128)(2,1)S(1)} %copy-done.6, bf16[3200,512]{1,0:T(8,128)(2,1)} %collective-permute-done.5.turned_other, bf16[208,1664]{1,0:T(8,128)(2,1)} %own_half_of_weight.1.refs_0_, ...), custom_call_target="tpu_custom_call" | custom-call | flops 99999997952 | bytes 100000000 | tf_op jit(solution)/shard_map/grad_out_rows/pallas_call | solution.py:268
  59.6 1.2 copy-done.8
  60.9 1.0 collective-permute-done.6.refs_0_
  61.9 1.3 collective-permute-done.7.refs_1_
  63.4 1.6 %collective-permute-start.10 = (bf16[112,1664]{1,0:T(8,128)(2,1)S(1)}, bf16[112,1664]{1,0:T(8,128)(2,1)S(1)}, u32[]{:S(2)}, u32[]{:S(2)}) collective-permute-start(bf16[112,1664]{1,0:T(8,128)(2,1)S(1)} %slice.18), channel_id=1, source_target_pairs={{0,2},{2,4},{4,6},{6,7},{7,5},{5,3},{3,1},{1,0},{8,10},{10,12},{12... | collective-permute-start | bytes 1118216 | tf_op jit(solution)/shard_map/ppermute | solution.py:486
  65.6 1.5 %copy-done.9 = bf16[8,208,448]{2,1,0:T(8,128)(2,1)S(1)} copy-done((bf16[8,208,448]{2,1,0:T(8,128)(2,1)S(1)}, bf16[8,208,448]{2,1,0:T(8,128)(2,1)}, u32[]{:S(2)}) %copy-start.9) | copy-done | bytes 1490968
  67.1 5.7 %projection_partial.3 = (f32[208,896]{1,0:T(8,128)S(1)}, f32[208,896]{1,0:T(8,128)S(1)}, f32[208,896]{1,0:T(8,128)S(1)}) custom-call(s32[3]{0:T(128)S(1)} %pad_add_fusion.3.order, s32[2]{0:T(128)S(1)} %pad_add_fusion.1.starts, bf16[8,208,448]{2,1,0:T(8,128)(2,1)S(1)} %bitcast.21, bf16[8,208,448]{2,1,0:T(8,128)(2,1)S(1)} %copy-done.9, ...), custom_call_target="tpu_custom_call" | custom-call | flops 99999997952 | bytes 100000000 | tf_op jit(solution)/shard_map/projection_partial/pallas_call | solution.py:377
  72.8 0.7 collective-permute-start.16
  73.7 1.5 %collective-permute-start.17 = (bf16[2,208,448]{2,1,0:T(8,128)(2,1)S(1)}, bf16[2,208,448]{2,1,0:T(8,128)(2,1)S(1)}, u32[]{:S(2)}, u32[]{:S(2)}) collective-permute-start(bf16[2,208,448]{2,1,0:T(8,128)(2,1)S(1)} %copy-done.14), channel_id=1, source_target_pairs={{0,16},{8,24},{16,0},{24,8},{1,17},{9,25},{17,1},{25,9},{2,18},{10... | collective-permute-start | bytes 1118216 | tf_op jit(solution)/shard_map/ppermute | solution.py:422
  75.2 1.0 collective-permute-start.15
  76.2 1.0 collective-permute-start.21
  77.2 2.1 %collective-permute-done.16 = bf16[96,896]{1,0:T(8,128)(2,1)S(1)} collective-permute-done((bf16[96,896]{1,0:T(8,128)(2,1)S(1)}, bf16[96,896]{1,0:T(8,128)(2,1)S(1)}, u32[]{:S(2)}, u32[]{:S(2)}) %collective-permute-start.16) | collective-permute-done | bytes 172064 | tf_op jit(solution)/shard_map/ppermute | solution.py:502
  79.4 2.4 %collective-permute-done.15 = bf16[112,896]{1,0:T(8,128)(2,1)S(1)} collective-permute-done((bf16[112,896]{1,0:T(8,128)(2,1)S(1)}, bf16[112,896]{1,0:T(8,128)(2,1)S(1)}, u32[]{:S(2)}, u32[]{:S(2)}) %collective-permute-start.15) | collective-permute-done | bytes 200736 | tf_op jit(solution)/shard_map/ppermute | solution.py:501
  81.8 4.6 %collective-permute-done.17.refs_2_ = bf16[2,208,448]{2,1,0:T(8,128)(2,1)S(1)} collective-permute-done((bf16[2,208,448]{2,1,0:T(8,128)(2,1)S(1)}, bf16[2,208,448]{2,1,0:T(8,128)(2,1)S(1)}, u32[]{:S(2)}, u32[]{:S(2)}) %collective-permute-start.17) | collective-permute-done | bytes 372768 | tf_op jit(solution)/shard_map/ppermute | solution.py:422
  86.4 5.7 %grad_out_rows.3 = (f32[8,208,448]{2,1,0:T(8,128)}, bf16[8,208,448]{2,1,0:T(8,128)(2,1)}) custom-call(s32[4]{0:T(128)S(1)} %pad_add_fusion.4.info, bf16[3200,512]{1,0:T(8,128)(2,1)S(1)} %copy-done.7, bf16[3200,512]{1,0:T(8,128)(2,1)} %collective-permute-done.5.turned_other, ...), custom_call_target="tpu_custom_call", output_to_operand_aliasing={{0}: (7, {}), {1}: (8, {})} | custom-call | flops 99999997952 | bytes 100000000 | tf_op jit(solution)/shard_map/grad_out_rows/pallas_call | solution.py:268
  92.1 1.4 %collective-permute-start.19 = (bf16[208,896]{1,0:T(8,128)(2,1)S(1)}, bf16[208,896]{1,0:T(8,128)(2,1)S(1)}, u32[]{:S(2)}, u32[]{:S(2)}) collective-permute-start(bf16[208,896]{1,0:T(8,128)(2,1)S(1)} %add_convert_fusion.5), channel_id=1, source_target_pairs={{0,2},{2,4},{4,6},{6,7},{7,5},{5,3},{3,1},{1,0},{8,10},{10,12},{12... | collective-permute-start | bytes 1118216 | tf_op jit(solution)/shard_map/ppermute | solution.py:539
  94.2 4.9 %projection_partial.4 = (f32[208,896]{1,0:T(8,128)S(1)}, f32[208,896]{1,0:T(8,128)S(1)}) custom-call(s32[2]{0:T(128)S(1)} %pad_add_fusion.2.order, s32[2]{0:T(128)S(1)} %pad_add_fusion.1.starts, bf16[8,208,448]{2,1,0:T(8,128)(2,1)S(1)} %bitcast.22, bf16[8,208,448]{2,1,0:T(8,128)(2,1)S(1)} %copy-done.10, ...), custom_call_target="tpu_custom_call" | custom-call | flops 99999997952 | bytes 100000000 | tf_op jit(solution)/shard_map/projection_partial/pallas_call | solution.py:377
  99.1 4.1 %collective-permute-done.19 = bf16[208,896]{1,0:T(8,128)(2,1)S(1)} collective-permute-done((bf16[208,896]{1,0:T(8,128)(2,1)S(1)}, bf16[208,896]{1,0:T(8,128)(2,1)S(1)}, u32[]{:S(2)}, u32[]{:S(2)}) %collective-permute-start.19) | collective-permute-done | bytes 372768 | tf_op jit(solution)/shard_map/ppermute | solution.py:539
  103.3 0.8 add_convert_fusion.3
  104.4 0.8 add_convert_fusion.2
  105.8 1.5 %collective-permute-start.23 = (bf16[208,896]{1,0:T(8,128)(2,1)}, bf16[208,896]{1,0:T(8,128)(2,1)S(1)}, u32[]{:S(2)}, u32[]{:S(2)}) collective-permute-start(bf16[208,896]{1,0:T(8,128)(2,1)} %add_convert_fusion.3), channel_id=1, source_target_pairs={{0,2},{2,4},{4,6},{6,7},{7,5},{5,3},{3,1},{1,0},{8,10},{10,12},{12... | collective-permute-start | bytes 1118216 | tf_op jit(solution)/shard_map/ppermute | solution.py:539
  107.8 5.7 %projection_partial.5 = (f32[208,896]{1,0:T(8,128)S(1)}, f32[208,896]{1,0:T(8,128)S(1)}, f32[208,896]{1,0:T(8,128)S(1)}) custom-call(s32[3]{0:T(128)S(1)} %pad_add_fusion.order, s32[2]{0:T(128)S(1)} %pad_add_fusion.1.starts, bf16[8,208,448]{2,1,0:T(8,128)(2,1)S(1)} %bitcast.23, bf16[8,208,448]{2,1,0:T(8,128)(2,1)S(1)} %copy-done.11, ...), custom_call_target="tpu_custom_call" | custom-call | flops 99999997952 | bytes 100000000 | tf_op jit(solution)/shard_map/projection_partial/pallas_call | solution.py:377
  113.5 3.1 %collective-permute-done.23 = bf16[208,896]{1,0:T(8,128)(2,1)S(1)} collective-permute-done((bf16[208,896]{1,0:T(8,128)(2,1)}, bf16[208,896]{1,0:T(8,128)(2,1)S(1)}, u32[]{:S(2)}, u32[]{:S(2)}) %collective-permute-start.23) | collective-permute-done | bytes 372768 | tf_op jit(solution)/shard_map/ppermute | solution.py:539
  116.7 0.8 add_convert_fusion.1
  117.9 0.8 add_convert_fusion
  118.8 5.9 %attention_backward.3.rest_0_ = bf16[3,448,1664]{2,1,0:T(8,128)(2,1)} custom-call(bf16[3,448,1664]{2,1,0:T(8,128)(2,1)} %qkv.7, f32[1664,448]{1,0:T(8,128)} %bitcast.27, bf16[1664,448]{1,0:T(8,128)(2,1)S(1)} %bitcast.24, f32[13,256,256]{2,1,0:T(8,128)} %get-tuple-element.115.main_probs, f32[13,192,192]{2,1,0:T(8,128)} %get-tuple-element.116.slot_probs), custom_call_target="tpu_custom_call" | custom-call | flops 99999997952 | bytes 100000000 | tf_op jit(solution)/shard_map/attention_backward/pallas_call | solution.py:200
  124.6 1.5 %collective-permute-start.26 = (bf16[208,896]{1,0:T(8,128)(2,1)}, bf16[208,896]{1,0:T(8,128)(2,1)}, u32[]{:S(2)}, u32[]{:S(2)}) collective-permute-start(bf16[208,896]{1,0:T(8,128)(2,1)} %add_convert_fusion.1), channel_id=1, source_target_pairs={{0,2},{2,4},{4,6},{6,7},{7,5},{5,3},{3,1},{1,0},{8,10},{10,12},{12... | collective-permute-start | bytes 1118216 | tf_op jit(solution)/shard_map/ppermute | solution.py:539
  126.7 3.9 %attention_backward.4.rest_0_ = bf16[3,448,1664]{2,1,0:T(8,128)(2,1)} custom-call(bf16[3,448,1664]{2,1,0:T(8,128)(2,1)} %qkv.7, f32[1664,448]{1,0:T(8,128)} %bitcast.28, bf16[1664,448]{1,0:T(8,128)(2,1)S(1)} %bitcast.25, f32[13,256,256]{2,1,0:T(8,128)} %get-tuple-element.115.main_probs, ...), custom_call_target="tpu_custom_call", output_to_operand_aliasing={{}: (5, {})} | custom-call | flops 99999997952 | bytes 100000000 | tf_op jit(solution)/shard_map/attention_backward/pallas_call | solution.py:200
  130.5 3.8 %attention_backward.5 = bf16[3,448,1664]{2,1,0:T(8,128)(2,1)} custom-call(bf16[3,448,1664]{2,1,0:T(8,128)(2,1)} %qkv.7, f32[1664,448]{1,0:T(8,128)} %bitcast.29, bf16[1664,448]{1,0:T(8,128)(2,1)S(1)} %bitcast.26, f32[13,256,256]{2,1,0:T(8,128)} %get-tuple-element.115.main_probs, ...), custom_call_target="tpu_custom_call", output_to_operand_aliasing={{}: (5, {})} | custom-call | flops 99999997952 | bytes 100000000 | tf_op jit(solution)/shard_map/attention_backward/pallas_call | solution.py:200
  134.4 1.3 collective-permute-done.27.came_down
  135.7 2.2 %last_sum.1 = f32[208,800]{1,0:T(8,128)} custom-call(s32[1]{0:T(128)} %bitcast.17.start, f32[208,896]{1,0:T(8,128)S(1)} %get-tuple-element.121.term, bf16[208,896]{1,0:T(8,128)(2,1)} %collective-permute-done.26.came_up, bf16[208,896]{1,0:T(8,128)(2,1)} %collective-permute-done.27.came_down), custom_call_target="tpu_custom_call" | custom-call | flops 1000 | bytes 1000 | tf_op jit(solution)/shard_map/last_sum/pallas_call | solution.py:330
  (71 shorter events, 6.2 us)
Async XLA Ops:
  0.6 14.6 %copy-start = (s32[4,1,4]{2,1,0:T(1,128)S(1)}, s32[4,1,4]{2,1,0:T(1,128)}, u32[]{:S(2)}) copy-start(s32[4,1,4]{2,1,0:T(1,128)} %param.9) | copy-start | bytes 196
  0.7 1.3 copy-start.4
  2.8 22.0 %collective-permute-start = (bf16[208,1664]{1,0:T(8,128)(2,1)}, bf16[208,1664]{1,0:T(8,128)(2,1)}, u32[]{:S(2)}, u32[]{:S(2)}) collective-permute-start(bf16[208,1664]{1,0:T(8,128)(2,1)} %own_half_of_weight.1.refs_0_), channel_id=1, source_target_pairs={{0,2},{2,4},{4,6},{6,7},{7,5},{5,3},{3,1},{1,0},{8,10},{10,12},{12... | collective-permute-start | bytes 2076680 | tf_op jit(solution)/shard_map/ppermute | solution.py:443
  5.9 19.0 %collective-permute-start.1 = (bf16[208,1664]{1,0:T(8,128)(2,1)}, bf16[208,1664]{1,0:T(8,128)(2,1)}, u32[]{:S(2)}, u32[]{:S(2)}) collective-permute-start(bf16[208,1664]{1,0:T(8,128)(2,1)} %own_half_of_weight.1.refs_0_), channel_id=1, source_target_pairs={{0,1},{2,0},{4,2},{6,4},{7,6},{5,7},{3,5},{1,3},{8,9},{10,8},{12,1... | collective-permute-start | bytes 2076680 | tf_op jit(solution)/shard_map/ppermute | solution.py:444
  12.8 12.1 %copy-start.5 = (bf16[3200,512]{1,0:T(8,128)(2,1)}, bf16[3200,512]{1,0:T(8,128)(2,1)S(1)}, u32[]{:S(2)}) copy-start(bf16[3200,512]{1,0:T(8,128)(2,1)S(1)} %get-tuple-element.69.turned) | copy-start | bytes 9830404
  12.8 30.9 %collective-permute-start.4 = (bf16[448,3200]{1,0:T(8,128)(2,1)}, bf16[448,3200]{1,0:T(8,128)(2,1)}, u32[]{:S(2)}, u32[]{:S(2)}) collective-permute-start(bf16[448,3200]{1,0:T(8,128)(2,1)} %get-tuple-element.68.refs_4_), channel_id=1, source_target_pairs={{0,8},{8,0},{16,24},{24,16},{1,9},{9,1},{17,25},{25,17},{2,10},{10... | collective-permute-start | bytes 8601608 | tf_op jit(solution)/shard_map/ppermute | solution.py:422
  12.8 30.9 %collective-permute-start.5 = (bf16[3200,512]{1,0:T(8,128)(2,1)S(1)}, bf16[3200,512]{1,0:T(8,128)(2,1)}, u32[]{:S(2)}, u32[]{:S(2)}) collective-permute-start(bf16[3200,512]{1,0:T(8,128)(2,1)S(1)} %get-tuple-element.69.turned), channel_id=1, source_target_pairs={{0,8},{8,0},{16,24},{24,16},{1,9},{9,1},{17,25},{25,17},{2,10},{10... | collective-permute-start | bytes 9830408 | tf_op jit(solution)/shard_map/ppermute | solution.py:422
  13.3 35.8 %collective-permute-start.8 = (bf16[448,1664]{1,0:T(8,128)(2,1)}, bf16[448,1664]{1,0:T(8,128)(2,1)}, u32[]{:S(2)}, u32[]{:S(2)}) collective-permute-start(bf16[448,1664]{1,0:T(8,128)(2,1)} %get-tuple-element.74), channel_id=1, source_target_pairs={{0,16},{8,24},{16,0},{24,8},{1,17},{9,25},{17,1},{25,9},{2,18},{10... | collective-permute-start | bytes 4472840 | tf_op jit(solution)/shard_map/ppermute | solution.py:422
  24.9 17.5 %collective-permute-start.2 = (bf16[208,1664]{1,0:T(8,128)(2,1)}, bf16[208,1664]{1,0:T(8,128)(2,1)}, u32[]{:S(2)}, u32[]{:S(2)}) collective-permute-start(bf16[208,1664]{1,0:T(8,128)(2,1)} %collective-permute-done.refs_1_), channel_id=1, source_target_pairs={{0,2},{2,4},{4,6},{6,7},{7,5},{5,3},{3,1},{1,0},{8,10},{10,12},{12... | collective-permute-start | bytes 2076680 | tf_op jit(solution)/shard_map/ppermute | solution.py:470
  26.5 17.2 %collective-permute-start.3 = (bf16[208,1664]{1,0:T(8,128)(2,1)}, bf16[208,1664]{1,0:T(8,128)(2,1)}, u32[]{:S(2)}, u32[]{:S(2)}) collective-permute-start(bf16[208,1664]{1,0:T(8,128)(2,1)} %collective-permute-done.1.refs_2_), channel_id=1, source_target_pairs={{0,1},{2,0},{4,2},{6,4},{7,6},{5,7},{3,5},{1,3},{8,9},{10,8},{12,1... | collective-permute-start | bytes 2076680 | tf_op jit(solution)/shard_map/ppermute | solution.py:471
  27.1 1.5 %copy-start.2 = (bf16[1664,448]{1,0:T(8,128)(2,1)S(1)}, bf16[1664,448]{1,0:T(8,128)(2,1)}, u32[]{:S(2)}) copy-start(bf16[1664,448]{1,0:T(8,128)(2,1)} %get-tuple-element.63) | copy-start | bytes 4472836
  31.4 0.9 copy-start.12
  32.2 0.8 copy-start.13
  42.4 20.8 %collective-permute-start.12 = (bf16[3,208,448]{2,1,0:T(8,128)(2,1)}, bf16[3,208,448]{2,1,0:T(8,128)(2,1)}, u32[]{:S(2)}, u32[]{:S(2)}) collective-permute-start(bf16[3,208,448]{2,1,0:T(8,128)(2,1)} %copy-done.12), channel_id=1, source_target_pairs={{0,16},{8,24},{16,0},{24,8},{1,17},{9,25},{17,1},{25,9},{2,18},{10... | collective-permute-start | bytes 1677320 | tf_op jit(solution)/shard_map/ppermute | solution.py:422
  43.7 15.9 %collective-permute-start.9 = (bf16[8,208,448]{2,1,0:T(8,128)(2,1)}, bf16[8,208,448]{2,1,0:T(8,128)(2,1)S(1)}, u32[]{:S(2)}, u32[]{:S(2)}) collective-permute-start(bf16[8,208,448]{2,1,0:T(8,128)(2,1)} %bitcast.19), channel_id=1, source_target_pairs={{0,8},{8,0},{16,24},{24,16},{1,9},{9,1},{17,25},{25,17},{2,10},{10... | collective-permute-start | bytes 4472840 | tf_op jit(solution)/shard_map/ppermute | solution.py:422
  43.7 18.1 %collective-permute-start.6 = (bf16[208,1664]{1,0:T(8,128)(2,1)}, bf16[208,1664]{1,0:T(8,128)(2,1)S(1)}, u32[]{:S(2)}, u32[]{:S(2)}) collective-permute-start(bf16[208,1664]{1,0:T(8,128)(2,1)} %collective-permute-done.2.refs_3_), channel_id=1, source_target_pairs={{0,2},{2,4},{4,6},{6,7},{7,5},{5,3},{3,1},{1,0},{8,10},{10,12},{12... | collective-permute-start | bytes 2076680 | tf_op jit(solution)/shard_map/ppermute | solution.py:482
  45.4 17.8 %collective-permute-start.7 = (bf16[208,1664]{1,0:T(8,128)(2,1)}, bf16[208,1664]{1,0:T(8,128)(2,1)S(1)}, u32[]{:S(2)}, u32[]{:S(2)}) collective-permute-start(bf16[208,1664]{1,0:T(8,128)(2,1)} %collective-permute-done.3.refs_4_), channel_id=1, source_target_pairs={{0,1},{2,0},{4,2},{6,4},{7,6},{5,7},{3,5},{1,3},{8,9},{10,8},{12,1... | collective-permute-start | bytes 2076680 | tf_op jit(solution)/shard_map/ppermute | solution.py:483
  49.1 16.5 %copy-start.3 = (bf16[1664,448]{1,0:T(8,128)(2,1)S(1)}, bf16[1664,448]{1,0:T(8,128)(2,1)}, u32[]{:S(2)}) copy-start(bf16[1664,448]{1,0:T(8,128)(2,1)} %get-tuple-element.63) | copy-start | bytes 4472836
  49.1 16.5 %collective-permute-start.14 = (bf16[448,1664]{1,0:T(8,128)(2,1)}, bf16[448,1664]{1,0:T(8,128)(2,1)}, u32[]{:S(2)}, u32[]{:S(2)}) collective-permute-start(bf16[448,1664]{1,0:T(8,128)(2,1)} %collective-permute-done.8.refs_6_), channel_id=1, source_target_pairs={{0,8},{8,0},{16,24},{24,16},{1,9},{9,1},{17,25},{25,17},{2,10},{10... | collective-permute-start | bytes 4472840 | tf_op jit(solution)/shard_map/ppermute | solution.py:422
  49.1 2.1 %copy-start.6 = (bf16[3200,512]{1,0:T(8,128)(2,1)S(1)}, bf16[3200,512]{1,0:T(8,128)(2,1)}, u32[]{:S(2)}) copy-start(bf16[3200,512]{1,0:T(8,128)(2,1)} %copy-done.5) | copy-start | bytes 9830404
  59.6 1.2 copy-start.8
  63.2 2.4 %collective-permute-start.13 = (bf16[3,208,448]{2,1,0:T(8,128)(2,1)}, bf16[3,208,448]{2,1,0:T(8,128)(2,1)}, u32[]{:S(2)}, u32[]{:S(2)}) collective-permute-start(bf16[3,208,448]{2,1,0:T(8,128)(2,1)} %collective-permute-done.12.refs_2_), channel_id=1, source_target_pairs={{0,8},{8,0},{16,24},{24,16},{1,9},{9,1},{17,25},{25,17},{2,10},{10... | collective-permute-start | bytes 1677320 | tf_op jit(solution)/shard_map/ppermute | solution.py:422
  63.4 10.3 %copy-start.14 = (bf16[2,208,448]{2,1,0:T(8,128)(2,1)S(1)}, bf16[2,208,448]{2,1,0:T(8,128)(2,1)}, u32[]{:S(2)}) copy-start(bf16[2,208,448]{2,1,0:T(8,128)(2,1)} %copy-done.13) | copy-start | bytes 1118212
  63.4 11.8 %collective-permute-start.10 = (bf16[112,1664]{1,0:T(8,128)(2,1)S(1)}, bf16[112,1664]{1,0:T(8,128)(2,1)S(1)}, u32[]{:S(2)}, u32[]{:S(2)}) collective-permute-start(bf16[112,1664]{1,0:T(8,128)(2,1)S(1)} %slice.18), channel_id=1, source_target_pairs={{0,2},{2,4},{4,6},{6,7},{7,5},{5,3},{3,1},{1,0},{8,10},{10,12},{12... | collective-permute-start | bytes 1118216 | tf_op jit(solution)/shard_map/ppermute | solution.py:486
  65.0 10.2 %collective-permute-start.11 = (bf16[96,1664]{1,0:T(8,128)(2,1)S(1)}, bf16[96,1664]{1,0:T(8,128)(2,1)S(1)}, u32[]{:S(2)}, u32[]{:S(2)}) collective-permute-start(bf16[96,1664]{1,0:T(8,128)(2,1)S(1)} %slice.19), channel_id=1, source_target_pairs={{0,1},{2,0},{4,2},{6,4},{7,6},{5,7},{3,5},{1,3},{8,9},{10,8},{12,1... | collective-permute-start | bytes 958472 | tf_op jit(solution)/shard_map/ppermute | solution.py:487
  65.6 1.5 %copy-start.9 = (bf16[8,208,448]{2,1,0:T(8,128)(2,1)S(1)}, bf16[8,208,448]{2,1,0:T(8,128)(2,1)}, u32[]{:S(2)}) copy-start(bf16[8,208,448]{2,1,0:T(8,128)(2,1)} %copy-done.8) | copy-start | bytes 4472836
  72.7 13.7 %copy-start.7 = (bf16[3200,512]{1,0:T(8,128)(2,1)S(1)}, bf16[3200,512]{1,0:T(8,128)(2,1)}, u32[]{:S(2)}) copy-start(bf16[3200,512]{1,0:T(8,128)(2,1)} %copy-done.5) | copy-start | bytes 9830404
  72.8 6.5 %collective-permute-start.16 = (bf16[96,896]{1,0:T(8,128)(2,1)S(1)}, bf16[96,896]{1,0:T(8,128)(2,1)S(1)}, u32[]{:S(2)}, u32[]{:S(2)}) collective-permute-start(bf16[96,896]{1,0:T(8,128)(2,1)S(1)} %slice.23), channel_id=1, source_target_pairs={{0,1},{2,0},{4,2},{6,4},{7,6},{5,7},{3,5},{1,3},{8,9},{10,8},{12,1... | collective-permute-start | bytes 516104 | tf_op jit(solution)/shard_map/ppermute | solution.py:502
  73.7 12.7 %collective-permute-start.17 = (bf16[2,208,448]{2,1,0:T(8,128)(2,1)S(1)}, bf16[2,208,448]{2,1,0:T(8,128)(2,1)S(1)}, u32[]{:S(2)}, u32[]{:S(2)}) collective-permute-start(bf16[2,208,448]{2,1,0:T(8,128)(2,1)S(1)} %copy-done.14), channel_id=1, source_target_pairs={{0,16},{8,24},{16,0},{24,8},{1,17},{9,25},{17,1},{25,9},{2,18},{10... | collective-permute-start | bytes 1118216 | tf_op jit(solution)/shard_map/ppermute | solution.py:422
  75.2 6.5 %collective-permute-start.15 = (bf16[112,896]{1,0:T(8,128)(2,1)S(1)}, bf16[112,896]{1,0:T(8,128)(2,1)S(1)}, u32[]{:S(2)}, u32[]{:S(2)}) collective-permute-start(bf16[112,896]{1,0:T(8,128)(2,1)S(1)} %slice.22), channel_id=1, source_target_pairs={{0,2},{2,4},{4,6},{6,7},{7,5},{5,3},{3,1},{1,0},{8,10},{10,12},{12... | collective-permute-start | bytes 602120 | tf_op jit(solution)/shard_map/ppermute | solution.py:501
  76.2 29.0 %collective-permute-start.21 = (bf16[3,208,448]{2,1,0:T(8,128)(2,1)}, bf16[3,208,448]{2,1,0:T(8,128)(2,1)}, u32[]{:S(2)}, u32[]{:S(2)}) collective-permute-start(bf16[3,208,448]{2,1,0:T(8,128)(2,1)} %get-tuple-element.100), channel_id=1, source_target_pairs={{0,16},{8,24},{16,0},{24,8},{1,17},{9,25},{17,1},{25,9},{2,18},{10... | collective-permute-start | bytes 1677320 | tf_op jit(solution)/shard_map/ppermute | solution.py:422
  81.8 12.4 %copy-start.10 = (bf16[8,208,448]{2,1,0:T(8,128)(2,1)S(1)}, bf16[8,208,448]{2,1,0:T(8,128)(2,1)}, u32[]{:S(2)}) copy-start(bf16[8,208,448]{2,1,0:T(8,128)(2,1)} %copy-done.8) | copy-start | bytes 4472836
  86.4 7.8 %collective-permute-start.18 = (bf16[2,208,448]{2,1,0:T(8,128)(2,1)S(1)}, bf16[2,208,448]{2,1,0:T(8,128)(2,1)S(1)}, u32[]{:S(2)}, u32[]{:S(2)}) collective-permute-start(bf16[2,208,448]{2,1,0:T(8,128)(2,1)S(1)} %collective-permute-done.17.refs_2_), channel_id=1, source_target_pairs={{0,8},{8,0},{16,24},{24,16},{1,9},{9,1},{17,25},{25,17},{2,10},{10... | collective-permute-start | bytes 1118216 | tf_op jit(solution)/shard_map/ppermute | solution.py:422
  92.1 11.2 %collective-permute-start.19 = (bf16[208,896]{1,0:T(8,128)(2,1)S(1)}, bf16[208,896]{1,0:T(8,128)(2,1)S(1)}, u32[]{:S(2)}, u32[]{:S(2)}) collective-permute-start(bf16[208,896]{1,0:T(8,128)(2,1)S(1)} %add_convert_fusion.5), channel_id=1, source_target_pairs={{0,2},{2,4},{4,6},{6,7},{7,5},{5,3},{3,1},{1,0},{8,10},{10,12},{12... | collective-permute-start | bytes 1118216 | tf_op jit(solution)/shard_map/ppermute | solution.py:539
  93.6 10.8 %collective-permute-start.20 = (bf16[208,896]{1,0:T(8,128)(2,1)S(1)}, bf16[208,896]{1,0:T(8,128)(2,1)S(1)}, u32[]{:S(2)}, u32[]{:S(2)}) collective-permute-start(bf16[208,896]{1,0:T(8,128)(2,1)S(1)} %add_convert_fusion.4), channel_id=1, source_target_pairs={{0,1},{2,0},{4,2},{6,4},{7,6},{5,7},{3,5},{1,3},{8,9},{10,8},{12,1... | collective-permute-start | bytes 1118216 | tf_op jit(solution)/shard_map/ppermute | solution.py:540
  99.1 8.7 %copy-start.11 = (bf16[8,208,448]{2,1,0:T(8,128)(2,1)S(1)}, bf16[8,208,448]{2,1,0:T(8,128)(2,1)}, u32[]{:S(2)}) copy-start(bf16[8,208,448]{2,1,0:T(8,128)(2,1)} %copy-done.8) | copy-start | bytes 4472836
  105.2 2.6 %collective-permute-start.22 = (bf16[3,208,448]{2,1,0:T(8,128)(2,1)}, bf16[3,208,448]{2,1,0:T(8,128)(2,1)}, u32[]{:S(2)}, u32[]{:S(2)}) collective-permute-start(bf16[3,208,448]{2,1,0:T(8,128)(2,1)} %collective-permute-done.21.refs_2_), channel_id=1, source_target_pairs={{0,8},{8,0},{16,24},{24,16},{1,9},{9,1},{17,25},{25,17},{2,10},{10... | collective-permute-start | bytes 1677320 | tf_op jit(solution)/shard_map/ppermute | solution.py:422
  105.3 13.5 %collective-permute-start.25 = (bf16[8,208,448]{2,1,0:T(8,128)(2,1)}, bf16[8,208,448]{2,1,0:T(8,128)(2,1)S(1)}, u32[]{:S(2)}, u32[]{:S(2)}) collective-permute-start(bf16[8,208,448]{2,1,0:T(8,128)(2,1)} %get-tuple-element.114), channel_id=1, source_target_pairs={{0,8},{8,0},{16,24},{24,16},{1,9},{9,1},{17,25},{25,17},{2,10},{10... | collective-permute-start | bytes 4472840 | tf_op jit(solution)/shard_map/ppermute | solution.py:422
  105.8 10.9 %collective-permute-start.23 = (bf16[208,896]{1,0:T(8,128)(2,1)}, bf16[208,896]{1,0:T(8,128)(2,1)S(1)}, u32[]{:S(2)}, u32[]{:S(2)}) collective-permute-start(bf16[208,896]{1,0:T(8,128)(2,1)} %add_convert_fusion.3), channel_id=1, source_target_pairs={{0,2},{2,4},{4,6},{6,7},{7,5},{5,3},{3,1},{1,0},{8,10},{10,12},{12... | collective-permute-start | bytes 1118216 | tf_op jit(solution)/shard_map/ppermute | solution.py:539
  107.4 10.6 %collective-permute-start.24 = (bf16[208,896]{1,0:T(8,128)(2,1)}, bf16[208,896]{1,0:T(8,128)(2,1)S(1)}, u32[]{:S(2)}, u32[]{:S(2)}) collective-permute-start(bf16[208,896]{1,0:T(8,128)(2,1)} %add_convert_fusion.2), channel_id=1, source_target_pairs={{0,1},{2,0},{4,2},{6,4},{7,6},{5,7},{3,5},{1,3},{8,9},{10,8},{12,1... | collective-permute-start | bytes 1118216 | tf_op jit(solution)/shard_map/ppermute | solution.py:540
  124.6 9.8 %collective-permute-start.26 = (bf16[208,896]{1,0:T(8,128)(2,1)}, bf16[208,896]{1,0:T(8,128)(2,1)}, u32[]{:S(2)}, u32[]{:S(2)}) collective-permute-start(bf16[208,896]{1,0:T(8,128)(2,1)} %add_convert_fusion.1), channel_id=1, source_target_pairs={{0,2},{2,4},{4,6},{6,7},{7,5},{5,3},{3,1},{1,0},{8,10},{10,12},{12... | collective-permute-start | bytes 1118216 | tf_op jit(solution)/shard_map/ppermute | solution.py:539
  126.2 9.5 %collective-permute-start.27 = (bf16[208,896]{1,0:T(8,128)(2,1)}, bf16[208,896]{1,0:T(8,128)(2,1)}, u32[]{:S(2)}, u32[]{:S(2)}) collective-permute-start(bf16[208,896]{1,0:T(8,128)(2,1)} %add_convert_fusion), channel_id=1, source_target_pairs={{0,1},{2,0},{4,2},{6,4},{7,6},{5,7},{3,5},{1,3},{8,9},{10,8},{12,1... | collective-permute-start | bytes 1118216 | tf_op jit(solution)/shard_map/ppermute | solution.py:540
  130.5 7.4 %copy-start.1 = (s32[4,1,4]{2,1,0:T(1,128)S(1)}, s32[4,1,4]{2,1,0:T(1,128)}, u32[]{:S(2)}) copy-start(s32[4,1,4]{2,1,0:T(1,128)} %param.9) | copy-start | bytes 196

commit v3 on v2

--- a/solution.py
+++ b/solution.py
@@ -12,9 +12,11 @@
 SLOT = 96
 LANE = 128
 FACTOR = HS ** (-0.5)
-VMEM_BYTES = 32 * 1024 * 1024
-LONG = pl.CostEstimate(flops=10 ** 11, bytes_accessed=10 ** 8, transcendentals=0)
-SHORT = pl.CostEstimate(flops=1000, bytes_accessed=1000, transcendentals=0)
+VMEM_BYTES = 20 * 1024 * 1024
+
+
+def lasting(microseconds):
+    return pl.CostEstimate(flops=int(microseconds * 575000000), bytes_accessed=1000, transcendentals=0)
 
 
 def dot(left, right, left_dim, right_dim):
@@ -25,49 +27,75 @@
     return pltpu.with_memory_space_constraint(array, pltpu.HBM)
 
 
-def prepare_kernel(steps, width, starts, cotangent, layer_scale, scaled, turned, *windows):
-    block = cotangent.shape[1]
-    values = cotangent[...].astype(jnp.float32) * layer_scale[...]
-    at = pl.ds(pl.multiple_of(pl.program_id(0) * block, LANE), block)
-    scaled[:, at] = values.astype(jnp.bfloat16)
-    spare = jnp.zeros((turned.shape[1] - values.shape[0], block), jnp.float32)
-    turned[...] = jnp.concatenate([values, spare], axis=0).T.astype(jnp.bfloat16)
-
-    @pl.when(pl.program_id(0) == steps - 1)
-    def _():
-        for k, window in enumerate(windows):
-            window[...] = scaled[:, pl.ds(pl.multiple_of(starts[k], LANE), width)]
-
-
-def prepare(starts, cotangent, layer_scale, peers, width):
+def window_kernel(peers, starts, cotangent, layer_scale, *refs):
+    windows, (held, sems) = refs[:-2], refs[-2:]
+    parts = len(windows) // peers
+    width = held.shape[2]
+    copies = []
+    for k in range(peers):
+        at = pl.ds(pl.multiple_of(starts[k], LANE), width)
+        first = 0
+        for part in range(parts):
+            rows = pl.ds(first, windows[part].shape[0])
+            copies.append(pltpu.make_async_copy(cotangent.at[rows, at], held.at[k, rows], sems.at[k, part]))
+            first += windows[part].shape[0]
+    for copy in copies:
+        copy.start()
+    for k in range(peers):
+        scale = layer_scale[:, pl.ds(pl.multiple_of(starts[k], LANE), width)]
+        first = 0
+        for part in range(parts):
+            copies[k * parts + part].wait()
+            window = windows[k * parts + part]
+            values = held[k, first:first + window.shape[0], :].astype(jnp.float32)
+            window[...] = (values * scale).astype(jnp.bfloat16)
+            first += window.shape[0]
+
+
+def peer_windows(starts, cotangent, layer_scale, peers, width):
+    rows, total = cotangent.shape
+    parts = (rows // 48 * 16 + 16, rows - rows // 48 * 16 - 16)
+    arrays = pl.pallas_call(
+        functools.partial(window_kernel, peers),
+        grid_spec=pltpu.PrefetchScalarGridSpec(
+            num_scalar_prefetch=1,
+            grid=(1,),
+            in_specs=[pl.BlockSpec(memory_space=pl.ANY), pl.BlockSpec((1, total), lambda i, s: (0, 0))],
+            out_specs=[pl.BlockSpec((part, width), lambda i, s: (0, 0)) for part in parts] * peers,
+            scratch_shapes=[
+                pltpu.VMEM((peers, rows, width), jnp.bfloat16),
+                pltpu.SemaphoreType.DMA((peers, len(parts))),
+            ],
+        ),
+        out_shape=[pltpu.HBM((part, width), jnp.bfloat16) for part in parts] * peers,
+        compiler_params=pltpu.CompilerParams(vmem_limit_bytes=VMEM_BYTES),
+        cost_estimate=lasting(60),
+        name="peer_windows",
+    )(starts, in_hbm(cotangent), layer_scale)
+    return [arrays[part::len(parts)] for part in range(len(parts))]
+
+
+def prepare_kernel(cotangent, layer_scale, turned):
+    values = (cotangent[...].astype(jnp.float32) * layer_scale[...]).astype(jnp.bfloat16)
+    spare = jnp.zeros((turned.shape[1] - values.shape[0], values.shape[1]), jnp.bfloat16)
+    turned[...] = jnp.concatenate([values, spare], axis=0).T
+
+
+def prepare(cotangent, layer_scale):
     rows, total = cotangent.shape
     lanes = -(-rows // LANE) * LANE
     steps = 5
     block = total // steps
     return pl.pallas_call(
-        functools.partial(prepare_kernel, steps, width),
-        grid_spec=pltpu.PrefetchScalarGridSpec(
-            num_scalar_prefetch=1,
-            grid=(steps,),
-            in_specs=[
-                pl.BlockSpec((rows, block), lambda i, s: (0, i)),
-                pl.BlockSpec((1, block), lambda i, s: (0, i)),
-            ],
-            out_specs=[
-                pl.BlockSpec((rows, total), lambda i, s: (0, 0)),
-                pl.BlockSpec((block, lanes), lambda i, s: (i, 0)),
-            ]
-            + [pl.BlockSpec((rows, width), lambda i, s: (0, 0))] * peers,
-        ),
-        out_shape=[
-            jax.ShapeDtypeStruct((rows, total), jnp.bfloat16),
-            jax.ShapeDtypeStruct((total, lanes), jnp.bfloat16),
-        ]
-        + [jax.ShapeDtypeStruct((rows, width), jnp.bfloat16)] * peers,
-        compiler_params=pltpu.CompilerParams(vmem_limit_bytes=VMEM_BYTES),
-        cost_estimate=LONG,
+        prepare_kernel,
+        grid=(steps,),
+        in_specs=[pl.BlockSpec((rows, block), lambda i: (0, i)), pl.BlockSpec((1, block), lambda i: (0, i))],
+        out_specs=pl.BlockSpec((block, lanes), lambda i: (i, 0)),
+        out_shape=pltpu.HBM((total, lanes), jnp.bfloat16),
+        compiler_params=pltpu.CompilerParams(vmem_limit_bytes=VMEM_BYTES),
+        cost_estimate=lasting(60),
         name="scaled_cotangent",
-    )(starts, in_hbm(cotangent), layer_scale.reshape(1, total))
+    )(in_hbm(cotangent), layer_scale)
 
 
 def arrange_kernel(sizes, order, attended, *refs):
@@ -91,14 +119,42 @@
             num_scalar_prefetch=1,
             grid=(1,),
             in_specs=[pl.BlockSpec(memory_space=pl.ANY)],
-            out_specs=[pl.BlockSpec(memory_space=pl.ANY)] * len(sizes),
+            out_specs=[pl.BlockSpec((size, depth, rows), lambda i, o: (0, 0, 0)) for size in sizes],
             scratch_shapes=[pltpu.SemaphoreType.DMA((sum(sizes),))],
         ),
         out_shape=[jax.ShapeDtypeStruct((size, depth, rows), attended.dtype) for size in sizes],
         compiler_params=pltpu.CompilerParams(vmem_limit_bytes=VMEM_BYTES),
-        cost_estimate=SHORT,
+        cost_estimate=lasting(2),
         name="attended_chunks",
-    )(order, attended)
+    )(order, in_hbm(attended))
+
+
+def far_kernel(up, down, out_up, out_down, sems):
+    cut = out_up.shape[0]
+    copies = [
+        pltpu.make_async_copy(up.at[pl.ds(0, cut)], out_up, sems.at[0]),
+        pltpu.make_async_copy(down.at[pl.ds(cut, out_down.shape[0])], out_down, sems.at[1]),
+    ]
+    for copy in copies:
+        copy.start()
+    for copy in copies:
+        copy.wait()
+
+
+def far_parts(up, down, cut):
+    depth, width = up.shape
+    sizes = (cut, depth - cut)
+    return pl.pallas_call(
+        far_kernel,
+        grid=(1,),
+        in_specs=[pl.BlockSpec(memory_space=pl.ANY)] * 2,
+        out_specs=[pl.BlockSpec((size, width), lambda i: (0, 0)) for size in sizes],
+        out_shape=[jax.ShapeDtypeStruct((size, width), up.dtype) for size in sizes],
+        scratch_shapes=[pltpu.SemaphoreType.DMA((2,))],
+        compiler_params=pltpu.CompilerParams(vmem_limit_bytes=VMEM_BYTES),
+        cost_estimate=lasting(1),
+        name="far_parts",
+    )(up, down)
 
 
 PAIR = 2
@@ -165,9 +221,9 @@
             pltpu.HBM((heads, 2 * SLOT, 2 * SLOT), jnp.float32),
         ],
         compiler_params=pltpu.CompilerParams(vmem_limit_bytes=VMEM_BYTES),
-        cost_estimate=LONG,
+        cost_estimate=lasting(60),
         name="attention_forward",
-    )(counts, in_hbm(qkv))
+    )(counts, qkv)
 
 
 def backward_kernel(qkv, grad_mine, grad_other, main_probs, slot_probs, *rest):
@@ -211,9 +267,9 @@
         out_shape=pltpu.HBM(qkv.shape, jnp.bfloat16),
         input_output_aliases={5: 0} if held else {},
         compiler_params=pltpu.CompilerParams(vmem_limit_bytes=VMEM_BYTES),
-        cost_estimate=LONG,
+        cost_estimate=lasting(2 * (high - low)),
         name="attention_backward",
-    )(in_hbm(qkv), in_hbm(grad_mine), grad_other, in_hbm(main_probs), in_hbm(slot_probs), *map(in_hbm, held))
+    )(qkv, grad_mine, grad_other, main_probs, slot_probs, *map(in_hbm, held))
 
 
 def grad_out_kernel(sizes, split, total, info, turned, turned_other, *refs):
@@ -257,7 +313,7 @@
         store.wait()
 
 
-def grad_out_rows(info, turned, turned_other, rows, pieces, shards, held):
+def grad_out_rows(info, turned, turned_other, rows, pieces, shards, held, after=()):
     total, lanes = turned.shape
     split = pieces[0][0].shape[1]
     depth = sum(p.shape[0] for p in pieces[0])
@@ -270,7 +326,7 @@
         grid_spec=pltpu.PrefetchScalarGridSpec(
             num_scalar_prefetch=1,
             grid=(1,),
-            in_specs=[pl.BlockSpec(memory_space=pl.ANY)] * (2 + len(arrays) + len(held)),
+            in_specs=[pl.BlockSpec(memory_space=pl.ANY)] * (2 + len(arrays) + len(held) + len(after)),
             out_specs=[pl.BlockSpec(memory_space=pl.ANY)] * 2,
             scratch_shapes=[
                 pltpu.VMEM((2, split, lanes), jnp.bfloat16),
@@ -287,9 +343,9 @@
         ],
         input_output_aliases={3 + len(arrays) + i: i for i in range(len(held))},
         compiler_params=pltpu.CompilerParams(vmem_limit_bytes=VMEM_BYTES),
-        cost_estimate=LONG,
+        cost_estimate=lasting(0.2 if held else 1.5 * len(pieces)),
         name="grad_out_rows",
-    )(info, turned, turned_other, *arrays, *map(in_hbm, held))
+    )(info, in_hbm(turned), turned_other, *arrays, *map(in_hbm, held), *after)
 
 
 def half_kernel(starts, weight, out, sem):
@@ -310,9 +366,9 @@
         ),
         out_shape=jax.ShapeDtypeStruct((weight.shape[0], width), weight.dtype),
         compiler_params=pltpu.CompilerParams(vmem_limit_bytes=VMEM_BYTES),
-        cost_estimate=SHORT,
+        cost_estimate=lasting(1),
         name="own_half_of_weight",
-    )(start, weight)
+    )(start, in_hbm(weight))
 
 
 def finish_kernel(offsets, start, term, came_up, came_down, out):
@@ -337,21 +393,31 @@
         ),
         out_shape=jax.ShapeDtypeStruct((depth, owned), jnp.float32),
         compiler_params=pltpu.CompilerParams(vmem_limit_bytes=VMEM_BYTES),
-        cost_estimate=SHORT,
+        cost_estimate=lasting(2),
         name="last_sum",
     )(start, term, came_up, came_down)
 
 
-def partial_kernel(sources, count, window, order, starts, *refs):
-    attended, columns = refs[:sources], refs[sources:2 * sources]
-    outs, (chunks, held, sems) = refs[2 * sources:-3], refs[-3:]
-    depth = chunks.shape[2]
+def partial_kernel(chosen, sources, parts, count, window, order, start, *refs):
+    attended, columns = refs[:sources], refs[sources:sources * (1 + parts)]
+    chunks, held, sems = refs[-3:]
+    bases = refs[sources * (1 + parts):-3 - count]
+    outs = refs[-3 - count:-3]
+    depth, rows = chunks.shape[2:]
+    at = pl.ds(pl.multiple_of(start[0], LANE), window)
     copies = []
     for i in range(sources):
-        at = pl.ds(pl.multiple_of(starts[min(i // 2, 1)], LANE), window)
-        some = [pltpu.make_async_copy(columns[i].at[:, at], held.at[i], sems.at[i, count])]
+        some, first = [], 0
+        for part in range(parts):
+            source = columns[i * parts + part]
+            if chosen:
+                some.append(pltpu.make_async_copy(source.at[at], held.at[i], sems.at[i, count + part]))
+            else:
+                target = held.at[i, pl.ds(first, source.shape[0])]
+                some.append(pltpu.make_async_copy(source.at[:, at], target, sems.at[i, count + part]))
+            first += source.shape[0]
         for j in range(count):
-            source = attended[i].at[order[j] if i < 2 else j]
+            source = attended[i].at[order[j] if chosen else j]
             some.append(pltpu.make_async_copy(source, chunks.at[i, j], sems.at[i, j]))
         copies.append(some)
     for some in copies:
@@ -362,36 +428,42 @@
         for copy in some:
             copy.wait()
         if together:
-            product = dot(chunks[i].reshape(count * depth, chunks.shape[3]), held[i], 1, 0)
+            tall = chunks[i].reshape(count * depth, rows)
+            product = dot(tall, held[i][:, :rows], 1, 1) if chosen else dot(tall, held[i], 1, 0)
         for j, out in enumerate(outs):
-            part = product[j * depth:(j + 1) * depth] if together else dot(chunks[i, j], held[i], 1, 0)
+            if together:
+                part = product[j * depth:(j + 1) * depth]
+            else:
+                part = dot(chunks[i, j], held[i][:, :rows], 1, 1) if chosen else dot(chunks[i, j], held[i], 1, 0)
             if i == 0:
-                out[...] = part
+                out[...] = bases[j][...] + part if bases else part
             else:
                 out[...] += part
 
 
-def partial_products(order, starts, attended, columns, window):
+def partial_products(order, start, attended, columns, window, bases=()):
     _, depth, rows = attended[0].shape
+    parts = len(columns) // len(attended)
     count, sources = order.shape[0], len(attended)
-    return pl.pallas_call(
-        functools.partial(partial_kernel, sources, count, window),
+    block = pl.BlockSpec((depth, window), lambda j, o, s: (0, 0))
+    return pl.pallas_call(
+        functools.partial(partial_kernel, not bases, sources, parts, count, window),
         grid_spec=pltpu.PrefetchScalarGridSpec(
             num_scalar_prefetch=2,
             grid=(1,),
-            in_specs=[pl.BlockSpec(memory_space=pl.ANY)] * (2 * sources),
-            out_specs=[pl.BlockSpec((depth, window), lambda j, o, s: (0, 0))] * count,
+            in_specs=[pl.BlockSpec(memory_space=pl.ANY)] * (sources * (1 + parts)) + [block] * len(bases),
+            out_specs=[block] * count,
             scratch_shapes=[
                 pltpu.VMEM((sources, count, depth, rows), jnp.bfloat16),
-                pltpu.VMEM((sources, rows, window), jnp.bfloat16),
-                pltpu.SemaphoreType.DMA((sources, count + 1)),
+                pltpu.VMEM((sources, rows, window) if bases else (sources, window, columns[0].shape[1]), jnp.bfloat16),
+                pltpu.SemaphoreType.DMA((sources, count + parts)),
             ],
         ),
-        out_shape=[jax.ShapeDtypeStruct((depth, window), jnp.float32)] * count,
-        compiler_params=pltpu.CompilerParams(vmem_limit_bytes=VMEM_BYTES),
-        cost_estimate=LONG,
-        name="projection_partial",
-    )(order, starts, *attended, *columns)
+        out_shape=[(jax.ShapeDtypeStruct if bases else pltpu.HBM)((depth, window), jnp.float32)] * count,
+        compiler_params=pltpu.CompilerParams(vmem_limit_bytes=VMEM_BYTES),
+        cost_estimate=lasting(0.2 if bases else 6),
+        name="projection_peers" if bases else "projection_chip",
+    )(order, start, *attended, *columns, *map(in_hbm, bases))
 
 
 def windows_of(groups, owned, total):
@@ -444,101 +516,113 @@
     down.append(lax.ppermute(down[-1], "fsdp", behind))
 
     mine, cotangent = lax.optimization_barrier((mine, cotangent))
-    scaled, turned, *sent = prepare(
-        table([chip_start(chip ^ k) for k in range(1, peers)] or [0]), cotangent, layer_scale, peers - 1, chip_width
+    scales = layer_scale.reshape(1, total)
+    sent = peer_windows(
+        table([chip_start(chip ^ k) for k in range(1, peers)] or [0]), cotangent, scales, peers - 1, chip_width
     )
-    columns = [scaled, swap(scaled, 1)]
-    turned_other = swap(turned, 1)
+    sent, cotangent = lax.optimization_barrier((sent, cotangent))
+    came_columns = [[swap(array, 2 * k) for k, array in enumerate(part, 1)] for part in sent]
+    turned = prepare(cotangent, scales)
     attended, main_probs, slot_probs = forward(counts, query_key_value)
     attended = attended.reshape(shards, depth, rows)
     near = [[o, -o] for o in range(half - 1, 0, -1)]
     groups = [[half] + near[0]] + near[1:-1] + [near[-1] + [0]]
-    came_columns = [swap(sent[k - 1], 2 * k) for k in range(1, peers)]
     flat = table([shard_at(o) for group in groups for o in group])
     sizes = [len(group) for group in groups]
     orders = [flat[sum(sizes[:g]):sum(sizes[:g + 1])] for g in range(len(groups))]
+
+    def rows_of(some, held, after=()):
+        info = table([core] + [shard_at(o) for _, o in some])
+        return grad_out_rows(info, turned, turned_other, rows, [p for p, _ in some], shards, held, after)
+
+    up[1], down[1], attended, came_columns[0], turned = lax.optimization_barrier(
+        (up[1], down[1], attended, came_columns[0], turned)
+    )
+    turned_other = swap(turned, 1)
+    other_columns = [[swap(array, 1) for array in came_columns[0]]]
+    attended_other = swap(attended, 1)
     chunks = list(arrange(flat, attended, sizes))
-    came = [[swap(chunks[0], 2 * k) for k in range(1, peers)]]
-
-    def rows_of(some, held):
-        info = table([core] + [shard_at(o) for _, o in some])
-        return grad_out_rows(info, turned, turned_other, rows, [p for p, _ in some], shards, held)
-
-    up[1], down[1], attended = lax.optimization_barrier((up[1], down[1], attended))
-    both = [attended, swap(attended, 1)]
     for _ in range(half - 3):
         up.append(lax.ppermute(up[-1], "fsdp", ahead))
         down.append(lax.ppermute(down[-1], "fsdp", behind))
-    up[-1], down[-1], columns[1], turned_other = lax.optimization_barrier((up[-1], down[-1], columns[1], turned_other))
-    came_columns, near_up, near_down, chunks = lax.optimization_barrier((came_columns, up[-1], down[-1], chunks))
+    up[-1], down[-1], turned_other, attended_other = lax.optimization_barrier(
+        (up[-1], down[-1], turned_other, attended_other)
+    )
+
+    bases = partial_products(
+        flat, starts[:1], [in_hbm(attended), attended_other], [in_hbm(turned), turned_other], window
+    )
+    late, chunks, *bases = lax.optimization_barrier((came_columns[1], chunks, *bases))
+    came = [[swap(chunks[0], 2 * k) for k in range(1, peers)]]
+    other_columns.append([swap(array, 1) for array in late])
+    came_columns[1] = late
     came.append([swap(chunks[1], 2 * k) for k in range(1, peers)])
+    columns = []
+    for k in range(peers - 1):
+        for arrays in (came_columns, other_columns):
+            columns += [part[k] for part in arrays]
     pieces = [([mine], 0)]
     for step in range(1, half - 1):
-        last = step == half - 2
-        pieces += [([near_up if last else up[step]], -step), ([near_down if last else down[step]], step)]
+        pieces += [([up[step]], -step), ([down[step]], step)]
     grad_out = rows_of(pieces, None)
-    for c in came_columns:
-        columns += [c, swap(c, 1)]
     up.append(lax.ppermute(up[-1], "fsdp", ahead))
     down.append(lax.ppermute(down[-1], "fsdp", behind))
-    up[-1], down[-1], grad_out, both[1] = lax.optimization_barrier((up[-1], down[-1], grad_out, both[1]))
-    came[0], near_up, near_down = lax.optimization_barrier((came[0], up[-1], down[-1]))
-    far_up = lax.ppermute(up[-1][:cut], "fsdp", ahead)
-    far_down = lax.ppermute(down[-1][cut:], "fsdp", behind)
-
-    def products(index):
-        taken = list(both)
-        for c in came[index]:
-            taken += [c, swap(c, 1)]
-        result = partial_products(orders[index], starts, taken, columns, window)
-        return {o: result[j] for j, o in enumerate(groups[index])}
-
-    terms = products(0)
+    up[-1], down[-1], grad_out, *bases = lax.optimization_barrier((up[-1], down[-1], grad_out, *bases))
+    bases = dict(zip([o for group in groups for o in group], bases))
+    if depth % 16 == 0:
+        far_up, far_down = far_parts(up[-1], down[-1], cut)
+    else:
+        far_up, far_down = up[-1][:cut], down[-1][cut:]
+    came[0], near_up, near_down, sent_up = lax.optimization_barrier((came[0], up[-1], down[-1], far_up))
+    far_up = lax.ppermute(far_up, "fsdp", ahead)
+    far_down = lax.ppermute(far_down, "fsdp", behind)
+
+    def both_cores(arrays):
+        return [a for c in arrays for a in (c, swap(c, 1))]
+
+    def products(index, taken):
+        group = groups[index]
+        if not taken:
+            return {o: bases[o] for o in group}
+        result = partial_products(orders[index], starts[1:], taken, columns, window, [bases[o] for o in group])
+        return dict(zip(group, result))
+
+    terms = products(0, both_cores(came[0]))
     first = terms[half].astype(jnp.bfloat16)
-    far_up, far_down, terms, chunks = lax.optimization_barrier((far_up, far_down, terms, chunks))
+    going_up, going_down, came[1], chunks, far_up, far_down = lax.optimization_barrier(
+        (first[:cut], first[cut:], came[1], chunks, far_up, far_down)
+    )
     came += [[swap(some, 2 * k) for k in range(1, peers)] for some in chunks[2:]]
-    going_up, going_down = first[:cut], first[cut:]
+    taken = both_cores(came[1])
     came_up = lax.ppermute(going_up, "fsdp", ahead)
     came_down = lax.ppermute(going_down, "fsdp", behind)
 
-    grad_out = rows_of([([near_up], 1 - half), ([near_down], half - 1), ([far_up, far_down], half)], grad_out)
-    grad_mine = grad_out[0].reshape(width, rows)
-    grad_other = swap(grad_out[1], 1).reshape(width, rows)
-    pairs = -(-(width // HS) // PAIR)
-    bounds = [0, 3, 5, pairs]
-
-    def back(index, held):
-        return backward(
-            query_key_value, grad_mine, grad_other, main_probs, slot_probs, bounds[index], bounds[index + 1], held
-        )
-
+    bounds = [0, 3, 5, -(-(width // HS) // PAIR)]
     grads = None
     for step in range(half, 1, -1):
         if step == half:
             came_up = jnp.pad(came_up, ((0, depth - cut), (0, 0)))
             came_down = jnp.pad(came_down, ((cut, 0), (0, 0)))
         else:
-            terms.update(products(half - step))
+            terms.update(products(half - step, taken))
         going_up = (terms[step - 1] + came_up.astype(jnp.float32)).astype(jnp.bfloat16)
         going_down = (terms[1 - step] + came_down.astype(jnp.float32)).astype(jnp.bfloat16)
-        beside = []
-        if step > 2:
-            beside.append(came[half - step + 1])
-        if step == 3:
-            beside.append(grad_mine)
-        if step == 2:
-            grads = back(0, grads)
-            beside.append(grads)
-        going_up, going_down, *beside = lax.optimization_barrier((going_up, going_down, *beside))
-        if step > 2:
-            came[half - step + 1] = beside[0]
-        if step == 3:
-            grad_mine = beside[1]
-        if step == 2:
-            grads = beside[0]
+        if step == half:
+            going_up, going_down, near_up = lax.optimization_barrier((going_up, going_down, near_up))
+            grad_out = rows_of([([near_up], 1 - half), ([near_down], half - 1), ([far_up, far_down], half)], grad_out, [sent_up])
+            grad_mine = grad_out[0].reshape(width, rows)
+            grad_other = swap(grad_out[1], 1).reshape(width, rows)
+        elif step > 2:
+            arrived = came[half - step + 1]
+            going_up, going_down, arrived, grad_mine = lax.optimization_barrier((going_up, going_down, arrived, grad_mine))
+            taken = both_cores(arrived)
+        else:
+            grads = backward(query_key_value, grad_mine, grad_other, main_probs, slot_probs, bounds[0], bounds[1], grads)
+            going_up, going_down, grads = lax.optimization_barrier((going_up, going_down, grads))
         came_up = lax.ppermute(going_up, "fsdp", ahead)
         came_down = lax.ppermute(going_down, "fsdp", behind)
-    grads = back(2, back(1, grads))
+    for low, high in zip(bounds[1:], bounds[2:]):
+        grads = backward(query_key_value, grad_mine, grad_other, main_probs, slot_probs, low, high, grads)
     came_up, came_down, grads = lax.optimization_barrier((came_up, came_down, grads))
     offsets = set()
     for m in range(members):

time: 139 us -> 139 us (level)
  Pallas kernels: 65.6 us -> 70 us
  local copies, waits for them, and re-layouts: 10.1 us -> 8.34 us
    pallas_call x4 -> x7, Pallas kernels: 22.4 us -> 34.2 us  [the longest x4 23.7 us: partial_products(): pl.pallas_call(functools.partial(partial_kernel, not bases, sources, part...]
    pallas_call x3, Pallas kernels: 13.5 us -> 8.14 us  [backward(): pl.pallas_call(backward_kernel, grid=(high - low,), in_specs=[pl.BlockSpe...]
    ppermute x4, waiting for transfers between devices: 9.8 us -> 5.97 us  [local(): came_up = lax.ppermute(going_up, 'fsdp', ahead)]
    pallas_call x1, Pallas kernels: 9.63 us -> 7.31 us  [forward(): pl.pallas_call(forward_kernel, grid_spec=pltpu.PrefetchScalarGridSpec(num...]
    unnamed x30 -> x34, local copies, waits for them, and re-layouts: 9.16 us -> 7.41 us
    ppermute x12 -> x13, waiting for transfers between devices: 8.01 us -> 9.23 us  [swap(): return lax.ppermute(array, 'dp', [(i, i ^ bit) for i in range(members)])]
    ppermute x12 -> x13, starting transfers between devices: 5.74 us -> 5.06 us  [swap(): return lax.ppermute(array, 'dp', [(i, i ^ bit) for i in range(members)])]
  transfers between devices with their start and end apart: 28 -> 29, of which waited for: 15 -> 12; matrix products, arithmetic and copies ran while one was open for 3% -> 3% of each run, Pallas kernels for 41% -> 47%
where the time goes in v3:
time: 139 us; the launch traced here: 138 us
  Pallas kernels  70 us (50%)
  waiting for transfers between devices  33.5 us (24%)
  starting transfers between devices  22.3 us (16%)
  local copies, waits for them, and re-layouts  8.34 us (6%)
  other arithmetic  3.23 us (2%)
    pallas_call x4, Pallas kernels, partial_products(): pl.pallas_call(functools.partial(partial_kernel, not bases, sources, part...  23.7 us
    pallas_call x2, Pallas kernels, grad_out_rows(): pl.pallas_call(functools.partial(grad_out_kernel, sizes, split, total), g...  14.9 us
    ppermute x3, waiting for transfers between devices, local(): up.append(lax.ppermute(up[-1], 'fsdp', ahead))  11.6 us
    ppermute x13, waiting for transfers between devices, swap(): return lax.ppermute(array, 'dp', [(i, i ^ bit) for i in range(members)])  9.23 us
    pallas_call x3, Pallas kernels, backward(): pl.pallas_call(backward_kernel, grid=(high - low,), in_specs=[pl.BlockSpe...  8.14 us
    unnamed x34, local copies, waits for them, and re-layouts  7.41 us
    pallas_call x1, Pallas kernels, forward(): pl.pallas_call(forward_kernel, grid_spec=pltpu.PrefetchScalarGridSpec(num...  7.31 us
    ppermute x3, starting transfers between devices, local(): up.append(lax.ppermute(up[-1], 'fsdp', ahead))  6.23 us
  transfers between devices with their start and end apart: 29, of which 12 were waited for; matrix products, arithmetic and copies ran while one was open for 3% of the time, Pallas kernels for 47%

profile of v3, /device:TPU:0, one launch (start us, length us, event | category | flops | bytes accessed | tf_op | source)
XLA Modules:
  0.0 138.3 jit_solution(9254295209647046727)
XLA Ops:
  0.7 1.1 own_half_of_weight.1.refs_0_
  1.8 3.1 %collective-permute-start.1 = (bf16[208,1664]{1,0:T(8,128)(2,1)S(1)}, bf16[208,1664]{1,0:T(8,128)(2,1)}, u32[]{:S(2)}, u32[]{:S(2)}) collective-permute-start(bf16[208,1664]{1,0:T(8,128)(2,1)S(1)} %own_half_of_weight.1.refs_0_), channel_id=1, source_target_pairs={{0,2},{2,4},{4,6},{6,7},{7,5},{5,3},{3,1},{1,0},{8,10},{10,12},{12... | collective-permute-start | bytes 2076680 | tf_op jit(solution)/shard_map/ppermute | solution.py:515
  4.9 0.7 reshape.18.layer_scale
  5.6 2.5 %peer_windows.1 = (bf16[160,1664]{1,0:T(8,128)(2,1)}, bf16[288,1664]{1,0:T(8,128)(2,1)}) custom-call(s32[1]{0:T(128)} %bitcast.9.starts, bf16[448,3200]{1,0:T(8,128)(2,1)} %cotangent.1, f32[1,3200]{1,0:T(1,128)S(1)} %reshape.18.layer_scale), custom_call_target="tpu_custom_call" | custom-call | flops 34500001792 | bytes 1000 | tf_op jit(solution)/shard_map/peer_windows/pallas_call | solution.py:58
  8.1 2.0 %collective-permute-start.3 = (bf16[160,1664]{1,0:T(8,128)(2,1)}, bf16[160,1664]{1,0:T(8,128)(2,1)S(1)}, u32[]{:S(2)}, u32[]{:S(2)}) collective-permute-start(bf16[160,1664]{1,0:T(8,128)(2,1)} %get-tuple-element.98), channel_id=1, source_target_pairs={{0,16},{8,24},{16,0},{24,8},{1,17},{9,25},{17,1},{25,9},{2,18},{10... | collective-permute-start | bytes 1597448 | tf_op jit(solution)/shard_map/ppermute | solution.py:494
  10.1 6.0 %scaled_cotangent.1.refs_2_.turned = bf16[3200,512]{1,0:T(8,128)(2,1)} custom-call(bf16[448,3200]{1,0:T(8,128)(2,1)} %cotangent.1, f32[1,3200]{1,0:T(1,128)S(1)} %reshape.18.layer_scale), custom_call_target="tpu_custom_call" | custom-call | flops 34500001792 | bytes 1000 | tf_op jit(solution)/shard_map/scaled_cotangent/pallas_call | solution.py:89
  16.2 7.3 %attention_forward.1 = (bf16[1664,448]{1,0:T(8,128)(2,1)}, f32[13,256,256]{2,1,0:T(8,128)}, f32[13,192,192]{2,1,0:T(8,128)}) custom-call(s32[4]{0:T(128)S(1)} %dynamic-slice_bitcast_fusion.counts, bf16[3,448,1664]{2,1,0:T(8,128)(2,1)S(1)} %copy-done.3), custom_call_target="tpu_custom_call" | custom-call | flops 34500001792 | bytes 1000 | tf_op jit(solution)/shard_map/attention_forward/pallas_call | solution.py:206
  24.1 1.6 %collective-permute-start.4 = (bf16[208,1664]{1,0:T(8,128)(2,1)}, bf16[208,1664]{1,0:T(8,128)(2,1)}, u32[]{:S(2)}, u32[]{:S(2)}) collective-permute-start(bf16[208,1664]{1,0:T(8,128)(2,1)} %collective-permute-done.1.refs_1_), channel_id=1, source_target_pairs={{0,2},{2,4},{4,6},{6,7},{7,5},{5,3},{3,1},{1,0},{8,10},{10,12},{12... | collective-permute-start | bytes 2076680 | tf_op jit(solution)/shard_map/ppermute | solution.py:546
  26.3 3.2 %attended_chunks.1 = (bf16[3,208,448]{2,1,0:T(8,128)(2,1)}, bf16[2,208,448]{2,1,0:T(8,128)(2,1)}, bf16[3,208,448]{2,1,0:T(8,128)(2,1)S(1)}) custom-call(s32[8]{0:T(128)S(1)} %stack.80.order, bf16[8,208,448]{2,1,0:T(8,128)(2,1)} %bitcast.26), custom_call_target="tpu_custom_call" | custom-call | flops 1150000000 | bytes 1000 | tf_op jit(solution)/shard_map/attended_chunks/pallas_call | solution.py:116
  29.5 0.9 copy-done.15
  30.3 11.6 %collective-permute-done.4.refs_3_ = bf16[208,1664]{1,0:T(8,128)(2,1)} collective-permute-done((bf16[208,1664]{1,0:T(8,128)(2,1)}, bf16[208,1664]{1,0:T(8,128)(2,1)}, u32[]{:S(2)}, u32[]{:S(2)}) %collective-permute-start.4) | collective-permute-done | bytes 692256 | tf_op jit(solution)/shard_map/ppermute | solution.py:546
  41.9 1.3 collective-permute-done.5.refs_4_
  43.2 1.6 %collective-permute-start.9 = (bf16[208,1664]{1,0:T(8,128)(2,1)}, bf16[208,1664]{1,0:T(8,128)(2,1)}, u32[]{:S(2)}, u32[]{:S(2)}) collective-permute-start(bf16[208,1664]{1,0:T(8,128)(2,1)} %collective-permute-done.4.refs_3_), channel_id=1, source_target_pairs={{0,2},{2,4},{4,6},{6,7},{7,5},{5,3},{3,1},{1,0},{8,10},{10,12},{12... | collective-permute-start | bytes 2076680 | tf_op jit(solution)/shard_map/ppermute | solution.py:568
  45.2 9.1 %projection_chip.1 = (f32[208,896]{1,0:T(8,128)}, f32[208,896]{1,0:T(8,128)}, f32[208,896]{1,0:T(8,128)}, f32[208,896]{1,0:T(8,128)}, f32[208,896]{1,0:T(8,128)}...) custom-call(s32[8]{0:T(128)S(1)} %stack.80.order, s32[1]{0:T(128)} %bitcast.13.start, ...), custom_call_target="tpu_custom_call" | custom-call | flops 3449999872 | bytes 1000 | tf_op jit(solution)/shard_map/projection_chip/pallas_call | solution.py:449
  54.4 0.6 collective-permute-start.8
  55.6 1.1 copy-done.14
  56.7 8.5 %grad_out_rows.2 = (f32[8,208,448]{2,1,0:T(8,128)}, bf16[8,208,448]{2,1,0:T(8,128)(2,1)}) custom-call(s32[6]{0:T(128)S(1)} %stack.83.info, bf16[3200,512]{1,0:T(8,128)(2,1)} %scaled_cotangent.1.refs_2_.turned, bf16[3200,512]{1,0:T(8,128)(2,1)} %collective-permute-done.6.refs_3_.turned_other, bf16[208,1664]{1,0:T(8,128)(2,1)S(1)} %copy-done.14, ...), custom_call_target="tpu_custom_call" | custom-call | flops 4312500224 | bytes 1000 | tf_op jit(solution)/shard_map/grad_out_rows/pallas_call | solution.py:324
  65.2 2.0 %far_parts.1 = (bf16[112,1664]{1,0:T(8,128)(2,1)}, bf16[96,1664]{1,0:T(8,128)(2,1)}) custom-call(bf16[208,1664]{1,0:T(8,128)(2,1)} %collective-permute-done.9.up.refs_0_, bf16[208,1664]{1,0:T(8,128)(2,1)} %collective-permute-done.10.down.refs_1_), custom_call_target="tpu_custom_call" | custom-call | flops 575000000 | bytes 1000 | tf_op jit(solution)/shard_map/far_parts/pallas_call | solution.py:147
  67.2 2.2 %collective-permute-done.8.refs_0_ = bf16[3,208,448]{2,1,0:T(8,128)(2,1)} collective-permute-done((bf16[3,208,448]{2,1,0:T(8,128)(2,1)}, bf16[3,208,448]{2,1,0:T(8,128)(2,1)}, u32[]{:S(2)}, u32[]{:S(2)}) %collective-permute-start.8) | collective-permute-done | bytes 559136 | tf_op jit(solution)/shard_map/ppermute | solution.py:494
  69.4 0.5 collective-permute-start.14
  69.9 1.6 %collective-permute-start.15 = (bf16[112,1664]{1,0:T(8,128)(2,1)}, bf16[112,1664]{1,0:T(8,128)(2,1)}, u32[]{:S(2)}, u32[]{:S(2)}) collective-permute-start(bf16[112,1664]{1,0:T(8,128)(2,1)} %get-tuple-element.163.refs_6_), channel_id=1, source_target_pairs={{0,2},{2,4},{4,6},{6,7},{7,5},{5,3},{3,1},{1,0},{8,10},{10,12},{12... | collective-permute-start | bytes 1118216 | tf_op jit(solution)/shard_map/ppermute | solution.py:577
  72.1 5.2 %projection_peers.3 = (f32[208,896]{1,0:T(8,128)S(1)}, f32[208,896]{1,0:T(8,128)S(1)}, f32[208,896]{1,0:T(8,128)S(1)}) custom-call(s32[3]{0:T(128)S(1)} %pad_add_fusion.2.order, s32[1]{0:T(128)} %bitcast.3.start, bf16[3,208,448]{2,1,0:T(8,128)(2,1)} %collective-permute-done.8.refs_0_, bf16[3,208,448]{2,1,0:T(8,128)(2,1)} %collective-permute-done.11.refs_1_, ...), custom_call_target="tpu_custom_call" | custom-call | flops 115000000 | bytes 1000 | tf_op jit(solution)/shard_map/projection_peers/pallas_call | solution.py:449
  77.4 4.6 %collective-permute-done.14.refs_0_ = bf16[2,208,448]{2,1,0:T(8,128)(2,1)} collective-permute-done((bf16[2,208,448]{2,1,0:T(8,128)(2,1)}, bf16[2,208,448]{2,1,0:T(8,128)(2,1)}, u32[]{:S(2)}, u32[]{:S(2)}) %collective-permute-start.14) | collective-permute-done | bytes 372768 | tf_op jit(solution)/shard_map/ppermute | solution.py:494
  81.9 0.6 collective-permute-start.19
  82.5 1.4 %collective-permute-start.18 = (bf16[112,896]{1,0:T(8,128)(2,1)S(1)}, bf16[112,896]{1,0:T(8,128)(2,1)S(1)}, u32[]{:S(2)}, u32[]{:S(2)}) collective-permute-start(bf16[112,896]{1,0:T(8,128)(2,1)S(1)} %slice.14), channel_id=1, source_target_pairs={{0,2},{2,4},{4,6},{6,7},{7,5},{5,3},{3,1},{1,0},{8,10},{10,12},{12... | collective-permute-start | bytes 602120 | tf_op jit(solution)/shard_map/ppermute | solution.py:597
  84.0 4.0 %collective-permute-done.19 = bf16[96,896]{1,0:T(8,128)(2,1)S(1)} collective-permute-done((bf16[96,896]{1,0:T(8,128)(2,1)S(1)}, bf16[96,896]{1,0:T(8,128)(2,1)S(1)}, u32[]{:S(2)}, u32[]{:S(2)}) %collective-permute-start.19) | collective-permute-done | bytes 172064 | tf_op jit(solution)/shard_map/ppermute | solution.py:598
  88.0 1.9 %collective-permute-done.18 = bf16[112,896]{1,0:T(8,128)(2,1)S(1)} collective-permute-done((bf16[112,896]{1,0:T(8,128)(2,1)S(1)}, bf16[112,896]{1,0:T(8,128)(2,1)S(1)}, u32[]{:S(2)}, u32[]{:S(2)}) %collective-permute-start.18) | collective-permute-done | bytes 200736 | tf_op jit(solution)/shard_map/ppermute | solution.py:597
  90.0 1.5 %collective-permute-start.20 = (bf16[208,896]{1,0:T(8,128)(2,1)S(1)}, bf16[208,896]{1,0:T(8,128)(2,1)S(1)}, u32[]{:S(2)}, u32[]{:S(2)}) collective-permute-start(bf16[208,896]{1,0:T(8,128)(2,1)S(1)} %add_convert_fusion.5), channel_id=1, source_target_pairs={{0,2},{2,4},{4,6},{6,7},{7,5},{5,3},{3,1},{1,0},{8,10},{10,12},{12... | collective-permute-start | bytes 1118216 | tf_op jit(solution)/shard_map/ppermute | solution.py:622
  91.6 0.7 collective-permute-start.22
  92.9 6.4 %grad_out_rows.3 = (f32[8,208,448]{2,1,0:T(8,128)}, bf16[8,208,448]{2,1,0:T(8,128)(2,1)}) custom-call(s32[4]{0:T(128)S(1)} %pad_add_fusion.3.info, bf16[3200,512]{1,0:T(8,128)(2,1)} %scaled_cotangent.1.refs_2_.turned, bf16[3200,512]{1,0:T(8,128)(2,1)} %collective-permute-done.6.refs_3_.turned_other, ...), custom_call_target="tpu_custom_call", output_to_operand_aliasing={{0}: (7, {}), {1}: (8, {})} | custom-call | flops 115000000 | bytes 1000 | tf_op jit(solution)/shard_map/grad_out_rows/pallas_call | solution.py:324
  99.4 4.3 %projection_peers.4 = (f32[208,896]{1,0:T(8,128)S(1)}, f32[208,896]{1,0:T(8,128)S(1)}) custom-call(s32[2]{0:T(128)S(1)} %pad_add_fusion.1.order, s32[1]{0:T(128)} %bitcast.3.start, bf16[2,208,448]{2,1,0:T(8,128)(2,1)} %collective-permute-done.14.refs_0_, bf16[2,208,448]{2,1,0:T(8,128)(2,1)S(1)} %collective-permute-done.17.refs_1_, ...), custom_call_target="tpu_custom_call" | custom-call | flops 115000000 | bytes 1000 | tf_op jit(solution)/shard_map/projection_peers/pallas_call | solution.py:449
  103.7 0.8 add_convert_fusion.3
  104.5 0.8 add_convert_fusion.2
  105.3 2.1 %collective-permute-done.22.refs_0_ = bf16[3,208,448]{2,1,0:T(8,128)(2,1)} collective-permute-done((bf16[3,208,448]{2,1,0:T(8,128)(2,1)S(1)}, bf16[3,208,448]{2,1,0:T(8,128)(2,1)}, u32[]{:S(2)}, u32[]{:S(2)}) %collective-permute-start.22) | collective-permute-done | bytes 559136 | tf_op jit(solution)/shard_map/ppermute | solution.py:494
  107.4 1.6 %collective-permute-start.24 = (bf16[208,896]{1,0:T(8,128)(2,1)}, bf16[208,896]{1,0:T(8,128)(2,1)}, u32[]{:S(2)}, u32[]{:S(2)}) collective-permute-start(bf16[208,896]{1,0:T(8,128)(2,1)} %add_convert_fusion.3), channel_id=1, source_target_pairs={{0,2},{2,4},{4,6},{6,7},{7,5},{5,3},{3,1},{1,0},{8,10},{10,12},{12... | collective-permute-start | bytes 1118216 | tf_op jit(solution)/shard_map/ppermute | solution.py:622
  109.8 1.3 copy-done.9
  111.2 1.8 %copy-done.12 = bf16[160,1664]{1,0:T(8,128)(2,1)S(1)} copy-done((bf16[160,1664]{1,0:T(8,128)(2,1)S(1)}, bf16[160,1664]{1,0:T(8,128)(2,1)}, u32[]{:S(2)}) %copy-start.12) | copy-done | bytes 532504
  113.0 5.1 %projection_peers.5 = (f32[208,896]{1,0:T(8,128)S(1)}, f32[208,896]{1,0:T(8,128)S(1)}, f32[208,896]{1,0:T(8,128)S(1)}) custom-call(s32[3]{0:T(128)S(1)} %pad_add_fusion.order, s32[1]{0:T(128)} %bitcast.3.start, bf16[3,208,448]{2,1,0:T(8,128)(2,1)} %collective-permute-done.22.refs_0_, bf16[3,208,448]{2,1,0:T(8,128)(2,1)} %collective-permute-done.23.refs_1_, ...), custom_call_target="tpu_custom_call" | custom-call | flops 115000000 | bytes 1000 | tf_op jit(solution)/shard_map/projection_peers/pallas_call | solution.py:449
  118.1 0.7 collective-permute-done.24
  118.8 1.1 add_convert_fusion.1
  120.1 2.3 %copy-done.4 = bf16[3,448,1664]{2,1,0:T(8,128)(2,1)S(1)} copy-done((bf16[3,448,1664]{2,1,0:T(8,128)(2,1)S(1)}, bf16[3,448,1664]{2,1,0:T(8,128)(2,1)}, u32[]{:S(2)}) %copy-start.4) | copy-done | bytes 4472856
  122.4 3.3 %attention_backward.3.rest_0_ = bf16[3,448,1664]{2,1,0:T(8,128)(2,1)} custom-call(bf16[3,448,1664]{2,1,0:T(8,128)(2,1)S(1)} %copy-done.4, f32[1664,448]{1,0:T(8,128)S(1)} %bitcast.19, bf16[1664,448]{1,0:T(8,128)(2,1)S(1)} %bitcast.22, f32[13,256,256]{2,1,0:T(8,128)S(1)} %copy-done.5, f32[13,192,192]{2,1,0:T(8,128)S(1)} %copy-done.6), custom_call_target="tpu_custom_call" | custom-call | flops 3449999872 | bytes 1000 | tf_op jit(solution)/shard_map/attention_backward/pallas_call | solution.py:256
  125.7 1.6 %collective-permute-start.27 = (bf16[208,896]{1,0:T(8,128)(2,1)S(1)}, bf16[208,896]{1,0:T(8,128)(2,1)S(1)}, u32[]{:S(2)}, u32[]{:S(2)}) collective-permute-start(bf16[208,896]{1,0:T(8,128)(2,1)S(1)} %add_convert_fusion.1), channel_id=1, source_target_pairs={{0,2},{2,4},{4,6},{6,7},{7,5},{5,3},{3,1},{1,0},{8,10},{10,12},{12... | collective-permute-start | bytes 1118216 | tf_op jit(solution)/shard_map/ppermute | solution.py:622
  127.7 2.5 %attention_backward.4.rest_0_ = bf16[3,448,1664]{2,1,0:T(8,128)(2,1)} custom-call(bf16[3,448,1664]{2,1,0:T(8,128)(2,1)S(1)} %copy-done.4, f32[1664,448]{1,0:T(8,128)S(1)} %bitcast.20, bf16[1664,448]{1,0:T(8,128)(2,1)S(1)} %bitcast.23, f32[13,256,256]{2,1,0:T(8,128)S(1)} %copy-done.5, f32[13,192,192]{2,1,0:T(8,128)S(1)} %copy-done.6, ...), custom_call_target="tpu_custom_call", output_to_operand_aliasing={{}: (5, {})} | custom-call | flops 2300000000 | bytes 1000 | tf_op jit(solution)/shard_map/attention_backward/pallas_call | solution.py:256
  130.2 2.4 %attention_backward.5 = bf16[3,448,1664]{2,1,0:T(8,128)(2,1)} custom-call(bf16[3,448,1664]{2,1,0:T(8,128)(2,1)S(1)} %copy-done.4, f32[1664,448]{1,0:T(8,128)S(1)} %bitcast.21, bf16[1664,448]{1,0:T(8,128)(2,1)S(1)} %bitcast.24, f32[13,256,256]{2,1,0:T(8,128)S(1)} %copy-done.5, f32[13,192,192]{2,1,0:T(8,128)S(1)} %copy-done.6, ...), custom_call_target="tpu_custom_call", output_to_operand_aliasing={{}: (5, {})} | custom-call | flops 2300000000 | bytes 1000 | tf_op jit(solution)/shard_map/attention_backward/pallas_call | solution.py:256
  132.6 3.3 %collective-permute-done.27.came_up = bf16[208,896]{1,0:T(8,128)(2,1)S(1)} collective-permute-done((bf16[208,896]{1,0:T(8,128)(2,1)S(1)}, bf16[208,896]{1,0:T(8,128)(2,1)S(1)}, u32[]{:S(2)}, u32[]{:S(2)}) %collective-permute-start.27) | collective-permute-done | bytes 372768 | tf_op jit(solution)/shard_map/ppermute | solution.py:622
  135.9 1.3 collective-permute-done.28.came_down
  137.2 1.1 last_sum.1
  (77 shorter events, 5.3 us)
Async XLA Ops:
  0.6 15.5 %copy-start = (s32[4,1,4]{2,1,0:T(1,128)S(1)}, s32[4,1,4]{2,1,0:T(1,128)}, u32[]{:S(2)}) copy-start(s32[4,1,4]{2,1,0:T(1,128)} %param.9) | copy-start | bytes 196
  1.8 6.3 %copy-start.13 = (bf16[208,1664]{1,0:T(8,128)(2,1)}, bf16[208,1664]{1,0:T(8,128)(2,1)S(1)}, u32[]{:S(2)}) copy-start(bf16[208,1664]{1,0:T(8,128)(2,1)S(1)} %own_half_of_weight.1.refs_0_) | copy-start | bytes 2076676
  1.8 21.7 %collective-permute-start.1 = (bf16[208,1664]{1,0:T(8,128)(2,1)S(1)}, bf16[208,1664]{1,0:T(8,128)(2,1)}, u32[]{:S(2)}, u32[]{:S(2)}) collective-permute-start(bf16[208,1664]{1,0:T(8,128)(2,1)S(1)} %own_half_of_weight.1.refs_0_), channel_id=1, source_target_pairs={{0,2},{2,4},{4,6},{6,7},{7,5},{5,3},{3,1},{1,0},{8,10},{10,12},{12... | collective-permute-start | bytes 2076680 | tf_op jit(solution)/shard_map/ppermute | solution.py:515
  4.9 18.6 %collective-permute-start.2 = (bf16[208,1664]{1,0:T(8,128)(2,1)S(1)}, bf16[208,1664]{1,0:T(8,128)(2,1)}, u32[]{:S(2)}, u32[]{:S(2)}) collective-permute-start(bf16[208,1664]{1,0:T(8,128)(2,1)S(1)} %own_half_of_weight.1.refs_0_), channel_id=1, source_target_pairs={{0,1},{2,0},{4,2},{6,4},{7,6},{5,7},{3,5},{1,3},{8,9},{10,8},{12,1... | collective-permute-start | bytes 2076680 | tf_op jit(solution)/shard_map/ppermute | solution.py:516
  8.1 15.4 %collective-permute-start.3 = (bf16[160,1664]{1,0:T(8,128)(2,1)}, bf16[160,1664]{1,0:T(8,128)(2,1)S(1)}, u32[]{:S(2)}, u32[]{:S(2)}) collective-permute-start(bf16[160,1664]{1,0:T(8,128)(2,1)} %get-tuple-element.98), channel_id=1, source_target_pairs={{0,16},{8,24},{16,0},{24,8},{1,17},{9,25},{17,1},{25,9},{2,18},{10... | collective-permute-start | bytes 1597448 | tf_op jit(solution)/shard_map/ppermute | solution.py:494
  10.1 6.0 %copy-start.3 = (bf16[3,448,1664]{2,1,0:T(8,128)(2,1)S(1)}, bf16[3,448,1664]{2,1,0:T(8,128)(2,1)}, u32[]{:S(2)}) copy-start(bf16[3,448,1664]{2,1,0:T(8,128)(2,1)} %qkv.7) | copy-start | bytes 13418500
  23.5 19.7 %collective-permute-start.6 = (bf16[3200,512]{1,0:T(8,128)(2,1)}, bf16[3200,512]{1,0:T(8,128)(2,1)}, u32[]{:S(2)}, u32[]{:S(2)}) collective-permute-start(bf16[3200,512]{1,0:T(8,128)(2,1)} %scaled_cotangent.1.refs_2_.turned), channel_id=1, source_target_pairs={{0,8},{8,0},{16,24},{24,16},{1,9},{9,1},{17,25},{25,17},{2,10},{10... | collective-permute-start | bytes 9830408 | tf_op jit(solution)/shard_map/ppermute | solution.py:494
  23.6 19.6 %collective-permute-start.7 = (bf16[8,208,448]{2,1,0:T(8,128)(2,1)}, bf16[8,208,448]{2,1,0:T(8,128)(2,1)S(1)}, u32[]{:S(2)}, u32[]{:S(2)}) collective-permute-start(bf16[8,208,448]{2,1,0:T(8,128)(2,1)} %bitcast.25), channel_id=1, source_target_pairs={{0,8},{8,0},{16,24},{24,16},{1,9},{9,1},{17,25},{25,17},{2,10},{10... | collective-permute-start | bytes 4472840 | tf_op jit(solution)/shard_map/ppermute | solution.py:494
  24.1 17.8 %collective-permute-start.4 = (bf16[208,1664]{1,0:T(8,128)(2,1)}, bf16[208,1664]{1,0:T(8,128)(2,1)}, u32[]{:S(2)}, u32[]{:S(2)}) collective-permute-start(bf16[208,1664]{1,0:T(8,128)(2,1)} %collective-permute-done.1.refs_1_), channel_id=1, source_target_pairs={{0,2},{2,4},{4,6},{6,7},{7,5},{5,3},{3,1},{1,0},{8,10},{10,12},{12... | collective-permute-start | bytes 2076680 | tf_op jit(solution)/shard_map/ppermute | solution.py:546
  25.6 17.5 %collective-permute-start.5 = (bf16[208,1664]{1,0:T(8,128)(2,1)}, bf16[208,1664]{1,0:T(8,128)(2,1)}, u32[]{:S(2)}, u32[]{:S(2)}) collective-permute-start(bf16[208,1664]{1,0:T(8,128)(2,1)} %collective-permute-done.2.refs_2_), channel_id=1, source_target_pairs={{0,1},{2,0},{4,2},{6,4},{7,6},{5,7},{3,5},{1,3},{8,9},{10,8},{12,1... | collective-permute-start | bytes 2076680 | tf_op jit(solution)/shard_map/ppermute | solution.py:547
  26.1 28.3 %collective-permute-start = (bf16[288,1664]{1,0:T(8,128)(2,1)}, bf16[288,1664]{1,0:T(8,128)(2,1)S(1)}, u32[]{:S(2)}, u32[]{:S(2)}) collective-permute-start(bf16[288,1664]{1,0:T(8,128)(2,1)} %get-tuple-element.96), channel_id=1, source_target_pairs={{0,16},{8,24},{16,0},{24,8},{1,17},{9,25},{17,1},{25,9},{2,18},{10... | collective-permute-start | bytes 2875400 | tf_op jit(solution)/shard_map/ppermute | solution.py:494
  29.5 0.9 copy-start.15
  43.2 22.0 %collective-permute-start.9 = (bf16[208,1664]{1,0:T(8,128)(2,1)}, bf16[208,1664]{1,0:T(8,128)(2,1)}, u32[]{:S(2)}, u32[]{:S(2)}) collective-permute-start(bf16[208,1664]{1,0:T(8,128)(2,1)} %collective-permute-done.4.refs_3_), channel_id=1, source_target_pairs={{0,2},{2,4},{4,6},{6,7},{7,5},{5,3},{3,1},{1,0},{8,10},{10,12},{12... | collective-permute-start | bytes 2076680 | tf_op jit(solution)/shard_map/ppermute | solution.py:568
  44.8 20.4 %collective-permute-start.10 = (bf16[208,1664]{1,0:T(8,128)(2,1)}, bf16[208,1664]{1,0:T(8,128)(2,1)}, u32[]{:S(2)}, u32[]{:S(2)}) collective-permute-start(bf16[208,1664]{1,0:T(8,128)(2,1)} %collective-permute-done.5.refs_4_), channel_id=1, source_target_pairs={{0,1},{2,0},{4,2},{6,4},{7,6},{5,7},{3,5},{1,3},{8,9},{10,8},{12,1... | collective-permute-start | bytes 2076680 | tf_op jit(solution)/shard_map/ppermute | solution.py:569
  54.4 15.0 %collective-permute-start.8 = (bf16[3,208,448]{2,1,0:T(8,128)(2,1)}, bf16[3,208,448]{2,1,0:T(8,128)(2,1)}, u32[]{:S(2)}, u32[]{:S(2)}) collective-permute-start(bf16[3,208,448]{2,1,0:T(8,128)(2,1)} %get-tuple-element.117), channel_id=1, source_target_pairs={{0,16},{8,24},{16,0},{24,8},{1,17},{9,25},{17,1},{25,9},{2,18},{10... | collective-permute-start | bytes 1677320 | tf_op jit(solution)/shard_map/ppermute | solution.py:494
  55.0 16.5 %collective-permute-start.12 = (bf16[160,1664]{1,0:T(8,128)(2,1)S(1)}, bf16[160,1664]{1,0:T(8,128)(2,1)S(1)}, u32[]{:S(2)}, u32[]{:S(2)}) collective-permute-start(bf16[160,1664]{1,0:T(8,128)(2,1)S(1)} %collective-permute-done.3.refs_2_), channel_id=1, source_target_pairs={{0,8},{8,0},{16,24},{24,16},{1,9},{9,1},{17,25},{25,17},{2,10},{10... | collective-permute-start | bytes 1597448 | tf_op jit(solution)/shard_map/ppermute | solution.py:494
  55.1 17.0 %collective-permute-start.13 = (bf16[288,1664]{1,0:T(8,128)(2,1)S(1)}, bf16[288,1664]{1,0:T(8,128)(2,1)S(1)}, u32[]{:S(2)}, u32[]{:S(2)}) collective-permute-start(bf16[288,1664]{1,0:T(8,128)(2,1)S(1)} %collective-permute-done.refs_3_), channel_id=1, source_target_pairs={{0,8},{8,0},{16,24},{24,16},{1,9},{9,1},{17,25},{25,17},{2,10},{10... | collective-permute-start | bytes 2875400 | tf_op jit(solution)/shard_map/ppermute | solution.py:494
  55.6 1.1 copy-start.14
  69.4 2.7 %collective-permute-start.11 = (bf16[3,208,448]{2,1,0:T(8,128)(2,1)}, bf16[3,208,448]{2,1,0:T(8,128)(2,1)}, u32[]{:S(2)}, u32[]{:S(2)}) collective-permute-start(bf16[3,208,448]{2,1,0:T(8,128)(2,1)} %collective-permute-done.8.refs_0_), channel_id=1, source_target_pairs={{0,8},{8,0},{16,24},{24,16},{1,9},{9,1},{17,25},{25,17},{2,10},{10... | collective-permute-start | bytes 1677320 | tf_op jit(solution)/shard_map/ppermute | solution.py:494
  69.4 12.5 %collective-permute-start.14 = (bf16[2,208,448]{2,1,0:T(8,128)(2,1)}, bf16[2,208,448]{2,1,0:T(8,128)(2,1)}, u32[]{:S(2)}, u32[]{:S(2)}) collective-permute-start(bf16[2,208,448]{2,1,0:T(8,128)(2,1)} %get-tuple-element.141), channel_id=1, source_target_pairs={{0,16},{8,24},{16,0},{24,8},{1,17},{9,25},{17,1},{25,9},{2,18},{10... | collective-permute-start | bytes 1118216 | tf_op jit(solution)/shard_map/ppermute | solution.py:494
  69.9 12.0 %collective-permute-start.15 = (bf16[112,1664]{1,0:T(8,128)(2,1)}, bf16[112,1664]{1,0:T(8,128)(2,1)}, u32[]{:S(2)}, u32[]{:S(2)}) collective-permute-start(bf16[112,1664]{1,0:T(8,128)(2,1)} %get-tuple-element.163.refs_6_), channel_id=1, source_target_pairs={{0,2},{2,4},{4,6},{6,7},{7,5},{5,3},{3,1},{1,0},{8,10},{10,12},{12... | collective-permute-start | bytes 1118216 | tf_op jit(solution)/shard_map/ppermute | solution.py:577
  71.5 5.8 %copy-start.10 = (bf16[160,1664]{1,0:T(8,128)(2,1)}, bf16[160,1664]{1,0:T(8,128)(2,1)S(1)}, u32[]{:S(2)}) copy-start(bf16[160,1664]{1,0:T(8,128)(2,1)S(1)} %collective-permute-done.12.refs_4_) | copy-start | bytes 1597444
  71.5 10.4 %collective-permute-start.16 = (bf16[96,1664]{1,0:T(8,128)(2,1)}, bf16[96,1664]{1,0:T(8,128)(2,1)S(1)}, u32[]{:S(2)}, u32[]{:S(2)}) collective-permute-start(bf16[96,1664]{1,0:T(8,128)(2,1)} %get-tuple-element.143), channel_id=1, source_target_pairs={{0,1},{2,0},{4,2},{6,4},{7,6},{5,7},{3,5},{1,3},{8,9},{10,8},{12,1... | collective-permute-start | bytes 958472 | tf_op jit(solution)/shard_map/ppermute | solution.py:578
  72.0 5.3 %copy-start.7 = (bf16[288,1664]{1,0:T(8,128)(2,1)}, bf16[288,1664]{1,0:T(8,128)(2,1)S(1)}, u32[]{:S(2)}) copy-start(bf16[288,1664]{1,0:T(8,128)(2,1)S(1)} %collective-permute-done.13.refs_5_) | copy-start | bytes 2875396
  77.2 14.4 %copy-start.16 = (bf16[3,208,448]{2,1,0:T(8,128)(2,1)S(1)}, bf16[3,208,448]{2,1,0:T(8,128)(2,1)}, u32[]{:S(2)}) copy-start(bf16[3,208,448]{2,1,0:T(8,128)(2,1)} %copy-done.15) | copy-start | bytes 1677316
  81.9 6.0 %collective-permute-start.19 = (bf16[96,896]{1,0:T(8,128)(2,1)S(1)}, bf16[96,896]{1,0:T(8,128)(2,1)S(1)}, u32[]{:S(2)}, u32[]{:S(2)}) collective-permute-start(bf16[96,896]{1,0:T(8,128)(2,1)S(1)} %slice.15), channel_id=1, source_target_pairs={{0,1},{2,0},{4,2},{6,4},{7,6},{5,7},{3,5},{1,3},{8,9},{10,8},{12,1... | collective-permute-start | bytes 516104 | tf_op jit(solution)/shard_map/ppermute | solution.py:598
  82.5 16.8 %collective-permute-start.17 = (bf16[2,208,448]{2,1,0:T(8,128)(2,1)}, bf16[2,208,448]{2,1,0:T(8,128)(2,1)S(1)}, u32[]{:S(2)}, u32[]{:S(2)}) collective-permute-start(bf16[2,208,448]{2,1,0:T(8,128)(2,1)} %collective-permute-done.14.refs_0_), channel_id=1, source_target_pairs={{0,8},{8,0},{16,24},{24,16},{1,9},{9,1},{17,25},{25,17},{2,10},{10... | collective-permute-start | bytes 1118216 | tf_op jit(solution)/shard_map/ppermute | solution.py:494
  82.5 7.4 %collective-permute-start.18 = (bf16[112,896]{1,0:T(8,128)(2,1)S(1)}, bf16[112,896]{1,0:T(8,128)(2,1)S(1)}, u32[]{:S(2)}, u32[]{:S(2)}) collective-permute-start(bf16[112,896]{1,0:T(8,128)(2,1)S(1)} %slice.14), channel_id=1, source_target_pairs={{0,2},{2,4},{4,6},{6,7},{7,5},{5,3},{3,1},{1,0},{8,10},{10,12},{12... | collective-permute-start | bytes 602120 | tf_op jit(solution)/shard_map/ppermute | solution.py:597
  90.0 13.7 %collective-permute-start.20 = (bf16[208,896]{1,0:T(8,128)(2,1)S(1)}, bf16[208,896]{1,0:T(8,128)(2,1)S(1)}, u32[]{:S(2)}, u32[]{:S(2)}) collective-permute-start(bf16[208,896]{1,0:T(8,128)(2,1)S(1)} %add_convert_fusion.5), channel_id=1, source_target_pairs={{0,2},{2,4},{4,6},{6,7},{7,5},{5,3},{3,1},{1,0},{8,10},{10,12},{12... | collective-permute-start | bytes 1118216 | tf_op jit(solution)/shard_map/ppermute | solution.py:622
  91.6 15.8 %collective-permute-start.22 = (bf16[3,208,448]{2,1,0:T(8,128)(2,1)S(1)}, bf16[3,208,448]{2,1,0:T(8,128)(2,1)}, u32[]{:S(2)}, u32[]{:S(2)}) collective-permute-start(bf16[3,208,448]{2,1,0:T(8,128)(2,1)S(1)} %copy-done.16), channel_id=1, source_target_pairs={{0,16},{8,24},{16,0},{24,8},{1,17},{9,25},{17,1},{25,9},{2,18},{10... | collective-permute-start | bytes 1677320 | tf_op jit(solution)/shard_map/ppermute | solution.py:494
  92.2 12.3 %collective-permute-start.21 = (bf16[208,896]{1,0:T(8,128)(2,1)S(1)}, bf16[208,896]{1,0:T(8,128)(2,1)S(1)}, u32[]{:S(2)}, u32[]{:S(2)}) collective-permute-start(bf16[208,896]{1,0:T(8,128)(2,1)S(1)} %add_convert_fusion.4), channel_id=1, source_target_pairs={{0,1},{2,0},{4,2},{6,4},{7,6},{5,7},{3,5},{1,3},{8,9},{10,8},{12,1... | collective-permute-start | bytes 1118216 | tf_op jit(solution)/shard_map/ppermute | solution.py:623
  92.8 6.5 %copy-start.8 = (bf16[288,1664]{1,0:T(8,128)(2,1)S(1)}, bf16[288,1664]{1,0:T(8,128)(2,1)}, u32[]{:S(2)}) copy-start(bf16[288,1664]{1,0:T(8,128)(2,1)} %copy-done.7) | copy-start | bytes 2875396
  92.9 6.6 %copy-start.11 = (bf16[160,1664]{1,0:T(8,128)(2,1)S(1)}, bf16[160,1664]{1,0:T(8,128)(2,1)}, u32[]{:S(2)}) copy-start(bf16[160,1664]{1,0:T(8,128)(2,1)} %copy-done.10) | copy-start | bytes 1597444
  99.3 20.8 %collective-permute-start.26 = (bf16[8,208,448]{2,1,0:T(8,128)(2,1)}, bf16[8,208,448]{2,1,0:T(8,128)(2,1)S(1)}, u32[]{:S(2)}, u32[]{:S(2)}) collective-permute-start(bf16[8,208,448]{2,1,0:T(8,128)(2,1)} %get-tuple-element.174), channel_id=1, source_target_pairs={{0,8},{8,0},{16,24},{24,16},{1,9},{9,1},{17,25},{25,17},{2,10},{10... | collective-permute-start | bytes 4472840 | tf_op jit(solution)/shard_map/ppermute | solution.py:494
  107.4 2.4 %collective-permute-start.23 = (bf16[3,208,448]{2,1,0:T(8,128)(2,1)}, bf16[3,208,448]{2,1,0:T(8,128)(2,1)}, u32[]{:S(2)}, u32[]{:S(2)}) collective-permute-start(bf16[3,208,448]{2,1,0:T(8,128)(2,1)} %collective-permute-done.22.refs_0_), channel_id=1, source_target_pairs={{0,8},{8,0},{16,24},{24,16},{1,9},{9,1},{17,25},{25,17},{2,10},{10... | collective-permute-start | bytes 1677320 | tf_op jit(solution)/shard_map/ppermute | solution.py:494
  107.4 11.4 %collective-permute-start.24 = (bf16[208,896]{1,0:T(8,128)(2,1)}, bf16[208,896]{1,0:T(8,128)(2,1)}, u32[]{:S(2)}, u32[]{:S(2)}) collective-permute-start(bf16[208,896]{1,0:T(8,128)(2,1)} %add_convert_fusion.3), channel_id=1, source_target_pairs={{0,2},{2,4},{4,6},{6,7},{7,5},{5,3},{3,1},{1,0},{8,10},{10,12},{12... | collective-permute-start | bytes 1118216 | tf_op jit(solution)/shard_map/ppermute | solution.py:622
  109.0 11.0 %collective-permute-start.25 = (bf16[208,896]{1,0:T(8,128)(2,1)}, bf16[208,896]{1,0:T(8,128)(2,1)S(1)}, u32[]{:S(2)}, u32[]{:S(2)}) collective-permute-start(bf16[208,896]{1,0:T(8,128)(2,1)} %add_convert_fusion.2), channel_id=1, source_target_pairs={{0,1},{2,0},{4,2},{6,4},{7,6},{5,7},{3,5},{1,3},{8,9},{10,8},{12,1... | collective-permute-start | bytes 1118216 | tf_op jit(solution)/shard_map/ppermute | solution.py:623
  109.5 10.6 %copy-start.2 = (f32[8,208,448]{2,1,0:T(8,128)S(1)}, f32[8,208,448]{2,1,0:T(8,128)}, u32[]{:S(2)}) copy-start(f32[8,208,448]{2,1,0:T(8,128)} %get-tuple-element.164) | copy-start | bytes 8945668
  109.5 10.6 %copy-start.5 = (f32[13,256,256]{2,1,0:T(8,128)S(1)}, f32[13,256,256]{2,1,0:T(8,128)}, u32[]{:S(2)}) copy-start(f32[13,256,256]{2,1,0:T(8,128)} %get-tuple-element.175.main_probs) | copy-start | bytes 10223620
  109.5 10.6 %copy-start.6 = (f32[13,192,192]{2,1,0:T(8,128)S(1)}, f32[13,192,192]{2,1,0:T(8,128)}, u32[]{:S(2)}) copy-start(f32[13,192,192]{2,1,0:T(8,128)} %get-tuple-element.176.slot_probs) | copy-start | bytes 5750788
  109.8 1.3 copy-start.9
  111.2 1.8 %copy-start.12 = (bf16[160,1664]{1,0:T(8,128)(2,1)S(1)}, bf16[160,1664]{1,0:T(8,128)(2,1)}, u32[]{:S(2)}) copy-start(bf16[160,1664]{1,0:T(8,128)(2,1)} %copy-done.10) | copy-start | bytes 1597444
  120.1 2.3 %copy-start.4 = (bf16[3,448,1664]{2,1,0:T(8,128)(2,1)S(1)}, bf16[3,448,1664]{2,1,0:T(8,128)(2,1)}, u32[]{:S(2)}) copy-start(bf16[3,448,1664]{2,1,0:T(8,128)(2,1)} %qkv.7) | copy-start | bytes 13418500
  125.7 10.2 %collective-permute-start.27 = (bf16[208,896]{1,0:T(8,128)(2,1)S(1)}, bf16[208,896]{1,0:T(8,128)(2,1)S(1)}, u32[]{:S(2)}, u32[]{:S(2)}) collective-permute-start(bf16[208,896]{1,0:T(8,128)(2,1)S(1)} %add_convert_fusion.1), channel_id=1, source_target_pairs={{0,2},{2,4},{4,6},{6,7},{7,5},{5,3},{3,1},{1,0},{8,10},{10,12},{12... | collective-permute-start | bytes 1118216 | tf_op jit(solution)/shard_map/ppermute | solution.py:622
  127.3 9.9 %collective-permute-start.28 = (bf16[208,896]{1,0:T(8,128)(2,1)S(1)}, bf16[208,896]{1,0:T(8,128)(2,1)S(1)}, u32[]{:S(2)}, u32[]{:S(2)}) collective-permute-start(bf16[208,896]{1,0:T(8,128)(2,1)S(1)} %add_convert_fusion), channel_id=1, source_target_pairs={{0,1},{2,0},{4,2},{6,4},{7,6},{5,7},{3,5},{1,3},{8,9},{10,8},{12,1... | collective-permute-start | bytes 1118216 | tf_op jit(solution)/shard_map/ppermute | solution.py:623
  130.2 8.1 %copy-start.1 = (s32[4,1,4]{2,1,0:T(1,128)S(1)}, s32[4,1,4]{2,1,0:T(1,128)}, u32[]{:S(2)}) copy-start(s32[4,1,4]{2,1,0:T(1,128)} %param.9) | copy-start | bytes 196

commit v4 on v3

--- a/solution.py
+++ b/solution.py
@@ -461,7 +461,7 @@
         ),
         out_shape=[(jax.ShapeDtypeStruct if bases else pltpu.HBM)((depth, window), jnp.float32)] * count,
         compiler_params=pltpu.CompilerParams(vmem_limit_bytes=VMEM_BYTES),
-        cost_estimate=lasting(0.2 if bases else 6),
+        cost_estimate=lasting(3 if bases else 6),
         name="projection_peers" if bases else "projection_chip",
     )(order, start, *attended, *columns, *map(in_hbm, bases))
 
@@ -545,14 +545,15 @@
     for _ in range(half - 3):
         up.append(lax.ppermute(up[-1], "fsdp", ahead))
         down.append(lax.ppermute(down[-1], "fsdp", behind))
-    up[-1], down[-1], turned_other, attended_other = lax.optimization_barrier(
-        (up[-1], down[-1], turned_other, attended_other)
-    )
-
     bases = partial_products(
         flat, starts[:1], [in_hbm(attended), attended_other], [in_hbm(turned), turned_other], window
     )
-    late, chunks, *bases = lax.optimization_barrier((came_columns[1], chunks, *bases))
+    up[-1], down[-1], turned_other, attended_other, *bases = lax.optimization_barrier(
+        (up[-1], down[-1], turned_other, attended_other, *bases)
+    )
+    bases = dict(zip([o for group in groups for o in group], bases))
+
+    late, chunks = lax.optimization_barrier((came_columns[1], chunks))
     came = [[swap(chunks[0], 2 * k) for k in range(1, peers)]]
     other_columns.append([swap(array, 1) for array in late])
     came_columns[1] = late
@@ -567,8 +568,7 @@
     grad_out = rows_of(pieces, None)
     up.append(lax.ppermute(up[-1], "fsdp", ahead))
     down.append(lax.ppermute(down[-1], "fsdp", behind))
-    up[-1], down[-1], grad_out, *bases = lax.optimization_barrier((up[-1], down[-1], grad_out, *bases))
-    bases = dict(zip([o for group in groups for o in group], bases))
+    up[-1], down[-1], grad_out = lax.optimization_barrier((up[-1], down[-1], grad_out))
     if depth % 16 == 0:
         far_up, far_down = far_parts(up[-1], down[-1], cut)
     else:
@@ -601,10 +601,10 @@
     grads = None
     for step in range(half, 1, -1):
         if step == half:
+            came_up, came_down, following = lax.optimization_barrier((came_up, came_down, products(1, taken)))
+            terms.update(following)
             came_up = jnp.pad(came_up, ((0, depth - cut), (0, 0)))
             came_down = jnp.pad(came_down, ((cut, 0), (0, 0)))
-        else:
-            terms.update(products(half - step, taken))
         going_up = (terms[step - 1] + came_up.astype(jnp.float32)).astype(jnp.bfloat16)
         going_down = (terms[1 - step] + came_down.astype(jnp.float32)).astype(jnp.bfloat16)
         if step == half:
@@ -615,13 +615,12 @@
         elif step > 2:
             arrived = came[half - step + 1]
             going_up, going_down, arrived, grad_mine = lax.optimization_barrier((going_up, going_down, arrived, grad_mine))
-            taken = both_cores(arrived)
+            terms.update(products(half - step + 1, both_cores(arrived)))
         else:
-            grads = backward(query_key_value, grad_mine, grad_other, main_probs, slot_probs, bounds[0], bounds[1], grads)
-            going_up, going_down, grads = lax.optimization_barrier((going_up, going_down, grads))
+            going_up, going_down = lax.optimization_barrier((going_up, going_down))
         came_up = lax.ppermute(going_up, "fsdp", ahead)
         came_down = lax.ppermute(going_down, "fsdp", behind)
-    for low, high in zip(bounds[1:], bounds[2:]):
+    for low, high in zip(bounds, bounds[1:]):
         grads = backward(query_key_value, grad_mine, grad_other, main_probs, slot_probs, low, high, grads)
     came_up, came_down, grads = lax.optimization_barrier((came_up, came_down, grads))
     offsets = set()

time: 139 us -> 131 us (0.942)
  waiting for transfers between devices: 33.5 us -> 21.3 us
  local copies, waits for them, and re-layouts: 8.34 us -> 11.7 us
    ppermute x3, waiting for transfers between devices: 11.6 us -> 0.55 us  [local(): up.append(lax.ppermute(up[-1], 'fsdp', ahead))]
    ppermute x13, waiting for transfers between devices: 9.23 us -> 15.3 us  [swap(): return lax.ppermute(array, 'dp', [(i, i ^ bit) for i in range(members)])]
    ppermute x4, waiting for transfers between devices: 5.97 us -> 1.15 us  [local(): came_up = lax.ppermute(going_up, 'fsdp', ahead)]
    unnamed x34 -> x38, local copies, waits for them, and re-layouts: 7.41 us -> 10.8 us
    ppermute x4, waiting for transfers between devices: 5.4 us -> 2.72 us  [local(): came_down = lax.ppermute(going_down, 'fsdp', behind)]
  transfers between devices with their start and end apart: 29 -> 29, of which waited for: 12 -> 12; matrix products, arithmetic and copies ran while one was open for 3% -> 3% of each run, Pallas kernels for 47% -> 52%
where the time goes in v4:
time: 131 us
  Pallas kernels  70 us (53%)
  starting transfers between devices  23.5 us (18%)
  waiting for transfers between devices  21.3 us (16%)
  local copies, waits for them, and re-layouts  11.7 us (9%)
  other arithmetic  3.26 us (2%)
    pallas_call x4, Pallas kernels, partial_products(): pl.pallas_call(functools.partial(partial_kernel, not bases, sources, part...  23.7 us
    ppermute x13, waiting for transfers between devices, swap(): return lax.ppermute(array, 'dp', [(i, i ^ bit) for i in range(members)])  15.3 us
    pallas_call x2, Pallas kernels, grad_out_rows(): pl.pallas_call(functools.partial(grad_out_kernel, sizes, split, total), g...  14.7 us
    unnamed x38, local copies, waits for them, and re-layouts  10.8 us
    pallas_call x3, Pallas kernels, backward(): pl.pallas_call(backward_kernel, grid=(high - low,), in_specs=[pl.BlockSpe...  8.4 us
    pallas_call x1, Pallas kernels, forward(): pl.pallas_call(forward_kernel, grid_spec=pltpu.PrefetchScalarGridSpec(num...  7.35 us
    ppermute x3, starting transfers between devices, local(): up.append(lax.ppermute(up[-1], 'fsdp', ahead))  6.64 us
    ppermute x4, starting transfers between devices, local(): came_up = lax.ppermute(going_up, 'fsdp', ahead)  6.21 us
  transfers between devices with their start and end apart: 29, of which 12 were waited for; matrix products, arithmetic and copies ran while one was open for 3% of the time, Pallas kernels for 52%

profile of v4, /device:TPU:0, one launch (start us, length us, event | category | flops | bytes accessed | tf_op | source)
XLA Modules:
  0.0 130.7 jit_solution(6232472864835915712)
XLA Ops:
  0.7 1.1 own_half_of_weight.1.refs_0_
  1.8 3.1 %collective-permute-start.1 = (bf16[208,1664]{1,0:T(8,128)(2,1)S(1)}, bf16[208,1664]{1,0:T(8,128)(2,1)S(1)}, u32[]{:S(2)}, u32[]{:S(2)}) collective-permute-start(bf16[208,1664]{1,0:T(8,128)(2,1)S(1)} %own_half_of_weight.1.refs_0_), channel_id=1, source_target_pairs={{0,2},{2,4},{4,6},{6,7},{7,5},{5,3},{3,1},{1,0},{8,10},{10,12},{12... | collective-permute-start | bytes 2076680 | tf_op jit(solution)/shard_map/ppermute | solution.py:515
  4.9 0.7 reshape.18.layer_scale
  5.6 2.5 %peer_windows.1 = (bf16[160,1664]{1,0:T(8,128)(2,1)}, bf16[288,1664]{1,0:T(8,128)(2,1)}) custom-call(s32[1]{0:T(128)} %bitcast.7.starts, bf16[448,3200]{1,0:T(8,128)(2,1)} %cotangent.1, f32[1,3200]{1,0:T(1,128)S(1)} %reshape.18.layer_scale), custom_call_target="tpu_custom_call" | custom-call | flops 34500001792 | bytes 1000 | tf_op jit(solution)/shard_map/peer_windows/pallas_call | solution.py:58
  8.1 2.0 %collective-permute-start.3 = (bf16[160,1664]{1,0:T(8,128)(2,1)}, bf16[160,1664]{1,0:T(8,128)(2,1)S(1)}, u32[]{:S(2)}, u32[]{:S(2)}) collective-permute-start(bf16[160,1664]{1,0:T(8,128)(2,1)} %get-tuple-element.92), channel_id=1, source_target_pairs={{0,16},{8,24},{16,0},{24,8},{1,17},{9,25},{17,1},{25,9},{2,18},{10... | collective-permute-start | bytes 1597448 | tf_op jit(solution)/shard_map/ppermute | solution.py:494
  10.1 6.0 %scaled_cotangent.1.refs_2_.turned = bf16[3200,512]{1,0:T(8,128)(2,1)} custom-call(bf16[448,3200]{1,0:T(8,128)(2,1)} %cotangent.1, f32[1,3200]{1,0:T(1,128)S(1)} %reshape.18.layer_scale), custom_call_target="tpu_custom_call" | custom-call | flops 34500001792 | bytes 1000 | tf_op jit(solution)/shard_map/scaled_cotangent/pallas_call | solution.py:89
  16.1 7.4 %attention_forward.1 = (bf16[1664,448]{1,0:T(8,128)(2,1)}, f32[13,256,256]{2,1,0:T(8,128)}, f32[13,192,192]{2,1,0:T(8,128)}) custom-call(s32[4]{0:T(128)S(1)} %dynamic-slice_bitcast_fusion.counts, bf16[3,448,1664]{2,1,0:T(8,128)(2,1)S(1)} %copy-done.3), custom_call_target="tpu_custom_call" | custom-call | flops 34500001792 | bytes 1000 | tf_op jit(solution)/shard_map/attention_forward/pallas_call | solution.py:206
  23.5 0.9 copy-done.13
  25.2 2.0 %collective-permute-start.5 = (bf16[208,1664]{1,0:T(8,128)(2,1)}, bf16[208,1664]{1,0:T(8,128)(2,1)}, u32[]{:S(2)}, u32[]{:S(2)}) collective-permute-start(bf16[208,1664]{1,0:T(8,128)(2,1)} %copy-done.13), channel_id=1, source_target_pairs={{0,2},{2,4},{4,6},{6,7},{7,5},{5,3},{3,1},{1,0},{8,10},{10,12},{12... | collective-permute-start | bytes 2076680 | tf_op jit(solution)/shard_map/ppermute | solution.py:546
  27.3 5.4 %collective-permute-done.8.refs_1_ = bf16[8,208,448]{2,1,0:T(8,128)(2,1)S(1)} collective-permute-done((bf16[8,208,448]{2,1,0:T(8,128)(2,1)}, bf16[8,208,448]{2,1,0:T(8,128)(2,1)S(1)}, u32[]{:S(2)}, u32[]{:S(2)}) %collective-permute-start.8) | collective-permute-done | bytes 1490976 | tf_op jit(solution)/shard_map/ppermute | solution.py:494
  33.2 9.1 %projection_chip.1 = (f32[208,896]{1,0:T(8,128)}, f32[208,896]{1,0:T(8,128)}, f32[208,896]{1,0:T(8,128)}, f32[208,896]{1,0:T(8,128)}, f32[208,896]{1,0:T(8,128)}...) custom-call(s32[8]{0:T(128)S(1)} %stack.79.order, s32[1]{0:T(128)} %bitcast.13.start, ...), custom_call_target="tpu_custom_call" | custom-call | flops 3449999872 | bytes 1000 | tf_op jit(solution)/shard_map/projection_chip/pallas_call | solution.py:449
  42.9 1.5 %collective-permute-done.6.refs_4_ = bf16[208,1664]{1,0:T(8,128)(2,1)} collective-permute-done((bf16[208,1664]{1,0:T(8,128)(2,1)}, bf16[208,1664]{1,0:T(8,128)(2,1)}, u32[]{:S(2)}, u32[]{:S(2)}) %collective-permute-start.6) | collective-permute-done | bytes 692256 | tf_op jit(solution)/shard_map/ppermute | solution.py:547
  44.4 1.6 %collective-permute-start.9 = (bf16[208,1664]{1,0:T(8,128)(2,1)}, bf16[208,1664]{1,0:T(8,128)(2,1)}, u32[]{:S(2)}, u32[]{:S(2)}) collective-permute-start(bf16[208,1664]{1,0:T(8,128)(2,1)} %collective-permute-done.5.refs_3_), channel_id=1, source_target_pairs={{0,2},{2,4},{4,6},{6,7},{7,5},{5,3},{3,1},{1,0},{8,10},{10,12},{12... | collective-permute-start | bytes 2076680 | tf_op jit(solution)/shard_map/ppermute | solution.py:569
  46.4 3.1 %attended_chunks.1 = (bf16[3,208,448]{2,1,0:T(8,128)(2,1)}, bf16[2,208,448]{2,1,0:T(8,128)(2,1)}, bf16[3,208,448]{2,1,0:T(8,128)(2,1)S(1)}) custom-call(s32[8]{0:T(128)S(1)} %stack.79.order, bf16[8,208,448]{2,1,0:T(8,128)(2,1)} %bitcast.27), custom_call_target="tpu_custom_call" | custom-call | flops 1150000000 | bytes 1000 | tf_op jit(solution)/shard_map/attended_chunks/pallas_call | solution.py:116
  49.5 0.9 copy-done.17
  50.4 1.5 %collective-permute-start.4 = (bf16[3,208,448]{2,1,0:T(8,128)(2,1)}, bf16[3,208,448]{2,1,0:T(8,128)(2,1)}, u32[]{:S(2)}, u32[]{:S(2)}) collective-permute-start(bf16[3,208,448]{2,1,0:T(8,128)(2,1)} %get-tuple-element.98), channel_id=1, source_target_pairs={{0,16},{8,24},{16,0},{24,8},{1,17},{9,25},{17,1},{25,9},{2,18},{10... | collective-permute-start | bytes 1677320 | tf_op jit(solution)/shard_map/ppermute | solution.py:494
  52.5 1.1 copy-done.12
  53.6 1.1 copy-done.14
  54.7 1.1 copy-done.16
  55.8 8.2 %grad_out_rows.2 = (f32[8,208,448]{2,1,0:T(8,128)}, bf16[8,208,448]{2,1,0:T(8,128)(2,1)}) custom-call(s32[6]{0:T(128)S(1)} %stack.82.info, bf16[3200,512]{1,0:T(8,128)(2,1)} %scaled_cotangent.1.refs_2_.turned, bf16[3200,512]{1,0:T(8,128)(2,1)} %collective-permute-done.7.refs_3_.turned_other, bf16[208,1664]{1,0:T(8,128)(2,1)S(1)} %copy-done.12, ...), custom_call_target="tpu_custom_call" | custom-call | flops 4312500224 | bytes 1000 | tf_op jit(solution)/shard_map/grad_out_rows/pallas_call | solution.py:324
  64.0 2.0 %far_parts.1 = (bf16[112,1664]{1,0:T(8,128)(2,1)}, bf16[96,1664]{1,0:T(8,128)(2,1)}) custom-call(bf16[208,1664]{1,0:T(8,128)(2,1)} %collective-permute-done.9.up.refs_0_, bf16[208,1664]{1,0:T(8,128)(2,1)} %collective-permute-done.10.down.refs_1_), custom_call_target="tpu_custom_call" | custom-call | flops 575000000 | bytes 1000 | tf_op jit(solution)/shard_map/far_parts/pallas_call | solution.py:147
  66.7 1.6 %collective-permute-start.15 = (bf16[112,1664]{1,0:T(8,128)(2,1)}, bf16[112,1664]{1,0:T(8,128)(2,1)}, u32[]{:S(2)}, u32[]{:S(2)}) collective-permute-start(bf16[112,1664]{1,0:T(8,128)(2,1)} %get-tuple-element.152.refs_6_), channel_id=1, source_target_pairs={{0,2},{2,4},{4,6},{6,7},{7,5},{5,3},{3,1},{1,0},{8,10},{10,12},{12... | collective-permute-start | bytes 1118216 | tf_op jit(solution)/shard_map/ppermute | solution.py:577
  68.9 5.2 %projection_peers.3 = (f32[208,896]{1,0:T(8,128)S(1)}, f32[208,896]{1,0:T(8,128)S(1)}, f32[208,896]{1,0:T(8,128)S(1)}) custom-call(s32[3]{0:T(128)S(1)} %pad_add_fusion.1.order, s32[1]{0:T(128)} %bitcast.3.start, bf16[3,208,448]{2,1,0:T(8,128)(2,1)} %collective-permute-done.4.refs_0_, bf16[3,208,448]{2,1,0:T(8,128)(2,1)} %collective-permute-done.11.refs_1_, ...), custom_call_target="tpu_custom_call" | custom-call | flops 1724999936 | bytes 1000 | tf_op jit(solution)/shard_map/projection_peers/pallas_call | solution.py:449
  74.1 4.5 %collective-permute-done.14.refs_0_ = bf16[2,208,448]{2,1,0:T(8,128)(2,1)} collective-permute-done((bf16[2,208,448]{2,1,0:T(8,128)(2,1)}, bf16[2,208,448]{2,1,0:T(8,128)(2,1)}, u32[]{:S(2)}, u32[]{:S(2)}) %collective-permute-start.14) | collective-permute-done | bytes 372768 | tf_op jit(solution)/shard_map/ppermute | solution.py:494
  78.7 1.6 %collective-permute-start.17 = (bf16[112,896]{1,0:T(8,128)(2,1)S(1)}, bf16[112,896]{1,0:T(8,128)(2,1)S(1)}, u32[]{:S(2)}, u32[]{:S(2)}) collective-permute-start(bf16[112,896]{1,0:T(8,128)(2,1)S(1)} %slice.14), channel_id=1, source_target_pairs={{0,2},{2,4},{4,6},{6,7},{7,5},{5,3},{3,1},{1,0},{8,10},{10,12},{12... | collective-permute-start | bytes 602120 | tf_op jit(solution)/shard_map/ppermute | solution.py:597
  80.9 4.3 %projection_peers.4 = (f32[208,896]{1,0:T(8,128)S(1)}, f32[208,896]{1,0:T(8,128)S(1)}) custom-call(s32[2]{0:T(128)S(1)} %pad_add_fusion.2.order, s32[1]{0:T(128)} %bitcast.3.start, bf16[2,208,448]{2,1,0:T(8,128)(2,1)} %collective-permute-done.14.refs_0_, bf16[2,208,448]{2,1,0:T(8,128)(2,1)S(1)} %collective-permute-done.19.refs_1_, ...), custom_call_target="tpu_custom_call" | custom-call | flops 1724999936 | bytes 1000 | tf_op jit(solution)/shard_map/projection_peers/pallas_call | solution.py:449
  85.1 1.6 %collective-permute-done.18 = bf16[96,896]{1,0:T(8,128)(2,1)S(1)} collective-permute-done((bf16[96,896]{1,0:T(8,128)(2,1)S(1)}, bf16[96,896]{1,0:T(8,128)(2,1)S(1)}, u32[]{:S(2)}, u32[]{:S(2)}) %collective-permute-start.18) | collective-permute-done | bytes 172064 | tf_op jit(solution)/shard_map/ppermute | solution.py:598
  86.9 1.7 %collective-permute-start.20 = (bf16[208,896]{1,0:T(8,128)(2,1)S(1)}, bf16[208,896]{1,0:T(8,128)(2,1)S(1)}, u32[]{:S(2)}, u32[]{:S(2)}) collective-permute-start(bf16[208,896]{1,0:T(8,128)(2,1)S(1)} %get-tuple-element.142), channel_id=1, source_target_pairs={{0,2},{2,4},{4,6},{6,7},{7,5},{5,3},{3,1},{1,0},{8,10},{10,12},{12... | collective-permute-start | bytes 1118216 | tf_op jit(solution)/shard_map/ppermute | solution.py:621
  88.6 0.6 collective-permute-start.22
  89.8 6.5 %grad_out_rows.3 = (f32[8,208,448]{2,1,0:T(8,128)}, bf16[8,208,448]{2,1,0:T(8,128)(2,1)}) custom-call(s32[4]{0:T(128)S(1)} %pad_add_fusion.3.info, bf16[3200,512]{1,0:T(8,128)(2,1)} %scaled_cotangent.1.refs_2_.turned, bf16[3200,512]{1,0:T(8,128)(2,1)} %collective-permute-done.7.refs_3_.turned_other, ...), custom_call_target="tpu_custom_call", output_to_operand_aliasing={{0}: (7, {}), {1}: (8, {})} | custom-call | flops 115000000 | bytes 1000 | tf_op jit(solution)/shard_map/grad_out_rows/pallas_call | solution.py:324
  96.3 0.6 collective-permute-done.20
  96.9 0.8 add_convert_fusion.3
  97.7 0.9 collective-permute-done.21
  98.6 0.8 add_convert_fusion.2
  99.4 4.6 %collective-permute-done.22.refs_0_ = bf16[3,208,448]{2,1,0:T(8,128)(2,1)} collective-permute-done((bf16[3,208,448]{2,1,0:T(8,128)(2,1)S(1)}, bf16[3,208,448]{2,1,0:T(8,128)(2,1)}, u32[]{:S(2)}, u32[]{:S(2)}) %collective-permute-start.22) | collective-permute-done | bytes 559136 | tf_op jit(solution)/shard_map/ppermute | solution.py:494
  104.0 1.5 %collective-permute-start.24 = (bf16[208,896]{1,0:T(8,128)(2,1)}, bf16[208,896]{1,0:T(8,128)(2,1)}, u32[]{:S(2)}, u32[]{:S(2)}) collective-permute-start(bf16[208,896]{1,0:T(8,128)(2,1)} %add_convert_fusion.3), channel_id=1, source_target_pairs={{0,2},{2,4},{4,6},{6,7},{7,5},{5,3},{3,1},{1,0},{8,10},{10,12},{12... | collective-permute-start | bytes 1118216 | tf_op jit(solution)/shard_map/ppermute | solution.py:621
  106.5 1.6 %copy-done.8 = bf16[288,1664]{1,0:T(8,128)(2,1)S(1)} copy-done((bf16[288,1664]{1,0:T(8,128)(2,1)S(1)}, bf16[288,1664]{1,0:T(8,128)(2,1)}, u32[]{:S(2)}) %copy-start.8) | copy-done | bytes 958488
  108.0 1.7 %copy-done.10 = bf16[160,1664]{1,0:T(8,128)(2,1)S(1)} copy-done((bf16[160,1664]{1,0:T(8,128)(2,1)S(1)}, bf16[160,1664]{1,0:T(8,128)(2,1)}, u32[]{:S(2)}) %copy-start.10) | copy-done | bytes 532504
  109.7 5.2 %projection_peers.5 = (f32[208,896]{1,0:T(8,128)S(1)}, f32[208,896]{1,0:T(8,128)S(1)}, f32[208,896]{1,0:T(8,128)S(1)}) custom-call(s32[3]{0:T(128)S(1)} %pad_add_fusion.order, s32[1]{0:T(128)} %bitcast.3.start, bf16[3,208,448]{2,1,0:T(8,128)(2,1)} %collective-permute-done.22.refs_0_, bf16[3,208,448]{2,1,0:T(8,128)(2,1)} %collective-permute-done.23.refs_1_, ...), custom_call_target="tpu_custom_call" | custom-call | flops 1724999936 | bytes 1000 | tf_op jit(solution)/shard_map/projection_peers/pallas_call | solution.py:449
  114.9 0.6 collective-permute-done.24
  115.4 1.1 add_convert_fusion.1
  116.8 1.4 %collective-permute-start.26 = (bf16[208,896]{1,0:T(8,128)(2,1)S(1)}, bf16[208,896]{1,0:T(8,128)(2,1)S(1)}, u32[]{:S(2)}, u32[]{:S(2)}) collective-permute-start(bf16[208,896]{1,0:T(8,128)(2,1)S(1)} %add_convert_fusion.1), channel_id=1, source_target_pairs={{0,2},{2,4},{4,6},{6,7},{7,5},{5,3},{3,1},{1,0},{8,10},{10,12},{12... | collective-permute-start | bytes 1118216 | tf_op jit(solution)/shard_map/ppermute | solution.py:621
  118.2 0.7 collective-permute-start.27
  118.9 2.3 %copy-done.4 = bf16[3,448,1664]{2,1,0:T(8,128)(2,1)S(1)} copy-done((bf16[3,448,1664]{2,1,0:T(8,128)(2,1)S(1)}, bf16[3,448,1664]{2,1,0:T(8,128)(2,1)}, u32[]{:S(2)}) %copy-start.4) | copy-done | bytes 4472856
  121.2 3.4 %attention_backward.3.rest_0_ = bf16[3,448,1664]{2,1,0:T(8,128)(2,1)} custom-call(bf16[3,448,1664]{2,1,0:T(8,128)(2,1)S(1)} %copy-done.4, f32[1664,448]{1,0:T(8,128)S(1)} %bitcast.19, bf16[1664,448]{1,0:T(8,128)(2,1)S(1)} %bitcast.22, f32[13,256,256]{2,1,0:T(8,128)S(1)} %copy-done.5, f32[13,192,192]{2,1,0:T(8,128)S(1)} %copy-done.6), custom_call_target="tpu_custom_call" | custom-call | flops 3449999872 | bytes 1000 | tf_op jit(solution)/shard_map/attention_backward/pallas_call | solution.py:256
  124.6 2.5 %attention_backward.4.rest_0_ = bf16[3,448,1664]{2,1,0:T(8,128)(2,1)} custom-call(bf16[3,448,1664]{2,1,0:T(8,128)(2,1)S(1)} %copy-done.4, f32[1664,448]{1,0:T(8,128)S(1)} %bitcast.20, bf16[1664,448]{1,0:T(8,128)(2,1)S(1)} %bitcast.23, f32[13,256,256]{2,1,0:T(8,128)S(1)} %copy-done.5, f32[13,192,192]{2,1,0:T(8,128)S(1)} %copy-done.6, ...), custom_call_target="tpu_custom_call", output_to_operand_aliasing={{}: (5, {})} | custom-call | flops 2300000000 | bytes 1000 | tf_op jit(solution)/shard_map/attention_backward/pallas_call | solution.py:256
  127.1 2.5 %attention_backward.5 = bf16[3,448,1664]{2,1,0:T(8,128)(2,1)} custom-call(bf16[3,448,1664]{2,1,0:T(8,128)(2,1)S(1)} %copy-done.4, f32[1664,448]{1,0:T(8,128)S(1)} %bitcast.21, bf16[1664,448]{1,0:T(8,128)(2,1)S(1)} %bitcast.24, f32[13,256,256]{2,1,0:T(8,128)S(1)} %copy-done.5, f32[13,192,192]{2,1,0:T(8,128)S(1)} %copy-done.6, ...), custom_call_target="tpu_custom_call", output_to_operand_aliasing={{}: (5, {})} | custom-call | flops 2300000000 | bytes 1000 | tf_op jit(solution)/shard_map/attention_backward/pallas_call | solution.py:256
  129.6 1.1 last_sum.1
  (80 shorter events, 6.9 us)
Async XLA Ops:
  0.6 15.5 %copy-start = (s32[4,1,4]{2,1,0:T(1,128)S(1)}, s32[4,1,4]{2,1,0:T(1,128)}, u32[]{:S(2)}) copy-start(s32[4,1,4]{2,1,0:T(1,128)} %param.9) | copy-start | bytes 196
  1.8 6.3 %copy-start.11 = (bf16[208,1664]{1,0:T(8,128)(2,1)}, bf16[208,1664]{1,0:T(8,128)(2,1)S(1)}, u32[]{:S(2)}) copy-start(bf16[208,1664]{1,0:T(8,128)(2,1)S(1)} %own_half_of_weight.1.refs_0_) | copy-start | bytes 2076676
  1.8 21.7 %collective-permute-start.1 = (bf16[208,1664]{1,0:T(8,128)(2,1)S(1)}, bf16[208,1664]{1,0:T(8,128)(2,1)S(1)}, u32[]{:S(2)}, u32[]{:S(2)}) collective-permute-start(bf16[208,1664]{1,0:T(8,128)(2,1)S(1)} %own_half_of_weight.1.refs_0_), channel_id=1, source_target_pairs={{0,2},{2,4},{4,6},{6,7},{7,5},{5,3},{3,1},{1,0},{8,10},{10,12},{12... | collective-permute-start | bytes 2076680 | tf_op jit(solution)/shard_map/ppermute | solution.py:515
  4.9 18.6 %collective-permute-start.2 = (bf16[208,1664]{1,0:T(8,128)(2,1)S(1)}, bf16[208,1664]{1,0:T(8,128)(2,1)S(1)}, u32[]{:S(2)}, u32[]{:S(2)}) collective-permute-start(bf16[208,1664]{1,0:T(8,128)(2,1)S(1)} %own_half_of_weight.1.refs_0_), channel_id=1, source_target_pairs={{0,1},{2,0},{4,2},{6,4},{7,6},{5,7},{3,5},{1,3},{8,9},{10,8},{12,1... | collective-permute-start | bytes 2076680 | tf_op jit(solution)/shard_map/ppermute | solution.py:516
  8.1 15.4 %collective-permute-start.3 = (bf16[160,1664]{1,0:T(8,128)(2,1)}, bf16[160,1664]{1,0:T(8,128)(2,1)S(1)}, u32[]{:S(2)}, u32[]{:S(2)}) collective-permute-start(bf16[160,1664]{1,0:T(8,128)(2,1)} %get-tuple-element.92), channel_id=1, source_target_pairs={{0,16},{8,24},{16,0},{24,8},{1,17},{9,25},{17,1},{25,9},{2,18},{10... | collective-permute-start | bytes 1597448 | tf_op jit(solution)/shard_map/ppermute | solution.py:494
  10.1 6.0 %copy-start.3 = (bf16[3,448,1664]{2,1,0:T(8,128)(2,1)S(1)}, bf16[3,448,1664]{2,1,0:T(8,128)(2,1)}, u32[]{:S(2)}) copy-start(bf16[3,448,1664]{2,1,0:T(8,128)(2,1)} %qkv.7) | copy-start | bytes 13418500
  23.5 0.9 copy-start.13
  23.5 1.1 copy-start.15
  24.6 8.6 %collective-permute-start.7 = (bf16[3200,512]{1,0:T(8,128)(2,1)}, bf16[3200,512]{1,0:T(8,128)(2,1)}, u32[]{:S(2)}, u32[]{:S(2)}) collective-permute-start(bf16[3200,512]{1,0:T(8,128)(2,1)} %scaled_cotangent.1.refs_2_.turned), channel_id=1, source_target_pairs={{0,8},{8,0},{16,24},{24,16},{1,9},{9,1},{17,25},{25,17},{2,10},{10... | collective-permute-start | bytes 9830408 | tf_op jit(solution)/shard_map/ppermute | solution.py:494
  24.6 8.1 %collective-permute-start.8 = (bf16[8,208,448]{2,1,0:T(8,128)(2,1)}, bf16[8,208,448]{2,1,0:T(8,128)(2,1)S(1)}, u32[]{:S(2)}, u32[]{:S(2)}) collective-permute-start(bf16[8,208,448]{2,1,0:T(8,128)(2,1)} %bitcast.25), channel_id=1, source_target_pairs={{0,8},{8,0},{16,24},{24,16},{1,9},{9,1},{17,25},{25,17},{2,10},{10... | collective-permute-start | bytes 4472840 | tf_op jit(solution)/shard_map/ppermute | solution.py:494
  25.1 25.3 %collective-permute-start = (bf16[288,1664]{1,0:T(8,128)(2,1)}, bf16[288,1664]{1,0:T(8,128)(2,1)S(1)}, u32[]{:S(2)}, u32[]{:S(2)}) collective-permute-start(bf16[288,1664]{1,0:T(8,128)(2,1)} %get-tuple-element.90), channel_id=1, source_target_pairs={{0,16},{8,24},{16,0},{24,8},{1,17},{9,25},{17,1},{25,9},{2,18},{10... | collective-permute-start | bytes 2875400 | tf_op jit(solution)/shard_map/ppermute | solution.py:494
  25.2 17.7 %collective-permute-start.5 = (bf16[208,1664]{1,0:T(8,128)(2,1)}, bf16[208,1664]{1,0:T(8,128)(2,1)}, u32[]{:S(2)}, u32[]{:S(2)}) collective-permute-start(bf16[208,1664]{1,0:T(8,128)(2,1)} %copy-done.13), channel_id=1, source_target_pairs={{0,2},{2,4},{4,6},{6,7},{7,5},{5,3},{3,1},{1,0},{8,10},{10,12},{12... | collective-permute-start | bytes 2076680 | tf_op jit(solution)/shard_map/ppermute | solution.py:546
  27.2 17.2 %collective-permute-start.6 = (bf16[208,1664]{1,0:T(8,128)(2,1)}, bf16[208,1664]{1,0:T(8,128)(2,1)}, u32[]{:S(2)}, u32[]{:S(2)}) collective-permute-start(bf16[208,1664]{1,0:T(8,128)(2,1)} %copy-done.15), channel_id=1, source_target_pairs={{0,1},{2,0},{4,2},{6,4},{7,6},{5,7},{3,5},{1,3},{8,9},{10,8},{12,1... | collective-permute-start | bytes 2076680 | tf_op jit(solution)/shard_map/ppermute | solution.py:547
  44.4 19.6 %collective-permute-start.9 = (bf16[208,1664]{1,0:T(8,128)(2,1)}, bf16[208,1664]{1,0:T(8,128)(2,1)}, u32[]{:S(2)}, u32[]{:S(2)}) collective-permute-start(bf16[208,1664]{1,0:T(8,128)(2,1)} %collective-permute-done.5.refs_3_), channel_id=1, source_target_pairs={{0,2},{2,4},{4,6},{6,7},{7,5},{5,3},{3,1},{1,0},{8,10},{10,12},{12... | collective-permute-start | bytes 2076680 | tf_op jit(solution)/shard_map/ppermute | solution.py:569
  46.0 18.1 %collective-permute-start.10 = (bf16[208,1664]{1,0:T(8,128)(2,1)}, bf16[208,1664]{1,0:T(8,128)(2,1)}, u32[]{:S(2)}, u32[]{:S(2)}) collective-permute-start(bf16[208,1664]{1,0:T(8,128)(2,1)} %collective-permute-done.6.refs_4_), channel_id=1, source_target_pairs={{0,1},{2,0},{4,2},{6,4},{7,6},{5,7},{3,5},{1,3},{8,9},{10,8},{12,1... | collective-permute-start | bytes 2076680 | tf_op jit(solution)/shard_map/ppermute | solution.py:570
  49.5 0.9 copy-start.17
  50.4 15.6 %collective-permute-start.4 = (bf16[3,208,448]{2,1,0:T(8,128)(2,1)}, bf16[3,208,448]{2,1,0:T(8,128)(2,1)}, u32[]{:S(2)}, u32[]{:S(2)}) collective-permute-start(bf16[3,208,448]{2,1,0:T(8,128)(2,1)} %get-tuple-element.98), channel_id=1, source_target_pairs={{0,16},{8,24},{16,0},{24,8},{1,17},{9,25},{17,1},{25,9},{2,18},{10... | collective-permute-start | bytes 1677320 | tf_op jit(solution)/shard_map/ppermute | solution.py:494
  52.0 16.3 %collective-permute-start.12 = (bf16[160,1664]{1,0:T(8,128)(2,1)S(1)}, bf16[160,1664]{1,0:T(8,128)(2,1)S(1)}, u32[]{:S(2)}, u32[]{:S(2)}) collective-permute-start(bf16[160,1664]{1,0:T(8,128)(2,1)S(1)} %collective-permute-done.3.refs_2_), channel_id=1, source_target_pairs={{0,8},{8,0},{16,24},{24,16},{1,9},{9,1},{17,25},{25,17},{2,10},{10... | collective-permute-start | bytes 1597448 | tf_op jit(solution)/shard_map/ppermute | solution.py:494
  52.0 16.9 %collective-permute-start.13 = (bf16[288,1664]{1,0:T(8,128)(2,1)S(1)}, bf16[288,1664]{1,0:T(8,128)(2,1)S(1)}, u32[]{:S(2)}, u32[]{:S(2)}) collective-permute-start(bf16[288,1664]{1,0:T(8,128)(2,1)S(1)} %collective-permute-done.refs_3_), channel_id=1, source_target_pairs={{0,8},{8,0},{16,24},{24,16},{1,9},{9,1},{17,25},{25,17},{2,10},{10... | collective-permute-start | bytes 2875400 | tf_op jit(solution)/shard_map/ppermute | solution.py:494
  52.5 1.1 copy-start.12
  53.6 1.1 copy-start.14
  54.7 1.1 copy-start.16
  66.1 2.8 %collective-permute-start.11 = (bf16[3,208,448]{2,1,0:T(8,128)(2,1)}, bf16[3,208,448]{2,1,0:T(8,128)(2,1)}, u32[]{:S(2)}, u32[]{:S(2)}) collective-permute-start(bf16[3,208,448]{2,1,0:T(8,128)(2,1)} %collective-permute-done.4.refs_0_), channel_id=1, source_target_pairs={{0,8},{8,0},{16,24},{24,16},{1,9},{9,1},{17,25},{25,17},{2,10},{10... | collective-permute-start | bytes 1677320 | tf_op jit(solution)/shard_map/ppermute | solution.py:494
  66.2 12.5 %collective-permute-start.14 = (bf16[2,208,448]{2,1,0:T(8,128)(2,1)}, bf16[2,208,448]{2,1,0:T(8,128)(2,1)}, u32[]{:S(2)}, u32[]{:S(2)}) collective-permute-start(bf16[2,208,448]{2,1,0:T(8,128)(2,1)} %get-tuple-element.126), channel_id=1, source_target_pairs={{0,16},{8,24},{16,0},{24,8},{1,17},{9,25},{17,1},{25,9},{2,18},{10... | collective-permute-start | bytes 1118216 | tf_op jit(solution)/shard_map/ppermute | solution.py:494
  66.7 11.9 %collective-permute-start.15 = (bf16[112,1664]{1,0:T(8,128)(2,1)}, bf16[112,1664]{1,0:T(8,128)(2,1)}, u32[]{:S(2)}, u32[]{:S(2)}) collective-permute-start(bf16[112,1664]{1,0:T(8,128)(2,1)} %get-tuple-element.152.refs_6_), channel_id=1, source_target_pairs={{0,2},{2,4},{4,6},{6,7},{7,5},{5,3},{3,1},{1,0},{8,10},{10,12},{12... | collective-permute-start | bytes 1118216 | tf_op jit(solution)/shard_map/ppermute | solution.py:577
  68.3 12.5 %copy-start.9 = (bf16[160,1664]{1,0:T(8,128)(2,1)}, bf16[160,1664]{1,0:T(8,128)(2,1)S(1)}, u32[]{:S(2)}) copy-start(bf16[160,1664]{1,0:T(8,128)(2,1)S(1)} %collective-permute-done.12.refs_4_) | copy-start | bytes 1597444
  68.3 10.4 %collective-permute-start.16 = (bf16[96,1664]{1,0:T(8,128)(2,1)}, bf16[96,1664]{1,0:T(8,128)(2,1)S(1)}, u32[]{:S(2)}, u32[]{:S(2)}) collective-permute-start(bf16[96,1664]{1,0:T(8,128)(2,1)} %get-tuple-element.128), channel_id=1, source_target_pairs={{0,1},{2,0},{4,2},{6,4},{7,6},{5,7},{3,5},{1,3},{8,9},{10,8},{12,1... | collective-permute-start | bytes 958472 | tf_op jit(solution)/shard_map/ppermute | solution.py:578
  68.9 12.0 %copy-start.7 = (bf16[288,1664]{1,0:T(8,128)(2,1)}, bf16[288,1664]{1,0:T(8,128)(2,1)S(1)}, u32[]{:S(2)}) copy-start(bf16[288,1664]{1,0:T(8,128)(2,1)S(1)} %collective-permute-done.13.refs_5_) | copy-start | bytes 2875396
  78.7 2.2 %collective-permute-start.19 = (bf16[2,208,448]{2,1,0:T(8,128)(2,1)}, bf16[2,208,448]{2,1,0:T(8,128)(2,1)S(1)}, u32[]{:S(2)}, u32[]{:S(2)}) collective-permute-start(bf16[2,208,448]{2,1,0:T(8,128)(2,1)} %collective-permute-done.14.refs_0_), channel_id=1, source_target_pairs={{0,8},{8,0},{16,24},{24,16},{1,9},{9,1},{17,25},{25,17},{2,10},{10... | collective-permute-start | bytes 1118216 | tf_op jit(solution)/shard_map/ppermute | solution.py:494
  78.7 8.1 %collective-permute-start.17 = (bf16[112,896]{1,0:T(8,128)(2,1)S(1)}, bf16[112,896]{1,0:T(8,128)(2,1)S(1)}, u32[]{:S(2)}, u32[]{:S(2)}) collective-permute-start(bf16[112,896]{1,0:T(8,128)(2,1)S(1)} %slice.14), channel_id=1, source_target_pairs={{0,2},{2,4},{4,6},{6,7},{7,5},{5,3},{3,1},{1,0},{8,10},{10,12},{12... | collective-permute-start | bytes 602120 | tf_op jit(solution)/shard_map/ppermute | solution.py:597
  80.3 6.5 %collective-permute-start.18 = (bf16[96,896]{1,0:T(8,128)(2,1)S(1)}, bf16[96,896]{1,0:T(8,128)(2,1)S(1)}, u32[]{:S(2)}, u32[]{:S(2)}) collective-permute-start(bf16[96,896]{1,0:T(8,128)(2,1)S(1)} %slice.15), channel_id=1, source_target_pairs={{0,1},{2,0},{4,2},{6,4},{7,6},{5,7},{3,5},{1,3},{8,9},{10,8},{12,1... | collective-permute-start | bytes 516104 | tf_op jit(solution)/shard_map/ppermute | solution.py:598
  80.9 7.7 %copy-start.18 = (bf16[3,208,448]{2,1,0:T(8,128)(2,1)S(1)}, bf16[3,208,448]{2,1,0:T(8,128)(2,1)}, u32[]{:S(2)}) copy-start(bf16[3,208,448]{2,1,0:T(8,128)(2,1)} %copy-done.17) | copy-start | bytes 1677316
  86.9 10.0 %collective-permute-start.20 = (bf16[208,896]{1,0:T(8,128)(2,1)S(1)}, bf16[208,896]{1,0:T(8,128)(2,1)S(1)}, u32[]{:S(2)}, u32[]{:S(2)}) collective-permute-start(bf16[208,896]{1,0:T(8,128)(2,1)S(1)} %get-tuple-element.142), channel_id=1, source_target_pairs={{0,2},{2,4},{4,6},{6,7},{7,5},{5,3},{3,1},{1,0},{8,10},{10,12},{12... | collective-permute-start | bytes 1118216 | tf_op jit(solution)/shard_map/ppermute | solution.py:621
  88.6 15.5 %collective-permute-start.22 = (bf16[3,208,448]{2,1,0:T(8,128)(2,1)S(1)}, bf16[3,208,448]{2,1,0:T(8,128)(2,1)}, u32[]{:S(2)}, u32[]{:S(2)}) collective-permute-start(bf16[3,208,448]{2,1,0:T(8,128)(2,1)S(1)} %copy-done.18), channel_id=1, source_target_pairs={{0,16},{8,24},{16,0},{24,8},{1,17},{9,25},{17,1},{25,9},{2,18},{10... | collective-permute-start | bytes 1677320 | tf_op jit(solution)/shard_map/ppermute | solution.py:494
  89.2 9.4 %collective-permute-start.21 = (bf16[208,896]{1,0:T(8,128)(2,1)S(1)}, bf16[208,896]{1,0:T(8,128)(2,1)S(1)}, u32[]{:S(2)}, u32[]{:S(2)}) collective-permute-start(bf16[208,896]{1,0:T(8,128)(2,1)S(1)} %get-tuple-element.144), channel_id=1, source_target_pairs={{0,1},{2,0},{4,2},{6,4},{7,6},{5,7},{3,5},{1,3},{8,9},{10,8},{12,1... | collective-permute-start | bytes 1118216 | tf_op jit(solution)/shard_map/ppermute | solution.py:622
  96.3 22.6 %collective-permute-start.28 = (bf16[8,208,448]{2,1,0:T(8,128)(2,1)}, bf16[8,208,448]{2,1,0:T(8,128)(2,1)S(1)}, u32[]{:S(2)}, u32[]{:S(2)}) collective-permute-start(bf16[8,208,448]{2,1,0:T(8,128)(2,1)} %get-tuple-element.165), channel_id=1, source_target_pairs={{0,8},{8,0},{16,24},{24,16},{1,9},{9,1},{17,25},{25,17},{2,10},{10... | collective-permute-start | bytes 4472840 | tf_op jit(solution)/shard_map/ppermute | solution.py:494
  104.0 2.4 %collective-permute-start.23 = (bf16[3,208,448]{2,1,0:T(8,128)(2,1)}, bf16[3,208,448]{2,1,0:T(8,128)(2,1)}, u32[]{:S(2)}, u32[]{:S(2)}) collective-permute-start(bf16[3,208,448]{2,1,0:T(8,128)(2,1)} %collective-permute-done.22.refs_0_), channel_id=1, source_target_pairs={{0,8},{8,0},{16,24},{24,16},{1,9},{9,1},{17,25},{25,17},{2,10},{10... | collective-permute-start | bytes 1677320 | tf_op jit(solution)/shard_map/ppermute | solution.py:494
  104.0 11.4 %collective-permute-start.24 = (bf16[208,896]{1,0:T(8,128)(2,1)}, bf16[208,896]{1,0:T(8,128)(2,1)}, u32[]{:S(2)}, u32[]{:S(2)}) collective-permute-start(bf16[208,896]{1,0:T(8,128)(2,1)} %add_convert_fusion.3), channel_id=1, source_target_pairs={{0,2},{2,4},{4,6},{6,7},{7,5},{5,3},{3,1},{1,0},{8,10},{10,12},{12... | collective-permute-start | bytes 1118216 | tf_op jit(solution)/shard_map/ppermute | solution.py:621
  105.6 13.2 %copy-start.2 = (f32[8,208,448]{2,1,0:T(8,128)S(1)}, f32[8,208,448]{2,1,0:T(8,128)}, u32[]{:S(2)}) copy-start(f32[8,208,448]{2,1,0:T(8,128)} %get-tuple-element.153) | copy-start | bytes 8945668
  105.6 13.2 %copy-start.5 = (f32[13,256,256]{2,1,0:T(8,128)S(1)}, f32[13,256,256]{2,1,0:T(8,128)}, u32[]{:S(2)}) copy-start(f32[13,256,256]{2,1,0:T(8,128)} %get-tuple-element.166.main_probs) | copy-start | bytes 10223620
  105.6 13.2 %copy-start.6 = (f32[13,192,192]{2,1,0:T(8,128)S(1)}, f32[13,192,192]{2,1,0:T(8,128)}, u32[]{:S(2)}) copy-start(f32[13,192,192]{2,1,0:T(8,128)} %get-tuple-element.167.slot_probs) | copy-start | bytes 5750788
  105.6 11.1 %collective-permute-start.25 = (bf16[208,896]{1,0:T(8,128)(2,1)}, bf16[208,896]{1,0:T(8,128)(2,1)S(1)}, u32[]{:S(2)}, u32[]{:S(2)}) collective-permute-start(bf16[208,896]{1,0:T(8,128)(2,1)} %add_convert_fusion.2), channel_id=1, source_target_pairs={{0,1},{2,0},{4,2},{6,4},{7,6},{5,7},{3,5},{1,3},{8,9},{10,8},{12,1... | collective-permute-start | bytes 1118216 | tf_op jit(solution)/shard_map/ppermute | solution.py:622
  106.5 1.6 %copy-start.8 = (bf16[288,1664]{1,0:T(8,128)(2,1)S(1)}, bf16[288,1664]{1,0:T(8,128)(2,1)}, u32[]{:S(2)}) copy-start(bf16[288,1664]{1,0:T(8,128)(2,1)} %copy-done.7) | copy-start | bytes 2875396
  108.0 1.7 %copy-start.10 = (bf16[160,1664]{1,0:T(8,128)(2,1)S(1)}, bf16[160,1664]{1,0:T(8,128)(2,1)}, u32[]{:S(2)}) copy-start(bf16[160,1664]{1,0:T(8,128)(2,1)} %copy-done.9) | copy-start | bytes 1597444
  116.8 12.8 %collective-permute-start.26 = (bf16[208,896]{1,0:T(8,128)(2,1)S(1)}, bf16[208,896]{1,0:T(8,128)(2,1)S(1)}, u32[]{:S(2)}, u32[]{:S(2)}) collective-permute-start(bf16[208,896]{1,0:T(8,128)(2,1)S(1)} %add_convert_fusion.1), channel_id=1, source_target_pairs={{0,2},{2,4},{4,6},{6,7},{7,5},{5,3},{3,1},{1,0},{8,10},{10,12},{12... | collective-permute-start | bytes 1118216 | tf_op jit(solution)/shard_map/ppermute | solution.py:621
  118.2 11.4 %collective-permute-start.27 = (bf16[208,896]{1,0:T(8,128)(2,1)S(1)}, bf16[208,896]{1,0:T(8,128)(2,1)S(1)}, u32[]{:S(2)}, u32[]{:S(2)}) collective-permute-start(bf16[208,896]{1,0:T(8,128)(2,1)S(1)} %add_convert_fusion), channel_id=1, source_target_pairs={{0,1},{2,0},{4,2},{6,4},{7,6},{5,7},{3,5},{1,3},{8,9},{10,8},{12,1... | collective-permute-start | bytes 1118216 | tf_op jit(solution)/shard_map/ppermute | solution.py:622
  118.9 2.3 %copy-start.4 = (bf16[3,448,1664]{2,1,0:T(8,128)(2,1)S(1)}, bf16[3,448,1664]{2,1,0:T(8,128)(2,1)}, u32[]{:S(2)}) copy-start(bf16[3,448,1664]{2,1,0:T(8,128)(2,1)} %qkv.7) | copy-start | bytes 13418500
  127.1 3.6 %copy-start.1 = (s32[4,1,4]{2,1,0:T(1,128)S(1)}, s32[4,1,4]{2,1,0:T(1,128)}, u32[]{:S(2)}) copy-start(s32[4,1,4]{2,1,0:T(1,128)} %param.9) | copy-start | bytes 196

commit v5 on v4

--- a/solution.py
+++ b/solution.py
@@ -400,9 +400,9 @@
 
 def partial_kernel(chosen, sources, parts, count, window, order, start, *refs):
     attended, columns = refs[:sources], refs[sources:sources * (1 + parts)]
-    chunks, held, sems = refs[-3:]
-    bases = refs[sources * (1 + parts):-3 - count]
-    outs = refs[-3 - count:-3]
+    chunks, held, sums, sems = refs[-4:]
+    bases = refs[sources * (1 + parts):-4 - count]
+    outs = refs[-4 - count:-4]
     depth, rows = chunks.shape[2:]
     at = pl.ds(pl.multiple_of(start[0], LANE), window)
     copies = []
@@ -436,9 +436,13 @@
             else:
                 part = dot(chunks[i, j], held[i][:, :rows], 1, 1) if chosen else dot(chunks[i, j], held[i], 1, 0)
             if i == 0:
-                out[...] = bases[j][...] + part if bases else part
+                total = bases[j][...].astype(jnp.float32) + part if bases else part
             else:
-                out[...] += part
+                total = sums[j] + part
+            if i < sources - 1:
+                sums[j] = total
+            else:
+                out[...] = total.astype(out.dtype)
 
 
 def partial_products(order, start, attended, columns, window, bases=()):
@@ -456,10 +460,13 @@
             scratch_shapes=[
                 pltpu.VMEM((sources, count, depth, rows), jnp.bfloat16),
                 pltpu.VMEM((sources, rows, window) if bases else (sources, window, columns[0].shape[1]), jnp.bfloat16),
+                pltpu.VMEM((count, depth, window), jnp.float32),
                 pltpu.SemaphoreType.DMA((sources, count + parts)),
             ],
         ),
-        out_shape=[(jax.ShapeDtypeStruct if bases else pltpu.HBM)((depth, window), jnp.float32)] * count,
+        out_shape=[
+            jax.ShapeDtypeStruct((depth, window), jnp.float32) if bases else pltpu.HBM((depth, window), jnp.bfloat16)
+        ] * count,
         compiler_params=pltpu.CompilerParams(vmem_limit_bytes=VMEM_BYTES),
         cost_estimate=lasting(3 if bases else 6),
         name="projection_peers" if bases else "projection_chip",
@@ -542,6 +549,7 @@
     other_columns = [[swap(array, 1) for array in came_columns[0]]]
     attended_other = swap(attended, 1)
     chunks = list(arrange(flat, attended, sizes))
+    attended_other, chunks = lax.optimization_barrier((attended_other, chunks))
     for _ in range(half - 3):
         up.append(lax.ppermute(up[-1], "fsdp", ahead))
         down.append(lax.ppermute(down[-1], "fsdp", behind))
@@ -611,7 +619,8 @@
             going_up, going_down, near_up = lax.optimization_barrier((going_up, going_down, near_up))
             grad_out = rows_of([([near_up], 1 - half), ([near_down], half - 1), ([far_up, far_down], half)], grad_out, [sent_up])
             grad_mine = grad_out[0].reshape(width, rows)
-            grad_other = swap(grad_out[1], 1).reshape(width, rows)
+            came[2], grad_other = lax.optimization_barrier((came[2], grad_out[1]))
+            grad_other = swap(grad_other, 1).reshape(width, rows)
         elif step > 2:
             arrived = came[half - step + 1]
             going_up, going_down, arrived, grad_mine = lax.optimization_barrier((going_up, going_down, arrived, grad_mine))

time: 131 us -> 127 us (0.969)
  waiting for transfers between devices: 21.3 us -> 14.7 us
  local copies, waits for them, and re-layouts: 11.7 us -> 16.3 us
  Pallas kernels: 70 us -> 66.9 us
    ppermute x13, waiting for transfers between devices: 15.3 us -> 8.13 us  [swap(): return lax.ppermute(array, 'dp', [(i, i ^ bit) for i in range(members)])]
    unnamed x38 -> x48, local copies, waits for them, and re-layouts: 10.8 us -> 15.4 us
    pallas_call x4, Pallas kernels: 23.7 us -> 21.2 us  [partial_products(): pl.pallas_call(functools.partial(partial_kernel, not bases, sources, part...]
    ppermute x4, waiting for transfers between devices: 2.72 us -> 1 us  [local(): came_down = lax.ppermute(going_down, 'fsdp', behind)]
    ppermute x3, waiting for transfers between devices: 0.55 us -> 2.26 us  [local(): up.append(lax.ppermute(up[-1], 'fsdp', ahead))]
  transfers between devices with their start and end apart: 29 -> 29, of which waited for: 12 -> 12; matrix products, arithmetic and copies ran while one was open for 3% -> 3% of each run, Pallas kernels for 52% -> 51%
where the time goes in v5:
time: 127 us; the launch traced here: 126 us
  Pallas kernels  66.9 us (53%)
  starting transfers between devices  23.4 us (18%)
  local copies, waits for them, and re-layouts  16.3 us (13%)
  waiting for transfers between devices  14.7 us (12%)
  other arithmetic  3.27 us (3%)
    pallas_call x4, Pallas kernels, partial_products(): pl.pallas_call(functools.partial(partial_kernel, not bases, sources, part...  21.2 us
    unnamed x48, local copies, waits for them, and re-layouts  15.4 us
    pallas_call x2, Pallas kernels, grad_out_rows(): pl.pallas_call(functools.partial(grad_out_kernel, sizes, split, total), g...  14.2 us
    pallas_call x3, Pallas kernels, backward(): pl.pallas_call(backward_kernel, grid=(high - low,), in_specs=[pl.BlockSpe...  8.29 us
    ppermute x13, waiting for transfers between devices, swap(): return lax.ppermute(array, 'dp', [(i, i ^ bit) for i in range(members)])  8.13 us
    pallas_call x1, Pallas kernels, forward(): pl.pallas_call(forward_kernel, grid_spec=pltpu.PrefetchScalarGridSpec(num...  7.34 us
    ppermute x3, starting transfers between devices, local(): up.append(lax.ppermute(up[-1], 'fsdp', ahead))  6.64 us
    ppermute x13, starting transfers between devices, swap(): return lax.ppermute(array, 'dp', [(i, i ^ bit) for i in range(members)])  6.03 us
  transfers between devices with their start and end apart: 29, of which 12 were waited for; matrix products, arithmetic and copies ran while one was open for 3% of the time, Pallas kernels for 51%

profile of v5, /device:TPU:0, one launch (start us, length us, event | category | flops | bytes accessed | tf_op | source)
XLA Modules:
  0.0 125.6 jit_solution(13826168381926263637)
XLA Ops:
  0.7 1.1 own_half_of_weight.1.refs_0_
  1.8 3.1 %collective-permute-start.1 = (bf16[208,1664]{1,0:T(8,128)(2,1)S(1)}, bf16[208,1664]{1,0:T(8,128)(2,1)S(1)}, u32[]{:S(2)}, u32[]{:S(2)}) collective-permute-start(bf16[208,1664]{1,0:T(8,128)(2,1)S(1)} %own_half_of_weight.1.refs_0_), channel_id=1, source_target_pairs={{0,2},{2,4},{4,6},{6,7},{7,5},{5,3},{3,1},{1,0},{8,10},{10,12},{12... | collective-permute-start | bytes 2076680 | tf_op jit(solution)/shard_map/ppermute | solution.py:522
  5.6 2.6 %peer_windows.1 = (bf16[160,1664]{1,0:T(8,128)(2,1)}, bf16[288,1664]{1,0:T(8,128)(2,1)}) custom-call(s32[1]{0:T(128)} %bitcast.7.starts, bf16[448,3200]{1,0:T(8,128)(2,1)} %cotangent.1, f32[1,3200]{1,0:T(1,128)S(1)} %reshape.18.layer_scale), custom_call_target="tpu_custom_call" | custom-call | flops 34500001792 | bytes 1000 | tf_op jit(solution)/shard_map/peer_windows/pallas_call | solution.py:58
  8.2 2.0 %collective-permute-start.3 = (bf16[160,1664]{1,0:T(8,128)(2,1)}, bf16[160,1664]{1,0:T(8,128)(2,1)S(1)}, u32[]{:S(2)}, u32[]{:S(2)}) collective-permute-start(bf16[160,1664]{1,0:T(8,128)(2,1)} %get-tuple-element.98), channel_id=1, source_target_pairs={{0,16},{8,24},{16,0},{24,8},{1,17},{9,25},{17,1},{25,9},{2,18},{10... | collective-permute-start | bytes 1597448 | tf_op jit(solution)/shard_map/ppermute | solution.py:501
  10.2 6.0 %scaled_cotangent.1.refs_2_.turned = bf16[3200,512]{1,0:T(8,128)(2,1)} custom-call(bf16[448,3200]{1,0:T(8,128)(2,1)} %cotangent.1, f32[1,3200]{1,0:T(1,128)S(1)} %reshape.18.layer_scale), custom_call_target="tpu_custom_call" | custom-call | flops 34500001792 | bytes 1000 | tf_op jit(solution)/shard_map/scaled_cotangent/pallas_call | solution.py:89
  16.2 7.3 %attention_forward.1 = (bf16[1664,448]{1,0:T(8,128)(2,1)}, f32[13,256,256]{2,1,0:T(8,128)}, f32[13,192,192]{2,1,0:T(8,128)}) custom-call(s32[4]{0:T(128)S(1)} %dynamic-slice_bitcast_fusion.counts, bf16[3,448,1664]{2,1,0:T(8,128)(2,1)S(1)} %copy-done.2), custom_call_target="tpu_custom_call" | custom-call | flops 34500001792 | bytes 1000 | tf_op jit(solution)/shard_map/attention_forward/pallas_call | solution.py:206
  25.5 2.0 %collective-permute-start.6 = (bf16[208,1664]{1,0:T(8,128)(2,1)}, bf16[208,1664]{1,0:T(8,128)(2,1)}, u32[]{:S(2)}, u32[]{:S(2)}) collective-permute-start(bf16[208,1664]{1,0:T(8,128)(2,1)} %copy-done.8), channel_id=1, source_target_pairs={{0,2},{2,4},{4,6},{6,7},{7,5},{5,3},{3,1},{1,0},{8,10},{10,12},{12... | collective-permute-start | bytes 2076680 | tf_op jit(solution)/shard_map/ppermute | solution.py:554
  27.6 3.1 %attended_chunks.1 = (bf16[3,208,448]{2,1,0:T(8,128)(2,1)}, bf16[2,208,448]{2,1,0:T(8,128)(2,1)}, bf16[3,208,448]{2,1,0:T(8,128)(2,1)S(1)}) custom-call(s32[8]{0:T(128)S(1)} %stack.79.order, bf16[8,208,448]{2,1,0:T(8,128)(2,1)} %bitcast.26), custom_call_target="tpu_custom_call" | custom-call | flops 1150000000 | bytes 1000 | tf_op jit(solution)/shard_map/attended_chunks/pallas_call | solution.py:116
  30.7 0.9 copy-done.12
  31.6 1.5 %collective-permute-done.4.refs_1_ = bf16[8,208,448]{2,1,0:T(8,128)(2,1)} collective-permute-done((bf16[8,208,448]{2,1,0:T(8,128)(2,1)}, bf16[8,208,448]{2,1,0:T(8,128)(2,1)}, u32[]{:S(2)}, u32[]{:S(2)}) %collective-permute-start.4) | collective-permute-done | bytes 1490976 | tf_op jit(solution)/shard_map/ppermute | solution.py:501
  33.3 7.5 %projection_chip.1 = (bf16[208,896]{1,0:T(8,128)(2,1)}, bf16[208,896]{1,0:T(8,128)(2,1)}, bf16[208,896]{1,0:T(8,128)(2,1)}, bf16[208,896]{1,0:T(8,128)(2,1)}, bf...) custom-call(s32[8]{0:T(128)S(1)} %stack.79.order, ...), custom_call_target="tpu_custom_call" | custom-call | flops 3449999872 | bytes 1000 | tf_op jit(solution)/shard_map/projection_chip/pallas_call | solution.py:453
  40.9 2.3 %collective-permute-done.6.refs_3_ = bf16[208,1664]{1,0:T(8,128)(2,1)} collective-permute-done((bf16[208,1664]{1,0:T(8,128)(2,1)}, bf16[208,1664]{1,0:T(8,128)(2,1)}, u32[]{:S(2)}, u32[]{:S(2)}) %collective-permute-start.6) | collective-permute-done | bytes 692256 | tf_op jit(solution)/shard_map/ppermute | solution.py:554
  43.1 1.5 %collective-permute-done.7.refs_4_ = bf16[208,1664]{1,0:T(8,128)(2,1)} collective-permute-done((bf16[208,1664]{1,0:T(8,128)(2,1)}, bf16[208,1664]{1,0:T(8,128)(2,1)}, u32[]{:S(2)}, u32[]{:S(2)}) %collective-permute-start.7) | collective-permute-done | bytes 692256 | tf_op jit(solution)/shard_map/ppermute | solution.py:555
  44.6 1.6 %collective-permute-start.9 = (bf16[208,1664]{1,0:T(8,128)(2,1)}, bf16[208,1664]{1,0:T(8,128)(2,1)}, u32[]{:S(2)}, u32[]{:S(2)}) collective-permute-start(bf16[208,1664]{1,0:T(8,128)(2,1)} %collective-permute-done.6.refs_3_), channel_id=1, source_target_pairs={{0,2},{2,4},{4,6},{6,7},{7,5},{5,3},{3,1},{1,0},{8,10},{10,12},{12... | collective-permute-start | bytes 2076680 | tf_op jit(solution)/shard_map/ppermute | solution.py:577
  46.7 2.1 %collective-permute-done.refs_3_ = bf16[288,1664]{1,0:T(8,128)(2,1)} collective-permute-done((bf16[288,1664]{1,0:T(8,128)(2,1)}, bf16[288,1664]{1,0:T(8,128)(2,1)}, u32[]{:S(2)}, u32[]{:S(2)}) %collective-permute-start) | collective-permute-done | bytes 958496 | tf_op jit(solution)/shard_map/ppermute | solution.py:501
  49.7 1.1 copy-done.7
  50.8 1.1 copy-done.9
  51.9 1.1 copy-done.11
  53.0 8.1 %grad_out_rows.2 = (f32[8,208,448]{2,1,0:T(8,128)}, bf16[8,208,448]{2,1,0:T(8,128)(2,1)}) custom-call(s32[6]{0:T(128)S(1)} %stack.82.info, bf16[3200,512]{1,0:T(8,128)(2,1)} %scaled_cotangent.1.refs_2_.turned, bf16[3200,512]{1,0:T(8,128)(2,1)S(1)} %collective-permute-done.8.refs_3_.turned_other, bf16[208,1664]{1,0:T(8,128)(2,1)S(1)} %copy-done.7, ...), custom_call_target="tpu_custom_call" | custom-call | flops 4312500224 | bytes 1000 | tf_op jit(solution)/shard_map/grad_out_rows/pallas_call | solution.py:324
  61.1 1.1 collective-permute-done.10.down.refs_1_
  62.2 1.9 %far_parts.1 = (bf16[112,1664]{1,0:T(8,128)(2,1)}, bf16[96,1664]{1,0:T(8,128)(2,1)}) custom-call(bf16[208,1664]{1,0:T(8,128)(2,1)} %collective-permute-done.9.up.refs_0_, bf16[208,1664]{1,0:T(8,128)(2,1)} %collective-permute-done.10.down.refs_1_), custom_call_target="tpu_custom_call" | custom-call | flops 575000000 | bytes 1000 | tf_op jit(solution)/shard_map/far_parts/pallas_call | solution.py:147
  64.6 1.2 collective-permute-start.14
  65.8 1.6 %collective-permute-start.15 = (bf16[112,1664]{1,0:T(8,128)(2,1)}, bf16[112,1664]{1,0:T(8,128)(2,1)}, u32[]{:S(2)}, u32[]{:S(2)}) collective-permute-start(bf16[112,1664]{1,0:T(8,128)(2,1)} %get-tuple-element.162.refs_6_), channel_id=1, source_target_pairs={{0,2},{2,4},{4,6},{6,7},{7,5},{5,3},{3,1},{1,0},{8,10},{10,12},{12... | collective-permute-start | bytes 1118216 | tf_op jit(solution)/shard_map/ppermute | solution.py:585
  68.8 1.0 copy-done.17
  69.8 1.0 copy-done.21
  70.8 4.8 %projection_peers.3 = (f32[208,896]{1,0:T(8,128)S(1)}, f32[208,896]{1,0:T(8,128)S(1)}, f32[208,896]{1,0:T(8,128)S(1)}) custom-call(s32[3]{0:T(128)S(1)} %pad_add_fusion.1.order, s32[1]{0:T(128)} %bitcast.3.start, bf16[3,208,448]{2,1,0:T(8,128)(2,1)} %collective-permute-done.5.refs_0_, bf16[3,208,448]{2,1,0:T(8,128)(2,1)} %collective-permute-done.11.refs_1_, ...), custom_call_target="tpu_custom_call" | custom-call | flops 1724999936 | bytes 1000 | tf_op jit(solution)/shard_map/projection_peers/pallas_call | solution.py:453
  75.8 1.3 %collective-permute-done.14.refs_0_ = bf16[2,208,448]{2,1,0:T(8,128)(2,1)} collective-permute-done((bf16[2,208,448]{2,1,0:T(8,128)(2,1)}, bf16[2,208,448]{2,1,0:T(8,128)(2,1)}, u32[]{:S(2)}, u32[]{:S(2)}) %collective-permute-start.14) | collective-permute-done | bytes 372768 | tf_op jit(solution)/shard_map/ppermute | solution.py:501
  77.9 1.5 %collective-permute-start.17 = (bf16[112,896]{1,0:T(8,128)(2,1)S(1)}, bf16[112,896]{1,0:T(8,128)(2,1)S(1)}, u32[]{:S(2)}, u32[]{:S(2)}) collective-permute-start(bf16[112,896]{1,0:T(8,128)(2,1)S(1)} %slice.14), channel_id=1, source_target_pairs={{0,2},{2,4},{4,6},{6,7},{7,5},{5,3},{3,1},{1,0},{8,10},{10,12},{12... | collective-permute-start | bytes 602120 | tf_op jit(solution)/shard_map/ppermute | solution.py:605
  80.0 0.8 collective-permute-start.22
  80.8 4.1 %projection_peers.4 = (f32[208,896]{1,0:T(8,128)S(1)}, f32[208,896]{1,0:T(8,128)S(1)}) custom-call(s32[2]{0:T(128)S(1)} %pad_add_fusion.2.order, s32[1]{0:T(128)} %bitcast.3.start, bf16[2,208,448]{2,1,0:T(8,128)(2,1)} %collective-permute-done.14.refs_0_, bf16[2,208,448]{2,1,0:T(8,128)(2,1)S(1)} %collective-permute-done.19.refs_1_, ...), custom_call_target="tpu_custom_call" | custom-call | flops 1724999936 | bytes 1000 | tf_op jit(solution)/shard_map/projection_peers/pallas_call | solution.py:453
  84.9 1.0 collective-permute-done.18
  86.0 1.0 collective-permute-start.20
  87.1 1.0 collective-permute-start.21
  88.2 6.0 %grad_out_rows.3 = (f32[8,208,448]{2,1,0:T(8,128)}, bf16[8,208,448]{2,1,0:T(8,128)(2,1)}) custom-call(s32[4]{0:T(128)S(1)} %pad_add_fusion.3.info, bf16[3200,512]{1,0:T(8,128)(2,1)} %scaled_cotangent.1.refs_2_.turned, bf16[3200,512]{1,0:T(8,128)(2,1)S(1)} %collective-permute-done.8.refs_3_.turned_other, ...), custom_call_target="tpu_custom_call", output_to_operand_aliasing={{0}: (7, {}), {1}: (8, {})} | custom-call | flops 115000000 | bytes 1000 | tf_op jit(solution)/shard_map/grad_out_rows/pallas_call | solution.py:324
  94.2 2.1 %collective-permute-done.22.refs_0_ = bf16[3,208,448]{2,1,0:T(8,128)(2,1)} collective-permute-done((bf16[3,208,448]{2,1,0:T(8,128)(2,1)S(1)}, bf16[3,208,448]{2,1,0:T(8,128)(2,1)}, u32[]{:S(2)}, u32[]{:S(2)}) %collective-permute-start.22) | collective-permute-done | bytes 559136 | tf_op jit(solution)/shard_map/ppermute | solution.py:501
  97.2 0.8 add_convert_fusion.2
  98.5 1.5 %collective-permute-start.24 = (bf16[208,896]{1,0:T(8,128)(2,1)}, bf16[208,896]{1,0:T(8,128)(2,1)}, u32[]{:S(2)}, u32[]{:S(2)}) collective-permute-start(bf16[208,896]{1,0:T(8,128)(2,1)} %add_convert_fusion.3), channel_id=1, source_target_pairs={{0,2},{2,4},{4,6},{6,7},{7,5},{5,3},{3,1},{1,0},{8,10},{10,12},{12... | collective-permute-start | bytes 1118216 | tf_op jit(solution)/shard_map/ppermute | solution.py:630
  101.9 1.8 %copy-done.15 = bf16[3,208,448]{2,1,0:T(8,128)(2,1)S(1)} copy-done((bf16[3,208,448]{2,1,0:T(8,128)(2,1)S(1)}, bf16[3,208,448]{2,1,0:T(8,128)(2,1)}, u32[]{:S(2)}) %copy-start.15) | copy-done | bytes 559128
  103.7 1.0 copy-done.19
  104.8 1.0 copy-done.23
  105.8 4.8 %projection_peers.5 = (f32[208,896]{1,0:T(8,128)S(1)}, f32[208,896]{1,0:T(8,128)S(1)}, f32[208,896]{1,0:T(8,128)S(1)}) custom-call(s32[3]{0:T(128)S(1)} %pad_add_fusion.order, s32[1]{0:T(128)} %bitcast.3.start, bf16[3,208,448]{2,1,0:T(8,128)(2,1)} %collective-permute-done.22.refs_0_, bf16[3,208,448]{2,1,0:T(8,128)(2,1)S(1)} %copy-done.15, ...), custom_call_target="tpu_custom_call" | custom-call | flops 1724999936 | bytes 1000 | tf_op jit(solution)/shard_map/projection_peers/pallas_call | solution.py:453
  110.6 1.1 add_convert_fusion.1
  111.8 1.5 %collective-permute-start.26 = (bf16[208,896]{1,0:T(8,128)(2,1)S(1)}, bf16[208,896]{1,0:T(8,128)(2,1)S(1)}, u32[]{:S(2)}, u32[]{:S(2)}) collective-permute-start(bf16[208,896]{1,0:T(8,128)(2,1)S(1)} %add_convert_fusion.1), channel_id=1, source_target_pairs={{0,2},{2,4},{4,6},{6,7},{7,5},{5,3},{3,1},{1,0},{8,10},{10,12},{12... | collective-permute-start | bytes 1118216 | tf_op jit(solution)/shard_map/ppermute | solution.py:630
  113.9 2.3 %copy-done.3 = bf16[3,448,1664]{2,1,0:T(8,128)(2,1)S(1)} copy-done((bf16[3,448,1664]{2,1,0:T(8,128)(2,1)S(1)}, bf16[3,448,1664]{2,1,0:T(8,128)(2,1)}, u32[]{:S(2)}) %copy-start.3) | copy-done | bytes 4472856
  116.2 3.4 %attention_backward.3.rest_0_ = bf16[3,448,1664]{2,1,0:T(8,128)(2,1)} custom-call(bf16[3,448,1664]{2,1,0:T(8,128)(2,1)S(1)} %copy-done.3, f32[1664,448]{1,0:T(8,128)S(1)} %bitcast.19, bf16[1664,448]{1,0:T(8,128)(2,1)S(1)} %bitcast.22, f32[13,256,256]{2,1,0:T(8,128)S(1)} %copy-done.4, f32[13,192,192]{2,1,0:T(8,128)S(1)} %copy-done.5), custom_call_target="tpu_custom_call" | custom-call | flops 3449999872 | bytes 1000 | tf_op jit(solution)/shard_map/attention_backward/pallas_call | solution.py:256
  119.5 2.5 %attention_backward.4.rest_0_ = bf16[3,448,1664]{2,1,0:T(8,128)(2,1)} custom-call(bf16[3,448,1664]{2,1,0:T(8,128)(2,1)S(1)} %copy-done.3, f32[1664,448]{1,0:T(8,128)S(1)} %bitcast.20, bf16[1664,448]{1,0:T(8,128)(2,1)S(1)} %bitcast.23, f32[13,256,256]{2,1,0:T(8,128)S(1)} %copy-done.4, f32[13,192,192]{2,1,0:T(8,128)S(1)} %copy-done.5, ...), custom_call_target="tpu_custom_call", output_to_operand_aliasing={{}: (5, {})} | custom-call | flops 2300000000 | bytes 1000 | tf_op jit(solution)/shard_map/attention_backward/pallas_call | solution.py:256
  122.0 2.4 %attention_backward.5 = bf16[3,448,1664]{2,1,0:T(8,128)(2,1)} custom-call(bf16[3,448,1664]{2,1,0:T(8,128)(2,1)S(1)} %copy-done.3, f32[1664,448]{1,0:T(8,128)S(1)} %bitcast.21, bf16[1664,448]{1,0:T(8,128)(2,1)S(1)} %bitcast.24, f32[13,256,256]{2,1,0:T(8,128)S(1)} %copy-done.4, f32[13,192,192]{2,1,0:T(8,128)S(1)} %copy-done.5, ...), custom_call_target="tpu_custom_call", output_to_operand_aliasing={{}: (5, {})} | custom-call | flops 2300000000 | bytes 1000 | tf_op jit(solution)/shard_map/attention_backward/pallas_call | solution.py:256
  124.5 1.1 last_sum.1
  (90 shorter events, 11.7 us)
Async XLA Ops:
  0.6 15.6 %copy-start = (s32[4,1,4]{2,1,0:T(1,128)S(1)}, s32[4,1,4]{2,1,0:T(1,128)}, u32[]{:S(2)}) copy-start(s32[4,1,4]{2,1,0:T(1,128)} %param.9) | copy-start | bytes 196
  1.8 6.4 %copy-start.6 = (bf16[208,1664]{1,0:T(8,128)(2,1)}, bf16[208,1664]{1,0:T(8,128)(2,1)S(1)}, u32[]{:S(2)}) copy-start(bf16[208,1664]{1,0:T(8,128)(2,1)S(1)} %own_half_of_weight.1.refs_0_) | copy-start | bytes 2076676
  1.8 21.8 %collective-permute-start.1 = (bf16[208,1664]{1,0:T(8,128)(2,1)S(1)}, bf16[208,1664]{1,0:T(8,128)(2,1)S(1)}, u32[]{:S(2)}, u32[]{:S(2)}) collective-permute-start(bf16[208,1664]{1,0:T(8,128)(2,1)S(1)} %own_half_of_weight.1.refs_0_), channel_id=1, source_target_pairs={{0,2},{2,4},{4,6},{6,7},{7,5},{5,3},{3,1},{1,0},{8,10},{10,12},{12... | collective-permute-start | bytes 2076680 | tf_op jit(solution)/shard_map/ppermute | solution.py:522
  4.9 18.7 %collective-permute-start.2 = (bf16[208,1664]{1,0:T(8,128)(2,1)S(1)}, bf16[208,1664]{1,0:T(8,128)(2,1)S(1)}, u32[]{:S(2)}, u32[]{:S(2)}) collective-permute-start(bf16[208,1664]{1,0:T(8,128)(2,1)S(1)} %own_half_of_weight.1.refs_0_), channel_id=1, source_target_pairs={{0,1},{2,0},{4,2},{6,4},{7,6},{5,7},{3,5},{1,3},{8,9},{10,8},{12,1... | collective-permute-start | bytes 2076680 | tf_op jit(solution)/shard_map/ppermute | solution.py:523
  8.2 15.4 %collective-permute-start.3 = (bf16[160,1664]{1,0:T(8,128)(2,1)}, bf16[160,1664]{1,0:T(8,128)(2,1)S(1)}, u32[]{:S(2)}, u32[]{:S(2)}) collective-permute-start(bf16[160,1664]{1,0:T(8,128)(2,1)} %get-tuple-element.98), channel_id=1, source_target_pairs={{0,16},{8,24},{16,0},{24,8},{1,17},{9,25},{17,1},{25,9},{2,18},{10... | collective-permute-start | bytes 1597448 | tf_op jit(solution)/shard_map/ppermute | solution.py:501
  10.2 6.0 %copy-start.2 = (bf16[3,448,1664]{2,1,0:T(8,128)(2,1)S(1)}, bf16[3,448,1664]{2,1,0:T(8,128)(2,1)}, u32[]{:S(2)}) copy-start(bf16[3,448,1664]{2,1,0:T(8,128)(2,1)} %qkv.7) | copy-start | bytes 13418500
  23.6 1.3 %copy-start.10 = (bf16[208,1664]{1,0:T(8,128)(2,1)}, bf16[208,1664]{1,0:T(8,128)(2,1)S(1)}, u32[]{:S(2)}) copy-start(bf16[208,1664]{1,0:T(8,128)(2,1)S(1)} %collective-permute-done.2.refs_2_) | copy-start | bytes 2076676
  24.8 8.5 %collective-permute-start.8 = (bf16[3200,512]{1,0:T(8,128)(2,1)}, bf16[3200,512]{1,0:T(8,128)(2,1)S(1)}, u32[]{:S(2)}, u32[]{:S(2)}) collective-permute-start(bf16[3200,512]{1,0:T(8,128)(2,1)} %scaled_cotangent.1.refs_2_.turned), channel_id=1, source_target_pairs={{0,8},{8,0},{16,24},{24,16},{1,9},{9,1},{17,25},{25,17},{2,10},{10... | collective-permute-start | bytes 9830408 | tf_op jit(solution)/shard_map/ppermute | solution.py:501
  24.8 8.3 %collective-permute-start.4 = (bf16[8,208,448]{2,1,0:T(8,128)(2,1)}, bf16[8,208,448]{2,1,0:T(8,128)(2,1)}, u32[]{:S(2)}, u32[]{:S(2)}) collective-permute-start(bf16[8,208,448]{2,1,0:T(8,128)(2,1)} %bitcast.25), channel_id=1, source_target_pairs={{0,8},{8,0},{16,24},{24,16},{1,9},{9,1},{17,25},{25,17},{2,10},{10... | collective-permute-start | bytes 4472840 | tf_op jit(solution)/shard_map/ppermute | solution.py:501
  25.4 23.5 %collective-permute-start = (bf16[288,1664]{1,0:T(8,128)(2,1)}, bf16[288,1664]{1,0:T(8,128)(2,1)}, u32[]{:S(2)}, u32[]{:S(2)}) collective-permute-start(bf16[288,1664]{1,0:T(8,128)(2,1)} %get-tuple-element.96), channel_id=1, source_target_pairs={{0,16},{8,24},{16,0},{24,8},{1,17},{9,25},{17,1},{25,9},{2,18},{10... | collective-permute-start | bytes 2875400 | tf_op jit(solution)/shard_map/ppermute | solution.py:501
  25.5 17.7 %collective-permute-start.6 = (bf16[208,1664]{1,0:T(8,128)(2,1)}, bf16[208,1664]{1,0:T(8,128)(2,1)}, u32[]{:S(2)}, u32[]{:S(2)}) collective-permute-start(bf16[208,1664]{1,0:T(8,128)(2,1)} %copy-done.8), channel_id=1, source_target_pairs={{0,2},{2,4},{4,6},{6,7},{7,5},{5,3},{3,1},{1,0},{8,10},{10,12},{12... | collective-permute-start | bytes 2076680 | tf_op jit(solution)/shard_map/ppermute | solution.py:554
  27.5 17.2 %collective-permute-start.7 = (bf16[208,1664]{1,0:T(8,128)(2,1)}, bf16[208,1664]{1,0:T(8,128)(2,1)}, u32[]{:S(2)}, u32[]{:S(2)}) collective-permute-start(bf16[208,1664]{1,0:T(8,128)(2,1)} %copy-done.10), channel_id=1, source_target_pairs={{0,1},{2,0},{4,2},{6,4},{7,6},{5,7},{3,5},{1,3},{8,9},{10,8},{12,1... | collective-permute-start | bytes 2076680 | tf_op jit(solution)/shard_map/ppermute | solution.py:555
  44.6 16.5 %collective-permute-start.9 = (bf16[208,1664]{1,0:T(8,128)(2,1)}, bf16[208,1664]{1,0:T(8,128)(2,1)}, u32[]{:S(2)}, u32[]{:S(2)}) collective-permute-start(bf16[208,1664]{1,0:T(8,128)(2,1)} %collective-permute-done.6.refs_3_), channel_id=1, source_target_pairs={{0,2},{2,4},{4,6},{6,7},{7,5},{5,3},{3,1},{1,0},{8,10},{10,12},{12... | collective-permute-start | bytes 2076680 | tf_op jit(solution)/shard_map/ppermute | solution.py:577
  46.2 16.0 %collective-permute-start.10 = (bf16[208,1664]{1,0:T(8,128)(2,1)}, bf16[208,1664]{1,0:T(8,128)(2,1)}, u32[]{:S(2)}, u32[]{:S(2)}) collective-permute-start(bf16[208,1664]{1,0:T(8,128)(2,1)} %collective-permute-done.7.refs_4_), channel_id=1, source_target_pairs={{0,1},{2,0},{4,2},{6,4},{7,6},{5,7},{3,5},{1,3},{8,9},{10,8},{12,1... | collective-permute-start | bytes 2076680 | tf_op jit(solution)/shard_map/ppermute | solution.py:578
  48.8 15.8 %collective-permute-start.5 = (bf16[3,208,448]{2,1,0:T(8,128)(2,1)}, bf16[3,208,448]{2,1,0:T(8,128)(2,1)}, u32[]{:S(2)}, u32[]{:S(2)}) collective-permute-start(bf16[3,208,448]{2,1,0:T(8,128)(2,1)} %get-tuple-element.107), channel_id=1, source_target_pairs={{0,16},{8,24},{16,0},{24,8},{1,17},{9,25},{17,1},{25,9},{2,18},{10... | collective-permute-start | bytes 1677320 | tf_op jit(solution)/shard_map/ppermute | solution.py:501
  49.2 18.2 %collective-permute-start.12 = (bf16[160,1664]{1,0:T(8,128)(2,1)}, bf16[160,1664]{1,0:T(8,128)(2,1)S(1)}, u32[]{:S(2)}, u32[]{:S(2)}) collective-permute-start(bf16[160,1664]{1,0:T(8,128)(2,1)} %copy-done.16), channel_id=1, source_target_pairs={{0,8},{8,0},{16,24},{24,16},{1,9},{9,1},{17,25},{25,17},{2,10},{10... | collective-permute-start | bytes 1597448 | tf_op jit(solution)/shard_map/ppermute | solution.py:501
  49.2 19.6 %collective-permute-start.13 = (bf16[288,1664]{1,0:T(8,128)(2,1)}, bf16[288,1664]{1,0:T(8,128)(2,1)}, u32[]{:S(2)}, u32[]{:S(2)}) collective-permute-start(bf16[288,1664]{1,0:T(8,128)(2,1)} %collective-permute-done.refs_3_), channel_id=1, source_target_pairs={{0,8},{8,0},{16,24},{24,16},{1,9},{9,1},{17,25},{25,17},{2,10},{10... | collective-permute-start | bytes 2875400 | tf_op jit(solution)/shard_map/ppermute | solution.py:501
  49.7 1.1 copy-start.7
  50.8 1.1 copy-start.9
  51.9 1.1 copy-start.11
  64.6 4.2 %collective-permute-start.11 = (bf16[3,208,448]{2,1,0:T(8,128)(2,1)}, bf16[3,208,448]{2,1,0:T(8,128)(2,1)}, u32[]{:S(2)}, u32[]{:S(2)}) collective-permute-start(bf16[3,208,448]{2,1,0:T(8,128)(2,1)} %collective-permute-done.5.refs_0_), channel_id=1, source_target_pairs={{0,8},{8,0},{16,24},{24,16},{1,9},{9,1},{17,25},{25,17},{2,10},{10... | collective-permute-start | bytes 1677320 | tf_op jit(solution)/shard_map/ppermute | solution.py:501
  64.6 12.5 %collective-permute-start.14 = (bf16[2,208,448]{2,1,0:T(8,128)(2,1)}, bf16[2,208,448]{2,1,0:T(8,128)(2,1)}, u32[]{:S(2)}, u32[]{:S(2)}) collective-permute-start(bf16[2,208,448]{2,1,0:T(8,128)(2,1)} %get-tuple-element.136), channel_id=1, source_target_pairs={{0,16},{8,24},{16,0},{24,8},{1,17},{9,25},{17,1},{25,9},{2,18},{10... | collective-permute-start | bytes 1118216 | tf_op jit(solution)/shard_map/ppermute | solution.py:501
  65.8 12.1 %collective-permute-start.15 = (bf16[112,1664]{1,0:T(8,128)(2,1)}, bf16[112,1664]{1,0:T(8,128)(2,1)}, u32[]{:S(2)}, u32[]{:S(2)}) collective-permute-start(bf16[112,1664]{1,0:T(8,128)(2,1)} %get-tuple-element.162.refs_6_), channel_id=1, source_target_pairs={{0,2},{2,4},{4,6},{6,7},{7,5},{5,3},{3,1},{1,0},{8,10},{10,12},{12... | collective-permute-start | bytes 1118216 | tf_op jit(solution)/shard_map/ppermute | solution.py:585
  68.2 9.6 %collective-permute-start.16 = (bf16[96,1664]{1,0:T(8,128)(2,1)}, bf16[96,1664]{1,0:T(8,128)(2,1)}, u32[]{:S(2)}, u32[]{:S(2)}) collective-permute-start(bf16[96,1664]{1,0:T(8,128)(2,1)} %get-tuple-element.138), channel_id=1, source_target_pairs={{0,1},{2,0},{4,2},{6,4},{7,6},{5,7},{3,5},{1,3},{8,9},{10,8},{12,1... | collective-permute-start | bytes 958472 | tf_op jit(solution)/shard_map/ppermute | solution.py:586
  68.7 1.0 copy-start.17
  69.8 1.0 copy-start.21
  70.8 9.1 %copy-start.13 = (bf16[3,208,448]{2,1,0:T(8,128)(2,1)S(1)}, bf16[3,208,448]{2,1,0:T(8,128)(2,1)}, u32[]{:S(2)}) copy-start(bf16[3,208,448]{2,1,0:T(8,128)(2,1)} %copy-done.12) | copy-start | bytes 1677316
  70.8 10.0 %copy-start.18 = (bf16[160,1664]{1,0:T(8,128)(2,1)S(1)}, bf16[160,1664]{1,0:T(8,128)(2,1)}, u32[]{:S(2)}) copy-start(bf16[160,1664]{1,0:T(8,128)(2,1)} %copy-done.16) | copy-start | bytes 1597444
  70.8 10.0 %copy-start.22 = (bf16[160,1664]{1,0:T(8,128)(2,1)S(1)}, bf16[160,1664]{1,0:T(8,128)(2,1)}, u32[]{:S(2)}) copy-start(bf16[160,1664]{1,0:T(8,128)(2,1)} %copy-done.20) | copy-start | bytes 1597444
  77.9 3.0 %collective-permute-start.19 = (bf16[2,208,448]{2,1,0:T(8,128)(2,1)}, bf16[2,208,448]{2,1,0:T(8,128)(2,1)S(1)}, u32[]{:S(2)}, u32[]{:S(2)}) collective-permute-start(bf16[2,208,448]{2,1,0:T(8,128)(2,1)} %collective-permute-done.14.refs_0_), channel_id=1, source_target_pairs={{0,8},{8,0},{16,24},{24,16},{1,9},{9,1},{17,25},{25,17},{2,10},{10... | collective-permute-start | bytes 1118216 | tf_op jit(solution)/shard_map/ppermute | solution.py:501
  77.9 8.0 %collective-permute-start.17 = (bf16[112,896]{1,0:T(8,128)(2,1)S(1)}, bf16[112,896]{1,0:T(8,128)(2,1)S(1)}, u32[]{:S(2)}, u32[]{:S(2)}) collective-permute-start(bf16[112,896]{1,0:T(8,128)(2,1)S(1)} %slice.14), channel_id=1, source_target_pairs={{0,2},{2,4},{4,6},{6,7},{7,5},{5,3},{3,1},{1,0},{8,10},{10,12},{12... | collective-permute-start | bytes 602120 | tf_op jit(solution)/shard_map/ppermute | solution.py:605
  79.4 6.5 %collective-permute-start.18 = (bf16[96,896]{1,0:T(8,128)(2,1)S(1)}, bf16[96,896]{1,0:T(8,128)(2,1)S(1)}, u32[]{:S(2)}, u32[]{:S(2)}) collective-permute-start(bf16[96,896]{1,0:T(8,128)(2,1)S(1)} %slice.15), channel_id=1, source_target_pairs={{0,1},{2,0},{4,2},{6,4},{7,6},{5,7},{3,5},{1,3},{8,9},{10,8},{12,1... | collective-permute-start | bytes 516104 | tf_op jit(solution)/shard_map/ppermute | solution.py:606
  80.0 16.3 %collective-permute-start.22 = (bf16[3,208,448]{2,1,0:T(8,128)(2,1)S(1)}, bf16[3,208,448]{2,1,0:T(8,128)(2,1)}, u32[]{:S(2)}, u32[]{:S(2)}) collective-permute-start(bf16[3,208,448]{2,1,0:T(8,128)(2,1)S(1)} %copy-done.13), channel_id=1, source_target_pairs={{0,16},{8,24},{16,0},{24,8},{1,17},{9,25},{17,1},{25,9},{2,18},{10... | collective-permute-start | bytes 1677320 | tf_op jit(solution)/shard_map/ppermute | solution.py:501
  86.0 10.3 %collective-permute-start.20 = (bf16[208,896]{1,0:T(8,128)(2,1)S(1)}, bf16[208,896]{1,0:T(8,128)(2,1)S(1)}, u32[]{:S(2)}, u32[]{:S(2)}) collective-permute-start(bf16[208,896]{1,0:T(8,128)(2,1)S(1)} %get-tuple-element.152), channel_id=1, source_target_pairs={{0,2},{2,4},{4,6},{6,7},{7,5},{5,3},{3,1},{1,0},{8,10},{10,12},{12... | collective-permute-start | bytes 1118216 | tf_op jit(solution)/shard_map/ppermute | solution.py:630
  87.1 10.1 %collective-permute-start.21 = (bf16[208,896]{1,0:T(8,128)(2,1)S(1)}, bf16[208,896]{1,0:T(8,128)(2,1)S(1)}, u32[]{:S(2)}, u32[]{:S(2)}) collective-permute-start(bf16[208,896]{1,0:T(8,128)(2,1)S(1)} %get-tuple-element.154), channel_id=1, source_target_pairs={{0,1},{2,0},{4,2},{6,4},{7,6},{5,7},{3,5},{1,3},{8,9},{10,8},{12,1... | collective-permute-start | bytes 1118216 | tf_op jit(solution)/shard_map/ppermute | solution.py:631
  96.3 17.6 %collective-permute-start.28 = (bf16[8,208,448]{2,1,0:T(8,128)(2,1)}, bf16[8,208,448]{2,1,0:T(8,128)(2,1)S(1)}, u32[]{:S(2)}, u32[]{:S(2)}) collective-permute-start(bf16[8,208,448]{2,1,0:T(8,128)(2,1)} %get-tuple-element.177), channel_id=1, source_target_pairs={{0,8},{8,0},{16,24},{24,16},{1,9},{9,1},{17,25},{25,17},{2,10},{10... | collective-permute-start | bytes 4472840 | tf_op jit(solution)/shard_map/ppermute | solution.py:501
  98.0 3.0 %collective-permute-start.23 = (bf16[3,208,448]{2,1,0:T(8,128)(2,1)}, bf16[3,208,448]{2,1,0:T(8,128)(2,1)S(1)}, u32[]{:S(2)}, u32[]{:S(2)}) collective-permute-start(bf16[3,208,448]{2,1,0:T(8,128)(2,1)} %collective-permute-done.22.refs_0_), channel_id=1, source_target_pairs={{0,8},{8,0},{16,24},{24,16},{1,9},{9,1},{17,25},{25,17},{2,10},{10... | collective-permute-start | bytes 1677320 | tf_op jit(solution)/shard_map/ppermute | solution.py:501
  98.5 12.1 %collective-permute-start.24 = (bf16[208,896]{1,0:T(8,128)(2,1)}, bf16[208,896]{1,0:T(8,128)(2,1)}, u32[]{:S(2)}, u32[]{:S(2)}) collective-permute-start(bf16[208,896]{1,0:T(8,128)(2,1)} %add_convert_fusion.3), channel_id=1, source_target_pairs={{0,2},{2,4},{4,6},{6,7},{7,5},{5,3},{3,1},{1,0},{8,10},{10,12},{12... | collective-permute-start | bytes 1118216 | tf_op jit(solution)/shard_map/ppermute | solution.py:630
  100.1 13.8 %copy-start.1 = (f32[8,208,448]{2,1,0:T(8,128)S(1)}, f32[8,208,448]{2,1,0:T(8,128)}, u32[]{:S(2)}) copy-start(f32[8,208,448]{2,1,0:T(8,128)} %get-tuple-element.165) | copy-start | bytes 8945668
  100.1 13.8 %copy-start.4 = (f32[13,256,256]{2,1,0:T(8,128)S(1)}, f32[13,256,256]{2,1,0:T(8,128)}, u32[]{:S(2)}) copy-start(f32[13,256,256]{2,1,0:T(8,128)} %get-tuple-element.178.main_probs) | copy-start | bytes 10223620
  100.1 13.8 %copy-start.5 = (f32[13,192,192]{2,1,0:T(8,128)S(1)}, f32[13,192,192]{2,1,0:T(8,128)}, u32[]{:S(2)}) copy-start(f32[13,192,192]{2,1,0:T(8,128)} %get-tuple-element.179.slot_probs) | copy-start | bytes 5750788
  100.1 11.6 %collective-permute-start.25 = (bf16[208,896]{1,0:T(8,128)(2,1)}, bf16[208,896]{1,0:T(8,128)(2,1)S(1)}, u32[]{:S(2)}, u32[]{:S(2)}) collective-permute-start(bf16[208,896]{1,0:T(8,128)(2,1)} %add_convert_fusion.2), channel_id=1, source_target_pairs={{0,1},{2,0},{4,2},{6,4},{7,6},{5,7},{3,5},{1,3},{8,9},{10,8},{12,1... | collective-permute-start | bytes 1118216 | tf_op jit(solution)/shard_map/ppermute | solution.py:631
  101.9 1.8 %copy-start.15 = (bf16[3,208,448]{2,1,0:T(8,128)(2,1)S(1)}, bf16[3,208,448]{2,1,0:T(8,128)(2,1)}, u32[]{:S(2)}) copy-start(bf16[3,208,448]{2,1,0:T(8,128)(2,1)} %copy-done.14) | copy-start | bytes 1677316
  103.7 1.0 copy-start.19
  104.8 1.0 copy-start.23
  111.8 12.7 %collective-permute-start.26 = (bf16[208,896]{1,0:T(8,128)(2,1)S(1)}, bf16[208,896]{1,0:T(8,128)(2,1)S(1)}, u32[]{:S(2)}, u32[]{:S(2)}) collective-permute-start(bf16[208,896]{1,0:T(8,128)(2,1)S(1)} %add_convert_fusion.1), channel_id=1, source_target_pairs={{0,2},{2,4},{4,6},{6,7},{7,5},{5,3},{3,1},{1,0},{8,10},{10,12},{12... | collective-permute-start | bytes 1118216 | tf_op jit(solution)/shard_map/ppermute | solution.py:630
  113.3 11.2 %collective-permute-start.27 = (bf16[208,896]{1,0:T(8,128)(2,1)S(1)}, bf16[208,896]{1,0:T(8,128)(2,1)S(1)}, u32[]{:S(2)}, u32[]{:S(2)}) collective-permute-start(bf16[208,896]{1,0:T(8,128)(2,1)S(1)} %add_convert_fusion), channel_id=1, source_target_pairs={{0,1},{2,0},{4,2},{6,4},{7,6},{5,7},{3,5},{1,3},{8,9},{10,8},{12,1... | collective-permute-start | bytes 1118216 | tf_op jit(solution)/shard_map/ppermute | solution.py:631
  113.9 2.3 %copy-start.3 = (bf16[3,448,1664]{2,1,0:T(8,128)(2,1)S(1)}, bf16[3,448,1664]{2,1,0:T(8,128)(2,1)}, u32[]{:S(2)}) copy-start(bf16[3,448,1664]{2,1,0:T(8,128)(2,1)} %qkv.7) | copy-start | bytes 13418500
  (5 other events, 4.4 us)

commit v6 on v4

--- a/solution.py
+++ b/solution.py
@@ -12,7 +12,7 @@
 SLOT = 96
 LANE = 128
 FACTOR = HS ** (-0.5)
-VMEM_BYTES = 20 * 1024 * 1024
+MIB = 1024 * 1024
 
 
 def lasting(microseconds):
@@ -68,7 +68,7 @@
             ],
         ),
         out_shape=[pltpu.HBM((part, width), jnp.bfloat16) for part in parts] * peers,
-        compiler_params=pltpu.CompilerParams(vmem_limit_bytes=VMEM_BYTES),
+        compiler_params=pltpu.CompilerParams(vmem_limit_bytes=8 * MIB),
         cost_estimate=lasting(60),
         name="peer_windows",
     )(starts, in_hbm(cotangent), layer_scale)
@@ -92,7 +92,7 @@
         in_specs=[pl.BlockSpec((rows, block), lambda i: (0, i)), pl.BlockSpec((1, block), lambda i: (0, i))],
         out_specs=pl.BlockSpec((block, lanes), lambda i: (i, 0)),
         out_shape=pltpu.HBM((total, lanes), jnp.bfloat16),
-        compiler_params=pltpu.CompilerParams(vmem_limit_bytes=VMEM_BYTES),
+        compiler_params=pltpu.CompilerParams(vmem_limit_bytes=8 * MIB),
         cost_estimate=lasting(60),
         name="scaled_cotangent",
     )(in_hbm(cotangent), layer_scale)
@@ -123,7 +123,7 @@
             scratch_shapes=[pltpu.SemaphoreType.DMA((sum(sizes),))],
         ),
         out_shape=[jax.ShapeDtypeStruct((size, depth, rows), attended.dtype) for size in sizes],
-        compiler_params=pltpu.CompilerParams(vmem_limit_bytes=VMEM_BYTES),
+        compiler_params=pltpu.CompilerParams(vmem_limit_bytes=6 * MIB),
         cost_estimate=lasting(2),
         name="attended_chunks",
     )(order, in_hbm(attended))
@@ -151,7 +151,7 @@
         out_specs=[pl.BlockSpec((size, width), lambda i: (0, 0)) for size in sizes],
         out_shape=[jax.ShapeDtypeStruct((size, width), up.dtype) for size in sizes],
         scratch_shapes=[pltpu.SemaphoreType.DMA((2,))],
-        compiler_params=pltpu.CompilerParams(vmem_limit_bytes=VMEM_BYTES),
+        compiler_params=pltpu.CompilerParams(vmem_limit_bytes=4 * MIB),
         cost_estimate=lasting(1),
         name="far_parts",
     )(up, down)
@@ -220,7 +220,7 @@
             pltpu.HBM((heads, MAIN, MAIN), jnp.float32),
             pltpu.HBM((heads, 2 * SLOT, 2 * SLOT), jnp.float32),
         ],
-        compiler_params=pltpu.CompilerParams(vmem_limit_bytes=VMEM_BYTES),
+        compiler_params=pltpu.CompilerParams(vmem_limit_bytes=12 * MIB),
         cost_estimate=lasting(60),
         name="attention_forward",
     )(counts, qkv)
@@ -266,7 +266,7 @@
         out_specs=pl.BlockSpec((3, rows, PAIR * HS), lambda h: (0, 0, h + low)),
         out_shape=pltpu.HBM(qkv.shape, jnp.bfloat16),
         input_output_aliases={5: 0} if held else {},
-        compiler_params=pltpu.CompilerParams(vmem_limit_bytes=VMEM_BYTES),
+        compiler_params=pltpu.CompilerParams(vmem_limit_bytes=14 * MIB),
         cost_estimate=lasting(2 * (high - low)),
         name="attention_backward",
     )(qkv, grad_mine, grad_other, main_probs, slot_probs, *map(in_hbm, held))
@@ -342,7 +342,7 @@
             pltpu.HBM((shards, depth, rows), jnp.bfloat16),
         ],
         input_output_aliases={3 + len(arrays) + i: i for i in range(len(held))},
-        compiler_params=pltpu.CompilerParams(vmem_limit_bytes=VMEM_BYTES),
+        compiler_params=pltpu.CompilerParams(vmem_limit_bytes=16 * MIB),
         cost_estimate=lasting(0.2 if held else 1.5 * len(pieces)),
         name="grad_out_rows",
     )(info, in_hbm(turned), turned_other, *arrays, *map(in_hbm, held), *after)
@@ -365,7 +365,7 @@
             scratch_shapes=[pltpu.SemaphoreType.DMA],
         ),
         out_shape=jax.ShapeDtypeStruct((weight.shape[0], width), weight.dtype),
-        compiler_params=pltpu.CompilerParams(vmem_limit_bytes=VMEM_BYTES),
+        compiler_params=pltpu.CompilerParams(vmem_limit_bytes=2 * MIB),
         cost_estimate=lasting(1),
         name="own_half_of_weight",
     )(start, in_hbm(weight))
@@ -392,7 +392,7 @@
             out_specs=pl.BlockSpec((depth, owned), lambda i, s: (0, 0)),
         ),
         out_shape=jax.ShapeDtypeStruct((depth, owned), jnp.float32),
-        compiler_params=pltpu.CompilerParams(vmem_limit_bytes=VMEM_BYTES),
+        compiler_params=pltpu.CompilerParams(vmem_limit_bytes=8 * MIB),
         cost_estimate=lasting(2),
         name="last_sum",
     )(start, term, came_up, came_down)
@@ -423,22 +423,22 @@
     for some in copies:
         for copy in some:
             copy.start()
-    together = depth % 16 == 0
-    for i, some in enumerate(copies):
-        for copy in some:
-            copy.wait()
-        if together:
-            tall = chunks[i].reshape(count * depth, rows)
-            product = dot(tall, held[i][:, :rows], 1, 1) if chosen else dot(tall, held[i], 1, 0)
-        for j, out in enumerate(outs):
-            if together:
-                part = product[j * depth:(j + 1) * depth]
-            else:
-                part = dot(chunks[i, j], held[i][:, :rows], 1, 1) if chosen else dot(chunks[i, j], held[i], 1, 0)
-            if i == 0:
-                out[...] = bases[j][...] + part if bases else part
-            else:
-                out[...] += part
+    most = 4 if depth % 16 == 0 else 1
+    for first in range(0, count, most):
+        some = min(most, count - first)
+        total = None
+        for i in range(sources):
+            if first == 0:
+                for copy in copies[i]:
+                    copy.wait()
+            tall = chunks[i, first:first + some].reshape(some * depth, rows) if some > 1 else chunks[i, first]
+            part = dot(tall, held[i][:, :rows], 1, 1) if chosen else dot(tall, held[i], 1, 0)
+            total = part if total is None else total + part
+        for j in range(some):
+            result = total[j * depth:(j + 1) * depth]
+            if bases:
+                result += bases[first + j][...].astype(jnp.float32)
+            outs[first + j][...] = result.astype(outs[first + j].dtype)
 
 
 def partial_products(order, start, attended, columns, window, bases=()):
@@ -459,8 +459,10 @@
                 pltpu.SemaphoreType.DMA((sources, count + parts)),
             ],
         ),
-        out_shape=[(jax.ShapeDtypeStruct if bases else pltpu.HBM)((depth, window), jnp.float32)] * count,
-        compiler_params=pltpu.CompilerParams(vmem_limit_bytes=VMEM_BYTES),
+        out_shape=[
+            jax.ShapeDtypeStruct((depth, window), jnp.float32) if bases else pltpu.HBM((depth, window), jnp.bfloat16)
+        ] * count,
+        compiler_params=pltpu.CompilerParams(vmem_limit_bytes=(16 if bases else 18) * MIB),
         cost_estimate=lasting(3 if bases else 6),
         name="projection_peers" if bases else "projection_chip",
     )(order, start, *attended, *columns, *map(in_hbm, bases))
@@ -542,6 +544,7 @@
     other_columns = [[swap(array, 1) for array in came_columns[0]]]
     attended_other = swap(attended, 1)
     chunks = list(arrange(flat, attended, sizes))
+    attended_other, chunks = lax.optimization_barrier((attended_other, chunks))
     for _ in range(half - 3):
         up.append(lax.ppermute(up[-1], "fsdp", ahead))
         down.append(lax.ppermute(down[-1], "fsdp", behind))
@@ -611,7 +614,8 @@
             going_up, going_down, near_up = lax.optimization_barrier((going_up, going_down, near_up))
             grad_out = rows_of([([near_up], 1 - half), ([near_down], half - 1), ([far_up, far_down], half)], grad_out, [sent_up])
             grad_mine = grad_out[0].reshape(width, rows)
-            grad_other = swap(grad_out[1], 1).reshape(width, rows)
+            came[2], grad_other = lax.optimization_barrier((came[2], grad_out[1]))
+            grad_other = swap(grad_other, 1).reshape(width, rows)
         elif step > 2:
             arrived = came[half - step + 1]
             going_up, going_down, arrived, grad_mine = lax.optimization_barrier((going_up, going_down, arrived, grad_mine))

time: 131 us -> 127 us (0.969)
  waiting for transfers between devices: 21.3 us -> 14.4 us
  local copies, waits for them, and re-layouts: 11.7 us -> 16.3 us
  Pallas kernels: 70 us -> 67.2 us
    ppermute x13, waiting for transfers between devices: 15.3 us -> 8.01 us  [swap(): return lax.ppermute(array, 'dp', [(i, i ^ bit) for i in range(members)])]
    unnamed x38 -> x48, local copies, waits for them, and re-layouts: 10.8 us -> 15.4 us
    pallas_call x4, Pallas kernels: 23.7 us -> 21.6 us  [partial_products(): pl.pallas_call(functools.partial(partial_kernel, not bases, sources, part...]
    ppermute x4, waiting for transfers between devices: 2.72 us -> 0.91 us  [local(): came_down = lax.ppermute(going_down, 'fsdp', behind)]
    ppermute x3, waiting for transfers between devices: 0.55 us -> 2.13 us  [local(): up.append(lax.ppermute(up[-1], 'fsdp', ahead))]
where the time goes in v6:
time: 127 us; the launch traced here: 126 us
  Pallas kernels  67.2 us (53%)
  starting transfers between devices  23.4 us (18%)
  local copies, waits for them, and re-layouts  16.3 us (13%)
  waiting for transfers between devices  14.4 us (11%)
  other arithmetic  3.26 us (3%)
    pallas_call x4, Pallas kernels, partial_products(): pl.pallas_call(functools.partial(partial_kernel, not bases, sources, part...  21.6 us
    unnamed x48, local copies, waits for them, and re-layouts  15.4 us
    pallas_call x2, Pallas kernels, grad_out_rows(): pl.pallas_call(functools.partial(grad_out_kernel, sizes, split, total), g...  14.2 us
    pallas_call x3, Pallas kernels, backward(): pl.pallas_call(backward_kernel, grid=(high - low,), in_specs=[pl.BlockSpe...  8.3 us
    ppermute x13, waiting for transfers between devices, swap(): return lax.ppermute(array, 'dp', [(i, i ^ bit) for i in range(members)])  8.01 us
    pallas_call x1, Pallas kernels, forward(): pl.pallas_call(forward_kernel, grid_spec=pltpu.PrefetchScalarGridSpec(num...  7.34 us
    ppermute x3, starting transfers between devices, local(): up.append(lax.ppermute(up[-1], 'fsdp', ahead))  6.64 us
    ppermute x13, starting transfers between devices, swap(): return lax.ppermute(array, 'dp', [(i, i ^ bit) for i in range(members)])  6.03 us
  transfers between devices with their start and end apart: 29, of which 12 were waited for; matrix products, arithmetic and copies ran while one was open for 3% of the time, Pallas kernels for 52%

profile of v6, /device:TPU:0, one launch (start us, length us, event | category | flops | bytes accessed | tf_op | source)
XLA Modules:
  0.0 125.6 jit_solution(5328804830325068230)
XLA Ops:
  0.7 1.1 own_half_of_weight.1.refs_0_
  1.8 3.1 %collective-permute-start.1 = (bf16[208,1664]{1,0:T(8,128)(2,1)S(1)}, bf16[208,1664]{1,0:T(8,128)(2,1)S(1)}, u32[]{:S(2)}, u32[]{:S(2)}) collective-permute-start(bf16[208,1664]{1,0:T(8,128)(2,1)S(1)} %own_half_of_weight.1.refs_0_), channel_id=1, source_target_pairs={{0,2},{2,4},{4,6},{6,7},{7,5},{5,3},{3,1},{1,0},{8,10},{10,12},{12... | collective-permute-start | bytes 2076680 | tf_op jit(solution)/shard_map/ppermute | solution.py:517
  5.6 2.6 %peer_windows.1 = (bf16[160,1664]{1,0:T(8,128)(2,1)}, bf16[288,1664]{1,0:T(8,128)(2,1)}) custom-call(s32[1]{0:T(128)} %bitcast.7.starts, bf16[448,3200]{1,0:T(8,128)(2,1)} %cotangent.1, f32[1,3200]{1,0:T(1,128)S(1)} %reshape.18.layer_scale), custom_call_target="tpu_custom_call" | custom-call | flops 34500001792 | bytes 1000 | tf_op jit(solution)/shard_map/peer_windows/pallas_call | solution.py:58
  8.2 2.0 %collective-permute-start.3 = (bf16[160,1664]{1,0:T(8,128)(2,1)}, bf16[160,1664]{1,0:T(8,128)(2,1)S(1)}, u32[]{:S(2)}, u32[]{:S(2)}) collective-permute-start(bf16[160,1664]{1,0:T(8,128)(2,1)} %get-tuple-element.98), channel_id=1, source_target_pairs={{0,16},{8,24},{16,0},{24,8},{1,17},{9,25},{17,1},{25,9},{2,18},{10... | collective-permute-start | bytes 1597448 | tf_op jit(solution)/shard_map/ppermute | solution.py:496
  10.2 6.0 %scaled_cotangent.1.refs_2_.turned = bf16[3200,512]{1,0:T(8,128)(2,1)} custom-call(bf16[448,3200]{1,0:T(8,128)(2,1)} %cotangent.1, f32[1,3200]{1,0:T(1,128)S(1)} %reshape.18.layer_scale), custom_call_target="tpu_custom_call" | custom-call | flops 34500001792 | bytes 1000 | tf_op jit(solution)/shard_map/scaled_cotangent/pallas_call | solution.py:89
  16.2 7.3 %attention_forward.1 = (bf16[1664,448]{1,0:T(8,128)(2,1)}, f32[13,256,256]{2,1,0:T(8,128)}, f32[13,192,192]{2,1,0:T(8,128)}) custom-call(s32[4]{0:T(128)S(1)} %dynamic-slice_bitcast_fusion.counts, bf16[3,448,1664]{2,1,0:T(8,128)(2,1)S(1)} %copy-done.2), custom_call_target="tpu_custom_call" | custom-call | flops 34500001792 | bytes 1000 | tf_op jit(solution)/shard_map/attention_forward/pallas_call | solution.py:206
  25.5 2.0 %collective-permute-start.6 = (bf16[208,1664]{1,0:T(8,128)(2,1)}, bf16[208,1664]{1,0:T(8,128)(2,1)}, u32[]{:S(2)}, u32[]{:S(2)}) collective-permute-start(bf16[208,1664]{1,0:T(8,128)(2,1)} %copy-done.8), channel_id=1, source_target_pairs={{0,2},{2,4},{4,6},{6,7},{7,5},{5,3},{3,1},{1,0},{8,10},{10,12},{12... | collective-permute-start | bytes 2076680 | tf_op jit(solution)/shard_map/ppermute | solution.py:549
  27.6 3.1 %attended_chunks.1 = (bf16[3,208,448]{2,1,0:T(8,128)(2,1)}, bf16[2,208,448]{2,1,0:T(8,128)(2,1)}, bf16[3,208,448]{2,1,0:T(8,128)(2,1)S(1)}) custom-call(s32[8]{0:T(128)S(1)} %stack.79.order, bf16[8,208,448]{2,1,0:T(8,128)(2,1)} %bitcast.26), custom_call_target="tpu_custom_call" | custom-call | flops 1150000000 | bytes 1000 | tf_op jit(solution)/shard_map/attended_chunks/pallas_call | solution.py:116
  30.7 0.9 copy-done.12
  31.6 1.5 %collective-permute-done.4.refs_1_ = bf16[8,208,448]{2,1,0:T(8,128)(2,1)} collective-permute-done((bf16[8,208,448]{2,1,0:T(8,128)(2,1)}, bf16[8,208,448]{2,1,0:T(8,128)(2,1)}, u32[]{:S(2)}, u32[]{:S(2)}) %collective-permute-start.4) | collective-permute-done | bytes 1490976 | tf_op jit(solution)/shard_map/ppermute | solution.py:496
  33.3 7.7 %projection_chip.1 = (bf16[208,896]{1,0:T(8,128)(2,1)}, bf16[208,896]{1,0:T(8,128)(2,1)}, bf16[208,896]{1,0:T(8,128)(2,1)}, bf16[208,896]{1,0:T(8,128)(2,1)}, bf...) custom-call(s32[8]{0:T(128)S(1)} %stack.79.order, ...), custom_call_target="tpu_custom_call" | custom-call | flops 3449999872 | bytes 1000 | tf_op jit(solution)/shard_map/projection_chip/pallas_call | solution.py:449
  41.0 2.1 %collective-permute-done.6.refs_3_ = bf16[208,1664]{1,0:T(8,128)(2,1)} collective-permute-done((bf16[208,1664]{1,0:T(8,128)(2,1)}, bf16[208,1664]{1,0:T(8,128)(2,1)}, u32[]{:S(2)}, u32[]{:S(2)}) %collective-permute-start.6) | collective-permute-done | bytes 692256 | tf_op jit(solution)/shard_map/ppermute | solution.py:549
  43.1 1.5 %collective-permute-done.7.refs_4_ = bf16[208,1664]{1,0:T(8,128)(2,1)} collective-permute-done((bf16[208,1664]{1,0:T(8,128)(2,1)}, bf16[208,1664]{1,0:T(8,128)(2,1)}, u32[]{:S(2)}, u32[]{:S(2)}) %collective-permute-start.7) | collective-permute-done | bytes 692256 | tf_op jit(solution)/shard_map/ppermute | solution.py:550
  44.6 1.6 %collective-permute-start.9 = (bf16[208,1664]{1,0:T(8,128)(2,1)}, bf16[208,1664]{1,0:T(8,128)(2,1)}, u32[]{:S(2)}, u32[]{:S(2)}) collective-permute-start(bf16[208,1664]{1,0:T(8,128)(2,1)} %collective-permute-done.6.refs_3_), channel_id=1, source_target_pairs={{0,2},{2,4},{4,6},{6,7},{7,5},{5,3},{3,1},{1,0},{8,10},{10,12},{12... | collective-permute-start | bytes 2076680 | tf_op jit(solution)/shard_map/ppermute | solution.py:572
  46.7 2.1 %collective-permute-done.refs_3_ = bf16[288,1664]{1,0:T(8,128)(2,1)} collective-permute-done((bf16[288,1664]{1,0:T(8,128)(2,1)}, bf16[288,1664]{1,0:T(8,128)(2,1)}, u32[]{:S(2)}, u32[]{:S(2)}) %collective-permute-start) | collective-permute-done | bytes 958496 | tf_op jit(solution)/shard_map/ppermute | solution.py:496
  49.7 1.1 copy-done.7
  50.8 1.1 copy-done.9
  51.9 1.1 copy-done.11
  53.0 8.1 %grad_out_rows.2 = (f32[8,208,448]{2,1,0:T(8,128)}, bf16[8,208,448]{2,1,0:T(8,128)(2,1)}) custom-call(s32[6]{0:T(128)S(1)} %stack.82.info, bf16[3200,512]{1,0:T(8,128)(2,1)} %scaled_cotangent.1.refs_2_.turned, bf16[3200,512]{1,0:T(8,128)(2,1)S(1)} %collective-permute-done.8.refs_3_.turned_other, bf16[208,1664]{1,0:T(8,128)(2,1)S(1)} %copy-done.7, ...), custom_call_target="tpu_custom_call" | custom-call | flops 4312500224 | bytes 1000 | tf_op jit(solution)/shard_map/grad_out_rows/pallas_call | solution.py:324
  61.1 1.1 collective-permute-done.10.down.refs_1_
  62.2 1.9 %far_parts.1 = (bf16[112,1664]{1,0:T(8,128)(2,1)}, bf16[96,1664]{1,0:T(8,128)(2,1)}) custom-call(bf16[208,1664]{1,0:T(8,128)(2,1)} %collective-permute-done.9.up.refs_0_, bf16[208,1664]{1,0:T(8,128)(2,1)} %collective-permute-done.10.down.refs_1_), custom_call_target="tpu_custom_call" | custom-call | flops 575000000 | bytes 1000 | tf_op jit(solution)/shard_map/far_parts/pallas_call | solution.py:147
  64.6 1.2 collective-permute-start.14
  65.8 1.6 %collective-permute-start.15 = (bf16[112,1664]{1,0:T(8,128)(2,1)}, bf16[112,1664]{1,0:T(8,128)(2,1)}, u32[]{:S(2)}, u32[]{:S(2)}) collective-permute-start(bf16[112,1664]{1,0:T(8,128)(2,1)} %get-tuple-element.162.refs_6_), channel_id=1, source_target_pairs={{0,2},{2,4},{4,6},{6,7},{7,5},{5,3},{3,1},{1,0},{8,10},{10,12},{12... | collective-permute-start | bytes 1118216 | tf_op jit(solution)/shard_map/ppermute | solution.py:580
  68.8 1.0 copy-done.17
  69.8 1.0 copy-done.21
  70.8 5.0 %projection_peers.3 = (f32[208,896]{1,0:T(8,128)S(1)}, f32[208,896]{1,0:T(8,128)S(1)}, f32[208,896]{1,0:T(8,128)S(1)}) custom-call(s32[3]{0:T(128)S(1)} %pad_add_fusion.1.order, s32[1]{0:T(128)} %bitcast.3.start, bf16[3,208,448]{2,1,0:T(8,128)(2,1)} %collective-permute-done.5.refs_0_, bf16[3,208,448]{2,1,0:T(8,128)(2,1)} %collective-permute-done.11.refs_1_, ...), custom_call_target="tpu_custom_call" | custom-call | flops 1724999936 | bytes 1000 | tf_op jit(solution)/shard_map/projection_peers/pallas_call | solution.py:449
  75.9 1.2 collective-permute-done.14.refs_0_
  77.9 1.5 %collective-permute-start.17 = (bf16[112,896]{1,0:T(8,128)(2,1)S(1)}, bf16[112,896]{1,0:T(8,128)(2,1)S(1)}, u32[]{:S(2)}, u32[]{:S(2)}) collective-permute-start(bf16[112,896]{1,0:T(8,128)(2,1)S(1)} %slice.14), channel_id=1, source_target_pairs={{0,2},{2,4},{4,6},{6,7},{7,5},{5,3},{3,1},{1,0},{8,10},{10,12},{12... | collective-permute-start | bytes 602120 | tf_op jit(solution)/shard_map/ppermute | solution.py:600
  80.0 0.8 collective-permute-start.22
  80.8 4.2 %projection_peers.4 = (f32[208,896]{1,0:T(8,128)S(1)}, f32[208,896]{1,0:T(8,128)S(1)}) custom-call(s32[2]{0:T(128)S(1)} %pad_add_fusion.2.order, s32[1]{0:T(128)} %bitcast.3.start, bf16[2,208,448]{2,1,0:T(8,128)(2,1)} %collective-permute-done.14.refs_0_, bf16[2,208,448]{2,1,0:T(8,128)(2,1)S(1)} %collective-permute-done.19.refs_1_, ...), custom_call_target="tpu_custom_call" | custom-call | flops 1724999936 | bytes 1000 | tf_op jit(solution)/shard_map/projection_peers/pallas_call | solution.py:449
  85.0 0.9 collective-permute-done.18
  86.0 1.0 collective-permute-start.20
  87.1 1.0 collective-permute-start.21
  88.2 6.0 %grad_out_rows.3 = (f32[8,208,448]{2,1,0:T(8,128)}, bf16[8,208,448]{2,1,0:T(8,128)(2,1)}) custom-call(s32[4]{0:T(128)S(1)} %pad_add_fusion.3.info, bf16[3200,512]{1,0:T(8,128)(2,1)} %scaled_cotangent.1.refs_2_.turned, bf16[3200,512]{1,0:T(8,128)(2,1)S(1)} %collective-permute-done.8.refs_3_.turned_other, ...), custom_call_target="tpu_custom_call", output_to_operand_aliasing={{0}: (7, {}), {1}: (8, {})} | custom-call | flops 115000000 | bytes 1000 | tf_op jit(solution)/shard_map/grad_out_rows/pallas_call | solution.py:324
  94.2 2.1 %collective-permute-done.22.refs_0_ = bf16[3,208,448]{2,1,0:T(8,128)(2,1)} collective-permute-done((bf16[3,208,448]{2,1,0:T(8,128)(2,1)S(1)}, bf16[3,208,448]{2,1,0:T(8,128)(2,1)}, u32[]{:S(2)}, u32[]{:S(2)}) %collective-permute-start.22) | collective-permute-done | bytes 559136 | tf_op jit(solution)/shard_map/ppermute | solution.py:496
  97.1 0.8 add_convert_fusion.2
  98.5 1.5 %collective-permute-start.24 = (bf16[208,896]{1,0:T(8,128)(2,1)}, bf16[208,896]{1,0:T(8,128)(2,1)}, u32[]{:S(2)}, u32[]{:S(2)}) collective-permute-start(bf16[208,896]{1,0:T(8,128)(2,1)} %add_convert_fusion.3), channel_id=1, source_target_pairs={{0,2},{2,4},{4,6},{6,7},{7,5},{5,3},{3,1},{1,0},{8,10},{10,12},{12... | collective-permute-start | bytes 1118216 | tf_op jit(solution)/shard_map/ppermute | solution.py:625
  101.9 1.8 %copy-done.15 = bf16[3,208,448]{2,1,0:T(8,128)(2,1)S(1)} copy-done((bf16[3,208,448]{2,1,0:T(8,128)(2,1)S(1)}, bf16[3,208,448]{2,1,0:T(8,128)(2,1)}, u32[]{:S(2)}) %copy-start.15) | copy-done | bytes 559128
  103.7 1.0 copy-done.19
  104.8 1.0 copy-done.23
  105.8 4.8 %projection_peers.5 = (f32[208,896]{1,0:T(8,128)S(1)}, f32[208,896]{1,0:T(8,128)S(1)}, f32[208,896]{1,0:T(8,128)S(1)}) custom-call(s32[3]{0:T(128)S(1)} %pad_add_fusion.order, s32[1]{0:T(128)} %bitcast.3.start, bf16[3,208,448]{2,1,0:T(8,128)(2,1)} %collective-permute-done.22.refs_0_, bf16[3,208,448]{2,1,0:T(8,128)(2,1)S(1)} %copy-done.15, ...), custom_call_target="tpu_custom_call" | custom-call | flops 1724999936 | bytes 1000 | tf_op jit(solution)/shard_map/projection_peers/pallas_call | solution.py:449
  110.6 1.1 add_convert_fusion.1
  111.8 1.4 %collective-permute-start.26 = (bf16[208,896]{1,0:T(8,128)(2,1)S(1)}, bf16[208,896]{1,0:T(8,128)(2,1)S(1)}, u32[]{:S(2)}, u32[]{:S(2)}) collective-permute-start(bf16[208,896]{1,0:T(8,128)(2,1)S(1)} %add_convert_fusion.1), channel_id=1, source_target_pairs={{0,2},{2,4},{4,6},{6,7},{7,5},{5,3},{3,1},{1,0},{8,10},{10,12},{12... | collective-permute-start | bytes 1118216 | tf_op jit(solution)/shard_map/ppermute | solution.py:625
  113.9 2.3 %copy-done.3 = bf16[3,448,1664]{2,1,0:T(8,128)(2,1)S(1)} copy-done((bf16[3,448,1664]{2,1,0:T(8,128)(2,1)S(1)}, bf16[3,448,1664]{2,1,0:T(8,128)(2,1)}, u32[]{:S(2)}) %copy-start.3) | copy-done | bytes 4472856
  116.1 3.4 %attention_backward.3.rest_0_ = bf16[3,448,1664]{2,1,0:T(8,128)(2,1)} custom-call(bf16[3,448,1664]{2,1,0:T(8,128)(2,1)S(1)} %copy-done.3, f32[1664,448]{1,0:T(8,128)S(1)} %bitcast.19, bf16[1664,448]{1,0:T(8,128)(2,1)S(1)} %bitcast.22, f32[13,256,256]{2,1,0:T(8,128)S(1)} %copy-done.4, f32[13,192,192]{2,1,0:T(8,128)S(1)} %copy-done.5), custom_call_target="tpu_custom_call" | custom-call | flops 3449999872 | bytes 1000 | tf_op jit(solution)/shard_map/attention_backward/pallas_call | solution.py:256
  119.5 2.5 %attention_backward.4.rest_0_ = bf16[3,448,1664]{2,1,0:T(8,128)(2,1)} custom-call(bf16[3,448,1664]{2,1,0:T(8,128)(2,1)S(1)} %copy-done.3, f32[1664,448]{1,0:T(8,128)S(1)} %bitcast.20, bf16[1664,448]{1,0:T(8,128)(2,1)S(1)} %bitcast.23, f32[13,256,256]{2,1,0:T(8,128)S(1)} %copy-done.4, f32[13,192,192]{2,1,0:T(8,128)S(1)} %copy-done.5, ...), custom_call_target="tpu_custom_call", output_to_operand_aliasing={{}: (5, {})} | custom-call | flops 2300000000 | bytes 1000 | tf_op jit(solution)/shard_map/attention_backward/pallas_call | solution.py:256
  122.0 2.4 %attention_backward.5 = bf16[3,448,1664]{2,1,0:T(8,128)(2,1)} custom-call(bf16[3,448,1664]{2,1,0:T(8,128)(2,1)S(1)} %copy-done.3, f32[1664,448]{1,0:T(8,128)S(1)} %bitcast.21, bf16[1664,448]{1,0:T(8,128)(2,1)S(1)} %bitcast.24, f32[13,256,256]{2,1,0:T(8,128)S(1)} %copy-done.4, f32[13,192,192]{2,1,0:T(8,128)S(1)} %copy-done.5, ...), custom_call_target="tpu_custom_call", output_to_operand_aliasing={{}: (5, {})} | custom-call | flops 2300000000 | bytes 1000 | tf_op jit(solution)/shard_map/attention_backward/pallas_call | solution.py:256
  124.4 1.1 last_sum.1
  (90 shorter events, 11.7 us)
Async XLA Ops:
  0.6 15.6 %copy-start = (s32[4,1,4]{2,1,0:T(1,128)S(1)}, s32[4,1,4]{2,1,0:T(1,128)}, u32[]{:S(2)}) copy-start(s32[4,1,4]{2,1,0:T(1,128)} %param.9) | copy-start | bytes 196
  1.8 6.4 %copy-start.6 = (bf16[208,1664]{1,0:T(8,128)(2,1)}, bf16[208,1664]{1,0:T(8,128)(2,1)S(1)}, u32[]{:S(2)}) copy-start(bf16[208,1664]{1,0:T(8,128)(2,1)S(1)} %own_half_of_weight.1.refs_0_) | copy-start | bytes 2076676
  1.8 21.8 %collective-permute-start.1 = (bf16[208,1664]{1,0:T(8,128)(2,1)S(1)}, bf16[208,1664]{1,0:T(8,128)(2,1)S(1)}, u32[]{:S(2)}, u32[]{:S(2)}) collective-permute-start(bf16[208,1664]{1,0:T(8,128)(2,1)S(1)} %own_half_of_weight.1.refs_0_), channel_id=1, source_target_pairs={{0,2},{2,4},{4,6},{6,7},{7,5},{5,3},{3,1},{1,0},{8,10},{10,12},{12... | collective-permute-start | bytes 2076680 | tf_op jit(solution)/shard_map/ppermute | solution.py:517
  4.9 18.7 %collective-permute-start.2 = (bf16[208,1664]{1,0:T(8,128)(2,1)S(1)}, bf16[208,1664]{1,0:T(8,128)(2,1)S(1)}, u32[]{:S(2)}, u32[]{:S(2)}) collective-permute-start(bf16[208,1664]{1,0:T(8,128)(2,1)S(1)} %own_half_of_weight.1.refs_0_), channel_id=1, source_target_pairs={{0,1},{2,0},{4,2},{6,4},{7,6},{5,7},{3,5},{1,3},{8,9},{10,8},{12,1... | collective-permute-start | bytes 2076680 | tf_op jit(solution)/shard_map/ppermute | solution.py:518
  8.2 15.4 %collective-permute-start.3 = (bf16[160,1664]{1,0:T(8,128)(2,1)}, bf16[160,1664]{1,0:T(8,128)(2,1)S(1)}, u32[]{:S(2)}, u32[]{:S(2)}) collective-permute-start(bf16[160,1664]{1,0:T(8,128)(2,1)} %get-tuple-element.98), channel_id=1, source_target_pairs={{0,16},{8,24},{16,0},{24,8},{1,17},{9,25},{17,1},{25,9},{2,18},{10... | collective-permute-start | bytes 1597448 | tf_op jit(solution)/shard_map/ppermute | solution.py:496
  10.2 6.0 %copy-start.2 = (bf16[3,448,1664]{2,1,0:T(8,128)(2,1)S(1)}, bf16[3,448,1664]{2,1,0:T(8,128)(2,1)}, u32[]{:S(2)}) copy-start(bf16[3,448,1664]{2,1,0:T(8,128)(2,1)} %qkv.7) | copy-start | bytes 13418500
  23.6 1.3 %copy-start.10 = (bf16[208,1664]{1,0:T(8,128)(2,1)}, bf16[208,1664]{1,0:T(8,128)(2,1)S(1)}, u32[]{:S(2)}) copy-start(bf16[208,1664]{1,0:T(8,128)(2,1)S(1)} %collective-permute-done.2.refs_2_) | copy-start | bytes 2076676
  24.8 8.5 %collective-permute-start.8 = (bf16[3200,512]{1,0:T(8,128)(2,1)}, bf16[3200,512]{1,0:T(8,128)(2,1)S(1)}, u32[]{:S(2)}, u32[]{:S(2)}) collective-permute-start(bf16[3200,512]{1,0:T(8,128)(2,1)} %scaled_cotangent.1.refs_2_.turned), channel_id=1, source_target_pairs={{0,8},{8,0},{16,24},{24,16},{1,9},{9,1},{17,25},{25,17},{2,10},{10... | collective-permute-start | bytes 9830408 | tf_op jit(solution)/shard_map/ppermute | solution.py:496
  24.8 8.3 %collective-permute-start.4 = (bf16[8,208,448]{2,1,0:T(8,128)(2,1)}, bf16[8,208,448]{2,1,0:T(8,128)(2,1)}, u32[]{:S(2)}, u32[]{:S(2)}) collective-permute-start(bf16[8,208,448]{2,1,0:T(8,128)(2,1)} %bitcast.25), channel_id=1, source_target_pairs={{0,8},{8,0},{16,24},{24,16},{1,9},{9,1},{17,25},{25,17},{2,10},{10... | collective-permute-start | bytes 4472840 | tf_op jit(solution)/shard_map/ppermute | solution.py:496
  25.4 23.5 %collective-permute-start = (bf16[288,1664]{1,0:T(8,128)(2,1)}, bf16[288,1664]{1,0:T(8,128)(2,1)}, u32[]{:S(2)}, u32[]{:S(2)}) collective-permute-start(bf16[288,1664]{1,0:T(8,128)(2,1)} %get-tuple-element.96), channel_id=1, source_target_pairs={{0,16},{8,24},{16,0},{24,8},{1,17},{9,25},{17,1},{25,9},{2,18},{10... | collective-permute-start | bytes 2875400 | tf_op jit(solution)/shard_map/ppermute | solution.py:496
  25.5 17.7 %collective-permute-start.6 = (bf16[208,1664]{1,0:T(8,128)(2,1)}, bf16[208,1664]{1,0:T(8,128)(2,1)}, u32[]{:S(2)}, u32[]{:S(2)}) collective-permute-start(bf16[208,1664]{1,0:T(8,128)(2,1)} %copy-done.8), channel_id=1, source_target_pairs={{0,2},{2,4},{4,6},{6,7},{7,5},{5,3},{3,1},{1,0},{8,10},{10,12},{12... | collective-permute-start | bytes 2076680 | tf_op jit(solution)/shard_map/ppermute | solution.py:549
  27.5 17.2 %collective-permute-start.7 = (bf16[208,1664]{1,0:T(8,128)(2,1)}, bf16[208,1664]{1,0:T(8,128)(2,1)}, u32[]{:S(2)}, u32[]{:S(2)}) collective-permute-start(bf16[208,1664]{1,0:T(8,128)(2,1)} %copy-done.10), channel_id=1, source_target_pairs={{0,1},{2,0},{4,2},{6,4},{7,6},{5,7},{3,5},{1,3},{8,9},{10,8},{12,1... | collective-permute-start | bytes 2076680 | tf_op jit(solution)/shard_map/ppermute | solution.py:550
  44.6 16.5 %collective-permute-start.9 = (bf16[208,1664]{1,0:T(8,128)(2,1)}, bf16[208,1664]{1,0:T(8,128)(2,1)}, u32[]{:S(2)}, u32[]{:S(2)}) collective-permute-start(bf16[208,1664]{1,0:T(8,128)(2,1)} %collective-permute-done.6.refs_3_), channel_id=1, source_target_pairs={{0,2},{2,4},{4,6},{6,7},{7,5},{5,3},{3,1},{1,0},{8,10},{10,12},{12... | collective-permute-start | bytes 2076680 | tf_op jit(solution)/shard_map/ppermute | solution.py:572
  46.2 16.0 %collective-permute-start.10 = (bf16[208,1664]{1,0:T(8,128)(2,1)}, bf16[208,1664]{1,0:T(8,128)(2,1)}, u32[]{:S(2)}, u32[]{:S(2)}) collective-permute-start(bf16[208,1664]{1,0:T(8,128)(2,1)} %collective-permute-done.7.refs_4_), channel_id=1, source_target_pairs={{0,1},{2,0},{4,2},{6,4},{7,6},{5,7},{3,5},{1,3},{8,9},{10,8},{12,1... | collective-permute-start | bytes 2076680 | tf_op jit(solution)/shard_map/ppermute | solution.py:573
  48.8 15.8 %collective-permute-start.5 = (bf16[3,208,448]{2,1,0:T(8,128)(2,1)}, bf16[3,208,448]{2,1,0:T(8,128)(2,1)}, u32[]{:S(2)}, u32[]{:S(2)}) collective-permute-start(bf16[3,208,448]{2,1,0:T(8,128)(2,1)} %get-tuple-element.107), channel_id=1, source_target_pairs={{0,16},{8,24},{16,0},{24,8},{1,17},{9,25},{17,1},{25,9},{2,18},{10... | collective-permute-start | bytes 1677320 | tf_op jit(solution)/shard_map/ppermute | solution.py:496
  49.2 18.2 %collective-permute-start.12 = (bf16[160,1664]{1,0:T(8,128)(2,1)}, bf16[160,1664]{1,0:T(8,128)(2,1)S(1)}, u32[]{:S(2)}, u32[]{:S(2)}) collective-permute-start(bf16[160,1664]{1,0:T(8,128)(2,1)} %copy-done.16), channel_id=1, source_target_pairs={{0,8},{8,0},{16,24},{24,16},{1,9},{9,1},{17,25},{25,17},{2,10},{10... | collective-permute-start | bytes 1597448 | tf_op jit(solution)/shard_map/ppermute | solution.py:496
  49.2 19.6 %collective-permute-start.13 = (bf16[288,1664]{1,0:T(8,128)(2,1)}, bf16[288,1664]{1,0:T(8,128)(2,1)}, u32[]{:S(2)}, u32[]{:S(2)}) collective-permute-start(bf16[288,1664]{1,0:T(8,128)(2,1)} %collective-permute-done.refs_3_), channel_id=1, source_target_pairs={{0,8},{8,0},{16,24},{24,16},{1,9},{9,1},{17,25},{25,17},{2,10},{10... | collective-permute-start | bytes 2875400 | tf_op jit(solution)/shard_map/ppermute | solution.py:496
  49.7 1.1 copy-start.7
  50.8 1.1 copy-start.9
  51.9 1.1 copy-start.11
  64.6 4.2 %collective-permute-start.11 = (bf16[3,208,448]{2,1,0:T(8,128)(2,1)}, bf16[3,208,448]{2,1,0:T(8,128)(2,1)}, u32[]{:S(2)}, u32[]{:S(2)}) collective-permute-start(bf16[3,208,448]{2,1,0:T(8,128)(2,1)} %collective-permute-done.5.refs_0_), channel_id=1, source_target_pairs={{0,8},{8,0},{16,24},{24,16},{1,9},{9,1},{17,25},{25,17},{2,10},{10... | collective-permute-start | bytes 1677320 | tf_op jit(solution)/shard_map/ppermute | solution.py:496
  64.6 12.5 %collective-permute-start.14 = (bf16[2,208,448]{2,1,0:T(8,128)(2,1)}, bf16[2,208,448]{2,1,0:T(8,128)(2,1)}, u32[]{:S(2)}, u32[]{:S(2)}) collective-permute-start(bf16[2,208,448]{2,1,0:T(8,128)(2,1)} %get-tuple-element.136), channel_id=1, source_target_pairs={{0,16},{8,24},{16,0},{24,8},{1,17},{9,25},{17,1},{25,9},{2,18},{10... | collective-permute-start | bytes 1118216 | tf_op jit(solution)/shard_map/ppermute | solution.py:496
  65.8 12.1 %collective-permute-start.15 = (bf16[112,1664]{1,0:T(8,128)(2,1)}, bf16[112,1664]{1,0:T(8,128)(2,1)}, u32[]{:S(2)}, u32[]{:S(2)}) collective-permute-start(bf16[112,1664]{1,0:T(8,128)(2,1)} %get-tuple-element.162.refs_6_), channel_id=1, source_target_pairs={{0,2},{2,4},{4,6},{6,7},{7,5},{5,3},{3,1},{1,0},{8,10},{10,12},{12... | collective-permute-start | bytes 1118216 | tf_op jit(solution)/shard_map/ppermute | solution.py:580
  68.2 9.6 %collective-permute-start.16 = (bf16[96,1664]{1,0:T(8,128)(2,1)}, bf16[96,1664]{1,0:T(8,128)(2,1)}, u32[]{:S(2)}, u32[]{:S(2)}) collective-permute-start(bf16[96,1664]{1,0:T(8,128)(2,1)} %get-tuple-element.138), channel_id=1, source_target_pairs={{0,1},{2,0},{4,2},{6,4},{7,6},{5,7},{3,5},{1,3},{8,9},{10,8},{12,1... | collective-permute-start | bytes 958472 | tf_op jit(solution)/shard_map/ppermute | solution.py:581
  68.7 1.0 copy-start.17
  69.8 1.0 copy-start.21
  70.8 9.1 %copy-start.13 = (bf16[3,208,448]{2,1,0:T(8,128)(2,1)S(1)}, bf16[3,208,448]{2,1,0:T(8,128)(2,1)}, u32[]{:S(2)}) copy-start(bf16[3,208,448]{2,1,0:T(8,128)(2,1)} %copy-done.12) | copy-start | bytes 1677316
  70.8 10.0 %copy-start.18 = (bf16[160,1664]{1,0:T(8,128)(2,1)S(1)}, bf16[160,1664]{1,0:T(8,128)(2,1)}, u32[]{:S(2)}) copy-start(bf16[160,1664]{1,0:T(8,128)(2,1)} %copy-done.16) | copy-start | bytes 1597444
  70.8 10.0 %copy-start.22 = (bf16[160,1664]{1,0:T(8,128)(2,1)S(1)}, bf16[160,1664]{1,0:T(8,128)(2,1)}, u32[]{:S(2)}) copy-start(bf16[160,1664]{1,0:T(8,128)(2,1)} %copy-done.20) | copy-start | bytes 1597444
  77.9 3.0 %collective-permute-start.19 = (bf16[2,208,448]{2,1,0:T(8,128)(2,1)}, bf16[2,208,448]{2,1,0:T(8,128)(2,1)S(1)}, u32[]{:S(2)}, u32[]{:S(2)}) collective-permute-start(bf16[2,208,448]{2,1,0:T(8,128)(2,1)} %collective-permute-done.14.refs_0_), channel_id=1, source_target_pairs={{0,8},{8,0},{16,24},{24,16},{1,9},{9,1},{17,25},{25,17},{2,10},{10... | collective-permute-start | bytes 1118216 | tf_op jit(solution)/shard_map/ppermute | solution.py:496
  77.9 8.0 %collective-permute-start.17 = (bf16[112,896]{1,0:T(8,128)(2,1)S(1)}, bf16[112,896]{1,0:T(8,128)(2,1)S(1)}, u32[]{:S(2)}, u32[]{:S(2)}) collective-permute-start(bf16[112,896]{1,0:T(8,128)(2,1)S(1)} %slice.14), channel_id=1, source_target_pairs={{0,2},{2,4},{4,6},{6,7},{7,5},{5,3},{3,1},{1,0},{8,10},{10,12},{12... | collective-permute-start | bytes 602120 | tf_op jit(solution)/shard_map/ppermute | solution.py:600
  79.4 6.5 %collective-permute-start.18 = (bf16[96,896]{1,0:T(8,128)(2,1)S(1)}, bf16[96,896]{1,0:T(8,128)(2,1)S(1)}, u32[]{:S(2)}, u32[]{:S(2)}) collective-permute-start(bf16[96,896]{1,0:T(8,128)(2,1)S(1)} %slice.15), channel_id=1, source_target_pairs={{0,1},{2,0},{4,2},{6,4},{7,6},{5,7},{3,5},{1,3},{8,9},{10,8},{12,1... | collective-permute-start | bytes 516104 | tf_op jit(solution)/shard_map/ppermute | solution.py:601
  80.0 16.3 %collective-permute-start.22 = (bf16[3,208,448]{2,1,0:T(8,128)(2,1)S(1)}, bf16[3,208,448]{2,1,0:T(8,128)(2,1)}, u32[]{:S(2)}, u32[]{:S(2)}) collective-permute-start(bf16[3,208,448]{2,1,0:T(8,128)(2,1)S(1)} %copy-done.13), channel_id=1, source_target_pairs={{0,16},{8,24},{16,0},{24,8},{1,17},{9,25},{17,1},{25,9},{2,18},{10... | collective-permute-start | bytes 1677320 | tf_op jit(solution)/shard_map/ppermute | solution.py:496
  86.0 10.3 %collective-permute-start.20 = (bf16[208,896]{1,0:T(8,128)(2,1)S(1)}, bf16[208,896]{1,0:T(8,128)(2,1)S(1)}, u32[]{:S(2)}, u32[]{:S(2)}) collective-permute-start(bf16[208,896]{1,0:T(8,128)(2,1)S(1)} %get-tuple-element.152), channel_id=1, source_target_pairs={{0,2},{2,4},{4,6},{6,7},{7,5},{5,3},{3,1},{1,0},{8,10},{10,12},{12... | collective-permute-start | bytes 1118216 | tf_op jit(solution)/shard_map/ppermute | solution.py:625
  87.1 10.1 %collective-permute-start.21 = (bf16[208,896]{1,0:T(8,128)(2,1)S(1)}, bf16[208,896]{1,0:T(8,128)(2,1)S(1)}, u32[]{:S(2)}, u32[]{:S(2)}) collective-permute-start(bf16[208,896]{1,0:T(8,128)(2,1)S(1)} %get-tuple-element.154), channel_id=1, source_target_pairs={{0,1},{2,0},{4,2},{6,4},{7,6},{5,7},{3,5},{1,3},{8,9},{10,8},{12,1... | collective-permute-start | bytes 1118216 | tf_op jit(solution)/shard_map/ppermute | solution.py:626
  96.3 17.5 %collective-permute-start.28 = (bf16[8,208,448]{2,1,0:T(8,128)(2,1)}, bf16[8,208,448]{2,1,0:T(8,128)(2,1)S(1)}, u32[]{:S(2)}, u32[]{:S(2)}) collective-permute-start(bf16[8,208,448]{2,1,0:T(8,128)(2,1)} %get-tuple-element.177), channel_id=1, source_target_pairs={{0,8},{8,0},{16,24},{24,16},{1,9},{9,1},{17,25},{25,17},{2,10},{10... | collective-permute-start | bytes 4472840 | tf_op jit(solution)/shard_map/ppermute | solution.py:496
  98.0 3.1 %collective-permute-start.23 = (bf16[3,208,448]{2,1,0:T(8,128)(2,1)}, bf16[3,208,448]{2,1,0:T(8,128)(2,1)S(1)}, u32[]{:S(2)}, u32[]{:S(2)}) collective-permute-start(bf16[3,208,448]{2,1,0:T(8,128)(2,1)} %collective-permute-done.22.refs_0_), channel_id=1, source_target_pairs={{0,8},{8,0},{16,24},{24,16},{1,9},{9,1},{17,25},{25,17},{2,10},{10... | collective-permute-start | bytes 1677320 | tf_op jit(solution)/shard_map/ppermute | solution.py:496
  98.5 12.1 %collective-permute-start.24 = (bf16[208,896]{1,0:T(8,128)(2,1)}, bf16[208,896]{1,0:T(8,128)(2,1)}, u32[]{:S(2)}, u32[]{:S(2)}) collective-permute-start(bf16[208,896]{1,0:T(8,128)(2,1)} %add_convert_fusion.3), channel_id=1, source_target_pairs={{0,2},{2,4},{4,6},{6,7},{7,5},{5,3},{3,1},{1,0},{8,10},{10,12},{12... | collective-permute-start | bytes 1118216 | tf_op jit(solution)/shard_map/ppermute | solution.py:625
  100.1 13.8 %copy-start.1 = (f32[8,208,448]{2,1,0:T(8,128)S(1)}, f32[8,208,448]{2,1,0:T(8,128)}, u32[]{:S(2)}) copy-start(f32[8,208,448]{2,1,0:T(8,128)} %get-tuple-element.165) | copy-start | bytes 8945668
  100.1 13.8 %copy-start.4 = (f32[13,256,256]{2,1,0:T(8,128)S(1)}, f32[13,256,256]{2,1,0:T(8,128)}, u32[]{:S(2)}) copy-start(f32[13,256,256]{2,1,0:T(8,128)} %get-tuple-element.178.main_probs) | copy-start | bytes 10223620
  100.1 13.8 %copy-start.5 = (f32[13,192,192]{2,1,0:T(8,128)S(1)}, f32[13,192,192]{2,1,0:T(8,128)}, u32[]{:S(2)}) copy-start(f32[13,192,192]{2,1,0:T(8,128)} %get-tuple-element.179.slot_probs) | copy-start | bytes 5750788
  100.1 11.6 %collective-permute-start.25 = (bf16[208,896]{1,0:T(8,128)(2,1)}, bf16[208,896]{1,0:T(8,128)(2,1)S(1)}, u32[]{:S(2)}, u32[]{:S(2)}) collective-permute-start(bf16[208,896]{1,0:T(8,128)(2,1)} %add_convert_fusion.2), channel_id=1, source_target_pairs={{0,1},{2,0},{4,2},{6,4},{7,6},{5,7},{3,5},{1,3},{8,9},{10,8},{12,1... | collective-permute-start | bytes 1118216 | tf_op jit(solution)/shard_map/ppermute | solution.py:626
  101.9 1.8 %copy-start.15 = (bf16[3,208,448]{2,1,0:T(8,128)(2,1)S(1)}, bf16[3,208,448]{2,1,0:T(8,128)(2,1)}, u32[]{:S(2)}) copy-start(bf16[3,208,448]{2,1,0:T(8,128)(2,1)} %copy-done.14) | copy-start | bytes 1677316
  103.7 1.0 copy-start.19
  104.8 1.0 copy-start.23
  111.8 12.7 %collective-permute-start.26 = (bf16[208,896]{1,0:T(8,128)(2,1)S(1)}, bf16[208,896]{1,0:T(8,128)(2,1)S(1)}, u32[]{:S(2)}, u32[]{:S(2)}) collective-permute-start(bf16[208,896]{1,0:T(8,128)(2,1)S(1)} %add_convert_fusion.1), channel_id=1, source_target_pairs={{0,2},{2,4},{4,6},{6,7},{7,5},{5,3},{3,1},{1,0},{8,10},{10,12},{12... | collective-permute-start | bytes 1118216 | tf_op jit(solution)/shard_map/ppermute | solution.py:625
  113.2 11.2 %collective-permute-start.27 = (bf16[208,896]{1,0:T(8,128)(2,1)S(1)}, bf16[208,896]{1,0:T(8,128)(2,1)S(1)}, u32[]{:S(2)}, u32[]{:S(2)}) collective-permute-start(bf16[208,896]{1,0:T(8,128)(2,1)S(1)} %add_convert_fusion), channel_id=1, source_target_pairs={{0,1},{2,0},{4,2},{6,4},{7,6},{5,7},{3,5},{1,3},{8,9},{10,8},{12,1... | collective-permute-start | bytes 1118216 | tf_op jit(solution)/shard_map/ppermute | solution.py:626
  113.9 2.3 %copy-start.3 = (bf16[3,448,1664]{2,1,0:T(8,128)(2,1)S(1)}, bf16[3,448,1664]{2,1,0:T(8,128)(2,1)}, u32[]{:S(2)}) copy-start(bf16[3,448,1664]{2,1,0:T(8,128)(2,1)} %qkv.7) | copy-start | bytes 13418500
  (5 other events, 4.4 us)

commit v7 on v6

--- a/solution.py
+++ b/solution.py
@@ -564,10 +564,11 @@
     columns = []
     for k in range(peers - 1):
         for arrays in (came_columns, other_columns):
-            columns += [part[k] for part in arrays]
+            columns += [in_hbm(part[k]) for part in arrays]
     pieces = [([mine], 0)]
     for step in range(1, half - 1):
         pieces += [([up[step]], -step), ([down[step]], step)]
+    pieces[:-2] = [([in_hbm(array) for array in arrays], o) for arrays, o in pieces[:-2]]
     grad_out = rows_of(pieces, None)
     up.append(lax.ppermute(up[-1], "fsdp", ahead))
     down.append(lax.ppermute(down[-1], "fsdp", behind))
@@ -619,7 +620,7 @@
         elif step > 2:
             arrived = came[half - step + 1]
             going_up, going_down, arrived, grad_mine = lax.optimization_barrier((going_up, going_down, arrived, grad_mine))
-            terms.update(products(half - step + 1, both_cores(arrived)))
+            terms.update(products(half - step + 1, [in_hbm(array) for array in both_cores(arrived)]))
         else:
             going_up, going_down = lax.optimization_barrier((going_up, going_down))
         came_up = lax.ppermute(going_up, "fsdp", ahead)

time: 127 us -> 123 us (0.969)
  local copies, waits for them, and re-layouts: 16.3 us -> 4.91 us
  waiting for transfers between devices: 14.4 us -> 24.3 us
  other arithmetic: 3.26 us -> 0.77 us
    unnamed x48 -> x20, local copies, waits for them, and re-layouts: 15.4 us -> 3.98 us
    ppermute x13, waiting for transfers between devices: 8.01 us -> 11.6 us  [swap(): return lax.ppermute(array, 'dp', [(i, i ^ bit) for i in range(members)])]
    ppermute x3, waiting for transfers between devices: 2.13 us -> 5.28 us  [local(): up.append(lax.ppermute(up[-1], 'fsdp', ahead))]
    ppermute x4, waiting for transfers between devices: 0.91 us -> 2.9 us  [local(): came_down = lax.ppermute(going_down, 'fsdp', behind)]
    ppermute x4, waiting for transfers between devices: 0.01 us -> 1.79 us  [local(): came_up = lax.ppermute(going_up, 'fsdp', ahead)]
    convert_element_type x2, other arithmetic: 1.89 us -> 0.15 us  [local(): (terms[step - 1] + came_up.astype(jnp.float32)).astype(jnp.bfloat16)]
  transfers between devices with their start and end apart: 29 -> 29, of which waited for: 12 -> 15; matrix products, arithmetic and copies ran while one was open for 3% -> 1% of each run, Pallas kernels for 52% -> 54%
where the time goes in v7:
time: 123 us; the launch traced here: 122 us
  Pallas kernels  67.6 us (55%)
  waiting for transfers between devices  24.3 us (20%)
  starting transfers between devices  23.5 us (19%)
  local copies, waits for them, and re-layouts  4.91 us (4%)
    pallas_call x4, Pallas kernels, partial_products(): pl.pallas_call(functools.partial(partial_kernel, not bases, sources, part...  22 us
    pallas_call x2, Pallas kernels, grad_out_rows(): pl.pallas_call(functools.partial(grad_out_kernel, sizes, split, total), g...  14.2 us
    ppermute x13, waiting for transfers between devices, swap(): return lax.ppermute(array, 'dp', [(i, i ^ bit) for i in range(members)])  11.6 us
    pallas_call x3, Pallas kernels, backward(): pl.pallas_call(backward_kernel, grid=(high - low,), in_specs=[pl.BlockSpe...  8.13 us
    pallas_call x1, Pallas kernels, forward(): pl.pallas_call(forward_kernel, grid_spec=pltpu.PrefetchScalarGridSpec(num...  7.37 us
    ppermute x3, starting transfers between devices, local(): up.append(lax.ppermute(up[-1], 'fsdp', ahead))  6.63 us
    ppermute x4, starting transfers between devices, local(): came_up = lax.ppermute(going_up, 'fsdp', ahead)  6.46 us
    pallas_call x1, Pallas kernels, prepare(): pl.pallas_call(prepare_kernel, grid=(steps,), in_specs=[pl.BlockSpec((row...  6.02 us
  transfers between devices with their start and end apart: 29, of which 15 were waited for; matrix products, arithmetic and copies ran while one was open for 1% of the time, Pallas kernels for 54%

profile of v7, /device:TPU:0, one launch (start us, length us, event | category | flops | bytes accessed | tf_op | source)
XLA Modules:
  0.0 122.1 jit_solution(11636893234897211549)
XLA Ops:
  0.7 1.1 own_half_of_weight.1.refs_0_
  1.8 3.1 %collective-permute-start.1 = (bf16[208,1664]{1,0:T(8,128)(2,1)S(1)}, bf16[208,1664]{1,0:T(8,128)(2,1)}, u32[]{:S(2)}, u32[]{:S(2)}) collective-permute-start(bf16[208,1664]{1,0:T(8,128)(2,1)S(1)} %own_half_of_weight.1.refs_0_), channel_id=1, source_target_pairs={{0,2},{2,4},{4,6},{6,7},{7,5},{5,3},{3,1},{1,0},{8,10},{10,12},{12... | collective-permute-start | bytes 2076680 | tf_op jit(solution)/shard_map/ppermute | solution.py:517
  4.9 0.7 reshape.18.layer_scale
  5.6 2.6 %peer_windows.1 = (bf16[160,1664]{1,0:T(8,128)(2,1)}, bf16[288,1664]{1,0:T(8,128)(2,1)}) custom-call(s32[1]{0:T(128)} %bitcast.7.starts, bf16[448,3200]{1,0:T(8,128)(2,1)} %cotangent.1, f32[1,3200]{1,0:T(1,128)S(1)} %reshape.18.layer_scale), custom_call_target="tpu_custom_call" | custom-call | flops 34500001792 | bytes 1000 | tf_op jit(solution)/shard_map/peer_windows/pallas_call | solution.py:58
  8.2 2.0 %collective-permute-start.3 = (bf16[160,1664]{1,0:T(8,128)(2,1)}, bf16[160,1664]{1,0:T(8,128)(2,1)}, u32[]{:S(2)}, u32[]{:S(2)}) collective-permute-start(bf16[160,1664]{1,0:T(8,128)(2,1)} %get-tuple-element.98), channel_id=1, source_target_pairs={{0,16},{8,24},{16,0},{24,8},{1,17},{9,25},{17,1},{25,9},{2,18},{10... | collective-permute-start | bytes 1597448 | tf_op jit(solution)/shard_map/ppermute | solution.py:496
  10.2 6.0 %scaled_cotangent.1.refs_2_.turned = bf16[3200,512]{1,0:T(8,128)(2,1)} custom-call(bf16[448,3200]{1,0:T(8,128)(2,1)} %cotangent.1, f32[1,3200]{1,0:T(1,128)S(1)} %reshape.18.layer_scale), custom_call_target="tpu_custom_call" | custom-call | flops 34500001792 | bytes 1000 | tf_op jit(solution)/shard_map/scaled_cotangent/pallas_call | solution.py:89
  16.2 7.4 %attention_forward.1 = (bf16[1664,448]{1,0:T(8,128)(2,1)}, f32[13,256,256]{2,1,0:T(8,128)}, f32[13,192,192]{2,1,0:T(8,128)}) custom-call(s32[4]{0:T(128)S(1)} %dynamic-slice_bitcast_fusion.counts, bf16[3,448,1664]{2,1,0:T(8,128)(2,1)S(1)} %copy-done.2), custom_call_target="tpu_custom_call" | custom-call | flops 34500001792 | bytes 1000 | tf_op jit(solution)/shard_map/attention_forward/pallas_call | solution.py:206
  23.7 0.5 collective-permute-start.4
  24.3 2.0 %collective-permute-start.6 = (bf16[208,1664]{1,0:T(8,128)(2,1)}, bf16[208,1664]{1,0:T(8,128)(2,1)}, u32[]{:S(2)}, u32[]{:S(2)}) collective-permute-start(bf16[208,1664]{1,0:T(8,128)(2,1)} %collective-permute-done.1.refs_1_), channel_id=1, source_target_pairs={{0,2},{2,4},{4,6},{6,7},{7,5},{5,3},{3,1},{1,0},{8,10},{10,12},{12... | collective-permute-start | bytes 2076680 | tf_op jit(solution)/shard_map/ppermute | solution.py:549
  26.4 3.1 %attended_chunks.1 = (bf16[3,208,448]{2,1,0:T(8,128)(2,1)}, bf16[2,208,448]{2,1,0:T(8,128)(2,1)}, bf16[3,208,448]{2,1,0:T(8,128)(2,1)S(1)}) custom-call(s32[8]{0:T(128)S(1)} %stack.79.order, bf16[8,208,448]{2,1,0:T(8,128)(2,1)} %bitcast.26), custom_call_target="tpu_custom_call" | custom-call | flops 1150000000 | bytes 1000 | tf_op jit(solution)/shard_map/attended_chunks/pallas_call | solution.py:116
  29.5 0.8 copy-done.7
  30.4 1.5 %collective-permute-done.4.refs_1_ = bf16[8,208,448]{2,1,0:T(8,128)(2,1)} collective-permute-done((bf16[8,208,448]{2,1,0:T(8,128)(2,1)}, bf16[8,208,448]{2,1,0:T(8,128)(2,1)}, u32[]{:S(2)}, u32[]{:S(2)}) %collective-permute-start.4) | collective-permute-done | bytes 1490976 | tf_op jit(solution)/shard_map/ppermute | solution.py:496
  32.1 7.7 %projection_chip.1 = (bf16[208,896]{1,0:T(8,128)(2,1)}, bf16[208,896]{1,0:T(8,128)(2,1)}, bf16[208,896]{1,0:T(8,128)(2,1)}, bf16[208,896]{1,0:T(8,128)(2,1)}, bf...) custom-call(s32[8]{0:T(128)S(1)} %stack.79.order, ...), custom_call_target="tpu_custom_call" | custom-call | flops 3449999872 | bytes 1000 | tf_op jit(solution)/shard_map/projection_chip/pallas_call | solution.py:449
  39.8 2.2 %collective-permute-done.6.refs_3_ = bf16[208,1664]{1,0:T(8,128)(2,1)} collective-permute-done((bf16[208,1664]{1,0:T(8,128)(2,1)}, bf16[208,1664]{1,0:T(8,128)(2,1)}, u32[]{:S(2)}, u32[]{:S(2)}) %collective-permute-start.6) | collective-permute-done | bytes 692256 | tf_op jit(solution)/shard_map/ppermute | solution.py:549
  42.0 1.5 %collective-permute-done.7.refs_4_ = bf16[208,1664]{1,0:T(8,128)(2,1)} collective-permute-done((bf16[208,1664]{1,0:T(8,128)(2,1)}, bf16[208,1664]{1,0:T(8,128)(2,1)}, u32[]{:S(2)}, u32[]{:S(2)}) %collective-permute-start.7) | collective-permute-done | bytes 692256 | tf_op jit(solution)/shard_map/ppermute | solution.py:550
  43.5 1.6 %collective-permute-start.9 = (bf16[208,1664]{1,0:T(8,128)(2,1)}, bf16[208,1664]{1,0:T(8,128)(2,1)}, u32[]{:S(2)}, u32[]{:S(2)}) collective-permute-start(bf16[208,1664]{1,0:T(8,128)(2,1)} %collective-permute-done.6.refs_3_), channel_id=1, source_target_pairs={{0,2},{2,4},{4,6},{6,7},{7,5},{5,3},{3,1},{1,0},{8,10},{10,12},{12... | collective-permute-start | bytes 2076680 | tf_op jit(solution)/shard_map/ppermute | solution.py:573
  45.6 2.1 %collective-permute-done.refs_3_ = bf16[288,1664]{1,0:T(8,128)(2,1)} collective-permute-done((bf16[288,1664]{1,0:T(8,128)(2,1)}, bf16[288,1664]{1,0:T(8,128)(2,1)}, u32[]{:S(2)}, u32[]{:S(2)}) %collective-permute-start) | collective-permute-done | bytes 958496 | tf_op jit(solution)/shard_map/ppermute | solution.py:496
  48.1 0.5 collective-permute-start.13
  48.6 8.2 %grad_out_rows.2 = (f32[8,208,448]{2,1,0:T(8,128)}, bf16[8,208,448]{2,1,0:T(8,128)(2,1)}) custom-call(s32[6]{0:T(128)S(1)} %stack.82.info, bf16[3200,512]{1,0:T(8,128)(2,1)} %scaled_cotangent.1.refs_2_.turned, bf16[3200,512]{1,0:T(8,128)(2,1)S(1)} %collective-permute-done.8.refs_3_.turned_other, bf16[208,1664]{1,0:T(8,128)(2,1)} %copy-done.6, ...), custom_call_target="tpu_custom_call" | custom-call | flops 4312500224 | bytes 1000 | tf_op jit(solution)/shard_map/grad_out_rows/pallas_call | solution.py:324
  56.8 3.1 %collective-permute-done.9.up.refs_0_ = bf16[208,1664]{1,0:T(8,128)(2,1)} collective-permute-done((bf16[208,1664]{1,0:T(8,128)(2,1)}, bf16[208,1664]{1,0:T(8,128)(2,1)}, u32[]{:S(2)}, u32[]{:S(2)}) %collective-permute-start.9) | collective-permute-done | bytes 692256 | tf_op jit(solution)/shard_map/ppermute | solution.py:573
  59.9 1.3 %collective-permute-done.10.down.refs_1_ = bf16[208,1664]{1,0:T(8,128)(2,1)} collective-permute-done((bf16[208,1664]{1,0:T(8,128)(2,1)}, bf16[208,1664]{1,0:T(8,128)(2,1)}, u32[]{:S(2)}, u32[]{:S(2)}) %collective-permute-start.10) | collective-permute-done | bytes 692256 | tf_op jit(solution)/shard_map/ppermute | solution.py:574
  61.2 1.9 %far_parts.1 = (bf16[112,1664]{1,0:T(8,128)(2,1)}, bf16[96,1664]{1,0:T(8,128)(2,1)}) custom-call(bf16[208,1664]{1,0:T(8,128)(2,1)} %collective-permute-done.9.up.refs_0_, bf16[208,1664]{1,0:T(8,128)(2,1)} %collective-permute-done.10.down.refs_1_), custom_call_target="tpu_custom_call" | custom-call | flops 575000000 | bytes 1000 | tf_op jit(solution)/shard_map/far_parts/pallas_call | solution.py:147
  63.5 1.2 %collective-permute-start.14 = (bf16[2,208,448]{2,1,0:T(8,128)(2,1)}, bf16[2,208,448]{2,1,0:T(8,128)(2,1)}, u32[]{:S(2)}, u32[]{:S(2)}) collective-permute-start(bf16[2,208,448]{2,1,0:T(8,128)(2,1)} %get-tuple-element.136), channel_id=1, source_target_pairs={{0,16},{8,24},{16,0},{24,8},{1,17},{9,25},{17,1},{25,9},{2,18},{10... | collective-permute-start | bytes 1118216 | tf_op jit(solution)/shard_map/ppermute | solution.py:496
  64.8 1.6 %collective-permute-start.15 = (bf16[112,1664]{1,0:T(8,128)(2,1)}, bf16[112,1664]{1,0:T(8,128)(2,1)}, u32[]{:S(2)}, u32[]{:S(2)}) collective-permute-start(bf16[112,1664]{1,0:T(8,128)(2,1)} %get-tuple-element.162.refs_6_), channel_id=1, source_target_pairs={{0,2},{2,4},{4,6},{6,7},{7,5},{5,3},{3,1},{1,0},{8,10},{10,12},{12... | collective-permute-start | bytes 1118216 | tf_op jit(solution)/shard_map/ppermute | solution.py:581
  66.9 5.1 %projection_peers.3 = (f32[208,896]{1,0:T(8,128)S(1)}, f32[208,896]{1,0:T(8,128)S(1)}, f32[208,896]{1,0:T(8,128)S(1)}) custom-call(s32[3]{0:T(128)S(1)} %pad_add_fusion.1.order, s32[1]{0:T(128)} %bitcast.3.start, bf16[3,208,448]{2,1,0:T(8,128)(2,1)} %collective-permute-done.5.refs_0_, bf16[3,208,448]{2,1,0:T(8,128)(2,1)} %collective-permute-done.11.refs_1_, ...), custom_call_target="tpu_custom_call" | custom-call | flops 1724999936 | bytes 1000 | tf_op jit(solution)/shard_map/projection_peers/pallas_call | solution.py:449
  72.1 4.0 %collective-permute-done.14.refs_0_ = bf16[2,208,448]{2,1,0:T(8,128)(2,1)} collective-permute-done((bf16[2,208,448]{2,1,0:T(8,128)(2,1)}, bf16[2,208,448]{2,1,0:T(8,128)(2,1)}, u32[]{:S(2)}, u32[]{:S(2)}) %collective-permute-start.14) | collective-permute-done | bytes 372768 | tf_op jit(solution)/shard_map/ppermute | solution.py:496
  76.1 1.6 %collective-permute-start.17 = (bf16[112,896]{1,0:T(8,128)(2,1)S(1)}, bf16[112,896]{1,0:T(8,128)(2,1)S(1)}, u32[]{:S(2)}, u32[]{:S(2)}) collective-permute-start(bf16[112,896]{1,0:T(8,128)(2,1)S(1)} %slice.14), channel_id=1, source_target_pairs={{0,2},{2,4},{4,6},{6,7},{7,5},{5,3},{3,1},{1,0},{8,10},{10,12},{12... | collective-permute-start | bytes 602120 | tf_op jit(solution)/shard_map/ppermute | solution.py:601
  78.3 1.2 collective-permute-start.22
  79.4 4.3 %projection_peers.4 = (f32[208,896]{1,0:T(8,128)S(1)}, f32[208,896]{1,0:T(8,128)S(1)}) custom-call(s32[2]{0:T(128)S(1)} %pad_add_fusion.2.order, s32[1]{0:T(128)} %bitcast.3.start, bf16[2,208,448]{2,1,0:T(8,128)(2,1)} %collective-permute-done.14.refs_0_, bf16[2,208,448]{2,1,0:T(8,128)(2,1)S(1)} %collective-permute-done.19.refs_1_, ...), custom_call_target="tpu_custom_call" | custom-call | flops 1724999936 | bytes 1000 | tf_op jit(solution)/shard_map/projection_peers/pallas_call | solution.py:449
  83.7 0.5 collective-permute-done.18
  84.3 1.6 %collective-permute-start.20 = (bf16[208,896]{1,0:T(8,128)(2,1)S(1)}, bf16[208,896]{1,0:T(8,128)(2,1)S(1)}, u32[]{:S(2)}, u32[]{:S(2)}) collective-permute-start(bf16[208,896]{1,0:T(8,128)(2,1)S(1)} %get-tuple-element.152), channel_id=1, source_target_pairs={{0,2},{2,4},{4,6},{6,7},{7,5},{5,3},{3,1},{1,0},{8,10},{10,12},{12... | collective-permute-start | bytes 1118216 | tf_op jit(solution)/shard_map/ppermute | solution.py:626
  86.5 6.0 %grad_out_rows.3 = (f32[8,208,448]{2,1,0:T(8,128)}, bf16[8,208,448]{2,1,0:T(8,128)(2,1)}) custom-call(s32[4]{0:T(128)S(1)} %pad_add_fusion.3.info, bf16[3200,512]{1,0:T(8,128)(2,1)} %scaled_cotangent.1.refs_2_.turned, bf16[3200,512]{1,0:T(8,128)(2,1)S(1)} %collective-permute-done.8.refs_3_.turned_other, ...), custom_call_target="tpu_custom_call", output_to_operand_aliasing={{0}: (7, {}), {1}: (8, {})} | custom-call | flops 115000000 | bytes 1000 | tf_op jit(solution)/shard_map/grad_out_rows/pallas_call | solution.py:324
  92.5 2.0 %collective-permute-done.22.refs_0_ = bf16[3,208,448]{2,1,0:T(8,128)(2,1)} collective-permute-done((bf16[3,208,448]{2,1,0:T(8,128)(2,1)S(1)}, bf16[3,208,448]{2,1,0:T(8,128)(2,1)}, u32[]{:S(2)}, u32[]{:S(2)}) %collective-permute-start.22) | collective-permute-done | bytes 559136 | tf_op jit(solution)/shard_map/ppermute | solution.py:496
  94.6 1.1 collective-permute-done.21
  95.9 1.6 %collective-permute-start.24 = (bf16[208,896]{1,0:T(8,128)(2,1)S(1)}, bf16[208,896]{1,0:T(8,128)(2,1)S(1)}, u32[]{:S(2)}, u32[]{:S(2)}) collective-permute-start(bf16[208,896]{1,0:T(8,128)(2,1)S(1)} %add_convert_fusion.3), channel_id=1, source_target_pairs={{0,2},{2,4},{4,6},{6,7},{7,5},{5,3},{3,1},{1,0},{8,10},{10,12},{12... | collective-permute-start | bytes 1118216 | tf_op jit(solution)/shard_map/ppermute | solution.py:626
  97.6 0.5 collective-permute-start.25
  98.1 1.2 collective-permute-done.23.refs_1_
  99.3 0.8 copy-done.9
  100.1 5.1 %projection_peers.5 = (f32[208,896]{1,0:T(8,128)S(1)}, f32[208,896]{1,0:T(8,128)S(1)}, f32[208,896]{1,0:T(8,128)S(1)}) custom-call(s32[3]{0:T(128)S(1)} %pad_add_fusion.order, s32[1]{0:T(128)} %bitcast.3.start, bf16[3,208,448]{2,1,0:T(8,128)(2,1)} %collective-permute-done.22.refs_0_, bf16[3,208,448]{2,1,0:T(8,128)(2,1)} %copy-done.9, ...), custom_call_target="tpu_custom_call" | custom-call | flops 1724999936 | bytes 1000 | tf_op jit(solution)/shard_map/projection_peers/pallas_call | solution.py:449
  105.2 1.8 %collective-permute-done.24 = bf16[208,896]{1,0:T(8,128)(2,1)S(1)} collective-permute-done((bf16[208,896]{1,0:T(8,128)(2,1)S(1)}, bf16[208,896]{1,0:T(8,128)(2,1)S(1)}, u32[]{:S(2)}, u32[]{:S(2)}) %collective-permute-start.24) | collective-permute-done | bytes 372768 | tf_op jit(solution)/shard_map/ppermute | solution.py:626
  107.0 1.3 %collective-permute-done.25 = bf16[208,896]{1,0:T(8,128)(2,1)S(1)} collective-permute-done((bf16[208,896]{1,0:T(8,128)(2,1)S(1)}, bf16[208,896]{1,0:T(8,128)(2,1)S(1)}, u32[]{:S(2)}, u32[]{:S(2)}) %collective-permute-start.25) | collective-permute-done | bytes 372768 | tf_op jit(solution)/shard_map/ppermute | solution.py:627
  108.4 1.6 %collective-permute-start.26 = (bf16[208,896]{1,0:T(8,128)(2,1)S(1)}, bf16[208,896]{1,0:T(8,128)(2,1)S(1)}, u32[]{:S(2)}, u32[]{:S(2)}) collective-permute-start(bf16[208,896]{1,0:T(8,128)(2,1)S(1)} %add_convert_fusion.1), channel_id=1, source_target_pairs={{0,2},{2,4},{4,6},{6,7},{7,5},{5,3},{3,1},{1,0},{8,10},{10,12},{12... | collective-permute-start | bytes 1118216 | tf_op jit(solution)/shard_map/ppermute | solution.py:626
  110.0 0.5 collective-permute-start.27
  110.5 2.3 %copy-done.3 = bf16[3,448,1664]{2,1,0:T(8,128)(2,1)S(1)} copy-done((bf16[3,448,1664]{2,1,0:T(8,128)(2,1)S(1)}, bf16[3,448,1664]{2,1,0:T(8,128)(2,1)}, u32[]{:S(2)}) %copy-start.3) | copy-done | bytes 4472856
  112.8 3.3 %attention_backward.3.rest_0_ = bf16[3,448,1664]{2,1,0:T(8,128)(2,1)} custom-call(bf16[3,448,1664]{2,1,0:T(8,128)(2,1)S(1)} %copy-done.3, f32[1664,448]{1,0:T(8,128)S(1)} %bitcast.19, bf16[1664,448]{1,0:T(8,128)(2,1)S(1)} %bitcast.22, f32[13,256,256]{2,1,0:T(8,128)S(1)} %copy-done.4, f32[13,192,192]{2,1,0:T(8,128)S(1)} %copy-done.5), custom_call_target="tpu_custom_call" | custom-call | flops 3449999872 | bytes 1000 | tf_op jit(solution)/shard_map/attention_backward/pallas_call | solution.py:256
  116.1 2.5 %attention_backward.4.rest_0_ = bf16[3,448,1664]{2,1,0:T(8,128)(2,1)} custom-call(bf16[3,448,1664]{2,1,0:T(8,128)(2,1)S(1)} %copy-done.3, f32[1664,448]{1,0:T(8,128)S(1)} %bitcast.20, bf16[1664,448]{1,0:T(8,128)(2,1)S(1)} %bitcast.23, f32[13,256,256]{2,1,0:T(8,128)S(1)} %copy-done.4, f32[13,192,192]{2,1,0:T(8,128)S(1)} %copy-done.5, ...), custom_call_target="tpu_custom_call", output_to_operand_aliasing={{}: (5, {})} | custom-call | flops 2300000000 | bytes 1000 | tf_op jit(solution)/shard_map/attention_backward/pallas_call | solution.py:256
  118.5 2.4 %attention_backward.5 = bf16[3,448,1664]{2,1,0:T(8,128)(2,1)} custom-call(bf16[3,448,1664]{2,1,0:T(8,128)(2,1)S(1)} %copy-done.3, f32[1664,448]{1,0:T(8,128)S(1)} %bitcast.21, bf16[1664,448]{1,0:T(8,128)(2,1)S(1)} %bitcast.24, f32[13,256,256]{2,1,0:T(8,128)S(1)} %copy-done.4, f32[13,192,192]{2,1,0:T(8,128)S(1)} %copy-done.5, ...), custom_call_target="tpu_custom_call", output_to_operand_aliasing={{}: (5, {})} | custom-call | flops 2300000000 | bytes 1000 | tf_op jit(solution)/shard_map/attention_backward/pallas_call | solution.py:256
  120.9 1.1 last_sum.1
  (62 shorter events, 4.1 us)
Async XLA Ops:
  0.6 15.6 %copy-start = (s32[4,1,4]{2,1,0:T(1,128)S(1)}, s32[4,1,4]{2,1,0:T(1,128)}, u32[]{:S(2)}) copy-start(s32[4,1,4]{2,1,0:T(1,128)} %param.9) | copy-start | bytes 196
  1.8 6.4 %copy-start.6 = (bf16[208,1664]{1,0:T(8,128)(2,1)}, bf16[208,1664]{1,0:T(8,128)(2,1)S(1)}, u32[]{:S(2)}) copy-start(bf16[208,1664]{1,0:T(8,128)(2,1)S(1)} %own_half_of_weight.1.refs_0_) | copy-start | bytes 2076676
  1.8 21.8 %collective-permute-start.1 = (bf16[208,1664]{1,0:T(8,128)(2,1)S(1)}, bf16[208,1664]{1,0:T(8,128)(2,1)}, u32[]{:S(2)}, u32[]{:S(2)}) collective-permute-start(bf16[208,1664]{1,0:T(8,128)(2,1)S(1)} %own_half_of_weight.1.refs_0_), channel_id=1, source_target_pairs={{0,2},{2,4},{4,6},{6,7},{7,5},{5,3},{3,1},{1,0},{8,10},{10,12},{12... | collective-permute-start | bytes 2076680 | tf_op jit(solution)/shard_map/ppermute | solution.py:517
  4.9 18.7 %collective-permute-start.2 = (bf16[208,1664]{1,0:T(8,128)(2,1)S(1)}, bf16[208,1664]{1,0:T(8,128)(2,1)}, u32[]{:S(2)}, u32[]{:S(2)}) collective-permute-start(bf16[208,1664]{1,0:T(8,128)(2,1)S(1)} %own_half_of_weight.1.refs_0_), channel_id=1, source_target_pairs={{0,1},{2,0},{4,2},{6,4},{7,6},{5,7},{3,5},{1,3},{8,9},{10,8},{12,1... | collective-permute-start | bytes 2076680 | tf_op jit(solution)/shard_map/ppermute | solution.py:518
  8.2 15.4 %collective-permute-start.3 = (bf16[160,1664]{1,0:T(8,128)(2,1)}, bf16[160,1664]{1,0:T(8,128)(2,1)}, u32[]{:S(2)}, u32[]{:S(2)}) collective-permute-start(bf16[160,1664]{1,0:T(8,128)(2,1)} %get-tuple-element.98), channel_id=1, source_target_pairs={{0,16},{8,24},{16,0},{24,8},{1,17},{9,25},{17,1},{25,9},{2,18},{10... | collective-permute-start | bytes 1597448 | tf_op jit(solution)/shard_map/ppermute | solution.py:496
  10.2 6.0 %copy-start.2 = (bf16[3,448,1664]{2,1,0:T(8,128)(2,1)S(1)}, bf16[3,448,1664]{2,1,0:T(8,128)(2,1)}, u32[]{:S(2)}) copy-start(bf16[3,448,1664]{2,1,0:T(8,128)(2,1)} %qkv.7) | copy-start | bytes 13418500
  23.6 8.6 %collective-permute-start.8 = (bf16[3200,512]{1,0:T(8,128)(2,1)}, bf16[3200,512]{1,0:T(8,128)(2,1)S(1)}, u32[]{:S(2)}, u32[]{:S(2)}) collective-permute-start(bf16[3200,512]{1,0:T(8,128)(2,1)} %scaled_cotangent.1.refs_2_.turned), channel_id=1, source_target_pairs={{0,8},{8,0},{16,24},{24,16},{1,9},{9,1},{17,25},{25,17},{2,10},{10... | collective-permute-start | bytes 9830408 | tf_op jit(solution)/shard_map/ppermute | solution.py:496
  23.7 8.2 %collective-permute-start.4 = (bf16[8,208,448]{2,1,0:T(8,128)(2,1)}, bf16[8,208,448]{2,1,0:T(8,128)(2,1)}, u32[]{:S(2)}, u32[]{:S(2)}) collective-permute-start(bf16[8,208,448]{2,1,0:T(8,128)(2,1)} %bitcast.25), channel_id=1, source_target_pairs={{0,8},{8,0},{16,24},{24,16},{1,9},{9,1},{17,25},{25,17},{2,10},{10... | collective-permute-start | bytes 4472840 | tf_op jit(solution)/shard_map/ppermute | solution.py:496
  24.2 23.5 %collective-permute-start = (bf16[288,1664]{1,0:T(8,128)(2,1)}, bf16[288,1664]{1,0:T(8,128)(2,1)}, u32[]{:S(2)}, u32[]{:S(2)}) collective-permute-start(bf16[288,1664]{1,0:T(8,128)(2,1)} %get-tuple-element.96), channel_id=1, source_target_pairs={{0,16},{8,24},{16,0},{24,8},{1,17},{9,25},{17,1},{25,9},{2,18},{10... | collective-permute-start | bytes 2875400 | tf_op jit(solution)/shard_map/ppermute | solution.py:496
  24.3 17.7 %collective-permute-start.6 = (bf16[208,1664]{1,0:T(8,128)(2,1)}, bf16[208,1664]{1,0:T(8,128)(2,1)}, u32[]{:S(2)}, u32[]{:S(2)}) collective-permute-start(bf16[208,1664]{1,0:T(8,128)(2,1)} %collective-permute-done.1.refs_1_), channel_id=1, source_target_pairs={{0,2},{2,4},{4,6},{6,7},{7,5},{5,3},{3,1},{1,0},{8,10},{10,12},{12... | collective-permute-start | bytes 2076680 | tf_op jit(solution)/shard_map/ppermute | solution.py:549
  26.3 17.3 %collective-permute-start.7 = (bf16[208,1664]{1,0:T(8,128)(2,1)}, bf16[208,1664]{1,0:T(8,128)(2,1)}, u32[]{:S(2)}, u32[]{:S(2)}) collective-permute-start(bf16[208,1664]{1,0:T(8,128)(2,1)} %collective-permute-done.2.refs_2_), channel_id=1, source_target_pairs={{0,1},{2,0},{4,2},{6,4},{7,6},{5,7},{3,5},{1,3},{8,9},{10,8},{12,1... | collective-permute-start | bytes 2076680 | tf_op jit(solution)/shard_map/ppermute | solution.py:550
  29.5 0.9 copy-start.7
  43.5 16.3 %collective-permute-start.9 = (bf16[208,1664]{1,0:T(8,128)(2,1)}, bf16[208,1664]{1,0:T(8,128)(2,1)}, u32[]{:S(2)}, u32[]{:S(2)}) collective-permute-start(bf16[208,1664]{1,0:T(8,128)(2,1)} %collective-permute-done.6.refs_3_), channel_id=1, source_target_pairs={{0,2},{2,4},{4,6},{6,7},{7,5},{5,3},{3,1},{1,0},{8,10},{10,12},{12... | collective-permute-start | bytes 2076680 | tf_op jit(solution)/shard_map/ppermute | solution.py:573
  45.1 16.1 %collective-permute-start.10 = (bf16[208,1664]{1,0:T(8,128)(2,1)}, bf16[208,1664]{1,0:T(8,128)(2,1)}, u32[]{:S(2)}, u32[]{:S(2)}) collective-permute-start(bf16[208,1664]{1,0:T(8,128)(2,1)} %collective-permute-done.7.refs_4_), channel_id=1, source_target_pairs={{0,1},{2,0},{4,2},{6,4},{7,6},{5,7},{3,5},{1,3},{8,9},{10,8},{12,1... | collective-permute-start | bytes 2076680 | tf_op jit(solution)/shard_map/ppermute | solution.py:574
  47.7 15.8 %collective-permute-start.5 = (bf16[3,208,448]{2,1,0:T(8,128)(2,1)}, bf16[3,208,448]{2,1,0:T(8,128)(2,1)}, u32[]{:S(2)}, u32[]{:S(2)}) collective-permute-start(bf16[3,208,448]{2,1,0:T(8,128)(2,1)} %get-tuple-element.107), channel_id=1, source_target_pairs={{0,16},{8,24},{16,0},{24,8},{1,17},{9,25},{17,1},{25,9},{2,18},{10... | collective-permute-start | bytes 1677320 | tf_op jit(solution)/shard_map/ppermute | solution.py:496
  48.1 18.3 %collective-permute-start.12 = (bf16[160,1664]{1,0:T(8,128)(2,1)}, bf16[160,1664]{1,0:T(8,128)(2,1)}, u32[]{:S(2)}, u32[]{:S(2)}) collective-permute-start(bf16[160,1664]{1,0:T(8,128)(2,1)} %collective-permute-done.3.refs_2_), channel_id=1, source_target_pairs={{0,8},{8,0},{16,24},{24,16},{1,9},{9,1},{17,25},{25,17},{2,10},{10... | collective-permute-start | bytes 1597448 | tf_op jit(solution)/shard_map/ppermute | solution.py:496
  48.1 18.8 %collective-permute-start.13 = (bf16[288,1664]{1,0:T(8,128)(2,1)}, bf16[288,1664]{1,0:T(8,128)(2,1)}, u32[]{:S(2)}, u32[]{:S(2)}) collective-permute-start(bf16[288,1664]{1,0:T(8,128)(2,1)} %collective-permute-done.refs_3_), channel_id=1, source_target_pairs={{0,8},{8,0},{16,24},{24,16},{1,9},{9,1},{17,25},{25,17},{2,10},{10... | collective-permute-start | bytes 2875400 | tf_op jit(solution)/shard_map/ppermute | solution.py:496
  63.5 3.4 %collective-permute-start.11 = (bf16[3,208,448]{2,1,0:T(8,128)(2,1)}, bf16[3,208,448]{2,1,0:T(8,128)(2,1)}, u32[]{:S(2)}, u32[]{:S(2)}) collective-permute-start(bf16[3,208,448]{2,1,0:T(8,128)(2,1)} %collective-permute-done.5.refs_0_), channel_id=1, source_target_pairs={{0,8},{8,0},{16,24},{24,16},{1,9},{9,1},{17,25},{25,17},{2,10},{10... | collective-permute-start | bytes 1677320 | tf_op jit(solution)/shard_map/ppermute | solution.py:496
  63.5 12.5 %collective-permute-start.14 = (bf16[2,208,448]{2,1,0:T(8,128)(2,1)}, bf16[2,208,448]{2,1,0:T(8,128)(2,1)}, u32[]{:S(2)}, u32[]{:S(2)}) collective-permute-start(bf16[2,208,448]{2,1,0:T(8,128)(2,1)} %get-tuple-element.136), channel_id=1, source_target_pairs={{0,16},{8,24},{16,0},{24,8},{1,17},{9,25},{17,1},{25,9},{2,18},{10... | collective-permute-start | bytes 1118216 | tf_op jit(solution)/shard_map/ppermute | solution.py:496
  64.8 11.3 %collective-permute-start.15 = (bf16[112,1664]{1,0:T(8,128)(2,1)}, bf16[112,1664]{1,0:T(8,128)(2,1)}, u32[]{:S(2)}, u32[]{:S(2)}) collective-permute-start(bf16[112,1664]{1,0:T(8,128)(2,1)} %get-tuple-element.162.refs_6_), channel_id=1, source_target_pairs={{0,2},{2,4},{4,6},{6,7},{7,5},{5,3},{3,1},{1,0},{8,10},{10,12},{12... | collective-permute-start | bytes 1118216 | tf_op jit(solution)/shard_map/ppermute | solution.py:581
  66.4 9.7 %collective-permute-start.16 = (bf16[96,1664]{1,0:T(8,128)(2,1)}, bf16[96,1664]{1,0:T(8,128)(2,1)}, u32[]{:S(2)}, u32[]{:S(2)}) collective-permute-start(bf16[96,1664]{1,0:T(8,128)(2,1)} %get-tuple-element.138), channel_id=1, source_target_pairs={{0,1},{2,0},{4,2},{6,4},{7,6},{5,7},{3,5},{1,3},{8,9},{10,8},{12,1... | collective-permute-start | bytes 958472 | tf_op jit(solution)/shard_map/ppermute | solution.py:582
  66.9 11.4 %copy-start.8 = (bf16[3,208,448]{2,1,0:T(8,128)(2,1)S(1)}, bf16[3,208,448]{2,1,0:T(8,128)(2,1)}, u32[]{:S(2)}) copy-start(bf16[3,208,448]{2,1,0:T(8,128)(2,1)} %copy-done.7) | copy-start | bytes 1677316
  76.1 3.3 %collective-permute-start.19 = (bf16[2,208,448]{2,1,0:T(8,128)(2,1)}, bf16[2,208,448]{2,1,0:T(8,128)(2,1)S(1)}, u32[]{:S(2)}, u32[]{:S(2)}) collective-permute-start(bf16[2,208,448]{2,1,0:T(8,128)(2,1)} %collective-permute-done.14.refs_0_), channel_id=1, source_target_pairs={{0,8},{8,0},{16,24},{24,16},{1,9},{9,1},{17,25},{25,17},{2,10},{10... | collective-permute-start | bytes 1118216 | tf_op jit(solution)/shard_map/ppermute | solution.py:496
  76.1 8.1 %collective-permute-start.17 = (bf16[112,896]{1,0:T(8,128)(2,1)S(1)}, bf16[112,896]{1,0:T(8,128)(2,1)S(1)}, u32[]{:S(2)}, u32[]{:S(2)}) collective-permute-start(bf16[112,896]{1,0:T(8,128)(2,1)S(1)} %slice.14), channel_id=1, source_target_pairs={{0,2},{2,4},{4,6},{6,7},{7,5},{5,3},{3,1},{1,0},{8,10},{10,12},{12... | collective-permute-start | bytes 602120 | tf_op jit(solution)/shard_map/ppermute | solution.py:601
  77.7 6.5 %collective-permute-start.18 = (bf16[96,896]{1,0:T(8,128)(2,1)S(1)}, bf16[96,896]{1,0:T(8,128)(2,1)S(1)}, u32[]{:S(2)}, u32[]{:S(2)}) collective-permute-start(bf16[96,896]{1,0:T(8,128)(2,1)S(1)} %slice.15), channel_id=1, source_target_pairs={{0,1},{2,0},{4,2},{6,4},{7,6},{5,7},{3,5},{1,3},{8,9},{10,8},{12,1... | collective-permute-start | bytes 516104 | tf_op jit(solution)/shard_map/ppermute | solution.py:602
  78.3 16.3 %collective-permute-start.22 = (bf16[3,208,448]{2,1,0:T(8,128)(2,1)S(1)}, bf16[3,208,448]{2,1,0:T(8,128)(2,1)}, u32[]{:S(2)}, u32[]{:S(2)}) collective-permute-start(bf16[3,208,448]{2,1,0:T(8,128)(2,1)S(1)} %copy-done.8), channel_id=1, source_target_pairs={{0,16},{8,24},{16,0},{24,8},{1,17},{9,25},{17,1},{25,9},{2,18},{10... | collective-permute-start | bytes 1677320 | tf_op jit(solution)/shard_map/ppermute | solution.py:496
  84.3 10.2 %collective-permute-start.20 = (bf16[208,896]{1,0:T(8,128)(2,1)S(1)}, bf16[208,896]{1,0:T(8,128)(2,1)S(1)}, u32[]{:S(2)}, u32[]{:S(2)}) collective-permute-start(bf16[208,896]{1,0:T(8,128)(2,1)S(1)} %get-tuple-element.152), channel_id=1, source_target_pairs={{0,2},{2,4},{4,6},{6,7},{7,5},{5,3},{3,1},{1,0},{8,10},{10,12},{12... | collective-permute-start | bytes 1118216 | tf_op jit(solution)/shard_map/ppermute | solution.py:626
  85.9 9.8 %collective-permute-start.21 = (bf16[208,896]{1,0:T(8,128)(2,1)S(1)}, bf16[208,896]{1,0:T(8,128)(2,1)S(1)}, u32[]{:S(2)}, u32[]{:S(2)}) collective-permute-start(bf16[208,896]{1,0:T(8,128)(2,1)S(1)} %get-tuple-element.154), channel_id=1, source_target_pairs={{0,1},{2,0},{4,2},{6,4},{7,6},{5,7},{3,5},{1,3},{8,9},{10,8},{12,1... | collective-permute-start | bytes 1118216 | tf_op jit(solution)/shard_map/ppermute | solution.py:627
  94.5 16.0 %collective-permute-start.28 = (bf16[8,208,448]{2,1,0:T(8,128)(2,1)}, bf16[8,208,448]{2,1,0:T(8,128)(2,1)S(1)}, u32[]{:S(2)}, u32[]{:S(2)}) collective-permute-start(bf16[8,208,448]{2,1,0:T(8,128)(2,1)} %get-tuple-element.177), channel_id=1, source_target_pairs={{0,8},{8,0},{16,24},{24,16},{1,9},{9,1},{17,25},{25,17},{2,10},{10... | collective-permute-start | bytes 4472840 | tf_op jit(solution)/shard_map/ppermute | solution.py:496
  95.8 3.5 %collective-permute-start.23 = (bf16[3,208,448]{2,1,0:T(8,128)(2,1)}, bf16[3,208,448]{2,1,0:T(8,128)(2,1)S(1)}, u32[]{:S(2)}, u32[]{:S(2)}) collective-permute-start(bf16[3,208,448]{2,1,0:T(8,128)(2,1)} %collective-permute-done.22.refs_0_), channel_id=1, source_target_pairs={{0,8},{8,0},{16,24},{24,16},{1,9},{9,1},{17,25},{25,17},{2,10},{10... | collective-permute-start | bytes 1677320 | tf_op jit(solution)/shard_map/ppermute | solution.py:496
  95.9 11.1 %collective-permute-start.24 = (bf16[208,896]{1,0:T(8,128)(2,1)S(1)}, bf16[208,896]{1,0:T(8,128)(2,1)S(1)}, u32[]{:S(2)}, u32[]{:S(2)}) collective-permute-start(bf16[208,896]{1,0:T(8,128)(2,1)S(1)} %add_convert_fusion.3), channel_id=1, source_target_pairs={{0,2},{2,4},{4,6},{6,7},{7,5},{5,3},{3,1},{1,0},{8,10},{10,12},{12... | collective-permute-start | bytes 1118216 | tf_op jit(solution)/shard_map/ppermute | solution.py:626
  97.6 12.9 %copy-start.1 = (f32[8,208,448]{2,1,0:T(8,128)S(1)}, f32[8,208,448]{2,1,0:T(8,128)}, u32[]{:S(2)}) copy-start(f32[8,208,448]{2,1,0:T(8,128)} %get-tuple-element.165) | copy-start | bytes 8945668
  97.6 12.9 %copy-start.4 = (f32[13,256,256]{2,1,0:T(8,128)S(1)}, f32[13,256,256]{2,1,0:T(8,128)}, u32[]{:S(2)}) copy-start(f32[13,256,256]{2,1,0:T(8,128)} %get-tuple-element.178.main_probs) | copy-start | bytes 10223620
  97.6 12.9 %copy-start.5 = (f32[13,192,192]{2,1,0:T(8,128)S(1)}, f32[13,192,192]{2,1,0:T(8,128)}, u32[]{:S(2)}) copy-start(f32[13,192,192]{2,1,0:T(8,128)} %get-tuple-element.179.slot_probs) | copy-start | bytes 5750788
  97.6 10.8 %collective-permute-start.25 = (bf16[208,896]{1,0:T(8,128)(2,1)S(1)}, bf16[208,896]{1,0:T(8,128)(2,1)S(1)}, u32[]{:S(2)}, u32[]{:S(2)}) collective-permute-start(bf16[208,896]{1,0:T(8,128)(2,1)S(1)} %add_convert_fusion.2), channel_id=1, source_target_pairs={{0,1},{2,0},{4,2},{6,4},{7,6},{5,7},{3,5},{1,3},{8,9},{10,8},{12,1... | collective-permute-start | bytes 1118216 | tf_op jit(solution)/shard_map/ppermute | solution.py:627
  99.3 0.8 copy-start.9
  108.4 12.5 %collective-permute-start.26 = (bf16[208,896]{1,0:T(8,128)(2,1)S(1)}, bf16[208,896]{1,0:T(8,128)(2,1)S(1)}, u32[]{:S(2)}, u32[]{:S(2)}) collective-permute-start(bf16[208,896]{1,0:T(8,128)(2,1)S(1)} %add_convert_fusion.1), channel_id=1, source_target_pairs={{0,2},{2,4},{4,6},{6,7},{7,5},{5,3},{3,1},{1,0},{8,10},{10,12},{12... | collective-permute-start | bytes 1118216 | tf_op jit(solution)/shard_map/ppermute | solution.py:626
  110.0 10.9 %collective-permute-start.27 = (bf16[208,896]{1,0:T(8,128)(2,1)S(1)}, bf16[208,896]{1,0:T(8,128)(2,1)S(1)}, u32[]{:S(2)}, u32[]{:S(2)}) collective-permute-start(bf16[208,896]{1,0:T(8,128)(2,1)S(1)} %add_convert_fusion), channel_id=1, source_target_pairs={{0,1},{2,0},{4,2},{6,4},{7,6},{5,7},{3,5},{1,3},{8,9},{10,8},{12,1... | collective-permute-start | bytes 1118216 | tf_op jit(solution)/shard_map/ppermute | solution.py:627
  110.5 2.3 %copy-start.3 = (bf16[3,448,1664]{2,1,0:T(8,128)(2,1)S(1)}, bf16[3,448,1664]{2,1,0:T(8,128)(2,1)}, u32[]{:S(2)}) copy-start(bf16[3,448,1664]{2,1,0:T(8,128)(2,1)} %qkv.7) | copy-start | bytes 13418500

commit v8 on v7

--- a/solution.py
+++ b/solution.py
@@ -54,7 +54,8 @@
 
 def peer_windows(starts, cotangent, layer_scale, peers, width):
     rows, total = cotangent.shape
-    parts = (rows // 48 * 16 + 16, rows - rows // 48 * 16 - 16)
+    first = rows * 2 // 5 // 16 * 16
+    parts = (first, rows - first)
     arrays = pl.pallas_call(
         functools.partial(window_kernel, peers),
         grid_spec=pltpu.PrefetchScalarGridSpec(
@@ -127,34 +128,6 @@
         cost_estimate=lasting(2),
         name="attended_chunks",
     )(order, in_hbm(attended))
-
-
-def far_kernel(up, down, out_up, out_down, sems):
-    cut = out_up.shape[0]
-    copies = [
-        pltpu.make_async_copy(up.at[pl.ds(0, cut)], out_up, sems.at[0]),
-        pltpu.make_async_copy(down.at[pl.ds(cut, out_down.shape[0])], out_down, sems.at[1]),
-    ]
-    for copy in copies:
-        copy.start()
-    for copy in copies:
-        copy.wait()
-
-
-def far_parts(up, down, cut):
-    depth, width = up.shape
-    sizes = (cut, depth - cut)
-    return pl.pallas_call(
-        far_kernel,
-        grid=(1,),
-        in_specs=[pl.BlockSpec(memory_space=pl.ANY)] * 2,
-        out_specs=[pl.BlockSpec((size, width), lambda i: (0, 0)) for size in sizes],
-        out_shape=[jax.ShapeDtypeStruct((size, width), up.dtype) for size in sizes],
-        scratch_shapes=[pltpu.SemaphoreType.DMA((2,))],
-        compiler_params=pltpu.CompilerParams(vmem_limit_bytes=4 * MIB),
-        cost_estimate=lasting(1),
-        name="far_parts",
-    )(up, down)
 
 
 PAIR = 2
@@ -269,7 +242,7 @@
         compiler_params=pltpu.CompilerParams(vmem_limit_bytes=14 * MIB),
         cost_estimate=lasting(2 * (high - low)),
         name="attention_backward",
-    )(qkv, grad_mine, grad_other, main_probs, slot_probs, *map(in_hbm, held))
+    )(qkv if held else in_hbm(qkv), grad_mine, grad_other, main_probs, slot_probs, *map(in_hbm, held))
 
 
 def grad_out_kernel(sizes, split, total, info, turned, turned_other, *refs):
@@ -313,7 +286,7 @@
         store.wait()
 
 
-def grad_out_rows(info, turned, turned_other, rows, pieces, shards, held, after=()):
+def grad_out_rows(info, turned, turned_other, rows, pieces, shards, held):
     total, lanes = turned.shape
     split = pieces[0][0].shape[1]
     depth = sum(p.shape[0] for p in pieces[0])
@@ -326,7 +299,7 @@
         grid_spec=pltpu.PrefetchScalarGridSpec(
             num_scalar_prefetch=1,
             grid=(1,),
-            in_specs=[pl.BlockSpec(memory_space=pl.ANY)] * (2 + len(arrays) + len(held) + len(after)),
+            in_specs=[pl.BlockSpec(memory_space=pl.ANY)] * (2 + len(arrays) + len(held)),
             out_specs=[pl.BlockSpec(memory_space=pl.ANY)] * 2,
             scratch_shapes=[
                 pltpu.VMEM((2, split, lanes), jnp.bfloat16),
@@ -345,7 +318,7 @@
         compiler_params=pltpu.CompilerParams(vmem_limit_bytes=16 * MIB),
         cost_estimate=lasting(0.2 if held else 1.5 * len(pieces)),
         name="grad_out_rows",
-    )(info, in_hbm(turned), turned_other, *arrays, *map(in_hbm, held), *after)
+    )(info, in_hbm(turned), turned_other, *arrays, *map(in_hbm, held))
 
 
 def half_kernel(starts, weight, out, sem):
@@ -398,7 +371,7 @@
     )(start, term, came_up, came_down)
 
 
-def partial_kernel(chosen, sources, parts, count, window, order, start, *refs):
+def partial_kernel(chosen, turned_round, sources, parts, count, window, order, start, *refs):
     attended, columns = refs[:sources], refs[sources:sources * (1 + parts)]
     chunks, held, sems = refs[-3:]
     bases = refs[sources * (1 + parts):-3 - count]
@@ -417,7 +390,7 @@
                 some.append(pltpu.make_async_copy(source.at[:, at], target, sems.at[i, count + part]))
             first += source.shape[0]
         for j in range(count):
-            source = attended[i].at[order[j] if chosen else j]
+            source = attended[i].at[order[j] if chosen else turned_round[j] if i % 2 else j]
             some.append(pltpu.make_async_copy(source, chunks.at[i, j], sems.at[i, j]))
         copies.append(some)
     for some in copies:
@@ -441,13 +414,13 @@
             outs[first + j][...] = result.astype(outs[first + j].dtype)
 
 
-def partial_products(order, start, attended, columns, window, bases=()):
+def partial_products(order, start, attended, columns, window, bases=(), turned_round=()):
     _, depth, rows = attended[0].shape
     parts = len(columns) // len(attended)
     count, sources = order.shape[0], len(attended)
     block = pl.BlockSpec((depth, window), lambda j, o, s: (0, 0))
     return pl.pallas_call(
-        functools.partial(partial_kernel, not bases, sources, parts, count, window),
+        functools.partial(partial_kernel, not bases, turned_round, sources, parts, count, window),
         grid_spec=pltpu.PrefetchScalarGridSpec(
             num_scalar_prefetch=2,
             grid=(1,),
@@ -486,17 +459,24 @@
     place = jnp.where(shard % 2 == 0, shard // 2, shards - 1 - shard // 2)
     ahead = [(ring[i], ring[(i + 1) % shards]) for i in range(shards)]
     behind = [(ring[i], ring[(i - 1) % shards]) for i in range(shards)]
+    ways = [ahead, behind]
+    streams = [
+        [(d * shards + a, d * shards + b) for d in range(members) for a, b in ways[(d + turn) % 2]] for turn in range(2)
+    ]
     half = shards // 2
     depth, total = proj_weight.shape
     rows, width = query_key_value.shape[1:]
     owned = total // members
     counts = lax.dynamic_index_in_dim(lengths[:, 0, :], member, 0, keepdims=False)
 
+    def send(array, stream):
+        return lax.ppermute(array, ("dp", "fsdp"), streams[stream])
+
     def swap(array, bit):
         return lax.ppermute(array, "dp", [(i, i ^ bit) for i in range(members)])
 
     def shard_at(offset):
-        at = (place + offset + shards) % shards
+        at = (place + (1 - 2 * core) * offset + shards) % shards
         return jnp.where(at < half, 2 * at, 2 * (shards - 1 - at) + 1)
 
     def table(values):
@@ -512,10 +492,9 @@
 
     split = -(-(total // LANE) // 2) * LANE
     mine = half_columns(table([core * (total - split)]), proj_weight, split)
-    cut = -(-depth // 32) * 16
     up, down = [mine], [mine]
-    up.append(lax.ppermute(up[-1], "fsdp", ahead))
-    down.append(lax.ppermute(down[-1], "fsdp", behind))
+    up.append(send(up[-1], 0))
+    down.append(send(down[-1], 1))
 
     mine, cotangent = lax.optimization_barrier((mine, cotangent))
     scales = layer_scale.reshape(1, total)
@@ -533,9 +512,9 @@
     sizes = [len(group) for group in groups]
     orders = [flat[sum(sizes[:g]):sum(sizes[:g + 1])] for g in range(len(groups))]
 
-    def rows_of(some, held, after=()):
+    def rows_of(some, held):
         info = table([core] + [shard_at(o) for _, o in some])
-        return grad_out_rows(info, turned, turned_other, rows, [p for p, _ in some], shards, held, after)
+        return grad_out_rows(info, turned, turned_other, rows, [p for p, _ in some], shards, held)
 
     up[1], down[1], attended, came_columns[0], turned = lax.optimization_barrier(
         (up[1], down[1], attended, came_columns[0], turned)
@@ -546,8 +525,8 @@
     chunks = list(arrange(flat, attended, sizes))
     attended_other, chunks = lax.optimization_barrier((attended_other, chunks))
     for _ in range(half - 3):
-        up.append(lax.ppermute(up[-1], "fsdp", ahead))
-        down.append(lax.ppermute(down[-1], "fsdp", behind))
+        up.append(send(up[-1], 0))
+        down.append(send(down[-1], 1))
     bases = partial_products(
         flat, starts[:1], [in_hbm(attended), attended_other], [in_hbm(turned), turned_other], window
     )
@@ -570,16 +549,11 @@
         pieces += [([up[step]], -step), ([down[step]], step)]
     pieces[:-2] = [([in_hbm(array) for array in arrays], o) for arrays, o in pieces[:-2]]
     grad_out = rows_of(pieces, None)
-    up.append(lax.ppermute(up[-1], "fsdp", ahead))
-    down.append(lax.ppermute(down[-1], "fsdp", behind))
+    up.append(send(up[-1], 0))
+    down.append(send(down[-1], 1))
     up[-1], down[-1], grad_out = lax.optimization_barrier((up[-1], down[-1], grad_out))
-    if depth % 16 == 0:
-        far_up, far_down = far_parts(up[-1], down[-1], cut)
-    else:
-        far_up, far_down = up[-1][:cut], down[-1][cut:]
-    came[0], near_up, near_down, sent_up = lax.optimization_barrier((came[0], up[-1], down[-1], far_up))
-    far_up = lax.ppermute(far_up, "fsdp", ahead)
-    far_down = lax.ppermute(far_down, "fsdp", behind)
+    far = send(up[-1], 0)
+    came[0], near_up, near_down = lax.optimization_barrier((came[0], up[-1], down[-1]))
 
     def both_cores(arrays):
         return [a for c in arrays for a in (c, swap(c, 1))]
@@ -588,32 +562,29 @@
         group = groups[index]
         if not taken:
             return {o: bases[o] for o in group}
-        result = partial_products(orders[index], starts[1:], taken, columns, window, [bases[o] for o in group])
+        turned_round = [group.index(-o) if -o in group else j for j, o in enumerate(group)]
+        result = partial_products(orders[index], starts[1:], taken, columns, window, [bases[o] for o in group], turned_round)
         return dict(zip(group, result))
 
     terms = products(0, both_cores(came[0]))
     first = terms[half].astype(jnp.bfloat16)
-    going_up, going_down, came[1], chunks, far_up, far_down = lax.optimization_barrier(
-        (first[:cut], first[cut:], came[1], chunks, far_up, far_down)
-    )
+    first, came[1], chunks, far = lax.optimization_barrier((first, came[1], chunks, far))
     came += [[swap(some, 2 * k) for k in range(1, peers)] for some in chunks[2:]]
     taken = both_cores(came[1])
-    came_up = lax.ppermute(going_up, "fsdp", ahead)
-    came_down = lax.ppermute(going_down, "fsdp", behind)
+    came_up, came_down = send(first, 0), None
 
     bounds = [0, 3, 5, -(-(width // HS) // PAIR)]
     grads = None
     for step in range(half, 1, -1):
         if step == half:
-            came_up, came_down, following = lax.optimization_barrier((came_up, came_down, products(1, taken)))
+            came_up, following = lax.optimization_barrier((came_up, products(1, taken)))
             terms.update(following)
-            came_up = jnp.pad(came_up, ((0, depth - cut), (0, 0)))
-            came_down = jnp.pad(came_down, ((cut, 0), (0, 0)))
         going_up = (terms[step - 1] + came_up.astype(jnp.float32)).astype(jnp.bfloat16)
-        going_down = (terms[1 - step] + came_down.astype(jnp.float32)).astype(jnp.bfloat16)
+        going_down = terms[1 - step] if came_down is None else terms[1 - step] + came_down.astype(jnp.float32)
+        going_down = going_down.astype(jnp.bfloat16)
         if step == half:
             going_up, going_down, near_up = lax.optimization_barrier((going_up, going_down, near_up))
-            grad_out = rows_of([([near_up], 1 - half), ([near_down], half - 1), ([far_up, far_down], half)], grad_out, [sent_up])
+            grad_out = rows_of([([near_up], 1 - half), ([near_down], half - 1), ([far], half)], grad_out)
             grad_mine = grad_out[0].reshape(width, rows)
             came[2], grad_other = lax.optimization_barrier((came[2], grad_out[1]))
             grad_other = swap(grad_other, 1).reshape(width, rows)
@@ -623,8 +594,7 @@
             terms.update(products(half - step + 1, [in_hbm(array) for array in both_cores(arrived)]))
         else:
             going_up, going_down = lax.optimization_barrier((going_up, going_down))
-        came_up = lax.ppermute(going_up, "fsdp", ahead)
-        came_down = lax.ppermute(going_down, "fsdp", behind)
+        came_up, came_down = send(going_up, 0), send(going_down, 1)
     for low, high in zip(bounds, bounds[1:]):
         grads = backward(query_key_value, grad_mine, grad_other, main_probs, slot_probs, low, high, grads)
     came_up, came_down, grads = lax.optimization_barrier((came_up, came_down, grads))

time: 123 us -> 120 us (0.976)
  local copies, waits for them, and re-layouts: 4.91 us -> 2.61 us
    unnamed x20 -> x22, local copies, waits for them, and re-layouts: 3.98 us -> 1.71 us
    ppermute x16 -> x14, starting transfers between devices: 17.5 us -> 15.4 us  [send(): return lax.ppermute(array, ('dp', 'fsdp'), streams[stream])]
    ppermute x13, starting transfers between devices: 5.98 us -> 8.11 us  [swap(): return lax.ppermute(array, 'dp', [(i, i ^ bit) for i in range(members)])]
    pallas_call x5 -> x4, Pallas kernels: 24 us -> 22.3 us  [partial_products(): pl.pallas_call(functools.partial(partial_kernel, not bases, turned_round,...]
    pallas_call x3, Pallas kernels: 8.13 us -> 9.73 us  [backward(): pl.pallas_call(backward_kernel, grid=(high - low,), in_specs=[pl.BlockSpe...]
    ppermute x16 -> x14, waiting for transfers between devices: 12.8 us -> 13.5 us  [send(): return lax.ppermute(array, ('dp', 'fsdp'), streams[stream])]
  transfers between devices with their start and end apart: 29 -> 27, of which waited for: 15 -> 13; matrix products, arithmetic and copies ran while one was open for 1% -> 1% of each run, Pallas kernels for 54% -> 55%
where the time goes in v8:
time: 120 us
  Pallas kernels  67.6 us (56%)
  waiting for transfers between devices  24.3 us (20%)
  starting transfers between devices  23.5 us (20%)
  local copies, waits for them, and re-layouts  2.61 us (2%)
    pallas_call x4, Pallas kernels, partial_products(): pl.pallas_call(functools.partial(partial_kernel, not bases, turned_round,...  22.3 us
    ppermute x14, starting transfers between devices, send(): return lax.ppermute(array, ('dp', 'fsdp'), streams[stream])  15.4 us
    pallas_call x2, Pallas kernels, grad_out_rows(): pl.pallas_call(functools.partial(grad_out_kernel, sizes, split, total), g...  14.3 us
    ppermute x14, waiting for transfers between devices, send(): return lax.ppermute(array, ('dp', 'fsdp'), streams[stream])  13.5 us
    ppermute x13, waiting for transfers between devices, swap(): return lax.ppermute(array, 'dp', [(i, i ^ bit) for i in range(members)])  10.7 us
    pallas_call x3, Pallas kernels, backward(): pl.pallas_call(backward_kernel, grid=(high - low,), in_specs=[pl.BlockSpe...  9.73 us
    ppermute x13, starting transfers between devices, swap(): return lax.ppermute(array, 'dp', [(i, i ^ bit) for i in range(members)])  8.11 us
    pallas_call x1, Pallas kernels, forward(): pl.pallas_call(forward_kernel, grid_spec=pltpu.PrefetchScalarGridSpec(num...  7.44 us
  transfers between devices with their start and end apart: 27, of which 13 were waited for; matrix products, arithmetic and copies ran while one was open for 1% of the time, Pallas kernels for 55%

profile of v8, /device:TPU:0, one launch (start us, length us, event | category | flops | bytes accessed | tf_op | source)
XLA Modules:
  0.0 119.6 jit_solution(18430456750089684384)
XLA Ops:
  0.7 1.1 own_half_of_weight.1.refs_0_
  1.8 3.1 %collective-permute-start.1 = (bf16[208,1664]{1,0:T(8,128)(2,1)S(1)}, bf16[208,1664]{1,0:T(8,128)(2,1)}, u32[]{:S(2)}, u32[]{:S(2)}) collective-permute-start(bf16[208,1664]{1,0:T(8,128)(2,1)S(1)} %own_half_of_weight.1.refs_0_), channel_id=1, source_target_pairs={{0,2},{2,4},{4,6},{6,7},{7,5},{5,3},{3,1},{1,0},{8,9},{10,8},{12,1... | collective-permute-start | bytes 2076680 | tf_op jit(solution)/shard_map/ppermute | solution.py:473
  4.9 0.7 reshape.18.layer_scale
  5.6 2.5 %peer_windows.1 = (bf16[176,1664]{1,0:T(8,128)(2,1)}, bf16[272,1664]{1,0:T(8,128)(2,1)}) custom-call(s32[1]{0:T(128)} %bitcast.7.starts, bf16[448,3200]{1,0:T(8,128)(2,1)} %cotangent.1, f32[1,3200]{1,0:T(1,128)S(1)} %reshape.18.layer_scale), custom_call_target="tpu_custom_call" | custom-call | flops 34500001792 | bytes 1000 | tf_op jit(solution)/shard_map/peer_windows/pallas_call | solution.py:59
  8.2 2.0 %collective-permute-start.3 = (bf16[176,1664]{1,0:T(8,128)(2,1)}, bf16[176,1664]{1,0:T(8,128)(2,1)}, u32[]{:S(2)}, u32[]{:S(2)}) collective-permute-start(bf16[176,1664]{1,0:T(8,128)(2,1)} %get-tuple-element.92), channel_id=1, source_target_pairs={{0,16},{8,24},{16,0},{24,8},{1,17},{9,25},{17,1},{25,9},{2,18},{10... | collective-permute-start | bytes 1757192 | tf_op jit(solution)/shard_map/ppermute | solution.py:476
  10.2 6.0 %scaled_cotangent.1.refs_2_.turned = bf16[3200,512]{1,0:T(8,128)(2,1)} custom-call(bf16[448,3200]{1,0:T(8,128)(2,1)} %cotangent.1, f32[1,3200]{1,0:T(1,128)S(1)} %reshape.18.layer_scale), custom_call_target="tpu_custom_call" | custom-call | flops 34500001792 | bytes 1000 | tf_op jit(solution)/shard_map/scaled_cotangent/pallas_call | solution.py:90
  16.2 7.4 %attention_forward.1 = (bf16[1664,448]{1,0:T(8,128)(2,1)}, f32[13,256,256]{2,1,0:T(8,128)}, f32[13,192,192]{2,1,0:T(8,128)}) custom-call(s32[4]{0:T(128)S(1)} %dynamic-slice_bitcast_fusion.counts, bf16[3,448,1664]{2,1,0:T(8,128)(2,1)S(1)} %copy-done.2), custom_call_target="tpu_custom_call" | custom-call | flops 34500001792 | bytes 1000 | tf_op jit(solution)/shard_map/attention_forward/pallas_call | solution.py:179
  23.7 0.5 collective-permute-start.4
  24.2 1.2 collective-permute-start
  25.4 1.6 %collective-permute-start.6 = (bf16[208,1664]{1,0:T(8,128)(2,1)}, bf16[208,1664]{1,0:T(8,128)(2,1)}, u32[]{:S(2)}, u32[]{:S(2)}) collective-permute-start(bf16[208,1664]{1,0:T(8,128)(2,1)} %collective-permute-done.1.refs_1_), channel_id=1, source_target_pairs={{0,2},{2,4},{4,6},{6,7},{7,5},{5,3},{3,1},{1,0},{8,9},{10,8},{12,1... | collective-permute-start | bytes 2076680 | tf_op jit(solution)/shard_map/ppermute | solution.py:473
  27.0 0.4 collective-permute-start.7
  27.5 3.1 %attended_chunks.1 = (bf16[3,208,448]{2,1,0:T(8,128)(2,1)}, bf16[2,208,448]{2,1,0:T(8,128)(2,1)}, bf16[3,208,448]{2,1,0:T(8,128)(2,1)S(1)}) custom-call(s32[8]{0:T(128)S(1)} %stack.79.order, bf16[8,208,448]{2,1,0:T(8,128)(2,1)} %bitcast.28), custom_call_target="tpu_custom_call" | custom-call | flops 1150000000 | bytes 1000 | tf_op jit(solution)/shard_map/attended_chunks/pallas_call | solution.py:117
  30.6 0.8 copy-done.6
  31.5 0.5 collective-permute-done.4.refs_1_
  32.2 7.7 %projection_chip.1 = (bf16[208,896]{1,0:T(8,128)(2,1)}, bf16[208,896]{1,0:T(8,128)(2,1)}, bf16[208,896]{1,0:T(8,128)(2,1)}, bf16[208,896]{1,0:T(8,128)(2,1)}, bf...) custom-call(s32[8]{0:T(128)S(1)} %stack.79.order, ...), custom_call_target="tpu_custom_call" | custom-call | flops 3449999872 | bytes 1000 | tf_op jit(solution)/shard_map/projection_chip/pallas_call | solution.py:422
  39.9 4.2 %collective-permute-done.6.refs_3_ = bf16[208,1664]{1,0:T(8,128)(2,1)} collective-permute-done((bf16[208,1664]{1,0:T(8,128)(2,1)}, bf16[208,1664]{1,0:T(8,128)(2,1)}, u32[]{:S(2)}, u32[]{:S(2)}) %collective-permute-start.6) | collective-permute-done | bytes 692256 | tf_op jit(solution)/shard_map/ppermute | solution.py:473
  44.1 0.6 collective-permute-start.9
  44.7 1.4 %collective-permute-start.10 = (bf16[208,1664]{1,0:T(8,128)(2,1)}, bf16[208,1664]{1,0:T(8,128)(2,1)}, u32[]{:S(2)}, u32[]{:S(2)}) collective-permute-start(bf16[208,1664]{1,0:T(8,128)(2,1)} %collective-permute-done.7.refs_4_), channel_id=1, source_target_pairs={{0,1},{2,0},{4,2},{6,4},{7,6},{5,7},{3,5},{1,3},{8,10},{10,12},{12... | collective-permute-start | bytes 2076680 | tf_op jit(solution)/shard_map/ppermute | solution.py:473
  46.1 0.5 collective-permute-done.refs_3_
  46.6 1.2 collective-permute-start.5
  47.9 0.5 collective-permute-start.13
  48.4 8.2 %grad_out_rows.2 = (f32[8,208,448]{2,1,0:T(8,128)}, bf16[8,208,448]{2,1,0:T(8,128)(2,1)}) custom-call(s32[6]{0:T(128)S(1)} %stack.82.info, bf16[3200,512]{1,0:T(8,128)(2,1)} %scaled_cotangent.1.refs_2_.turned, bf16[3200,512]{1,0:T(8,128)(2,1)S(1)} %collective-permute-done.8.refs_3_.turned_other, bf16[208,1664]{1,0:T(8,128)(2,1)} %copy-done.5, ...), custom_call_target="tpu_custom_call" | custom-call | flops 4312500224 | bytes 1000 | tf_op jit(solution)/shard_map/grad_out_rows/pallas_call | solution.py:297
  56.6 5.8 %collective-permute-done.9.refs_0_ = bf16[208,1664]{1,0:T(8,128)(2,1)} collective-permute-done((bf16[208,1664]{1,0:T(8,128)(2,1)}, bf16[208,1664]{1,0:T(8,128)(2,1)}, u32[]{:S(2)}, u32[]{:S(2)}) %collective-permute-start.9) | collective-permute-done | bytes 692256 | tf_op jit(solution)/shard_map/ppermute | solution.py:473
  62.6 1.4 %collective-permute-start.15 = (bf16[208,1664]{1,0:T(8,128)(2,1)}, bf16[208,1664]{1,0:T(8,128)(2,1)}, u32[]{:S(2)}, u32[]{:S(2)}) collective-permute-start(bf16[208,1664]{1,0:T(8,128)(2,1)} %collective-permute-done.9.refs_0_), channel_id=1, source_target_pairs={{0,2},{2,4},{4,6},{6,7},{7,5},{5,3},{3,1},{1,0},{8,9},{10,8},{12,1... | collective-permute-start | bytes 2076680 | tf_op jit(solution)/shard_map/ppermute | solution.py:473
  64.0 1.2 collective-permute-start.14
  65.3 5.1 %projection_peers.3 = (f32[208,896]{1,0:T(8,128)S(1)}, f32[208,896]{1,0:T(8,128)S(1)}, f32[208,896]{1,0:T(8,128)S(1)}) custom-call(s32[3]{0:T(128)S(1)} %pad_add_fusion.1.order, s32[1]{0:T(128)} %bitcast.3.start, bf16[3,208,448]{2,1,0:T(8,128)(2,1)} %collective-permute-done.5.refs_0_, bf16[3,208,448]{2,1,0:T(8,128)(2,1)} %collective-permute-done.11.refs_1_, ...), custom_call_target="tpu_custom_call" | custom-call | flops 1724999936 | bytes 1000 | tf_op jit(solution)/shard_map/projection_peers/pallas_call | solution.py:422
  70.4 5.8 %collective-permute-done.14.refs_0_ = bf16[2,208,448]{2,1,0:T(8,128)(2,1)} collective-permute-done((bf16[2,208,448]{2,1,0:T(8,128)(2,1)}, bf16[2,208,448]{2,1,0:T(8,128)(2,1)}, u32[]{:S(2)}, u32[]{:S(2)}) %collective-permute-start.14) | collective-permute-done | bytes 372768 | tf_op jit(solution)/shard_map/ppermute | solution.py:476
  76.3 0.5 collective-permute-start.16
  76.9 1.2 %collective-permute-start.20 = (bf16[3,208,448]{2,1,0:T(8,128)(2,1)S(1)}, bf16[3,208,448]{2,1,0:T(8,128)(2,1)}, u32[]{:S(2)}, u32[]{:S(2)}) collective-permute-start(bf16[3,208,448]{2,1,0:T(8,128)(2,1)S(1)} %copy-done.7), channel_id=1, source_target_pairs={{0,16},{8,24},{16,0},{24,8},{1,17},{9,25},{17,1},{25,9},{2,18},{10... | collective-permute-start | bytes 1677320 | tf_op jit(solution)/shard_map/ppermute | solution.py:476
  78.2 4.3 %projection_peers.4 = (f32[208,896]{1,0:T(8,128)S(1)}, f32[208,896]{1,0:T(8,128)S(1)}) custom-call(s32[2]{0:T(128)S(1)} %pad_add_fusion.2.order, s32[1]{0:T(128)} %bitcast.3.start, bf16[2,208,448]{2,1,0:T(8,128)(2,1)} %collective-permute-done.14.refs_0_, bf16[2,208,448]{2,1,0:T(8,128)(2,1)S(1)} %collective-permute-done.17.refs_1_, ...), custom_call_target="tpu_custom_call" | custom-call | flops 1724999936 | bytes 1000 | tf_op jit(solution)/shard_map/projection_peers/pallas_call | solution.py:422
  82.5 1.3 %collective-permute-done.16 = bf16[208,896]{1,0:T(8,128)(2,1)S(1)} collective-permute-done((bf16[208,896]{1,0:T(8,128)(2,1)S(1)}, bf16[208,896]{1,0:T(8,128)(2,1)S(1)}, u32[]{:S(2)}, u32[]{:S(2)}) %collective-permute-start.16) | collective-permute-done | bytes 372768 | tf_op jit(solution)/shard_map/ppermute | solution.py:473
  83.9 0.6 collective-permute-start.18
  84.5 1.5 %collective-permute-start.19 = (bf16[208,896]{1,0:T(8,128)(2,1)S(1)}, bf16[208,896]{1,0:T(8,128)(2,1)S(1)}, u32[]{:S(2)}, u32[]{:S(2)}) collective-permute-start(bf16[208,896]{1,0:T(8,128)(2,1)S(1)} %convert_element_type.39), channel_id=1, source_target_pairs={{0,1},{2,0},{4,2},{6,4},{7,6},{5,7},{3,5},{1,3},{8,10},{10,12},{12... | collective-permute-start | bytes 1118216 | tf_op jit(solution)/shard_map/ppermute | solution.py:473
  86.1 6.0 %grad_out_rows.3 = (f32[8,208,448]{2,1,0:T(8,128)}, bf16[8,208,448]{2,1,0:T(8,128)(2,1)}) custom-call(s32[4]{0:T(128)S(1)} %pad_add_fusion.3.info, bf16[3200,512]{1,0:T(8,128)(2,1)} %scaled_cotangent.1.refs_2_.turned, bf16[3200,512]{1,0:T(8,128)(2,1)S(1)} %collective-permute-done.8.refs_3_.turned_other, ...), custom_call_target="tpu_custom_call", output_to_operand_aliasing={{0}: (6, {}), {1}: (7, {})} | custom-call | flops 115000000 | bytes 1000 | tf_op jit(solution)/shard_map/grad_out_rows/pallas_call | solution.py:297
  92.1 2.2 %collective-permute-done.20.refs_0_ = bf16[3,208,448]{2,1,0:T(8,128)(2,1)} collective-permute-done((bf16[3,208,448]{2,1,0:T(8,128)(2,1)S(1)}, bf16[3,208,448]{2,1,0:T(8,128)(2,1)}, u32[]{:S(2)}, u32[]{:S(2)}) %collective-permute-start.20) | collective-permute-done | bytes 559136 | tf_op jit(solution)/shard_map/ppermute | solution.py:476
  94.3 0.9 collective-permute-done.18
  95.5 0.8 collective-permute-start.22
  96.4 1.3 %collective-permute-start.23 = (bf16[208,896]{1,0:T(8,128)(2,1)S(1)}, bf16[208,896]{1,0:T(8,128)(2,1)S(1)}, u32[]{:S(2)}, u32[]{:S(2)}) collective-permute-start(bf16[208,896]{1,0:T(8,128)(2,1)S(1)} %add_convert_fusion.2), channel_id=1, source_target_pairs={{0,1},{2,0},{4,2},{6,4},{7,6},{5,7},{3,5},{1,3},{8,10},{10,12},{12... | collective-permute-start | bytes 1118216 | tf_op jit(solution)/shard_map/ppermute | solution.py:473
  97.7 1.3 %collective-permute-done.21.refs_1_ = bf16[3,208,448]{2,1,0:T(8,128)(2,1)S(1)} collective-permute-done((bf16[3,208,448]{2,1,0:T(8,128)(2,1)}, bf16[3,208,448]{2,1,0:T(8,128)(2,1)S(1)}, u32[]{:S(2)}, u32[]{:S(2)}) %collective-permute-start.21) | collective-permute-done | bytes 559136 | tf_op jit(solution)/shard_map/ppermute | solution.py:476
  99.0 0.8 copy-done.8
  99.8 5.3 %projection_peers.5 = (f32[208,896]{1,0:T(8,128)S(1)}, f32[208,896]{1,0:T(8,128)S(1)}, f32[208,896]{1,0:T(8,128)S(1)}) custom-call(s32[3]{0:T(128)S(1)} %pad_add_fusion.order, s32[1]{0:T(128)} %bitcast.3.start, bf16[3,208,448]{2,1,0:T(8,128)(2,1)} %collective-permute-done.20.refs_0_, bf16[3,208,448]{2,1,0:T(8,128)(2,1)} %copy-done.8, ...), custom_call_target="tpu_custom_call" | custom-call | flops 1724999936 | bytes 1000 | tf_op jit(solution)/shard_map/projection_peers/pallas_call | solution.py:422
  105.1 1.3 %collective-permute-done.22 = bf16[208,896]{1,0:T(8,128)(2,1)S(1)} collective-permute-done((bf16[208,896]{1,0:T(8,128)(2,1)S(1)}, bf16[208,896]{1,0:T(8,128)(2,1)S(1)}, u32[]{:S(2)}, u32[]{:S(2)}) %collective-permute-start.22) | collective-permute-done | bytes 372768 | tf_op jit(solution)/shard_map/ppermute | solution.py:473
  106.6 0.9 collective-permute-start.24
  107.6 1.1 collective-permute-start.25
  108.7 4.8 %attention_backward.3.rest_0_ = bf16[3,448,1664]{2,1,0:T(8,128)(2,1)} custom-call(bf16[3,448,1664]{2,1,0:T(8,128)(2,1)} %qkv.7, f32[1664,448]{1,0:T(8,128)S(1)} %bitcast.19, bf16[1664,448]{1,0:T(8,128)(2,1)S(1)} %bitcast.24, f32[13,256,256]{2,1,0:T(8,128)S(1)} %copy-done.3, f32[13,192,192]{2,1,0:T(8,128)S(1)} %copy-done.4), custom_call_target="tpu_custom_call" | custom-call | flops 3449999872 | bytes 1000 | tf_op jit(solution)/shard_map/attention_backward/pallas_call | solution.py:229
  113.6 2.5 %attention_backward.4.rest_0_ = bf16[3,448,1664]{2,1,0:T(8,128)(2,1)} custom-call(bf16[3,448,1664]{2,1,0:T(8,128)(2,1)S(1)} %bitcast.23, f32[1664,448]{1,0:T(8,128)S(1)} %bitcast.20, bf16[1664,448]{1,0:T(8,128)(2,1)S(1)} %bitcast.25, f32[13,256,256]{2,1,0:T(8,128)S(1)} %copy-done.3, f32[13,192,192]{2,1,0:T(8,128)S(1)} %copy-done.4, ...), custom_call_target="tpu_custom_call", output_to_operand_aliasing={{}: (5, {})} | custom-call | flops 2300000000 | bytes 1000 | tf_op jit(solution)/shard_map/attention_backward/pallas_call | solution.py:229
  116.1 2.4 %attention_backward.5 = bf16[3,448,1664]{2,1,0:T(8,128)(2,1)} custom-call(bf16[3,448,1664]{2,1,0:T(8,128)(2,1)S(1)} %bitcast.23, f32[1664,448]{1,0:T(8,128)S(1)} %bitcast.21, bf16[1664,448]{1,0:T(8,128)(2,1)S(1)} %bitcast.26, f32[13,256,256]{2,1,0:T(8,128)S(1)} %copy-done.3, f32[13,192,192]{2,1,0:T(8,128)S(1)} %copy-done.4, ...), custom_call_target="tpu_custom_call", output_to_operand_aliasing={{}: (5, {})} | custom-call | flops 2300000000 | bytes 1000 | tf_op jit(solution)/shard_map/attention_backward/pallas_call | solution.py:229
  118.5 1.1 last_sum.1
  (59 shorter events, 1.9 us)
Async XLA Ops:
  0.6 15.6 %copy-start = (s32[4,1,4]{2,1,0:T(1,128)S(1)}, s32[4,1,4]{2,1,0:T(1,128)}, u32[]{:S(2)}) copy-start(s32[4,1,4]{2,1,0:T(1,128)} %param.9) | copy-start | bytes 196
  1.8 6.4 %copy-start.5 = (bf16[208,1664]{1,0:T(8,128)(2,1)}, bf16[208,1664]{1,0:T(8,128)(2,1)S(1)}, u32[]{:S(2)}) copy-start(bf16[208,1664]{1,0:T(8,128)(2,1)S(1)} %own_half_of_weight.1.refs_0_) | copy-start | bytes 2076676
  1.8 21.9 %collective-permute-start.1 = (bf16[208,1664]{1,0:T(8,128)(2,1)S(1)}, bf16[208,1664]{1,0:T(8,128)(2,1)}, u32[]{:S(2)}, u32[]{:S(2)}) collective-permute-start(bf16[208,1664]{1,0:T(8,128)(2,1)S(1)} %own_half_of_weight.1.refs_0_), channel_id=1, source_target_pairs={{0,2},{2,4},{4,6},{6,7},{7,5},{5,3},{3,1},{1,0},{8,9},{10,8},{12,1... | collective-permute-start | bytes 2076680 | tf_op jit(solution)/shard_map/ppermute | solution.py:473
  4.9 18.8 %collective-permute-start.2 = (bf16[208,1664]{1,0:T(8,128)(2,1)S(1)}, bf16[208,1664]{1,0:T(8,128)(2,1)}, u32[]{:S(2)}, u32[]{:S(2)}) collective-permute-start(bf16[208,1664]{1,0:T(8,128)(2,1)S(1)} %own_half_of_weight.1.refs_0_), channel_id=1, source_target_pairs={{0,1},{2,0},{4,2},{6,4},{7,6},{5,7},{3,5},{1,3},{8,10},{10,12},{12... | collective-permute-start | bytes 2076680 | tf_op jit(solution)/shard_map/ppermute | solution.py:473
  8.2 15.5 %collective-permute-start.3 = (bf16[176,1664]{1,0:T(8,128)(2,1)}, bf16[176,1664]{1,0:T(8,128)(2,1)}, u32[]{:S(2)}, u32[]{:S(2)}) collective-permute-start(bf16[176,1664]{1,0:T(8,128)(2,1)} %get-tuple-element.92), channel_id=1, source_target_pairs={{0,16},{8,24},{16,0},{24,8},{1,17},{9,25},{17,1},{25,9},{2,18},{10... | collective-permute-start | bytes 1757192 | tf_op jit(solution)/shard_map/ppermute | solution.py:476
  10.2 6.0 %copy-start.2 = (bf16[3,448,1664]{2,1,0:T(8,128)(2,1)S(1)}, bf16[3,448,1664]{2,1,0:T(8,128)(2,1)}, u32[]{:S(2)}) copy-start(bf16[3,448,1664]{2,1,0:T(8,128)(2,1)} %qkv.7) | copy-start | bytes 13418500
  23.7 8.6 %collective-permute-start.8 = (bf16[3200,512]{1,0:T(8,128)(2,1)}, bf16[3200,512]{1,0:T(8,128)(2,1)S(1)}, u32[]{:S(2)}, u32[]{:S(2)}) collective-permute-start(bf16[3200,512]{1,0:T(8,128)(2,1)} %scaled_cotangent.1.refs_2_.turned), channel_id=1, source_target_pairs={{0,8},{8,0},{16,24},{24,16},{1,9},{9,1},{17,25},{25,17},{2,10},{10... | collective-permute-start | bytes 9830408 | tf_op jit(solution)/shard_map/ppermute | solution.py:476
  23.7 8.2 %collective-permute-start.4 = (bf16[8,208,448]{2,1,0:T(8,128)(2,1)}, bf16[8,208,448]{2,1,0:T(8,128)(2,1)}, u32[]{:S(2)}, u32[]{:S(2)}) collective-permute-start(bf16[8,208,448]{2,1,0:T(8,128)(2,1)} %bitcast.27), channel_id=1, source_target_pairs={{0,8},{8,0},{16,24},{24,16},{1,9},{9,1},{17,25},{25,17},{2,10},{10... | collective-permute-start | bytes 4472840 | tf_op jit(solution)/shard_map/ppermute | solution.py:476
  24.2 22.4 %collective-permute-start = (bf16[272,1664]{1,0:T(8,128)(2,1)}, bf16[272,1664]{1,0:T(8,128)(2,1)}, u32[]{:S(2)}, u32[]{:S(2)}) collective-permute-start(bf16[272,1664]{1,0:T(8,128)(2,1)} %get-tuple-element.90), channel_id=1, source_target_pairs={{0,16},{8,24},{16,0},{24,8},{1,17},{9,25},{17,1},{25,9},{2,18},{10... | collective-permute-start | bytes 2715656 | tf_op jit(solution)/shard_map/ppermute | solution.py:476
  25.4 18.6 %collective-permute-start.6 = (bf16[208,1664]{1,0:T(8,128)(2,1)}, bf16[208,1664]{1,0:T(8,128)(2,1)}, u32[]{:S(2)}, u32[]{:S(2)}) collective-permute-start(bf16[208,1664]{1,0:T(8,128)(2,1)} %collective-permute-done.1.refs_1_), channel_id=1, source_target_pairs={{0,2},{2,4},{4,6},{6,7},{7,5},{5,3},{3,1},{1,0},{8,9},{10,8},{12,1... | collective-permute-start | bytes 2076680 | tf_op jit(solution)/shard_map/ppermute | solution.py:473
  27.0 17.1 %collective-permute-start.7 = (bf16[208,1664]{1,0:T(8,128)(2,1)}, bf16[208,1664]{1,0:T(8,128)(2,1)}, u32[]{:S(2)}, u32[]{:S(2)}) collective-permute-start(bf16[208,1664]{1,0:T(8,128)(2,1)} %collective-permute-done.2.refs_2_), channel_id=1, source_target_pairs={{0,1},{2,0},{4,2},{6,4},{7,6},{5,7},{3,5},{1,3},{8,10},{10,12},{12... | collective-permute-start | bytes 2076680 | tf_op jit(solution)/shard_map/ppermute | solution.py:473
  30.6 0.8 copy-start.6
  44.1 18.3 %collective-permute-start.9 = (bf16[208,1664]{1,0:T(8,128)(2,1)}, bf16[208,1664]{1,0:T(8,128)(2,1)}, u32[]{:S(2)}, u32[]{:S(2)}) collective-permute-start(bf16[208,1664]{1,0:T(8,128)(2,1)} %collective-permute-done.6.refs_3_), channel_id=1, source_target_pairs={{0,2},{2,4},{4,6},{6,7},{7,5},{5,3},{3,1},{1,0},{8,9},{10,8},{12,1... | collective-permute-start | bytes 2076680 | tf_op jit(solution)/shard_map/ppermute | solution.py:473
  44.7 17.7 %collective-permute-start.10 = (bf16[208,1664]{1,0:T(8,128)(2,1)}, bf16[208,1664]{1,0:T(8,128)(2,1)}, u32[]{:S(2)}, u32[]{:S(2)}) collective-permute-start(bf16[208,1664]{1,0:T(8,128)(2,1)} %collective-permute-done.7.refs_4_), channel_id=1, source_target_pairs={{0,1},{2,0},{4,2},{6,4},{7,6},{5,7},{3,5},{1,3},{8,10},{10,12},{12... | collective-permute-start | bytes 2076680 | tf_op jit(solution)/shard_map/ppermute | solution.py:473
  46.6 15.8 %collective-permute-start.5 = (bf16[3,208,448]{2,1,0:T(8,128)(2,1)}, bf16[3,208,448]{2,1,0:T(8,128)(2,1)}, u32[]{:S(2)}, u32[]{:S(2)}) collective-permute-start(bf16[3,208,448]{2,1,0:T(8,128)(2,1)} %get-tuple-element.101), channel_id=1, source_target_pairs={{0,16},{8,24},{16,0},{24,8},{1,17},{9,25},{17,1},{25,9},{2,18},{10... | collective-permute-start | bytes 1677320 | tf_op jit(solution)/shard_map/ppermute | solution.py:476
  47.9 17.4 %collective-permute-start.12 = (bf16[176,1664]{1,0:T(8,128)(2,1)}, bf16[176,1664]{1,0:T(8,128)(2,1)}, u32[]{:S(2)}, u32[]{:S(2)}) collective-permute-start(bf16[176,1664]{1,0:T(8,128)(2,1)} %collective-permute-done.3.refs_2_), channel_id=1, source_target_pairs={{0,8},{8,0},{16,24},{24,16},{1,9},{9,1},{17,25},{25,17},{2,10},{10... | collective-permute-start | bytes 1757192 | tf_op jit(solution)/shard_map/ppermute | solution.py:476
  47.9 17.4 %collective-permute-start.13 = (bf16[272,1664]{1,0:T(8,128)(2,1)}, bf16[272,1664]{1,0:T(8,128)(2,1)}, u32[]{:S(2)}, u32[]{:S(2)}) collective-permute-start(bf16[272,1664]{1,0:T(8,128)(2,1)} %collective-permute-done.refs_3_), channel_id=1, source_target_pairs={{0,8},{8,0},{16,24},{24,16},{1,9},{9,1},{17,25},{25,17},{2,10},{10... | collective-permute-start | bytes 2715656 | tf_op jit(solution)/shard_map/ppermute | solution.py:476
  62.5 2.8 %collective-permute-start.11 = (bf16[3,208,448]{2,1,0:T(8,128)(2,1)}, bf16[3,208,448]{2,1,0:T(8,128)(2,1)}, u32[]{:S(2)}, u32[]{:S(2)}) collective-permute-start(bf16[3,208,448]{2,1,0:T(8,128)(2,1)} %collective-permute-done.5.refs_0_), channel_id=1, source_target_pairs={{0,8},{8,0},{16,24},{24,16},{1,9},{9,1},{17,25},{25,17},{2,10},{10... | collective-permute-start | bytes 1677320 | tf_op jit(solution)/shard_map/ppermute | solution.py:476
  62.6 13.6 %collective-permute-start.15 = (bf16[208,1664]{1,0:T(8,128)(2,1)}, bf16[208,1664]{1,0:T(8,128)(2,1)}, u32[]{:S(2)}, u32[]{:S(2)}) collective-permute-start(bf16[208,1664]{1,0:T(8,128)(2,1)} %collective-permute-done.9.refs_0_), channel_id=1, source_target_pairs={{0,2},{2,4},{4,6},{6,7},{7,5},{5,3},{3,1},{1,0},{8,9},{10,8},{12,1... | collective-permute-start | bytes 2076680 | tf_op jit(solution)/shard_map/ppermute | solution.py:473
  64.0 12.2 %collective-permute-start.14 = (bf16[2,208,448]{2,1,0:T(8,128)(2,1)}, bf16[2,208,448]{2,1,0:T(8,128)(2,1)}, u32[]{:S(2)}, u32[]{:S(2)}) collective-permute-start(bf16[2,208,448]{2,1,0:T(8,128)(2,1)} %get-tuple-element.129), channel_id=1, source_target_pairs={{0,16},{8,24},{16,0},{24,8},{1,17},{9,25},{17,1},{25,9},{2,18},{10... | collective-permute-start | bytes 1118216 | tf_op jit(solution)/shard_map/ppermute | solution.py:476
  65.3 11.6 %copy-start.7 = (bf16[3,208,448]{2,1,0:T(8,128)(2,1)S(1)}, bf16[3,208,448]{2,1,0:T(8,128)(2,1)}, u32[]{:S(2)}) copy-start(bf16[3,208,448]{2,1,0:T(8,128)(2,1)} %copy-done.6) | copy-start | bytes 1677316
  76.3 2.0 %collective-permute-start.17 = (bf16[2,208,448]{2,1,0:T(8,128)(2,1)}, bf16[2,208,448]{2,1,0:T(8,128)(2,1)S(1)}, u32[]{:S(2)}, u32[]{:S(2)}) collective-permute-start(bf16[2,208,448]{2,1,0:T(8,128)(2,1)} %collective-permute-done.14.refs_0_), channel_id=1, source_target_pairs={{0,8},{8,0},{16,24},{24,16},{1,9},{9,1},{17,25},{25,17},{2,10},{10... | collective-permute-start | bytes 1118216 | tf_op jit(solution)/shard_map/ppermute | solution.py:476
  76.3 7.6 %collective-permute-start.16 = (bf16[208,896]{1,0:T(8,128)(2,1)S(1)}, bf16[208,896]{1,0:T(8,128)(2,1)S(1)}, u32[]{:S(2)}, u32[]{:S(2)}) collective-permute-start(bf16[208,896]{1,0:T(8,128)(2,1)S(1)} %convert_element_type.36), channel_id=1, source_target_pairs={{0,2},{2,4},{4,6},{6,7},{7,5},{5,3},{3,1},{1,0},{8,9},{10,8},{12,1... | collective-permute-start | bytes 1118216 | tf_op jit(solution)/shard_map/ppermute | solution.py:473
  76.9 17.4 %collective-permute-start.20 = (bf16[3,208,448]{2,1,0:T(8,128)(2,1)S(1)}, bf16[3,208,448]{2,1,0:T(8,128)(2,1)}, u32[]{:S(2)}, u32[]{:S(2)}) collective-permute-start(bf16[3,208,448]{2,1,0:T(8,128)(2,1)S(1)} %copy-done.7), channel_id=1, source_target_pairs={{0,16},{8,24},{16,0},{24,8},{1,17},{9,25},{17,1},{25,9},{2,18},{10... | collective-permute-start | bytes 1677320 | tf_op jit(solution)/shard_map/ppermute | solution.py:476
  83.9 11.3 %collective-permute-start.18 = (bf16[208,896]{1,0:T(8,128)(2,1)S(1)}, bf16[208,896]{1,0:T(8,128)(2,1)S(1)}, u32[]{:S(2)}, u32[]{:S(2)}) collective-permute-start(bf16[208,896]{1,0:T(8,128)(2,1)S(1)} %add_convert_fusion.4), channel_id=1, source_target_pairs={{0,2},{2,4},{4,6},{6,7},{7,5},{5,3},{3,1},{1,0},{8,9},{10,8},{12,1... | collective-permute-start | bytes 1118216 | tf_op jit(solution)/shard_map/ppermute | solution.py:473
  84.5 10.8 %collective-permute-start.19 = (bf16[208,896]{1,0:T(8,128)(2,1)S(1)}, bf16[208,896]{1,0:T(8,128)(2,1)S(1)}, u32[]{:S(2)}, u32[]{:S(2)}) collective-permute-start(bf16[208,896]{1,0:T(8,128)(2,1)S(1)} %convert_element_type.39), channel_id=1, source_target_pairs={{0,1},{2,0},{4,2},{6,4},{7,6},{5,7},{3,5},{1,3},{8,10},{10,12},{12... | collective-permute-start | bytes 1118216 | tf_op jit(solution)/shard_map/ppermute | solution.py:473
  94.3 14.4 %collective-permute-start.26 = (bf16[8,208,448]{2,1,0:T(8,128)(2,1)}, bf16[8,208,448]{2,1,0:T(8,128)(2,1)S(1)}, u32[]{:S(2)}, u32[]{:S(2)}) collective-permute-start(bf16[8,208,448]{2,1,0:T(8,128)(2,1)} %get-tuple-element.165), channel_id=1, source_target_pairs={{0,8},{8,0},{16,24},{24,16},{1,9},{9,1},{17,25},{25,17},{2,10},{10... | collective-permute-start | bytes 4472840 | tf_op jit(solution)/shard_map/ppermute | solution.py:476
  95.4 3.6 %collective-permute-start.21 = (bf16[3,208,448]{2,1,0:T(8,128)(2,1)}, bf16[3,208,448]{2,1,0:T(8,128)(2,1)S(1)}, u32[]{:S(2)}, u32[]{:S(2)}) collective-permute-start(bf16[3,208,448]{2,1,0:T(8,128)(2,1)} %collective-permute-done.20.refs_0_), channel_id=1, source_target_pairs={{0,8},{8,0},{16,24},{24,16},{1,9},{9,1},{17,25},{25,17},{2,10},{10... | collective-permute-start | bytes 1677320 | tf_op jit(solution)/shard_map/ppermute | solution.py:476
  95.5 10.9 %collective-permute-start.22 = (bf16[208,896]{1,0:T(8,128)(2,1)S(1)}, bf16[208,896]{1,0:T(8,128)(2,1)S(1)}, u32[]{:S(2)}, u32[]{:S(2)}) collective-permute-start(bf16[208,896]{1,0:T(8,128)(2,1)S(1)} %add_convert_fusion.3), channel_id=1, source_target_pairs={{0,2},{2,4},{4,6},{6,7},{7,5},{5,3},{3,1},{1,0},{8,9},{10,8},{12,1... | collective-permute-start | bytes 1118216 | tf_op jit(solution)/shard_map/ppermute | solution.py:473
  96.4 12.3 %copy-start.1 = (f32[8,208,448]{2,1,0:T(8,128)S(1)}, f32[8,208,448]{2,1,0:T(8,128)}, u32[]{:S(2)}) copy-start(f32[8,208,448]{2,1,0:T(8,128)} %get-tuple-element.153) | copy-start | bytes 8945668
  96.4 12.3 %copy-start.3 = (f32[13,256,256]{2,1,0:T(8,128)S(1)}, f32[13,256,256]{2,1,0:T(8,128)}, u32[]{:S(2)}) copy-start(f32[13,256,256]{2,1,0:T(8,128)} %get-tuple-element.166.main_probs) | copy-start | bytes 10223620
  96.4 12.3 %copy-start.4 = (f32[13,192,192]{2,1,0:T(8,128)S(1)}, f32[13,192,192]{2,1,0:T(8,128)}, u32[]{:S(2)}) copy-start(f32[13,192,192]{2,1,0:T(8,128)} %get-tuple-element.167.slot_probs) | copy-start | bytes 5750788
  96.4 10.2 %collective-permute-start.23 = (bf16[208,896]{1,0:T(8,128)(2,1)S(1)}, bf16[208,896]{1,0:T(8,128)(2,1)S(1)}, u32[]{:S(2)}, u32[]{:S(2)}) collective-permute-start(bf16[208,896]{1,0:T(8,128)(2,1)S(1)} %add_convert_fusion.2), channel_id=1, source_target_pairs={{0,1},{2,0},{4,2},{6,4},{7,6},{5,7},{3,5},{1,3},{8,10},{10,12},{12... | collective-permute-start | bytes 1118216 | tf_op jit(solution)/shard_map/ppermute | solution.py:473
  99.0 0.8 copy-start.8
  99.8 13.8 %slice-start = ((s8[4472832]{0:T(1024)(128)(4,1)}), s8[4194304]{0:T(1024)(128)(4,1)S(1)}, s32[]{:S(2)}) async-start(s8[4472832]{0:T(1024)(128)(4,1)} %bitcast.22), calls=%async_computation | async-start | bytes 8388608
  106.6 11.8 %collective-permute-start.24 = (bf16[208,896]{1,0:T(8,128)(2,1)S(1)}, bf16[208,896]{1,0:T(8,128)(2,1)S(1)}, u32[]{:S(2)}, u32[]{:S(2)}) collective-permute-start(bf16[208,896]{1,0:T(8,128)(2,1)S(1)} %add_convert_fusion.1), channel_id=1, source_target_pairs={{0,2},{2,4},{4,6},{6,7},{7,5},{5,3},{3,1},{1,0},{8,9},{10,8},{12,1... | collective-permute-start | bytes 1118216 | tf_op jit(solution)/shard_map/ppermute | solution.py:473
  107.6 10.9 %collective-permute-start.25 = (bf16[208,896]{1,0:T(8,128)(2,1)S(1)}, bf16[208,896]{1,0:T(8,128)(2,1)S(1)}, u32[]{:S(2)}, u32[]{:S(2)}) collective-permute-start(bf16[208,896]{1,0:T(8,128)(2,1)S(1)} %add_convert_fusion), channel_id=1, source_target_pairs={{0,1},{2,0},{4,2},{6,4},{7,6},{5,7},{3,5},{1,3},{8,10},{10,12},{12... | collective-permute-start | bytes 1118216 | tf_op jit(solution)/shard_map/ppermute | solution.py:473
  108.7 4.9 %slice-start.1 = ((s8[4472832]{0:T(1024)(128)(4,1)}), s8[278528]{0:T(1024)(128)(4,1)S(1)}, s32[]{:S(2)}) async-start(s8[4472832]{0:T(1024)(128)(4,1)} %bitcast.22), calls=%async_computation.1 | async-start | bytes 557056

commit v9 on v8

--- a/solution.py
+++ b/solution.py
@@ -372,9 +372,10 @@
 
 
 def partial_kernel(chosen, turned_round, sources, parts, count, window, order, start, *refs):
-    attended, columns = refs[:sources], refs[sources:sources * (1 + parts)]
+    per = 1 if chosen or len(turned_round) != 2 else 2
+    attended, columns = refs[:sources * per], refs[sources * per:sources * (per + parts)]
     chunks, held, sems = refs[-3:]
-    bases = refs[sources * (1 + parts):-3 - count]
+    bases = refs[sources * (per + parts):-3 - count]
     outs = refs[-3 - count:-3]
     depth, rows = chunks.shape[2:]
     at = pl.ds(pl.multiple_of(start[0], LANE), window)
@@ -390,7 +391,8 @@
                 some.append(pltpu.make_async_copy(source.at[:, at], target, sems.at[i, count + part]))
             first += source.shape[0]
         for j in range(count):
-            source = attended[i].at[order[j] if chosen else turned_round[j] if i % 2 else j]
+            at_j = order[j] if chosen else turned_round[j] if i % 2 else j
+            source = attended[i].at[at_j] if per == 1 else attended[i * per + at_j].at[0]
             some.append(pltpu.make_async_copy(source, chunks.at[i, j], sems.at[i, j]))
         copies.append(some)
     for some in copies:
@@ -416,15 +418,16 @@
 
 def partial_products(order, start, attended, columns, window, bases=(), turned_round=()):
     _, depth, rows = attended[0].shape
-    parts = len(columns) // len(attended)
-    count, sources = order.shape[0], len(attended)
+    per = 2 if len(turned_round) == 2 else 1
+    parts = len(columns) * per // len(attended)
+    count, sources = order.shape[0], len(attended) // per
     block = pl.BlockSpec((depth, window), lambda j, o, s: (0, 0))
     return pl.pallas_call(
         functools.partial(partial_kernel, not bases, turned_round, sources, parts, count, window),
         grid_spec=pltpu.PrefetchScalarGridSpec(
             num_scalar_prefetch=2,
             grid=(1,),
-            in_specs=[pl.BlockSpec(memory_space=pl.ANY)] * (sources * (1 + parts)) + [block] * len(bases),
+            in_specs=[pl.BlockSpec(memory_space=pl.ANY)] * (sources * (per + parts)) + [block] * len(bases),
             out_specs=[block] * count,
             scratch_shapes=[
                 pltpu.VMEM((sources, count, depth, rows), jnp.bfloat16),
@@ -522,7 +525,10 @@
     turned_other = swap(turned, 1)
     other_columns = [[swap(array, 1) for array in came_columns[0]]]
     attended_other = swap(attended, 1)
-    chunks = list(arrange(flat, attended, sizes))
+    chunks = list(arrange(flat, attended, [n for size in sizes for n in ([1, 1] if size == 2 else [size])]))
+    bounds = [0]
+    for size in sizes:
+        bounds.append(bounds[-1] + (2 if size == 2 else 1))
     attended_other, chunks = lax.optimization_barrier((attended_other, chunks))
     for _ in range(half - 3):
         up.append(send(up[-1], 0))
@@ -537,9 +543,9 @@
 
     late, chunks = lax.optimization_barrier((came_columns[1], chunks))
     came = [[swap(chunks[0], 2 * k) for k in range(1, peers)]]
+    halves = [[swap(chunks[1], 2 * k) for k in range(1, peers)]]
     other_columns.append([swap(array, 1) for array in late])
     came_columns[1] = late
-    came.append([swap(chunks[1], 2 * k) for k in range(1, peers)])
     columns = []
     for k in range(peers - 1):
         for arrays in (came_columns, other_columns):
@@ -556,7 +562,9 @@
     came[0], near_up, near_down = lax.optimization_barrier((came[0], up[-1], down[-1]))
 
     def both_cores(arrays):
-        return [a for c in arrays for a in (c, swap(c, 1))]
+        per = len(arrays) // max(peers - 1, 1)
+        held = [arrays[n:n + per] for n in range(0, len(arrays), per)]
+        return [a for some in held for a in (*some, *[swap(c, 1) for c in some])]
 
     def products(index, taken):
         group = groups[index]
@@ -568,22 +576,23 @@
 
     terms = products(0, both_cores(came[0]))
     first = terms[half].astype(jnp.bfloat16)
-    first, came[1], chunks, far = lax.optimization_barrier((first, came[1], chunks, far))
-    came += [[swap(some, 2 * k) for k in range(1, peers)] for some in chunks[2:]]
-    taken = both_cores(came[1])
+    first, halves[0], chunks, far = lax.optimization_barrier((first, halves[0], chunks, far))
+    halves.append([swap(chunks[2], 2 * k) for k in range(1, peers)])
+    came.append([pair[k] for k in range(peers - 1) for pair in halves])
     came_up, came_down = send(first, 0), None
 
-    bounds = [0, 3, 5, -(-(width // HS) // PAIR)]
+    steps = [0, 3, 5, -(-(width // HS) // PAIR)]
     grads = None
     for step in range(half, 1, -1):
-        if step == half:
-            came_up, following = lax.optimization_barrier((came_up, products(1, taken)))
-            terms.update(following)
         going_up = (terms[step - 1] + came_up.astype(jnp.float32)).astype(jnp.bfloat16)
         going_down = terms[1 - step] if came_down is None else terms[1 - step] + came_down.astype(jnp.float32)
         going_down = going_down.astype(jnp.bfloat16)
         if step == half:
-            going_up, going_down, near_up = lax.optimization_barrier((going_up, going_down, near_up))
+            going_up, going_down, near_up, chunks = lax.optimization_barrier((going_up, going_down, near_up, chunks))
+            for g in range(2, len(groups)):
+                came.append([swap(some, 2 * k) for k in range(1, peers) for some in chunks[bounds[g]:bounds[g + 1]]])
+            near_up, came[1] = lax.optimization_barrier((near_up, came[1]))
+            terms.update(products(1, both_cores(came[1])))
             grad_out = rows_of([([near_up], 1 - half), ([near_down], half - 1), ([far], half)], grad_out)
             grad_mine = grad_out[0].reshape(width, rows)
             came[2], grad_other = lax.optimization_barrier((came[2], grad_out[1]))
@@ -595,7 +604,7 @@
         else:
             going_up, going_down = lax.optimization_barrier((going_up, going_down))
         came_up, came_down = send(going_up, 0), send(going_down, 1)
-    for low, high in zip(bounds, bounds[1:]):
+    for low, high in zip(steps, steps[1:]):
         grads = backward(query_key_value, grad_mine, grad_other, main_probs, slot_probs, low, high, grads)
     came_up, came_down, grads = lax.optimization_barrier((came_up, came_down, grads))
     offsets = set()

time: 120 us -> 128 us (1.067)
  starting transfers between devices: 23.5 us -> 26.6 us
  waiting for transfers between devices: 24.3 us -> 27 us
  other arithmetic: 0.78 us -> 3.24 us
    ppermute x14, waiting for transfers between devices: 13.5 us -> 19.9 us  [send(): return lax.ppermute(array, ('dp', 'fsdp'), streams[stream])]
    ppermute x13 -> x15, waiting for transfers between devices: 10.7 us -> 7.1 us  [swap(): return lax.ppermute(array, 'dp', [(i, i ^ bit) for i in range(members)])]
    ppermute x13 -> x15, starting transfers between devices: 8.11 us -> 10.6 us  [swap(): return lax.ppermute(array, 'dp', [(i, i ^ bit) for i in range(members)])]
    convert_element_type x3, other arithmetic: 0.24 us -> 1.95 us  [local(): (terms[step - 1] + came_up.astype(jnp.float32)).astype(jnp.bfloat16)]
  transfers between devices with their start and end apart: 27 -> 29, of which waited for: 13 -> 12; matrix products, arithmetic and copies ran while one was open for 1% -> 3% of each run, Pallas kernels for 55% -> 51%
where the time goes in v9:
time: 128 us; the launch traced here: 127 us
  Pallas kernels  67.5 us (53%)
  waiting for transfers between devices  27 us (21%)
  starting transfers between devices  26.6 us (21%)
  other arithmetic  3.24 us (3%)
  local copies, waits for them, and re-layouts  1.79 us (1%)
    pallas_call x4, Pallas kernels, partial_products(): pl.pallas_call(functools.partial(partial_kernel, not bases, turned_round,...  22.3 us
    ppermute x14, waiting for transfers between devices, send(): return lax.ppermute(array, ('dp', 'fsdp'), streams[stream])  19.9 us
    ppermute x14, starting transfers between devices, send(): return lax.ppermute(array, ('dp', 'fsdp'), streams[stream])  16 us
    pallas_call x2, Pallas kernels, grad_out_rows(): pl.pallas_call(functools.partial(grad_out_kernel, sizes, split, total), g...  14.3 us
    ppermute x15, starting transfers between devices, swap(): return lax.ppermute(array, 'dp', [(i, i ^ bit) for i in range(members)])  10.6 us
    pallas_call x3, Pallas kernels, backward(): pl.pallas_call(backward_kernel, grid=(high - low,), in_specs=[pl.BlockSpe...  9.72 us
    pallas_call x1, Pallas kernels, forward(): pl.pallas_call(forward_kernel, grid_spec=pltpu.PrefetchScalarGridSpec(num...  7.37 us
    ppermute x15, waiting for transfers between devices, swap(): return lax.ppermute(array, 'dp', [(i, i ^ bit) for i in range(members)])  7.1 us
  transfers between devices with their start and end apart: 29, of which 12 were waited for; matrix products, arithmetic and copies ran while one was open for 3% of the time, Pallas kernels for 51%

profile of v9, /device:TPU:0, one launch (start us, length us, event | category | flops | bytes accessed | tf_op | source)
XLA Modules:
  0.0 127.0 jit_solution(6453122016787969943)
XLA Ops:
  0.7 1.1 own_half_of_weight.1.refs_0_
  1.8 3.1 %collective-permute-start.1 = (bf16[208,1664]{1,0:T(8,128)(2,1)S(1)}, bf16[208,1664]{1,0:T(8,128)(2,1)}, u32[]{:S(2)}, u32[]{:S(2)}) collective-permute-start(bf16[208,1664]{1,0:T(8,128)(2,1)S(1)} %own_half_of_weight.1.refs_0_), channel_id=1, source_target_pairs={{0,2},{2,4},{4,6},{6,7},{7,5},{5,3},{3,1},{1,0},{8,9},{10,8},{12,1... | collective-permute-start | bytes 2076680 | tf_op jit(solution)/shard_map/ppermute | solution.py:476
  4.9 0.7 reshape.18.layer_scale
  5.6 2.6 %peer_windows.1 = (bf16[176,1664]{1,0:T(8,128)(2,1)}, bf16[272,1664]{1,0:T(8,128)(2,1)}) custom-call(s32[1]{0:T(128)} %bitcast.9.starts, bf16[448,3200]{1,0:T(8,128)(2,1)} %cotangent.1, f32[1,3200]{1,0:T(1,128)S(1)} %reshape.18.layer_scale), custom_call_target="tpu_custom_call" | custom-call | flops 34500001792 | bytes 1000 | tf_op jit(solution)/shard_map/peer_windows/pallas_call | solution.py:59
  8.2 2.0 %collective-permute-start.3 = (bf16[176,1664]{1,0:T(8,128)(2,1)}, bf16[176,1664]{1,0:T(8,128)(2,1)}, u32[]{:S(2)}, u32[]{:S(2)}) collective-permute-start(bf16[176,1664]{1,0:T(8,128)(2,1)} %get-tuple-element.97), channel_id=1, source_target_pairs={{0,16},{8,24},{16,0},{24,8},{1,17},{9,25},{17,1},{25,9},{2,18},{10... | collective-permute-start | bytes 1757192 | tf_op jit(solution)/shard_map/ppermute | solution.py:479
  10.2 6.0 %scaled_cotangent.1.refs_2_.turned = bf16[3200,512]{1,0:T(8,128)(2,1)} custom-call(bf16[448,3200]{1,0:T(8,128)(2,1)} %cotangent.1, f32[1,3200]{1,0:T(1,128)S(1)} %reshape.18.layer_scale), custom_call_target="tpu_custom_call" | custom-call | flops 34500001792 | bytes 1000 | tf_op jit(solution)/shard_map/scaled_cotangent/pallas_call | solution.py:90
  16.2 7.4 %attention_forward.1 = (bf16[1664,448]{1,0:T(8,128)(2,1)}, f32[13,256,256]{2,1,0:T(8,128)}, f32[13,192,192]{2,1,0:T(8,128)}) custom-call(s32[4]{0:T(128)S(1)} %dynamic-slice_bitcast_fusion.counts, bf16[3,448,1664]{2,1,0:T(8,128)(2,1)S(1)} %copy-done.2), custom_call_target="tpu_custom_call" | custom-call | flops 34500001792 | bytes 1000 | tf_op jit(solution)/shard_map/attention_forward/pallas_call | solution.py:179
  24.2 1.3 collective-permute-start
  25.4 1.6 %collective-permute-start.6 = (bf16[208,1664]{1,0:T(8,128)(2,1)}, bf16[208,1664]{1,0:T(8,128)(2,1)}, u32[]{:S(2)}, u32[]{:S(2)}) collective-permute-start(bf16[208,1664]{1,0:T(8,128)(2,1)} %collective-permute-done.1.refs_1_), channel_id=1, source_target_pairs={{0,2},{2,4},{4,6},{6,7},{7,5},{5,3},{3,1},{1,0},{8,9},{10,8},{12,1... | collective-permute-start | bytes 2076680 | tf_op jit(solution)/shard_map/ppermute | solution.py:476
  27.5 3.0 %attended_chunks.1 = (bf16[3,208,448]{2,1,0:T(8,128)(2,1)}, bf16[1,208,448]{2,1,0:T(8,128)(2,1)}, bf16[1,208,448]{2,1,0:T(8,128)(2,1)S(1)}, bf16[3,208,448]{2,1,0:T(8,128)(2,1)S(1)}) custom-call(s32[8]{0:T(128)S(1)} %stack.80.order, bf16[8,208,448]{2,1,0:T(8,128)(2,1)} %bitcast.28), custom_call_target="tpu_custom_call" | custom-call | flops 1150000000 | bytes 1000 | tf_op jit(solution)/shard_map/attended_chunks/pallas_call | solution.py:117
  30.6 0.8 copy-done.6
  32.2 7.7 %projection_chip.1 = (bf16[208,896]{1,0:T(8,128)(2,1)}, bf16[208,896]{1,0:T(8,128)(2,1)}, bf16[208,896]{1,0:T(8,128)(2,1)}, bf16[208,896]{1,0:T(8,128)(2,1)}, bf...) custom-call(s32[8]{0:T(128)S(1)} %stack.80.order, ...), custom_call_target="tpu_custom_call" | custom-call | flops 3449999872 | bytes 1000 | tf_op jit(solution)/shard_map/projection_chip/pallas_call | solution.py:425
  39.8 4.3 %collective-permute-done.6.refs_3_ = bf16[208,1664]{1,0:T(8,128)(2,1)} collective-permute-done((bf16[208,1664]{1,0:T(8,128)(2,1)}, bf16[208,1664]{1,0:T(8,128)(2,1)}, u32[]{:S(2)}, u32[]{:S(2)}) %collective-permute-start.6) | collective-permute-done | bytes 692256 | tf_op jit(solution)/shard_map/ppermute | solution.py:476
  44.1 0.6 collective-permute-start.9
  44.7 1.4 %collective-permute-start.10 = (bf16[208,1664]{1,0:T(8,128)(2,1)}, bf16[208,1664]{1,0:T(8,128)(2,1)}, u32[]{:S(2)}, u32[]{:S(2)}) collective-permute-start(bf16[208,1664]{1,0:T(8,128)(2,1)} %collective-permute-done.7.refs_4_), channel_id=1, source_target_pairs={{0,1},{2,0},{4,2},{6,4},{7,6},{5,7},{3,5},{1,3},{8,10},{10,12},{12... | collective-permute-start | bytes 2076680 | tf_op jit(solution)/shard_map/ppermute | solution.py:476
  46.6 1.3 collective-permute-start.5
  47.9 0.5 collective-permute-start.13
  48.4 8.2 %grad_out_rows.2 = (f32[8,208,448]{2,1,0:T(8,128)}, bf16[8,208,448]{2,1,0:T(8,128)(2,1)}) custom-call(s32[6]{0:T(128)S(1)} %stack.83.info, bf16[3200,512]{1,0:T(8,128)(2,1)} %scaled_cotangent.1.refs_2_.turned, bf16[3200,512]{1,0:T(8,128)(2,1)S(1)} %collective-permute-done.8.refs_3_.turned_other, bf16[208,1664]{1,0:T(8,128)(2,1)} %copy-done.5, ...), custom_call_target="tpu_custom_call" | custom-call | flops 4312500224 | bytes 1000 | tf_op jit(solution)/shard_map/grad_out_rows/pallas_call | solution.py:297
  56.6 5.8 %collective-permute-done.9.refs_0_ = bf16[208,1664]{1,0:T(8,128)(2,1)} collective-permute-done((bf16[208,1664]{1,0:T(8,128)(2,1)}, bf16[208,1664]{1,0:T(8,128)(2,1)}, u32[]{:S(2)}, u32[]{:S(2)}) %collective-permute-start.9) | collective-permute-done | bytes 692256 | tf_op jit(solution)/shard_map/ppermute | solution.py:476
  62.6 1.3 %collective-permute-start.15 = (bf16[208,1664]{1,0:T(8,128)(2,1)}, bf16[208,1664]{1,0:T(8,128)(2,1)}, u32[]{:S(2)}, u32[]{:S(2)}) collective-permute-start(bf16[208,1664]{1,0:T(8,128)(2,1)} %collective-permute-done.9.refs_0_), channel_id=1, source_target_pairs={{0,2},{2,4},{4,6},{6,7},{7,5},{5,3},{3,1},{1,0},{8,9},{10,8},{12,1... | collective-permute-start | bytes 2076680 | tf_op jit(solution)/shard_map/ppermute | solution.py:476
  64.0 1.3 collective-permute-start.14
  65.3 5.1 %projection_peers.3 = (f32[208,896]{1,0:T(8,128)S(1)}, f32[208,896]{1,0:T(8,128)S(1)}, f32[208,896]{1,0:T(8,128)S(1)}) custom-call(s32[3]{0:T(128)S(1)} %pad_add_fusion.2.order, s32[1]{0:T(128)} %bitcast.3.start, bf16[3,208,448]{2,1,0:T(8,128)(2,1)} %collective-permute-done.5.refs_0_, bf16[3,208,448]{2,1,0:T(8,128)(2,1)} %collective-permute-done.11.refs_1_, ...), custom_call_target="tpu_custom_call" | custom-call | flops 1724999936 | bytes 1000 | tf_op jit(solution)/shard_map/projection_peers/pallas_call | solution.py:425
  70.4 1.2 collective-permute-done.14.refs_0_
  71.6 2.3 %collective-permute-done.15.refs_2_ = bf16[208,1664]{1,0:T(8,128)(2,1)} collective-permute-done((bf16[208,1664]{1,0:T(8,128)(2,1)}, bf16[208,1664]{1,0:T(8,128)(2,1)}, u32[]{:S(2)}, u32[]{:S(2)}) %collective-permute-start.15) | collective-permute-done | bytes 692256 | tf_op jit(solution)/shard_map/ppermute | solution.py:476
  73.9 1.3 %collective-permute-start.16 = (bf16[208,896]{1,0:T(8,128)(2,1)S(1)}, bf16[208,896]{1,0:T(8,128)(2,1)S(1)}, u32[]{:S(2)}, u32[]{:S(2)}) collective-permute-start(bf16[208,896]{1,0:T(8,128)(2,1)S(1)} %convert_element_type.36), channel_id=1, source_target_pairs={{0,2},{2,4},{4,6},{6,7},{7,5},{5,3},{3,1},{1,0},{8,9},{10,8},{12,1... | collective-permute-start | bytes 1118216 | tf_op jit(solution)/shard_map/ppermute | solution.py:476
  75.3 1.3 %collective-permute-start.17 = (bf16[1,208,448]{2,1,0:T(8,128)(2,1)S(1)}, bf16[1,208,448]{2,1,0:T(8,128)(2,1)S(1)}, u32[]{:S(2)}, u32[]{:S(2)}) collective-permute-start(bf16[1,208,448]{2,1,0:T(8,128)(2,1)S(1)} %get-tuple-element.143), channel_id=1, source_target_pairs={{0,16},{8,24},{16,0},{24,8},{1,17},{9,25},{17,1},{25,9},{2,18},{10... | collective-permute-start | bytes 559112 | tf_op jit(solution)/shard_map/ppermute | solution.py:479
  76.6 4.8 %collective-permute-done.16 = bf16[208,896]{1,0:T(8,128)(2,1)S(1)} collective-permute-done((bf16[208,896]{1,0:T(8,128)(2,1)S(1)}, bf16[208,896]{1,0:T(8,128)(2,1)S(1)}, u32[]{:S(2)}, u32[]{:S(2)}) %collective-permute-start.16) | collective-permute-done | bytes 372768 | tf_op jit(solution)/shard_map/ppermute | solution.py:476
  81.9 0.5 collective-permute-start.19
  82.4 1.1 collective-permute-start.20
  83.5 1.3 collective-permute-start.22
  84.9 0.9 collective-permute-start.21
  85.8 6.0 %grad_out_rows.3 = (f32[8,208,448]{2,1,0:T(8,128)}, bf16[8,208,448]{2,1,0:T(8,128)(2,1)}) custom-call(s32[4]{0:T(128)S(1)} %pad_add_fusion.3.info, bf16[3200,512]{1,0:T(8,128)(2,1)} %scaled_cotangent.1.refs_2_.turned, bf16[3200,512]{1,0:T(8,128)(2,1)S(1)} %collective-permute-done.8.refs_3_.turned_other, ...), custom_call_target="tpu_custom_call", output_to_operand_aliasing={{0}: (6, {}), {1}: (7, {})} | custom-call | flops 115000000 | bytes 1000 | tf_op jit(solution)/shard_map/grad_out_rows/pallas_call | solution.py:297
  91.9 4.3 %projection_peers.4 = (f32[208,896]{1,0:T(8,128)S(1)}, f32[208,896]{1,0:T(8,128)S(1)}) custom-call(s32[2]{0:T(128)S(1)} %pad_add_fusion.1.order, s32[1]{0:T(128)} %bitcast.3.start, bf16[1,208,448]{2,1,0:T(8,128)(2,1)} %collective-permute-done.14.refs_0_, bf16[1,208,448]{2,1,0:T(8,128)(2,1)S(1)} %collective-permute-done.17.refs_1_, ...), custom_call_target="tpu_custom_call" | custom-call | flops 1724999936 | bytes 1000 | tf_op jit(solution)/shard_map/projection_peers/pallas_call | solution.py:425
  96.1 0.8 add_convert_fusion.3
  96.9 3.1 %collective-permute-done.22.refs_0_ = bf16[3,208,448]{2,1,0:T(8,128)(2,1)} collective-permute-done((bf16[3,208,448]{2,1,0:T(8,128)(2,1)S(1)}, bf16[3,208,448]{2,1,0:T(8,128)(2,1)}, u32[]{:S(2)}, u32[]{:S(2)}) %collective-permute-start.22) | collective-permute-done | bytes 559136 | tf_op jit(solution)/shard_map/ppermute | solution.py:479
  100.1 0.8 add_convert_fusion.2
  100.9 0.5 collective-permute-start.23
  101.9 1.6 %collective-permute-start.25 = (bf16[208,896]{1,0:T(8,128)(2,1)}, bf16[208,896]{1,0:T(8,128)(2,1)S(1)}, u32[]{:S(2)}, u32[]{:S(2)}) collective-permute-start(bf16[208,896]{1,0:T(8,128)(2,1)} %add_convert_fusion.2), channel_id=1, source_target_pairs={{0,1},{2,0},{4,2},{6,4},{7,6},{5,7},{3,5},{1,3},{8,10},{10,12},{12... | collective-permute-start | bytes 1118216 | tf_op jit(solution)/shard_map/ppermute | solution.py:476
  103.6 1.4 %collective-permute-done.23.refs_1_ = bf16[3,208,448]{2,1,0:T(8,128)(2,1)} collective-permute-done((bf16[3,208,448]{2,1,0:T(8,128)(2,1)}, bf16[3,208,448]{2,1,0:T(8,128)(2,1)}, u32[]{:S(2)}, u32[]{:S(2)}) %collective-permute-start.23) | collective-permute-done | bytes 559136 | tf_op jit(solution)/shard_map/ppermute | solution.py:479
  104.9 5.3 %projection_peers.5 = (f32[208,896]{1,0:T(8,128)S(1)}, f32[208,896]{1,0:T(8,128)S(1)}, f32[208,896]{1,0:T(8,128)S(1)}) custom-call(s32[3]{0:T(128)S(1)} %pad_add_fusion.order, s32[1]{0:T(128)} %bitcast.3.start, bf16[3,208,448]{2,1,0:T(8,128)(2,1)} %collective-permute-done.22.refs_0_, bf16[3,208,448]{2,1,0:T(8,128)(2,1)} %collective-permute-done.23.refs_1_, ...), custom_call_target="tpu_custom_call" | custom-call | flops 1724999936 | bytes 1000 | tf_op jit(solution)/shard_map/projection_peers/pallas_call | solution.py:425
  110.2 2.7 %collective-permute-done.24 = bf16[208,896]{1,0:T(8,128)(2,1)} collective-permute-done((bf16[208,896]{1,0:T(8,128)(2,1)}, bf16[208,896]{1,0:T(8,128)(2,1)}, u32[]{:S(2)}, u32[]{:S(2)}) %collective-permute-start.24) | collective-permute-done | bytes 372768 | tf_op jit(solution)/shard_map/ppermute | solution.py:476
  112.9 1.1 add_convert_fusion.1
  114.1 0.5 collective-permute-start.26
  114.6 1.6 %collective-permute-start.27 = (bf16[208,896]{1,0:T(8,128)(2,1)S(1)}, bf16[208,896]{1,0:T(8,128)(2,1)S(1)}, u32[]{:S(2)}, u32[]{:S(2)}) collective-permute-start(bf16[208,896]{1,0:T(8,128)(2,1)S(1)} %add_convert_fusion), channel_id=1, source_target_pairs={{0,1},{2,0},{4,2},{6,4},{7,6},{5,7},{3,5},{1,3},{8,10},{10,12},{12... | collective-permute-start | bytes 1118216 | tf_op jit(solution)/shard_map/ppermute | solution.py:476
  116.2 4.8 %attention_backward.3.rest_0_ = bf16[3,448,1664]{2,1,0:T(8,128)(2,1)} custom-call(bf16[3,448,1664]{2,1,0:T(8,128)(2,1)} %qkv.7, f32[1664,448]{1,0:T(8,128)S(1)} %bitcast.19, bf16[1664,448]{1,0:T(8,128)(2,1)S(1)} %bitcast.24, f32[13,256,256]{2,1,0:T(8,128)S(1)} %copy-done.3, f32[13,192,192]{2,1,0:T(8,128)S(1)} %copy-done.4), custom_call_target="tpu_custom_call" | custom-call | flops 3449999872 | bytes 1000 | tf_op jit(solution)/shard_map/attention_backward/pallas_call | solution.py:229
  121.0 2.5 %attention_backward.4.rest_0_ = bf16[3,448,1664]{2,1,0:T(8,128)(2,1)} custom-call(bf16[3,448,1664]{2,1,0:T(8,128)(2,1)S(1)} %bitcast.23, f32[1664,448]{1,0:T(8,128)S(1)} %bitcast.20, bf16[1664,448]{1,0:T(8,128)(2,1)S(1)} %bitcast.25, f32[13,256,256]{2,1,0:T(8,128)S(1)} %copy-done.3, f32[13,192,192]{2,1,0:T(8,128)S(1)} %copy-done.4, ...), custom_call_target="tpu_custom_call", output_to_operand_aliasing={{}: (5, {})} | custom-call | flops 2300000000 | bytes 1000 | tf_op jit(solution)/shard_map/attention_backward/pallas_call | solution.py:229
  123.5 2.4 %attention_backward.5 = bf16[3,448,1664]{2,1,0:T(8,128)(2,1)} custom-call(bf16[3,448,1664]{2,1,0:T(8,128)(2,1)S(1)} %bitcast.23, f32[1664,448]{1,0:T(8,128)S(1)} %bitcast.21, bf16[1664,448]{1,0:T(8,128)(2,1)S(1)} %bitcast.26, f32[13,256,256]{2,1,0:T(8,128)S(1)} %copy-done.3, f32[13,192,192]{2,1,0:T(8,128)S(1)} %copy-done.4, ...), custom_call_target="tpu_custom_call", output_to_operand_aliasing={{}: (5, {})} | custom-call | flops 2300000000 | bytes 1000 | tf_op jit(solution)/shard_map/attention_backward/pallas_call | solution.py:229
  125.9 1.1 last_sum.1
  (63 shorter events, 3.9 us)
Async XLA Ops:
  0.6 15.6 %copy-start = (s32[4,1,4]{2,1,0:T(1,128)S(1)}, s32[4,1,4]{2,1,0:T(1,128)}, u32[]{:S(2)}) copy-start(s32[4,1,4]{2,1,0:T(1,128)} %param.9) | copy-start | bytes 196
  1.8 6.4 %copy-start.5 = (bf16[208,1664]{1,0:T(8,128)(2,1)}, bf16[208,1664]{1,0:T(8,128)(2,1)S(1)}, u32[]{:S(2)}) copy-start(bf16[208,1664]{1,0:T(8,128)(2,1)S(1)} %own_half_of_weight.1.refs_0_) | copy-start | bytes 2076676
  1.8 21.8 %collective-permute-start.1 = (bf16[208,1664]{1,0:T(8,128)(2,1)S(1)}, bf16[208,1664]{1,0:T(8,128)(2,1)}, u32[]{:S(2)}, u32[]{:S(2)}) collective-permute-start(bf16[208,1664]{1,0:T(8,128)(2,1)S(1)} %own_half_of_weight.1.refs_0_), channel_id=1, source_target_pairs={{0,2},{2,4},{4,6},{6,7},{7,5},{5,3},{3,1},{1,0},{8,9},{10,8},{12,1... | collective-permute-start | bytes 2076680 | tf_op jit(solution)/shard_map/ppermute | solution.py:476
  4.9 18.7 %collective-permute-start.2 = (bf16[208,1664]{1,0:T(8,128)(2,1)S(1)}, bf16[208,1664]{1,0:T(8,128)(2,1)}, u32[]{:S(2)}, u32[]{:S(2)}) collective-permute-start(bf16[208,1664]{1,0:T(8,128)(2,1)S(1)} %own_half_of_weight.1.refs_0_), channel_id=1, source_target_pairs={{0,1},{2,0},{4,2},{6,4},{7,6},{5,7},{3,5},{1,3},{8,10},{10,12},{12... | collective-permute-start | bytes 2076680 | tf_op jit(solution)/shard_map/ppermute | solution.py:476
  8.2 15.4 %collective-permute-start.3 = (bf16[176,1664]{1,0:T(8,128)(2,1)}, bf16[176,1664]{1,0:T(8,128)(2,1)}, u32[]{:S(2)}, u32[]{:S(2)}) collective-permute-start(bf16[176,1664]{1,0:T(8,128)(2,1)} %get-tuple-element.97), channel_id=1, source_target_pairs={{0,16},{8,24},{16,0},{24,8},{1,17},{9,25},{17,1},{25,9},{2,18},{10... | collective-permute-start | bytes 1757192 | tf_op jit(solution)/shard_map/ppermute | solution.py:479
  10.2 6.0 %copy-start.2 = (bf16[3,448,1664]{2,1,0:T(8,128)(2,1)S(1)}, bf16[3,448,1664]{2,1,0:T(8,128)(2,1)}, u32[]{:S(2)}) copy-start(bf16[3,448,1664]{2,1,0:T(8,128)(2,1)} %qkv.7) | copy-start | bytes 13418500
  23.6 8.6 %collective-permute-start.8 = (bf16[3200,512]{1,0:T(8,128)(2,1)}, bf16[3200,512]{1,0:T(8,128)(2,1)S(1)}, u32[]{:S(2)}, u32[]{:S(2)}) collective-permute-start(bf16[3200,512]{1,0:T(8,128)(2,1)} %scaled_cotangent.1.refs_2_.turned), channel_id=1, source_target_pairs={{0,8},{8,0},{16,24},{24,16},{1,9},{9,1},{17,25},{25,17},{2,10},{10... | collective-permute-start | bytes 9830408 | tf_op jit(solution)/shard_map/ppermute | solution.py:479
  23.7 8.2 %collective-permute-start.4 = (bf16[8,208,448]{2,1,0:T(8,128)(2,1)}, bf16[8,208,448]{2,1,0:T(8,128)(2,1)}, u32[]{:S(2)}, u32[]{:S(2)}) collective-permute-start(bf16[8,208,448]{2,1,0:T(8,128)(2,1)} %bitcast.27), channel_id=1, source_target_pairs={{0,8},{8,0},{16,24},{24,16},{1,9},{9,1},{17,25},{25,17},{2,10},{10... | collective-permute-start | bytes 4472840 | tf_op jit(solution)/shard_map/ppermute | solution.py:479
  24.2 22.4 %collective-permute-start = (bf16[272,1664]{1,0:T(8,128)(2,1)}, bf16[272,1664]{1,0:T(8,128)(2,1)}, u32[]{:S(2)}, u32[]{:S(2)}) collective-permute-start(bf16[272,1664]{1,0:T(8,128)(2,1)} %get-tuple-element.95), channel_id=1, source_target_pairs={{0,16},{8,24},{16,0},{24,8},{1,17},{9,25},{17,1},{25,9},{2,18},{10... | collective-permute-start | bytes 2715656 | tf_op jit(solution)/shard_map/ppermute | solution.py:479
  25.4 18.6 %collective-permute-start.6 = (bf16[208,1664]{1,0:T(8,128)(2,1)}, bf16[208,1664]{1,0:T(8,128)(2,1)}, u32[]{:S(2)}, u32[]{:S(2)}) collective-permute-start(bf16[208,1664]{1,0:T(8,128)(2,1)} %collective-permute-done.1.refs_1_), channel_id=1, source_target_pairs={{0,2},{2,4},{4,6},{6,7},{7,5},{5,3},{3,1},{1,0},{8,9},{10,8},{12,1... | collective-permute-start | bytes 2076680 | tf_op jit(solution)/shard_map/ppermute | solution.py:476
  27.0 17.1 %collective-permute-start.7 = (bf16[208,1664]{1,0:T(8,128)(2,1)}, bf16[208,1664]{1,0:T(8,128)(2,1)}, u32[]{:S(2)}, u32[]{:S(2)}) collective-permute-start(bf16[208,1664]{1,0:T(8,128)(2,1)} %collective-permute-done.2.refs_2_), channel_id=1, source_target_pairs={{0,1},{2,0},{4,2},{6,4},{7,6},{5,7},{3,5},{1,3},{8,10},{10,12},{12... | collective-permute-start | bytes 2076680 | tf_op jit(solution)/shard_map/ppermute | solution.py:476
  30.6 0.9 copy-start.6
  44.1 18.3 %collective-permute-start.9 = (bf16[208,1664]{1,0:T(8,128)(2,1)}, bf16[208,1664]{1,0:T(8,128)(2,1)}, u32[]{:S(2)}, u32[]{:S(2)}) collective-permute-start(bf16[208,1664]{1,0:T(8,128)(2,1)} %collective-permute-done.6.refs_3_), channel_id=1, source_target_pairs={{0,2},{2,4},{4,6},{6,7},{7,5},{5,3},{3,1},{1,0},{8,9},{10,8},{12,1... | collective-permute-start | bytes 2076680 | tf_op jit(solution)/shard_map/ppermute | solution.py:476
  44.7 17.7 %collective-permute-start.10 = (bf16[208,1664]{1,0:T(8,128)(2,1)}, bf16[208,1664]{1,0:T(8,128)(2,1)}, u32[]{:S(2)}, u32[]{:S(2)}) collective-permute-start(bf16[208,1664]{1,0:T(8,128)(2,1)} %collective-permute-done.7.refs_4_), channel_id=1, source_target_pairs={{0,1},{2,0},{4,2},{6,4},{7,6},{5,7},{3,5},{1,3},{8,10},{10,12},{12... | collective-permute-start | bytes 2076680 | tf_op jit(solution)/shard_map/ppermute | solution.py:476
  46.6 15.9 %collective-permute-start.5 = (bf16[3,208,448]{2,1,0:T(8,128)(2,1)}, bf16[3,208,448]{2,1,0:T(8,128)(2,1)}, u32[]{:S(2)}, u32[]{:S(2)}) collective-permute-start(bf16[3,208,448]{2,1,0:T(8,128)(2,1)} %get-tuple-element.108), channel_id=1, source_target_pairs={{0,16},{8,24},{16,0},{24,8},{1,17},{9,25},{17,1},{25,9},{2,18},{10... | collective-permute-start | bytes 1677320 | tf_op jit(solution)/shard_map/ppermute | solution.py:479
  47.9 17.4 %collective-permute-start.12 = (bf16[176,1664]{1,0:T(8,128)(2,1)}, bf16[176,1664]{1,0:T(8,128)(2,1)}, u32[]{:S(2)}, u32[]{:S(2)}) collective-permute-start(bf16[176,1664]{1,0:T(8,128)(2,1)} %collective-permute-done.3.refs_2_.refs_4_), channel_id=1, source_target_pairs={{0,8},{8,0},{16,24},{24,16},{1,9},{9,1},{17,25},{25,17},{2,10},{10... | collective-permute-start | bytes 1757192 | tf_op jit(solution)/shard_map/ppermute | solution.py:479
  47.9 17.4 %collective-permute-start.13 = (bf16[272,1664]{1,0:T(8,128)(2,1)}, bf16[272,1664]{1,0:T(8,128)(2,1)}, u32[]{:S(2)}, u32[]{:S(2)}) collective-permute-start(bf16[272,1664]{1,0:T(8,128)(2,1)} %collective-permute-done.refs_3_.refs_5_), channel_id=1, source_target_pairs={{0,8},{8,0},{16,24},{24,16},{1,9},{9,1},{17,25},{25,17},{2,10},{10... | collective-permute-start | bytes 2715656 | tf_op jit(solution)/shard_map/ppermute | solution.py:479
  62.4 2.9 %collective-permute-start.11 = (bf16[3,208,448]{2,1,0:T(8,128)(2,1)}, bf16[3,208,448]{2,1,0:T(8,128)(2,1)}, u32[]{:S(2)}, u32[]{:S(2)}) collective-permute-start(bf16[3,208,448]{2,1,0:T(8,128)(2,1)} %collective-permute-done.5.refs_0_), channel_id=1, source_target_pairs={{0,8},{8,0},{16,24},{24,16},{1,9},{9,1},{17,25},{25,17},{2,10},{10... | collective-permute-start | bytes 1677320 | tf_op jit(solution)/shard_map/ppermute | solution.py:479
  62.6 11.3 %collective-permute-start.15 = (bf16[208,1664]{1,0:T(8,128)(2,1)}, bf16[208,1664]{1,0:T(8,128)(2,1)}, u32[]{:S(2)}, u32[]{:S(2)}) collective-permute-start(bf16[208,1664]{1,0:T(8,128)(2,1)} %collective-permute-done.9.refs_0_), channel_id=1, source_target_pairs={{0,2},{2,4},{4,6},{6,7},{7,5},{5,3},{3,1},{1,0},{8,9},{10,8},{12,1... | collective-permute-start | bytes 2076680 | tf_op jit(solution)/shard_map/ppermute | solution.py:476
  64.0 7.6 %collective-permute-start.14 = (bf16[1,208,448]{2,1,0:T(8,128)(2,1)}, bf16[1,208,448]{2,1,0:T(8,128)(2,1)}, u32[]{:S(2)}, u32[]{:S(2)}) collective-permute-start(bf16[1,208,448]{2,1,0:T(8,128)(2,1)} %get-tuple-element.137), channel_id=1, source_target_pairs={{0,16},{8,24},{16,0},{24,8},{1,17},{9,25},{17,1},{25,9},{2,18},{10... | collective-permute-start | bytes 559112 | tf_op jit(solution)/shard_map/ppermute | solution.py:479
  70.4 13.1 %copy-start.7 = (bf16[3,208,448]{2,1,0:T(8,128)(2,1)S(1)}, bf16[3,208,448]{2,1,0:T(8,128)(2,1)}, u32[]{:S(2)}) copy-start(bf16[3,208,448]{2,1,0:T(8,128)(2,1)} %copy-done.6) | copy-start | bytes 1677316
  73.9 7.6 %collective-permute-start.16 = (bf16[208,896]{1,0:T(8,128)(2,1)S(1)}, bf16[208,896]{1,0:T(8,128)(2,1)S(1)}, u32[]{:S(2)}, u32[]{:S(2)}) collective-permute-start(bf16[208,896]{1,0:T(8,128)(2,1)S(1)} %convert_element_type.36), channel_id=1, source_target_pairs={{0,2},{2,4},{4,6},{6,7},{7,5},{5,3},{3,1},{1,0},{8,9},{10,8},{12,1... | collective-permute-start | bytes 1118216 | tf_op jit(solution)/shard_map/ppermute | solution.py:476
  75.3 6.5 %collective-permute-start.17 = (bf16[1,208,448]{2,1,0:T(8,128)(2,1)S(1)}, bf16[1,208,448]{2,1,0:T(8,128)(2,1)S(1)}, u32[]{:S(2)}, u32[]{:S(2)}) collective-permute-start(bf16[1,208,448]{2,1,0:T(8,128)(2,1)S(1)} %get-tuple-element.143), channel_id=1, source_target_pairs={{0,16},{8,24},{16,0},{24,8},{1,17},{9,25},{17,1},{25,9},{2,18},{10... | collective-permute-start | bytes 559112 | tf_op jit(solution)/shard_map/ppermute | solution.py:479
  81.9 10.0 %collective-permute-start.18 = (bf16[1,208,448]{2,1,0:T(8,128)(2,1)}, bf16[1,208,448]{2,1,0:T(8,128)(2,1)S(1)}, u32[]{:S(2)}, u32[]{:S(2)}) collective-permute-start(bf16[1,208,448]{2,1,0:T(8,128)(2,1)} %collective-permute-done.14.refs_0_), channel_id=1, source_target_pairs={{0,8},{8,0},{16,24},{24,16},{1,9},{9,1},{17,25},{25,17},{2,10},{10... | collective-permute-start | bytes 559112 | tf_op jit(solution)/shard_map/ppermute | solution.py:479
  81.9 10.0 %collective-permute-start.19 = (bf16[1,208,448]{2,1,0:T(8,128)(2,1)S(1)}, bf16[1,208,448]{2,1,0:T(8,128)(2,1)S(1)}, u32[]{:S(2)}, u32[]{:S(2)}) collective-permute-start(bf16[1,208,448]{2,1,0:T(8,128)(2,1)S(1)} %collective-permute-done.17.refs_1_), channel_id=1, source_target_pairs={{0,8},{8,0},{16,24},{24,16},{1,9},{9,1},{17,25},{25,17},{2,10},{10... | collective-permute-start | bytes 559112 | tf_op jit(solution)/shard_map/ppermute | solution.py:479
  82.4 13.8 %collective-permute-start.20 = (bf16[208,896]{1,0:T(8,128)(2,1)S(1)}, bf16[208,896]{1,0:T(8,128)(2,1)S(1)}, u32[]{:S(2)}, u32[]{:S(2)}) collective-permute-start(bf16[208,896]{1,0:T(8,128)(2,1)S(1)} %add_convert_fusion.4), channel_id=1, source_target_pairs={{0,2},{2,4},{4,6},{6,7},{7,5},{5,3},{3,1},{1,0},{8,9},{10,8},{12,1... | collective-permute-start | bytes 1118216 | tf_op jit(solution)/shard_map/ppermute | solution.py:476
  83.5 16.6 %collective-permute-start.22 = (bf16[3,208,448]{2,1,0:T(8,128)(2,1)S(1)}, bf16[3,208,448]{2,1,0:T(8,128)(2,1)}, u32[]{:S(2)}, u32[]{:S(2)}) collective-permute-start(bf16[3,208,448]{2,1,0:T(8,128)(2,1)S(1)} %copy-done.7), channel_id=1, source_target_pairs={{0,16},{8,24},{16,0},{24,8},{1,17},{9,25},{17,1},{25,9},{2,18},{10... | collective-permute-start | bytes 1677320 | tf_op jit(solution)/shard_map/ppermute | solution.py:479
  84.9 15.2 %collective-permute-start.21 = (bf16[208,896]{1,0:T(8,128)(2,1)S(1)}, bf16[208,896]{1,0:T(8,128)(2,1)S(1)}, u32[]{:S(2)}, u32[]{:S(2)}) collective-permute-start(bf16[208,896]{1,0:T(8,128)(2,1)S(1)} %convert_element_type.39), channel_id=1, source_target_pairs={{0,1},{2,0},{4,2},{6,4},{7,6},{5,7},{3,5},{1,3},{8,10},{10,12},{12... | collective-permute-start | bytes 1118216 | tf_op jit(solution)/shard_map/ppermute | solution.py:476
  91.8 8.2 %copy-start.8 = (bf16[8,208,448]{2,1,0:T(8,128)(2,1)S(1)}, bf16[8,208,448]{2,1,0:T(8,128)(2,1)}, u32[]{:S(2)}) copy-start(bf16[8,208,448]{2,1,0:T(8,128)(2,1)} %get-tuple-element.175) | copy-start | bytes 4472836
  100.1 16.1 %collective-permute-start.28 = (bf16[8,208,448]{2,1,0:T(8,128)(2,1)S(1)}, bf16[8,208,448]{2,1,0:T(8,128)(2,1)S(1)}, u32[]{:S(2)}, u32[]{:S(2)}) collective-permute-start(bf16[8,208,448]{2,1,0:T(8,128)(2,1)S(1)} %copy-done.8), channel_id=1, source_target_pairs={{0,8},{8,0},{16,24},{24,16},{1,9},{9,1},{17,25},{25,17},{2,10},{10... | collective-permute-start | bytes 4472840 | tf_op jit(solution)/shard_map/ppermute | solution.py:479
  100.9 4.0 %collective-permute-start.23 = (bf16[3,208,448]{2,1,0:T(8,128)(2,1)}, bf16[3,208,448]{2,1,0:T(8,128)(2,1)}, u32[]{:S(2)}, u32[]{:S(2)}) collective-permute-start(bf16[3,208,448]{2,1,0:T(8,128)(2,1)} %collective-permute-done.22.refs_0_), channel_id=1, source_target_pairs={{0,8},{8,0},{16,24},{24,16},{1,9},{9,1},{17,25},{25,17},{2,10},{10... | collective-permute-start | bytes 1677320 | tf_op jit(solution)/shard_map/ppermute | solution.py:479
  101.4 11.5 %collective-permute-start.24 = (bf16[208,896]{1,0:T(8,128)(2,1)}, bf16[208,896]{1,0:T(8,128)(2,1)}, u32[]{:S(2)}, u32[]{:S(2)}) collective-permute-start(bf16[208,896]{1,0:T(8,128)(2,1)} %add_convert_fusion.3), channel_id=1, source_target_pairs={{0,2},{2,4},{4,6},{6,7},{7,5},{5,3},{3,1},{1,0},{8,9},{10,8},{12,1... | collective-permute-start | bytes 1118216 | tf_op jit(solution)/shard_map/ppermute | solution.py:476
  101.9 14.2 %copy-start.1 = (f32[8,208,448]{2,1,0:T(8,128)S(1)}, f32[8,208,448]{2,1,0:T(8,128)}, u32[]{:S(2)}) copy-start(f32[8,208,448]{2,1,0:T(8,128)} %get-tuple-element.163) | copy-start | bytes 8945668
  101.9 14.2 %copy-start.3 = (f32[13,256,256]{2,1,0:T(8,128)S(1)}, f32[13,256,256]{2,1,0:T(8,128)}, u32[]{:S(2)}) copy-start(f32[13,256,256]{2,1,0:T(8,128)} %get-tuple-element.176.main_probs) | copy-start | bytes 10223620
  101.9 14.2 %copy-start.4 = (f32[13,192,192]{2,1,0:T(8,128)S(1)}, f32[13,192,192]{2,1,0:T(8,128)}, u32[]{:S(2)}) copy-start(f32[13,192,192]{2,1,0:T(8,128)} %get-tuple-element.177.slot_probs) | copy-start | bytes 5750788
  101.9 12.0 %collective-permute-start.25 = (bf16[208,896]{1,0:T(8,128)(2,1)}, bf16[208,896]{1,0:T(8,128)(2,1)S(1)}, u32[]{:S(2)}, u32[]{:S(2)}) collective-permute-start(bf16[208,896]{1,0:T(8,128)(2,1)} %add_convert_fusion.2), channel_id=1, source_target_pairs={{0,1},{2,0},{4,2},{6,4},{7,6},{5,7},{3,5},{1,3},{8,10},{10,12},{12... | collective-permute-start | bytes 1118216 | tf_op jit(solution)/shard_map/ppermute | solution.py:476
  104.9 16.1 %slice-start = ((s8[4472832]{0:T(1024)(128)(4,1)}), s8[4194304]{0:T(1024)(128)(4,1)S(1)}, s32[]{:S(2)}) async-start(s8[4472832]{0:T(1024)(128)(4,1)} %bitcast.22), calls=%async_computation | async-start | bytes 8388608
  114.1 11.8 %collective-permute-start.26 = (bf16[208,896]{1,0:T(8,128)(2,1)S(1)}, bf16[208,896]{1,0:T(8,128)(2,1)S(1)}, u32[]{:S(2)}, u32[]{:S(2)}) collective-permute-start(bf16[208,896]{1,0:T(8,128)(2,1)S(1)} %add_convert_fusion.1), channel_id=1, source_target_pairs={{0,2},{2,4},{4,6},{6,7},{7,5},{5,3},{3,1},{1,0},{8,9},{10,8},{12,1... | collective-permute-start | bytes 1118216 | tf_op jit(solution)/shard_map/ppermute | solution.py:476
  114.6 11.3 %collective-permute-start.27 = (bf16[208,896]{1,0:T(8,128)(2,1)S(1)}, bf16[208,896]{1,0:T(8,128)(2,1)S(1)}, u32[]{:S(2)}, u32[]{:S(2)}) collective-permute-start(bf16[208,896]{1,0:T(8,128)(2,1)S(1)} %add_convert_fusion), channel_id=1, source_target_pairs={{0,1},{2,0},{4,2},{6,4},{7,6},{5,7},{3,5},{1,3},{8,10},{10,12},{12... | collective-permute-start | bytes 1118216 | tf_op jit(solution)/shard_map/ppermute | solution.py:476
  116.2 4.9 %slice-start.1 = ((s8[4472832]{0:T(1024)(128)(4,1)}), s8[278528]{0:T(1024)(128)(4,1)S(1)}, s32[]{:S(2)}) async-start(s8[4472832]{0:T(1024)(128)(4,1)} %bitcast.22), calls=%async_computation.1 | async-start | bytes 557056

commit v10 on v8

--- a/solution.py
+++ b/solution.py
@@ -573,7 +573,7 @@
     taken = both_cores(came[1])
     came_up, came_down = send(first, 0), None
 
-    bounds = [0, 3, 5, -(-(width // HS) // PAIR)]
+    bounds = [0, 2, 5, -(-(width // HS) // PAIR)]
     grads = None
     for step in range(half, 1, -1):
         if step == half:

time: 120 us -> 120 us (level)
  transfers between devices with their start and end apart: 27 -> 27, of which waited for: 13 -> 13; matrix products, arithmetic and copies ran while one was open for 1% -> 1% of each run, Pallas kernels for 55% -> 54%
where the time goes in v10:
time: 120 us; the launch traced here: 119 us
  Pallas kernels  67.1 us (56%)
  waiting for transfers between devices  24.3 us (20%)
  starting transfers between devices  23.5 us (20%)
  local copies, waits for them, and re-layouts  2.61 us (2%)
    pallas_call x4, Pallas kernels, partial_products(): pl.pallas_call(functools.partial(partial_kernel, not bases, turned_round,...  22.3 us
    ppermute x14, starting transfers between devices, send(): return lax.ppermute(array, ('dp', 'fsdp'), streams[stream])  15.4 us
    pallas_call x2, Pallas kernels, grad_out_rows(): pl.pallas_call(functools.partial(grad_out_kernel, sizes, split, total), g...  14.3 us
    ppermute x14, waiting for transfers between devices, send(): return lax.ppermute(array, ('dp', 'fsdp'), streams[stream])  13.5 us
    ppermute x13, waiting for transfers between devices, swap(): return lax.ppermute(array, 'dp', [(i, i ^ bit) for i in range(members)])  10.7 us
    pallas_call x3, Pallas kernels, backward(): pl.pallas_call(backward_kernel, grid=(high - low,), in_specs=[pl.BlockSpe...  9.2 us
    ppermute x13, starting transfers between devices, swap(): return lax.ppermute(array, 'dp', [(i, i ^ bit) for i in range(members)])  8.11 us
    pallas_call x1, Pallas kernels, forward(): pl.pallas_call(forward_kernel, grid_spec=pltpu.PrefetchScalarGridSpec(num...  7.44 us
  transfers between devices with their start and end apart: 27, of which 13 were waited for; matrix products, arithmetic and copies ran while one was open for 1% of the time, Pallas kernels for 54%

profile of v10, /device:TPU:0, one launch (start us, length us, event | category | flops | bytes accessed | tf_op | source)
XLA Modules:
  0.0 119.1 jit_solution(6973722158457490065)
XLA Ops:
  0.7 1.1 own_half_of_weight.1.refs_0_
  1.8 3.1 %collective-permute-start.1 = (bf16[208,1664]{1,0:T(8,128)(2,1)S(1)}, bf16[208,1664]{1,0:T(8,128)(2,1)}, u32[]{:S(2)}, u32[]{:S(2)}) collective-permute-start(bf16[208,1664]{1,0:T(8,128)(2,1)S(1)} %own_half_of_weight.1.refs_0_), channel_id=1, source_target_pairs={{0,2},{2,4},{4,6},{6,7},{7,5},{5,3},{3,1},{1,0},{8,9},{10,8},{12,1... | collective-permute-start | bytes 2076680 | tf_op jit(solution)/shard_map/ppermute | solution.py:473
  4.9 0.7 reshape.18.layer_scale
  5.6 2.5 %peer_windows.1 = (bf16[176,1664]{1,0:T(8,128)(2,1)}, bf16[272,1664]{1,0:T(8,128)(2,1)}) custom-call(s32[1]{0:T(128)} %bitcast.7.starts, bf16[448,3200]{1,0:T(8,128)(2,1)} %cotangent.1, f32[1,3200]{1,0:T(1,128)S(1)} %reshape.18.layer_scale), custom_call_target="tpu_custom_call" | custom-call | flops 34500001792 | bytes 1000 | tf_op jit(solution)/shard_map/peer_windows/pallas_call | solution.py:59
  8.2 2.0 %collective-permute-start.3 = (bf16[176,1664]{1,0:T(8,128)(2,1)}, bf16[176,1664]{1,0:T(8,128)(2,1)}, u32[]{:S(2)}, u32[]{:S(2)}) collective-permute-start(bf16[176,1664]{1,0:T(8,128)(2,1)} %get-tuple-element.92), channel_id=1, source_target_pairs={{0,16},{8,24},{16,0},{24,8},{1,17},{9,25},{17,1},{25,9},{2,18},{10... | collective-permute-start | bytes 1757192 | tf_op jit(solution)/shard_map/ppermute | solution.py:476
  10.2 6.0 %scaled_cotangent.1.refs_2_.turned = bf16[3200,512]{1,0:T(8,128)(2,1)} custom-call(bf16[448,3200]{1,0:T(8,128)(2,1)} %cotangent.1, f32[1,3200]{1,0:T(1,128)S(1)} %reshape.18.layer_scale), custom_call_target="tpu_custom_call" | custom-call | flops 34500001792 | bytes 1000 | tf_op jit(solution)/shard_map/scaled_cotangent/pallas_call | solution.py:90
  16.2 7.4 %attention_forward.1 = (bf16[1664,448]{1,0:T(8,128)(2,1)}, f32[13,256,256]{2,1,0:T(8,128)}, f32[13,192,192]{2,1,0:T(8,128)}) custom-call(s32[4]{0:T(128)S(1)} %dynamic-slice_bitcast_fusion.counts, bf16[3,448,1664]{2,1,0:T(8,128)(2,1)S(1)} %copy-done.2), custom_call_target="tpu_custom_call" | custom-call | flops 34500001792 | bytes 1000 | tf_op jit(solution)/shard_map/attention_forward/pallas_call | solution.py:179
  23.7 0.5 collective-permute-start.4
  24.2 1.2 collective-permute-start
  25.4 1.6 %collective-permute-start.6 = (bf16[208,1664]{1,0:T(8,128)(2,1)}, bf16[208,1664]{1,0:T(8,128)(2,1)}, u32[]{:S(2)}, u32[]{:S(2)}) collective-permute-start(bf16[208,1664]{1,0:T(8,128)(2,1)} %collective-permute-done.1.refs_1_), channel_id=1, source_target_pairs={{0,2},{2,4},{4,6},{6,7},{7,5},{5,3},{3,1},{1,0},{8,9},{10,8},{12,1... | collective-permute-start | bytes 2076680 | tf_op jit(solution)/shard_map/ppermute | solution.py:473
  27.0 0.4 collective-permute-start.7
  27.5 3.1 %attended_chunks.1 = (bf16[3,208,448]{2,1,0:T(8,128)(2,1)}, bf16[2,208,448]{2,1,0:T(8,128)(2,1)}, bf16[3,208,448]{2,1,0:T(8,128)(2,1)S(1)}) custom-call(s32[8]{0:T(128)S(1)} %stack.79.order, bf16[8,208,448]{2,1,0:T(8,128)(2,1)} %bitcast.28), custom_call_target="tpu_custom_call" | custom-call | flops 1150000000 | bytes 1000 | tf_op jit(solution)/shard_map/attended_chunks/pallas_call | solution.py:117
  30.6 0.8 copy-done.6
  31.5 0.5 collective-permute-done.4.refs_1_
  32.2 7.7 %projection_chip.1 = (bf16[208,896]{1,0:T(8,128)(2,1)}, bf16[208,896]{1,0:T(8,128)(2,1)}, bf16[208,896]{1,0:T(8,128)(2,1)}, bf16[208,896]{1,0:T(8,128)(2,1)}, bf...) custom-call(s32[8]{0:T(128)S(1)} %stack.79.order, ...), custom_call_target="tpu_custom_call" | custom-call | flops 3449999872 | bytes 1000 | tf_op jit(solution)/shard_map/projection_chip/pallas_call | solution.py:422
  39.9 4.2 %collective-permute-done.6.refs_3_ = bf16[208,1664]{1,0:T(8,128)(2,1)} collective-permute-done((bf16[208,1664]{1,0:T(8,128)(2,1)}, bf16[208,1664]{1,0:T(8,128)(2,1)}, u32[]{:S(2)}, u32[]{:S(2)}) %collective-permute-start.6) | collective-permute-done | bytes 692256 | tf_op jit(solution)/shard_map/ppermute | solution.py:473
  44.1 0.6 collective-permute-start.9
  44.7 1.4 %collective-permute-start.10 = (bf16[208,1664]{1,0:T(8,128)(2,1)}, bf16[208,1664]{1,0:T(8,128)(2,1)}, u32[]{:S(2)}, u32[]{:S(2)}) collective-permute-start(bf16[208,1664]{1,0:T(8,128)(2,1)} %collective-permute-done.7.refs_4_), channel_id=1, source_target_pairs={{0,1},{2,0},{4,2},{6,4},{7,6},{5,7},{3,5},{1,3},{8,10},{10,12},{12... | collective-permute-start | bytes 2076680 | tf_op jit(solution)/shard_map/ppermute | solution.py:473
  46.1 0.5 collective-permute-done.refs_3_
  46.6 1.2 collective-permute-start.5
  47.9 0.5 collective-permute-start.13
  48.4 8.2 %grad_out_rows.2 = (f32[8,208,448]{2,1,0:T(8,128)}, bf16[8,208,448]{2,1,0:T(8,128)(2,1)}) custom-call(s32[6]{0:T(128)S(1)} %stack.82.info, bf16[3200,512]{1,0:T(8,128)(2,1)} %scaled_cotangent.1.refs_2_.turned, bf16[3200,512]{1,0:T(8,128)(2,1)S(1)} %collective-permute-done.8.refs_3_.turned_other, bf16[208,1664]{1,0:T(8,128)(2,1)} %copy-done.5, ...), custom_call_target="tpu_custom_call" | custom-call | flops 4312500224 | bytes 1000 | tf_op jit(solution)/shard_map/grad_out_rows/pallas_call | solution.py:297
  56.6 5.8 %collective-permute-done.9.refs_0_ = bf16[208,1664]{1,0:T(8,128)(2,1)} collective-permute-done((bf16[208,1664]{1,0:T(8,128)(2,1)}, bf16[208,1664]{1,0:T(8,128)(2,1)}, u32[]{:S(2)}, u32[]{:S(2)}) %collective-permute-start.9) | collective-permute-done | bytes 692256 | tf_op jit(solution)/shard_map/ppermute | solution.py:473
  62.6 1.4 %collective-permute-start.15 = (bf16[208,1664]{1,0:T(8,128)(2,1)}, bf16[208,1664]{1,0:T(8,128)(2,1)}, u32[]{:S(2)}, u32[]{:S(2)}) collective-permute-start(bf16[208,1664]{1,0:T(8,128)(2,1)} %collective-permute-done.9.refs_0_), channel_id=1, source_target_pairs={{0,2},{2,4},{4,6},{6,7},{7,5},{5,3},{3,1},{1,0},{8,9},{10,8},{12,1... | collective-permute-start | bytes 2076680 | tf_op jit(solution)/shard_map/ppermute | solution.py:473
  64.0 1.2 collective-permute-start.14
  65.3 5.1 %projection_peers.3 = (f32[208,896]{1,0:T(8,128)S(1)}, f32[208,896]{1,0:T(8,128)S(1)}, f32[208,896]{1,0:T(8,128)S(1)}) custom-call(s32[3]{0:T(128)S(1)} %pad_add_fusion.1.order, s32[1]{0:T(128)} %bitcast.3.start, bf16[3,208,448]{2,1,0:T(8,128)(2,1)} %collective-permute-done.5.refs_0_, bf16[3,208,448]{2,1,0:T(8,128)(2,1)} %collective-permute-done.11.refs_1_, ...), custom_call_target="tpu_custom_call" | custom-call | flops 1724999936 | bytes 1000 | tf_op jit(solution)/shard_map/projection_peers/pallas_call | solution.py:422
  70.4 5.8 %collective-permute-done.14.refs_0_ = bf16[2,208,448]{2,1,0:T(8,128)(2,1)} collective-permute-done((bf16[2,208,448]{2,1,0:T(8,128)(2,1)}, bf16[2,208,448]{2,1,0:T(8,128)(2,1)}, u32[]{:S(2)}, u32[]{:S(2)}) %collective-permute-start.14) | collective-permute-done | bytes 372768 | tf_op jit(solution)/shard_map/ppermute | solution.py:476
  76.3 0.5 collective-permute-start.16
  76.9 1.2 %collective-permute-start.20 = (bf16[3,208,448]{2,1,0:T(8,128)(2,1)S(1)}, bf16[3,208,448]{2,1,0:T(8,128)(2,1)}, u32[]{:S(2)}, u32[]{:S(2)}) collective-permute-start(bf16[3,208,448]{2,1,0:T(8,128)(2,1)S(1)} %copy-done.7), channel_id=1, source_target_pairs={{0,16},{8,24},{16,0},{24,8},{1,17},{9,25},{17,1},{25,9},{2,18},{10... | collective-permute-start | bytes 1677320 | tf_op jit(solution)/shard_map/ppermute | solution.py:476
  78.2 4.3 %projection_peers.4 = (f32[208,896]{1,0:T(8,128)S(1)}, f32[208,896]{1,0:T(8,128)S(1)}) custom-call(s32[2]{0:T(128)S(1)} %pad_add_fusion.2.order, s32[1]{0:T(128)} %bitcast.3.start, bf16[2,208,448]{2,1,0:T(8,128)(2,1)} %collective-permute-done.14.refs_0_, bf16[2,208,448]{2,1,0:T(8,128)(2,1)S(1)} %collective-permute-done.17.refs_1_, ...), custom_call_target="tpu_custom_call" | custom-call | flops 1724999936 | bytes 1000 | tf_op jit(solution)/shard_map/projection_peers/pallas_call | solution.py:422
  82.5 1.3 %collective-permute-done.16 = bf16[208,896]{1,0:T(8,128)(2,1)S(1)} collective-permute-done((bf16[208,896]{1,0:T(8,128)(2,1)S(1)}, bf16[208,896]{1,0:T(8,128)(2,1)S(1)}, u32[]{:S(2)}, u32[]{:S(2)}) %collective-permute-start.16) | collective-permute-done | bytes 372768 | tf_op jit(solution)/shard_map/ppermute | solution.py:473
  83.9 0.6 collective-permute-start.18
  84.5 1.5 %collective-permute-start.19 = (bf16[208,896]{1,0:T(8,128)(2,1)S(1)}, bf16[208,896]{1,0:T(8,128)(2,1)S(1)}, u32[]{:S(2)}, u32[]{:S(2)}) collective-permute-start(bf16[208,896]{1,0:T(8,128)(2,1)S(1)} %convert_element_type.39), channel_id=1, source_target_pairs={{0,1},{2,0},{4,2},{6,4},{7,6},{5,7},{3,5},{1,3},{8,10},{10,12},{12... | collective-permute-start | bytes 1118216 | tf_op jit(solution)/shard_map/ppermute | solution.py:473
  86.1 6.0 %grad_out_rows.3 = (f32[8,208,448]{2,1,0:T(8,128)}, bf16[8,208,448]{2,1,0:T(8,128)(2,1)}) custom-call(s32[4]{0:T(128)S(1)} %pad_add_fusion.3.info, bf16[3200,512]{1,0:T(8,128)(2,1)} %scaled_cotangent.1.refs_2_.turned, bf16[3200,512]{1,0:T(8,128)(2,1)S(1)} %collective-permute-done.8.refs_3_.turned_other, ...), custom_call_target="tpu_custom_call", output_to_operand_aliasing={{0}: (6, {}), {1}: (7, {})} | custom-call | flops 115000000 | bytes 1000 | tf_op jit(solution)/shard_map/grad_out_rows/pallas_call | solution.py:297
  92.1 2.2 %collective-permute-done.20.refs_0_ = bf16[3,208,448]{2,1,0:T(8,128)(2,1)} collective-permute-done((bf16[3,208,448]{2,1,0:T(8,128)(2,1)S(1)}, bf16[3,208,448]{2,1,0:T(8,128)(2,1)}, u32[]{:S(2)}, u32[]{:S(2)}) %collective-permute-start.20) | collective-permute-done | bytes 559136 | tf_op jit(solution)/shard_map/ppermute | solution.py:476
  94.3 0.9 collective-permute-done.18
  95.5 0.8 collective-permute-start.22
  96.4 1.3 %collective-permute-start.23 = (bf16[208,896]{1,0:T(8,128)(2,1)S(1)}, bf16[208,896]{1,0:T(8,128)(2,1)S(1)}, u32[]{:S(2)}, u32[]{:S(2)}) collective-permute-start(bf16[208,896]{1,0:T(8,128)(2,1)S(1)} %add_convert_fusion.2), channel_id=1, source_target_pairs={{0,1},{2,0},{4,2},{6,4},{7,6},{5,7},{3,5},{1,3},{8,10},{10,12},{12... | collective-permute-start | bytes 1118216 | tf_op jit(solution)/shard_map/ppermute | solution.py:473
  97.7 1.3 %collective-permute-done.21.refs_1_ = bf16[3,208,448]{2,1,0:T(8,128)(2,1)S(1)} collective-permute-done((bf16[3,208,448]{2,1,0:T(8,128)(2,1)}, bf16[3,208,448]{2,1,0:T(8,128)(2,1)S(1)}, u32[]{:S(2)}, u32[]{:S(2)}) %collective-permute-start.21) | collective-permute-done | bytes 559136 | tf_op jit(solution)/shard_map/ppermute | solution.py:476
  99.0 0.8 copy-done.8
  99.8 5.3 %projection_peers.5 = (f32[208,896]{1,0:T(8,128)S(1)}, f32[208,896]{1,0:T(8,128)S(1)}, f32[208,896]{1,0:T(8,128)S(1)}) custom-call(s32[3]{0:T(128)S(1)} %pad_add_fusion.order, s32[1]{0:T(128)} %bitcast.3.start, bf16[3,208,448]{2,1,0:T(8,128)(2,1)} %collective-permute-done.20.refs_0_, bf16[3,208,448]{2,1,0:T(8,128)(2,1)} %copy-done.8, ...), custom_call_target="tpu_custom_call" | custom-call | flops 1724999936 | bytes 1000 | tf_op jit(solution)/shard_map/projection_peers/pallas_call | solution.py:422
  105.1 1.3 %collective-permute-done.22 = bf16[208,896]{1,0:T(8,128)(2,1)S(1)} collective-permute-done((bf16[208,896]{1,0:T(8,128)(2,1)S(1)}, bf16[208,896]{1,0:T(8,128)(2,1)S(1)}, u32[]{:S(2)}, u32[]{:S(2)}) %collective-permute-start.22) | collective-permute-done | bytes 372768 | tf_op jit(solution)/shard_map/ppermute | solution.py:473
  106.6 0.9 collective-permute-start.24
  107.6 1.1 collective-permute-start.25
  108.7 3.5 %attention_backward.3.rest_0_ = bf16[3,448,1664]{2,1,0:T(8,128)(2,1)} custom-call(bf16[3,448,1664]{2,1,0:T(8,128)(2,1)} %qkv.7, f32[1664,448]{1,0:T(8,128)S(1)} %bitcast.19, bf16[1664,448]{1,0:T(8,128)(2,1)S(1)} %bitcast.24, f32[13,256,256]{2,1,0:T(8,128)S(1)} %copy-done.3, f32[13,192,192]{2,1,0:T(8,128)S(1)} %copy-done.4), custom_call_target="tpu_custom_call" | custom-call | flops 2300000000 | bytes 1000 | tf_op jit(solution)/shard_map/attention_backward/pallas_call | solution.py:229
  112.2 3.3 %attention_backward.4.rest_0_ = bf16[3,448,1664]{2,1,0:T(8,128)(2,1)} custom-call(bf16[3,448,1664]{2,1,0:T(8,128)(2,1)S(1)} %bitcast.23, f32[1664,448]{1,0:T(8,128)S(1)} %bitcast.20, bf16[1664,448]{1,0:T(8,128)(2,1)S(1)} %bitcast.25, f32[13,256,256]{2,1,0:T(8,128)S(1)} %copy-done.3, f32[13,192,192]{2,1,0:T(8,128)S(1)} %copy-done.4, ...), custom_call_target="tpu_custom_call", output_to_operand_aliasing={{}: (5, {})} | custom-call | flops 3449999872 | bytes 1000 | tf_op jit(solution)/shard_map/attention_backward/pallas_call | solution.py:229
  115.6 2.4 %attention_backward.5 = bf16[3,448,1664]{2,1,0:T(8,128)(2,1)} custom-call(bf16[3,448,1664]{2,1,0:T(8,128)(2,1)S(1)} %bitcast.23, f32[1664,448]{1,0:T(8,128)S(1)} %bitcast.21, bf16[1664,448]{1,0:T(8,128)(2,1)S(1)} %bitcast.26, f32[13,256,256]{2,1,0:T(8,128)S(1)} %copy-done.3, f32[13,192,192]{2,1,0:T(8,128)S(1)} %copy-done.4, ...), custom_call_target="tpu_custom_call", output_to_operand_aliasing={{}: (5, {})} | custom-call | flops 2300000000 | bytes 1000 | tf_op jit(solution)/shard_map/attention_backward/pallas_call | solution.py:229
  118.0 1.1 last_sum.1
  (59 shorter events, 1.9 us)
Async XLA Ops:
  0.6 15.6 %copy-start = (s32[4,1,4]{2,1,0:T(1,128)S(1)}, s32[4,1,4]{2,1,0:T(1,128)}, u32[]{:S(2)}) copy-start(s32[4,1,4]{2,1,0:T(1,128)} %param.9) | copy-start | bytes 196
  1.8 6.4 %copy-start.5 = (bf16[208,1664]{1,0:T(8,128)(2,1)}, bf16[208,1664]{1,0:T(8,128)(2,1)S(1)}, u32[]{:S(2)}) copy-start(bf16[208,1664]{1,0:T(8,128)(2,1)S(1)} %own_half_of_weight.1.refs_0_) | copy-start | bytes 2076676
  1.8 21.9 %collective-permute-start.1 = (bf16[208,1664]{1,0:T(8,128)(2,1)S(1)}, bf16[208,1664]{1,0:T(8,128)(2,1)}, u32[]{:S(2)}, u32[]{:S(2)}) collective-permute-start(bf16[208,1664]{1,0:T(8,128)(2,1)S(1)} %own_half_of_weight.1.refs_0_), channel_id=1, source_target_pairs={{0,2},{2,4},{4,6},{6,7},{7,5},{5,3},{3,1},{1,0},{8,9},{10,8},{12,1... | collective-permute-start | bytes 2076680 | tf_op jit(solution)/shard_map/ppermute | solution.py:473
  4.9 18.8 %collective-permute-start.2 = (bf16[208,1664]{1,0:T(8,128)(2,1)S(1)}, bf16[208,1664]{1,0:T(8,128)(2,1)}, u32[]{:S(2)}, u32[]{:S(2)}) collective-permute-start(bf16[208,1664]{1,0:T(8,128)(2,1)S(1)} %own_half_of_weight.1.refs_0_), channel_id=1, source_target_pairs={{0,1},{2,0},{4,2},{6,4},{7,6},{5,7},{3,5},{1,3},{8,10},{10,12},{12... | collective-permute-start | bytes 2076680 | tf_op jit(solution)/shard_map/ppermute | solution.py:473
  8.2 15.5 %collective-permute-start.3 = (bf16[176,1664]{1,0:T(8,128)(2,1)}, bf16[176,1664]{1,0:T(8,128)(2,1)}, u32[]{:S(2)}, u32[]{:S(2)}) collective-permute-start(bf16[176,1664]{1,0:T(8,128)(2,1)} %get-tuple-element.92), channel_id=1, source_target_pairs={{0,16},{8,24},{16,0},{24,8},{1,17},{9,25},{17,1},{25,9},{2,18},{10... | collective-permute-start | bytes 1757192 | tf_op jit(solution)/shard_map/ppermute | solution.py:476
  10.2 6.0 %copy-start.2 = (bf16[3,448,1664]{2,1,0:T(8,128)(2,1)S(1)}, bf16[3,448,1664]{2,1,0:T(8,128)(2,1)}, u32[]{:S(2)}) copy-start(bf16[3,448,1664]{2,1,0:T(8,128)(2,1)} %qkv.7) | copy-start | bytes 13418500
  23.7 8.6 %collective-permute-start.8 = (bf16[3200,512]{1,0:T(8,128)(2,1)}, bf16[3200,512]{1,0:T(8,128)(2,1)S(1)}, u32[]{:S(2)}, u32[]{:S(2)}) collective-permute-start(bf16[3200,512]{1,0:T(8,128)(2,1)} %scaled_cotangent.1.refs_2_.turned), channel_id=1, source_target_pairs={{0,8},{8,0},{16,24},{24,16},{1,9},{9,1},{17,25},{25,17},{2,10},{10... | collective-permute-start | bytes 9830408 | tf_op jit(solution)/shard_map/ppermute | solution.py:476
  23.7 8.2 %collective-permute-start.4 = (bf16[8,208,448]{2,1,0:T(8,128)(2,1)}, bf16[8,208,448]{2,1,0:T(8,128)(2,1)}, u32[]{:S(2)}, u32[]{:S(2)}) collective-permute-start(bf16[8,208,448]{2,1,0:T(8,128)(2,1)} %bitcast.27), channel_id=1, source_target_pairs={{0,8},{8,0},{16,24},{24,16},{1,9},{9,1},{17,25},{25,17},{2,10},{10... | collective-permute-start | bytes 4472840 | tf_op jit(solution)/shard_map/ppermute | solution.py:476
  24.2 22.4 %collective-permute-start = (bf16[272,1664]{1,0:T(8,128)(2,1)}, bf16[272,1664]{1,0:T(8,128)(2,1)}, u32[]{:S(2)}, u32[]{:S(2)}) collective-permute-start(bf16[272,1664]{1,0:T(8,128)(2,1)} %get-tuple-element.90), channel_id=1, source_target_pairs={{0,16},{8,24},{16,0},{24,8},{1,17},{9,25},{17,1},{25,9},{2,18},{10... | collective-permute-start | bytes 2715656 | tf_op jit(solution)/shard_map/ppermute | solution.py:476
  25.4 18.6 %collective-permute-start.6 = (bf16[208,1664]{1,0:T(8,128)(2,1)}, bf16[208,1664]{1,0:T(8,128)(2,1)}, u32[]{:S(2)}, u32[]{:S(2)}) collective-permute-start(bf16[208,1664]{1,0:T(8,128)(2,1)} %collective-permute-done.1.refs_1_), channel_id=1, source_target_pairs={{0,2},{2,4},{4,6},{6,7},{7,5},{5,3},{3,1},{1,0},{8,9},{10,8},{12,1... | collective-permute-start | bytes 2076680 | tf_op jit(solution)/shard_map/ppermute | solution.py:473
  27.0 17.1 %collective-permute-start.7 = (bf16[208,1664]{1,0:T(8,128)(2,1)}, bf16[208,1664]{1,0:T(8,128)(2,1)}, u32[]{:S(2)}, u32[]{:S(2)}) collective-permute-start(bf16[208,1664]{1,0:T(8,128)(2,1)} %collective-permute-done.2.refs_2_), channel_id=1, source_target_pairs={{0,1},{2,0},{4,2},{6,4},{7,6},{5,7},{3,5},{1,3},{8,10},{10,12},{12... | collective-permute-start | bytes 2076680 | tf_op jit(solution)/shard_map/ppermute | solution.py:473
  30.6 0.8 copy-start.6
  44.1 18.3 %collective-permute-start.9 = (bf16[208,1664]{1,0:T(8,128)(2,1)}, bf16[208,1664]{1,0:T(8,128)(2,1)}, u32[]{:S(2)}, u32[]{:S(2)}) collective-permute-start(bf16[208,1664]{1,0:T(8,128)(2,1)} %collective-permute-done.6.refs_3_), channel_id=1, source_target_pairs={{0,2},{2,4},{4,6},{6,7},{7,5},{5,3},{3,1},{1,0},{8,9},{10,8},{12,1... | collective-permute-start | bytes 2076680 | tf_op jit(solution)/shard_map/ppermute | solution.py:473
  44.7 17.7 %collective-permute-start.10 = (bf16[208,1664]{1,0:T(8,128)(2,1)}, bf16[208,1664]{1,0:T(8,128)(2,1)}, u32[]{:S(2)}, u32[]{:S(2)}) collective-permute-start(bf16[208,1664]{1,0:T(8,128)(2,1)} %collective-permute-done.7.refs_4_), channel_id=1, source_target_pairs={{0,1},{2,0},{4,2},{6,4},{7,6},{5,7},{3,5},{1,3},{8,10},{10,12},{12... | collective-permute-start | bytes 2076680 | tf_op jit(solution)/shard_map/ppermute | solution.py:473
  46.6 15.8 %collective-permute-start.5 = (bf16[3,208,448]{2,1,0:T(8,128)(2,1)}, bf16[3,208,448]{2,1,0:T(8,128)(2,1)}, u32[]{:S(2)}, u32[]{:S(2)}) collective-permute-start(bf16[3,208,448]{2,1,0:T(8,128)(2,1)} %get-tuple-element.101), channel_id=1, source_target_pairs={{0,16},{8,24},{16,0},{24,8},{1,17},{9,25},{17,1},{25,9},{2,18},{10... | collective-permute-start | bytes 1677320 | tf_op jit(solution)/shard_map/ppermute | solution.py:476
  47.9 17.4 %collective-permute-start.12 = (bf16[176,1664]{1,0:T(8,128)(2,1)}, bf16[176,1664]{1,0:T(8,128)(2,1)}, u32[]{:S(2)}, u32[]{:S(2)}) collective-permute-start(bf16[176,1664]{1,0:T(8,128)(2,1)} %collective-permute-done.3.refs_2_), channel_id=1, source_target_pairs={{0,8},{8,0},{16,24},{24,16},{1,9},{9,1},{17,25},{25,17},{2,10},{10... | collective-permute-start | bytes 1757192 | tf_op jit(solution)/shard_map/ppermute | solution.py:476
  47.9 17.4 %collective-permute-start.13 = (bf16[272,1664]{1,0:T(8,128)(2,1)}, bf16[272,1664]{1,0:T(8,128)(2,1)}, u32[]{:S(2)}, u32[]{:S(2)}) collective-permute-start(bf16[272,1664]{1,0:T(8,128)(2,1)} %collective-permute-done.refs_3_), channel_id=1, source_target_pairs={{0,8},{8,0},{16,24},{24,16},{1,9},{9,1},{17,25},{25,17},{2,10},{10... | collective-permute-start | bytes 2715656 | tf_op jit(solution)/shard_map/ppermute | solution.py:476
  62.5 2.8 %collective-permute-start.11 = (bf16[3,208,448]{2,1,0:T(8,128)(2,1)}, bf16[3,208,448]{2,1,0:T(8,128)(2,1)}, u32[]{:S(2)}, u32[]{:S(2)}) collective-permute-start(bf16[3,208,448]{2,1,0:T(8,128)(2,1)} %collective-permute-done.5.refs_0_), channel_id=1, source_target_pairs={{0,8},{8,0},{16,24},{24,16},{1,9},{9,1},{17,25},{25,17},{2,10},{10... | collective-permute-start | bytes 1677320 | tf_op jit(solution)/shard_map/ppermute | solution.py:476
  62.6 13.6 %collective-permute-start.15 = (bf16[208,1664]{1,0:T(8,128)(2,1)}, bf16[208,1664]{1,0:T(8,128)(2,1)}, u32[]{:S(2)}, u32[]{:S(2)}) collective-permute-start(bf16[208,1664]{1,0:T(8,128)(2,1)} %collective-permute-done.9.refs_0_), channel_id=1, source_target_pairs={{0,2},{2,4},{4,6},{6,7},{7,5},{5,3},{3,1},{1,0},{8,9},{10,8},{12,1... | collective-permute-start | bytes 2076680 | tf_op jit(solution)/shard_map/ppermute | solution.py:473
  64.0 12.2 %collective-permute-start.14 = (bf16[2,208,448]{2,1,0:T(8,128)(2,1)}, bf16[2,208,448]{2,1,0:T(8,128)(2,1)}, u32[]{:S(2)}, u32[]{:S(2)}) collective-permute-start(bf16[2,208,448]{2,1,0:T(8,128)(2,1)} %get-tuple-element.129), channel_id=1, source_target_pairs={{0,16},{8,24},{16,0},{24,8},{1,17},{9,25},{17,1},{25,9},{2,18},{10... | collective-permute-start | bytes 1118216 | tf_op jit(solution)/shard_map/ppermute | solution.py:476
  65.3 11.6 %copy-start.7 = (bf16[3,208,448]{2,1,0:T(8,128)(2,1)S(1)}, bf16[3,208,448]{2,1,0:T(8,128)(2,1)}, u32[]{:S(2)}) copy-start(bf16[3,208,448]{2,1,0:T(8,128)(2,1)} %copy-done.6) | copy-start | bytes 1677316
  76.3 2.0 %collective-permute-start.17 = (bf16[2,208,448]{2,1,0:T(8,128)(2,1)}, bf16[2,208,448]{2,1,0:T(8,128)(2,1)S(1)}, u32[]{:S(2)}, u32[]{:S(2)}) collective-permute-start(bf16[2,208,448]{2,1,0:T(8,128)(2,1)} %collective-permute-done.14.refs_0_), channel_id=1, source_target_pairs={{0,8},{8,0},{16,24},{24,16},{1,9},{9,1},{17,25},{25,17},{2,10},{10... | collective-permute-start | bytes 1118216 | tf_op jit(solution)/shard_map/ppermute | solution.py:476
  76.3 7.6 %collective-permute-start.16 = (bf16[208,896]{1,0:T(8,128)(2,1)S(1)}, bf16[208,896]{1,0:T(8,128)(2,1)S(1)}, u32[]{:S(2)}, u32[]{:S(2)}) collective-permute-start(bf16[208,896]{1,0:T(8,128)(2,1)S(1)} %convert_element_type.36), channel_id=1, source_target_pairs={{0,2},{2,4},{4,6},{6,7},{7,5},{5,3},{3,1},{1,0},{8,9},{10,8},{12,1... | collective-permute-start | bytes 1118216 | tf_op jit(solution)/shard_map/ppermute | solution.py:473
  76.9 17.4 %collective-permute-start.20 = (bf16[3,208,448]{2,1,0:T(8,128)(2,1)S(1)}, bf16[3,208,448]{2,1,0:T(8,128)(2,1)}, u32[]{:S(2)}, u32[]{:S(2)}) collective-permute-start(bf16[3,208,448]{2,1,0:T(8,128)(2,1)S(1)} %copy-done.7), channel_id=1, source_target_pairs={{0,16},{8,24},{16,0},{24,8},{1,17},{9,25},{17,1},{25,9},{2,18},{10... | collective-permute-start | bytes 1677320 | tf_op jit(solution)/shard_map/ppermute | solution.py:476
  83.9 11.3 %collective-permute-start.18 = (bf16[208,896]{1,0:T(8,128)(2,1)S(1)}, bf16[208,896]{1,0:T(8,128)(2,1)S(1)}, u32[]{:S(2)}, u32[]{:S(2)}) collective-permute-start(bf16[208,896]{1,0:T(8,128)(2,1)S(1)} %add_convert_fusion.4), channel_id=1, source_target_pairs={{0,2},{2,4},{4,6},{6,7},{7,5},{5,3},{3,1},{1,0},{8,9},{10,8},{12,1... | collective-permute-start | bytes 1118216 | tf_op jit(solution)/shard_map/ppermute | solution.py:473
  84.5 10.8 %collective-permute-start.19 = (bf16[208,896]{1,0:T(8,128)(2,1)S(1)}, bf16[208,896]{1,0:T(8,128)(2,1)S(1)}, u32[]{:S(2)}, u32[]{:S(2)}) collective-permute-start(bf16[208,896]{1,0:T(8,128)(2,1)S(1)} %convert_element_type.39), channel_id=1, source_target_pairs={{0,1},{2,0},{4,2},{6,4},{7,6},{5,7},{3,5},{1,3},{8,10},{10,12},{12... | collective-permute-start | bytes 1118216 | tf_op jit(solution)/shard_map/ppermute | solution.py:473
  94.3 14.4 %collective-permute-start.26 = (bf16[8,208,448]{2,1,0:T(8,128)(2,1)}, bf16[8,208,448]{2,1,0:T(8,128)(2,1)S(1)}, u32[]{:S(2)}, u32[]{:S(2)}) collective-permute-start(bf16[8,208,448]{2,1,0:T(8,128)(2,1)} %get-tuple-element.165), channel_id=1, source_target_pairs={{0,8},{8,0},{16,24},{24,16},{1,9},{9,1},{17,25},{25,17},{2,10},{10... | collective-permute-start | bytes 4472840 | tf_op jit(solution)/shard_map/ppermute | solution.py:476
  95.4 3.6 %collective-permute-start.21 = (bf16[3,208,448]{2,1,0:T(8,128)(2,1)}, bf16[3,208,448]{2,1,0:T(8,128)(2,1)S(1)}, u32[]{:S(2)}, u32[]{:S(2)}) collective-permute-start(bf16[3,208,448]{2,1,0:T(8,128)(2,1)} %collective-permute-done.20.refs_0_), channel_id=1, source_target_pairs={{0,8},{8,0},{16,24},{24,16},{1,9},{9,1},{17,25},{25,17},{2,10},{10... | collective-permute-start | bytes 1677320 | tf_op jit(solution)/shard_map/ppermute | solution.py:476
  95.5 10.9 %collective-permute-start.22 = (bf16[208,896]{1,0:T(8,128)(2,1)S(1)}, bf16[208,896]{1,0:T(8,128)(2,1)S(1)}, u32[]{:S(2)}, u32[]{:S(2)}) collective-permute-start(bf16[208,896]{1,0:T(8,128)(2,1)S(1)} %add_convert_fusion.3), channel_id=1, source_target_pairs={{0,2},{2,4},{4,6},{6,7},{7,5},{5,3},{3,1},{1,0},{8,9},{10,8},{12,1... | collective-permute-start | bytes 1118216 | tf_op jit(solution)/shard_map/ppermute | solution.py:473
  96.4 12.3 %copy-start.1 = (f32[8,208,448]{2,1,0:T(8,128)S(1)}, f32[8,208,448]{2,1,0:T(8,128)}, u32[]{:S(2)}) copy-start(f32[8,208,448]{2,1,0:T(8,128)} %get-tuple-element.153) | copy-start | bytes 8945668
  96.4 12.3 %copy-start.3 = (f32[13,256,256]{2,1,0:T(8,128)S(1)}, f32[13,256,256]{2,1,0:T(8,128)}, u32[]{:S(2)}) copy-start(f32[13,256,256]{2,1,0:T(8,128)} %get-tuple-element.166.main_probs) | copy-start | bytes 10223620
  96.4 12.3 %copy-start.4 = (f32[13,192,192]{2,1,0:T(8,128)S(1)}, f32[13,192,192]{2,1,0:T(8,128)}, u32[]{:S(2)}) copy-start(f32[13,192,192]{2,1,0:T(8,128)} %get-tuple-element.167.slot_probs) | copy-start | bytes 5750788
  96.4 10.2 %collective-permute-start.23 = (bf16[208,896]{1,0:T(8,128)(2,1)S(1)}, bf16[208,896]{1,0:T(8,128)(2,1)S(1)}, u32[]{:S(2)}, u32[]{:S(2)}) collective-permute-start(bf16[208,896]{1,0:T(8,128)(2,1)S(1)} %add_convert_fusion.2), channel_id=1, source_target_pairs={{0,1},{2,0},{4,2},{6,4},{7,6},{5,7},{3,5},{1,3},{8,10},{10,12},{12... | collective-permute-start | bytes 1118216 | tf_op jit(solution)/shard_map/ppermute | solution.py:473
  99.0 0.8 copy-start.8
  99.8 12.4 %slice-start = ((s8[4472832]{0:T(1024)(128)(4,1)}), s8[4194304]{0:T(1024)(128)(4,1)S(1)}, s32[]{:S(2)}) async-start(s8[4472832]{0:T(1024)(128)(4,1)} %bitcast.22), calls=%async_computation | async-start | bytes 8388608
  106.6 11.3 %collective-permute-start.24 = (bf16[208,896]{1,0:T(8,128)(2,1)S(1)}, bf16[208,896]{1,0:T(8,128)(2,1)S(1)}, u32[]{:S(2)}, u32[]{:S(2)}) collective-permute-start(bf16[208,896]{1,0:T(8,128)(2,1)S(1)} %add_convert_fusion.1), channel_id=1, source_target_pairs={{0,2},{2,4},{4,6},{6,7},{7,5},{5,3},{3,1},{1,0},{8,9},{10,8},{12,1... | collective-permute-start | bytes 1118216 | tf_op jit(solution)/shard_map/ppermute | solution.py:473
  107.6 10.4 %collective-permute-start.25 = (bf16[208,896]{1,0:T(8,128)(2,1)S(1)}, bf16[208,896]{1,0:T(8,128)(2,1)S(1)}, u32[]{:S(2)}, u32[]{:S(2)}) collective-permute-start(bf16[208,896]{1,0:T(8,128)(2,1)S(1)} %add_convert_fusion), channel_id=1, source_target_pairs={{0,1},{2,0},{4,2},{6,4},{7,6},{5,7},{3,5},{1,3},{8,10},{10,12},{12... | collective-permute-start | bytes 1118216 | tf_op jit(solution)/shard_map/ppermute | solution.py:473
  108.7 3.5 %slice-start.1 = ((s8[4472832]{0:T(1024)(128)(4,1)}), s8[278528]{0:T(1024)(128)(4,1)S(1)}, s32[]{:S(2)}) async-start(s8[4472832]{0:T(1024)(128)(4,1)} %bitcast.22), calls=%async_computation.1 | async-start | bytes 557056
